TPU v7x, 32 devices: a whole 2x2x4 slice. The times are simulated.
32 devices in a mesh: gx: 4 (over y, core), gy: 8 (over z, x).
Axes of the slice: x: 2, y: 2, z: 4, core: 2. Of those that a mesh axis runs over, the one named last changes fastest.
Arguments:
- coefficients: float32 [13, 56, 8192], P(None, None, ('gx', 'gy')), may hold values from -6 to 6
- jacobian: float32 [3, 3, 8192], P(None, None, ('gx', 'gy')), may hold values from -1 to 1
- face_normals: float32 [4, 3, 8192], P(None, None, ('gx', 'gy')), may hold values from -3 to 3
- wave_speed: float32 [8192], P(('gx', 'gy')), may hold values from 0.3 to 1.5
- star_mats: float32 [3, 13, 13], replicated, may hold values from -1.75 to 1.75
- deriv_mats: float32 [3, 56, 56], replicated, may hold values from -0.75 to 0.75
- stiff_mats: float32 [3, 56, 56], replicated, may hold values from -0.75 to 0.75
- source_mat: float32 [13, 13], replicated, may hold values from -4 to 4
- trace_mats: float32 [4, 21, 56], replicated, may hold values from -0.75 to 0.75
- lift_mats: float32 [4, 56, 21], replicated, may hold values from -1.25 to 1.25
- face_partner: int32 [4, 8192], P(None, ('gx', 'gy')), may hold values from -1 to 1535, as said below
- send_faces: int32 [8, 2048], P(None, ('gx', 'gy')), may hold values from 0 to 1023, as said below
- sea_face: int32 [8192], P(('gx', 'gy')), may hold values from 0 to 1023
- sea_row: int32 [8192, 1], P(('gx', 'gy')), may hold values from 0 to 7; in each aligned block of 256 rows (0 to 255, 256 to 511, ...) at most 64 rows name the same one
- sea_base: int32 [8192, 2], P(('gx', 'gy')), may hold values from 0 to 252
- interp_mat: float32 [16, 21], replicated, may hold values from -1.25 to 1.25
- water_depth: float32 [1024, 2048], P('gx', 'gy'), may hold values from 0.6 to 1.4
- momentum: float32 [2, 1024, 2048], P(None, 'gx', 'gy'), may hold values from -0.5 to 0.5
- bottom: float32 [1024, 2048], P('gx', 'gy'), may hold values from -0.3 to 0.3
Outputs:
- solid_final: float32 [13, 56, 8192], P(None, None, ('gx', 'gy'))
- ocean_final: float32 [3, 1024, 2048], P(None, 'gx', 'gy')
- bed_final: float32 [1024, 2048], P('gx', 'gy')
Inputs may be any that keep to these rules, and one draw needn't show every extreme that they name: `face_partner`: for each face of a device's elements: -1 on the domain's outer boundary, a code below 1024 naming a face of the same device, or 1024 + k * 64 + s for the face paired with the neighbouring device at offset k in slot s. Pairings are symmetric; a device shares exactly 64 faces with each neighbour that exists on the device grid. `send_faces`: entry (k, s) of a device is the code f * 256 + e of its face paired in slot s with the neighbouring device at offset k; the 512 codes of a device are distinct. `sea_row`: among the rows of one device no tile row is named more than 64 times.
All inputs are finite; a program needn't handle non-finite values.
Results may differ from a plain program's by a relative error of at most 0.0001.
Values sent between devices are 32-bit elements; how exact they have to be, the bound alone decides.
No kernel may reach another device: no remote copies, remote signals or barrier semaphores. Data moves between devices by JAX's collectives and lax.ppermute only.
A program may use at most 64 MiB of HBM per device.

v0:
```python
import functools

import jax
import jax.numpy as jnp
from jax import lax
from jax.experimental import pallas as pl
from jax.experimental.pallas import tpu as pltpu
from jax.sharding import PartitionSpec as P

FIELDS = 13
FACE_BASIS = 21
FACE_PAD = 24
POINTS = 16
ORD = 3
STEPS_OCEAN = 2
CAP = 64
TABLE = FIELDS * FACE_PAD
HALF = 160
WIDE = 2 * HALF
OCEAN_ROWS = 16
MARGIN = 16

step_solid = 0.4
step_ocean = 0.2
depth_floor = 0.5
vertical_field = 6
patch_side = 4

F32 = jnp.float32
BF16 = jnp.bfloat16
NT = (((1,), (1,)), ((), ()))
VMEM_LIMIT = 48 * 1024 * 1024


def iota(shape, dim):
    return lax.broadcasted_iota(jnp.int32, shape, dim)


def dot(a, b):
    return jnp.dot(a, b, preferred_element_type=F32)


def exact_dot(a, b):
    return jnp.dot(a, b, preferred_element_type=F32, precision=lax.Precision.HIGHEST)


def parts(x):
    high = x.astype(BF16)
    low = (x - high.astype(F32)).astype(BF16)
    return high, low


def both_parts(x):
    high = x.astype(BF16).astype(F32)
    return jnp.concatenate([high, x - high], axis=0).astype(BF16)


def folded(y):
    half = y.shape[0] // 2
    return y[:half] + y[half:]


def weights(w):
    return both_parts(w), w.astype(BF16)


def weighted(stack, high, x):
    x_high, x_low = parts(x)
    return folded(dot(stack, x_high)) + dot(high, x_low)


def selector(rows, columns, shift):
    return (iota((rows, columns), 1) == iota((rows, columns), 0) + shift).astype(F32)


def star_weights(mats):
    size = FIELDS * 8
    spread = ((iota((FIELDS, 2 * size), 1) % size) // 8 == iota((FIELDS, 2 * size), 0)).astype(F32)
    diagonal = iota((size, 2 * size), 0) % 8 == iota((size, 2 * size), 1) % 8
    first = iota((size, 2 * size), 1) < size
    high, low = [], []
    for mat in mats:
        wide = exact_dot(mat, spread)
        tall = jnp.concatenate(
            [jnp.broadcast_to(wide[g : g + 1], (8, 2 * size)) for g in range(FIELDS)], axis=0
        )
        tall = jnp.where(diagonal, tall, 0.0)
        top = tall.astype(BF16).astype(F32)
        high.append(top)
        low.append(jnp.where(first, tall - top, 0.0))
    return jnp.concatenate(high + low, axis=0).astype(BF16)


def side_by_side(mats):
    rows, columns = mats[0].shape
    total = len(mats) * columns
    return sum(exact_dot(m, selector(columns, total, i * columns)) for i, m in enumerate(mats))


def stacked_traces(trace_ref):
    basis = trace_ref.shape[2]
    place = (
        iota((FACE_PAD, FACE_BASIS), 0) == iota((FACE_PAD, FACE_BASIS), 1)
    ).astype(F32)
    return jnp.concatenate([exact_dot(place, trace_ref[f]) for f in range(4)], axis=0)


def spread_out(source, jac_ref, star, target, extra=None):
    basis = target.shape[1] // 3
    size = FIELDS * 8
    for j in range(basis // 8):
        x = jnp.concatenate(
            [source[g * basis + 8 * j : g * basis + 8 * j + 8, :] for g in range(FIELDS)], axis=0
        )
        y = folded(dot(star, both_parts(x)))
        for d in range(3):
            z = sum(jac_ref[d, c : c + 1, :] * y[c * size : (c + 1) * size] for c in range(3))
            for g in range(FIELDS):
                target[g, d * basis + 8 * j : d * basis + 8 * j + 8, :] = z[8 * g : 8 * g + 8]
        if extra is not None:
            for g in range(FIELDS):
                extra[g * basis + 8 * j : g * basis + 8 * j + 8, :] = y[
                    3 * size + 8 * g : 3 * size + 8 * g + 8
                ]


def derivative(source, target, jac_ref, star, basis_weights, spread_ref, relaxed_ref):
    basis = spread_ref.shape[1] // 3
    spread_out(source, jac_ref, star, spread_ref, relaxed_ref)
    for g in range(FIELDS):
        rows = slice(g * basis, (g + 1) * basis)
        target[rows, :] = -(weighted(*basis_weights, spread_ref[g]) + relaxed_ref[rows, :])


def unequal(place):
    a1 = jnp.where(place[0] % 2 == 0, 1, -1)
    c1 = jnp.where(place[1] % 2 == 0, 1, -1)
    return a1, c1


def column_block(a):
    return jnp.where(a > 0, 6, 1)


def row_block(c):
    return jnp.where(c > 0, 4, 3)


def front(
    place, q_ref, jac_ref, star_ref, source_ref, deriv_ref, trace_ref, send_ref,
    integral_ref, table_ref, p1_ref, p2_ref, q1_ref, q2_ref, spread_ref, relaxed_ref, d1_ref, d2_ref,
):
    basis = deriv_ref.shape[1]
    elements = q_ref.shape[1]
    star = star_weights([star_ref[0], star_ref[1], star_ref[2], source_ref[...]])
    basis_weights = weights(side_by_side([deriv_ref[d] for d in range(3)]))
    derivative(q_ref, d1_ref, jac_ref, star, basis_weights, spread_ref, relaxed_ref)
    derivative(d1_ref, d2_ref, jac_ref, star, basis_weights, spread_ref, relaxed_ref)
    first = step_solid
    second = first * step_solid / 2
    third = second * step_solid / 3
    trace = weights(stacked_traces(trace_ref))
    for g in range(FIELDS):
        rows = slice(g * basis, (g + 1) * basis)
        whole = first * q_ref[rows, :] + second * d1_ref[rows, :] + third * d2_ref[rows, :]
        integral_ref[rows, :] = whole
        faces = weighted(*trace, whole)
        for f in range(4):
            table_ref[g * FACE_PAD : (g + 1) * FACE_PAD, f * elements : (f + 1) * elements] = faces[
                f * FACE_PAD : (f + 1) * FACE_PAD
            ]
    a1, c1 = unequal(place)
    picks = [
        (p1_ref, 0, column_block(a1)),
        (p2_ref, 0, column_block(-a1)),
        (p1_ref, HALF, column_block(a1) + c1),
        (p1_ref, 2 * HALF, column_block(a1) - c1),
        (p2_ref, HALF, column_block(-a1) + c1),
        (p2_ref, 2 * HALF, column_block(-a1) - c1),
        (q1_ref, 0, row_block(c1)),
        (q2_ref, 0, row_block(-c1)),
    ]
    stack = table_parts(table_ref)
    left = iota((HALF, 2 * CAP), 1) < CAP
    codes = iota((4 * elements, 2 * CAP), 0)
    for n in range(0, 8, 2):
        wanted = jnp.concatenate(
            [send_ref[pl.ds(picks[n][2], 1), :], send_ref[pl.ds(picks[n + 1][2], 1), :]], axis=1
        )
        got = folded(dot(stack, (codes == wanted).astype(F32).astype(BF16)))
        low, high = got[:HALF], got[HALF:]
        ref, at, _ = picks[n]
        ref[at : at + HALF, :] = jnp.where(left, low, pltpu.roll(high, CAP, 1))
        ref, at, _ = picks[n + 1]
        ref[at : at + HALF, :] = jnp.where(left, pltpu.roll(low, CAP, 1), high)


def table_parts(table_ref):
    pad = jnp.zeros((WIDE - TABLE, table_ref.shape[1]), BF16)
    high, low = parts(table_ref[...])
    both = [high.astype(F32), pad.astype(F32), low.astype(F32), pad.astype(F32)]
    return jnp.concatenate(both, axis=0).astype(BF16)


def middle(
    q_ref, jac_ref, star_ref, stiff_ref, integral_ref, table_ref, partner_ref,
    base_ref, outer_ref, spread_ref,
):
    basis = stiff_ref.shape[1]
    elements = q_ref.shape[1]
    star = star_weights([star_ref[0], star_ref[1], star_ref[2]])
    basis_weights = weights(side_by_side([stiff_ref[d] for d in range(3)]))
    spread_out(integral_ref, jac_ref, star, spread_ref)
    for g in range(FIELDS):
        rows = slice(g * basis, (g + 1) * basis)
        base_ref[rows, :] = q_ref[rows, :] + weighted(*basis_weights, spread_ref[g])
    stack = table_parts(table_ref)
    codes = iota((4 * elements, elements), 0)
    for f in range(4):
        hot = (codes == partner_ref[f : f + 1, :]).astype(F32).astype(BF16)
        outer_ref[:, f * elements : (f + 1) * elements] = folded(dot(stack, hot))[:TABLE]


def back(
    place, base_ref, table_ref, outer_ref, partner_ref, normal_ref, speed_ref, star_ref, lift_ref,
    p1_ref, p2_ref, q1_ref, q2_ref, state_ref, flux_ref,
):
    basis = lift_ref.shape[1]
    elements = base_ref.shape[1]
    a1, c1 = unequal(place)
    blocks = [
        (p1_ref, 0, column_block(a1)),
        (p2_ref, 0, column_block(-a1)),
        (q1_ref, 0, row_block(c1)),
        (q1_ref, HALF, column_block(a1) + c1),
        (q1_ref, 2 * HALF, column_block(-a1) + c1),
        (q2_ref, 0, row_block(-c1)),
        (q2_ref, HALF, column_block(a1) - c1),
        (q2_ref, 2 * HALF, column_block(-a1) - c1),
    ]
    left = iota((HALF, 2 * CAP), 1) < CAP
    tops, bottoms = [], []
    for n in range(0, 8, 2):
        one = blocks[n][0][blocks[n][1] : blocks[n][1] + HALF, :]
        two = blocks[n + 1][0][blocks[n + 1][1] : blocks[n + 1][1] + HALF, :]
        tops.append(jnp.where(left, one, pltpu.roll(two, CAP, 1)))
        bottoms.append(jnp.where(left, pltpu.roll(one, CAP, 1), two))
    remote = jnp.concatenate(
        [jnp.concatenate(tops, axis=1), jnp.concatenate(bottoms, axis=1)], axis=0
    )
    remote = both_parts(remote)
    slot = iota((CAP, elements), 0)
    for f in range(4):
        wanted = partner_ref[f : f + 1, :] - 4 * elements
        hot = jnp.concatenate(
            [(slot + CAP * block[2] == wanted).astype(F32) for block in blocks], axis=0
        ).astype(BF16)
        columns = slice(f * elements, (f + 1) * elements)
        outer_ref[:, columns] += folded(dot(remote, hot))[:TABLE]
    star = star_weights([star_ref[0], star_ref[1], star_ref[2]])
    size = FIELDS * 8
    for part in range(FACE_PAD // 8):
        at = [slice(g * FACE_PAD + 8 * part, g * FACE_PAD + 8 * part + 8) for g in range(FIELDS)]
        for f in range(4):
            columns = slice(f * elements, (f + 1) * elements)
            inner = jnp.concatenate([table_ref[rows, columns] for rows in at], axis=0)
            outer = jnp.concatenate([outer_ref[rows, columns] for rows in at], axis=0)
            y = folded(dot(star, both_parts(inner + outer)))
            flux = 0.5 * speed_ref[...] * (inner - outer)
            for c in range(3):
                flux = flux + 0.5 * normal_ref[f, c : c + 1, :] * y[c * size : (c + 1) * size]
            for g in range(FIELDS):
                flux_ref[g, f * FACE_PAD + 8 * part : f * FACE_PAD + 8 * part + 8, :] = flux[
                    8 * g : 8 * g + 8
                ]
    place_lift = [
        exact_dot(lift_ref[f], selector(FACE_BASIS, 4 * FACE_PAD, f * FACE_PAD)) for f in range(4)
    ]
    lift = weights(sum(place_lift))
    for g in range(FIELDS):
        rows = slice(g * basis, (g + 1) * basis)
        state_ref[rows, :] = base_ref[rows, :] - weighted(*lift, flux_ref[g])


def rates_out(state_ref, trace_ref, interp_ref, sea_face_ref, sea_base_ref, sea_row_ref, out_ref):
    basis = trace_ref.shape[2]
    elements = state_ref.shape[1]
    faces = sea_face_ref.shape[1]
    tiles = out_ref.shape[0]
    vertical = state_ref[vertical_field * basis : (vertical_field + 1) * basis, :]
    sea = weighted(*weights(stacked_traces(trace_ref)), vertical)
    sea = jnp.concatenate([sea[f * FACE_PAD : (f + 1) * FACE_PAD] for f in range(4)], axis=1)
    hot = (iota((4 * elements, faces), 0) == sea_face_ref[...]).astype(F32).astype(BF16)
    coeffs = folded(dot(both_parts(sea), hot))[:FACE_BASIS]
    rates = exact_dot(interp_ref[...], coeffs)
    sent = both_parts(jnp.concatenate([rates, sea_base_ref[...]], axis=0))
    row = sea_row_ref[...]
    hits = (iota((faces, 128), 1) == row).astype(F32)
    before = (iota((faces, faces), 1) < iota((faces, faces), 0)).astype(F32)
    count = dot(before.astype(BF16), hits.astype(BF16))
    slot = jnp.sum(count * hits, axis=1, keepdims=True).astype(jnp.int32)
    lane = iota((faces, 2 * CAP), 1)
    mine = slot == lane % CAP
    left = iota((POINTS // 2, 2 * CAP), 1) < CAP
    left_1 = iota((1, 2 * CAP), 1) < CAP
    for j in range(tiles):
        edges = mine & (row == jnp.where(lane < CAP, j - 1, j + 1))
        inside = mine & (row == j)
        hot = jnp.concatenate([edges.astype(F32), inside.astype(F32)], axis=1).astype(BF16)
        got = folded(dot(sent, hot))
        near, own = got[:, : 2 * CAP], got[:, 2 * CAP :]
        out_ref[j, 0:POINTS, :] = near[:POINTS]
        out_ref[j, 16:24, :] = jnp.where(left, own[0:8], own[8:16])
        out_ref[j, 24:26, :] = near[POINTS : POINTS + 2]
        out_ref[j, 26:27, :] = jnp.where(left_1, own[16:17], own[17:18])
        out_ref[j, 27:32, :] = jnp.zeros((5, 2 * CAP), F32)


def forced(place, got_ref, forcing_ref, s1_ref, s2_ref):
    tiles = got_ref.shape[0]
    tile_x = forcing_ref.shape[0]
    tile_y = forcing_ref.shape[1] - 128
    left8 = iota((8, 2 * CAP), 1) < CAP
    left1 = iota((1, 2 * CAP), 1) < CAP
    tops, bottoms, xs, ys = [], [], [], []
    for s in range(0, tiles, 2):
        one, two = got_ref[s, 16:24, :], got_ref[s + 1, 16:24, :]
        tops.append(jnp.where(left8, one, pltpu.roll(two, CAP, 1)))
        bottoms.append(jnp.where(left8, pltpu.roll(one, CAP, 1), two))
        one, two = got_ref[s, 24:32, :], got_ref[s + 1, 24:32, :]
        xs.append(jnp.where(left8, one, pltpu.roll(two, CAP, 1))[2:3])
        ys.append(jnp.where(left8, pltpu.roll(one, CAP, 1), two)[2:3])
    lower, upper = jnp.concatenate(tops, axis=1), jnp.concatenate(bottoms, axis=1)
    x0, y0 = jnp.concatenate(xs, axis=1), jnp.concatenate(ys, axis=1)
    arrived = x0.shape[1]
    from_x = iota((tile_x, arrived), 0).astype(F32) - x0
    from_y = iota((tile_y, arrived), 0).astype(F32) - y0
    total = jnp.zeros((tile_x, tile_y), F32)
    for pr in range(patch_side):
        source = lower if pr < 2 else upper
        value = jnp.zeros((tile_y, arrived), F32)
        for pc in range(patch_side):
            at = (pr * patch_side + pc) % 8
            value = jnp.where(from_y == pc, source[at : at + 1], value)
        hot = (from_x == pr).astype(F32).astype(BF16)
        for value in parts(value):
            total += lax.dot_general(hot, value, NT, preferred_element_type=F32)
    forcing_ref[:, :tile_y] = total
    near = jnp.concatenate([got_ref[s, 0:POINTS, :] for s in range(tiles)], axis=1)
    x0 = jnp.concatenate([got_ref[s, 24:25, :] for s in range(tiles)], axis=1)
    y0 = jnp.concatenate([got_ref[s, 25:26, :] for s in range(tiles)], axis=1)
    arrived = x0.shape[1]
    from_x = iota((tile_x, arrived), 0).astype(F32) - x0
    rows = iota((8, arrived), 0)
    before = iota((8, arrived), 1) % (2 * CAP) < CAP
    high_y = jnp.where(before & (rows >= 6), (rows + (tile_y - 8)).astype(F32) - y0, -1.0)
    low_y = jnp.where(before | (rows >= 2), -1.0, rows.astype(F32) - y0)
    total = jnp.zeros((tile_x, 128), F32)
    blank = jnp.zeros((128 - 16, arrived), F32)
    for pr in range(patch_side):
        high, low = jnp.zeros((8, arrived), F32), jnp.zeros((8, arrived), F32)
        for pc in range(patch_side):
            at = pr * patch_side + pc
            high = jnp.where(high_y == pc, near[at : at + 1], high)
            low = jnp.where(low_y == pc, near[at : at + 1], low)
        hot = (from_x == pr).astype(F32).astype(BF16)
        for value in parts(jnp.concatenate([low, blank, high], axis=0)):
            total += lax.dot_general(hot, value, NT, preferred_element_type=F32)
    forcing_ref[:, tile_y:] = total
    a1, _ = unequal(place)
    head, tail = forcing_ref[0:8, :], forcing_ref[tile_x - 8 : tile_x, :]
    tail = pltpu.roll(tail, 2, 0)
    s1_ref[...] = jnp.where(a1 > 0, tail, head)
    s2_ref[...] = jnp.where(a1 > 0, head, tail)


def edges_out(place, depth_ref, momentum_ref, bottom_ref, p1_ref, p2_ref, q1_ref, q2_ref):
    arrays = [depth_ref[...], momentum_ref[0], momentum_ref[1], bottom_ref[...]]
    a1, c1 = unequal(place)
    tile_x, tile_y = depth_ref.shape
    row = iota((8, tile_y), 0)
    up = jnp.where(row < 2, row + (tile_y - 2), row - 2)
    down = jnp.where(row < 2, row, row + (tile_y - 4))
    wanted = jnp.where(c1 > 0, up, down)
    hot = ((row < 4) & (wanted == iota((8, tile_y), 1))).astype(F32)
    for i, array in enumerate(arrays):
        head, tail = array[0:2], array[tile_x - 2 : tile_x]
        one = jnp.where(a1 > 0, tail, head)
        two = jnp.where(a1 > 0, head, tail)
        columns = lax.dot_general(
            hot, array, NT, preferred_element_type=F32, precision=lax.Precision.HIGHEST
        )
        for h in range(2):
            at = slice(4 * i + 2 * h, 4 * i + 2 * h + 2)
            lanes = slice(128 * h, 128 * (h + 1))
            p1_ref[at, :] = one[:, lanes]
            p2_ref[at, :] = two[:, lanes]
            q1_ref[at, :] = columns[0:2, lanes]
            q2_ref[at, :] = columns[2:4, lanes]


def widened(place, depth_ref, momentum_ref, bottom_ref, p1_ref, p2_ref, q1_ref, q2_ref, out_ref):
    tile_x, tile_y = depth_ref.shape
    a1, c1 = unequal(place)
    arrays = [depth_ref[...], momentum_ref[0], momentum_ref[1], bottom_ref[...]]
    p1, p2, q1, q2 = p1_ref[...], p2_ref[...], q1_ref[...], q2_ref[...]
    below, above = jnp.where(a1 > 0, p2, p1), jnp.where(a1 > 0, p1, p2)
    before, after = jnp.where(c1 > 0, q2, q1), jnp.where(c1 > 0, q1, q2)
    n = OCEAN_ROWS

    def ends(rows):
        one, two = rows[n : 2 * n], rows[2 * n :]
        return jnp.where(a1 > 0, two, one), jnp.where(a1 > 0, one, two)

    before_below, before_above = ends(before)
    after_below, after_above = ends(after)
    lane = iota((2, 128), 1)
    low, high = lane < 2, lane >= 126
    for i, array in enumerate(arrays):
        first, second = slice(4 * i, 4 * i + 2), slice(4 * i + 2, 4 * i + 4)
        out_ref[i, 0:MARGIN, :] = jnp.zeros((MARGIN, tile_y + 128), F32)
        out_ref[i, MARGIN + tile_x :, :] = jnp.zeros((MARGIN, tile_y + 128), F32)
        out_ref[i, MARGIN : MARGIN + tile_x, :tile_y] = array
        for at, rows, left, right in (
            (MARGIN - 2, below, before_below, after_below),
            (MARGIN + tile_x, above, before_above, after_above),
        ):
            out_ref[i, at : at + 2, 0:128] = rows[first]
            out_ref[i, at : at + 2, 128:256] = rows[second]
            corner = jnp.where(low, right[first], jnp.where(high, left[second], 0.0))
            out_ref[i, at : at + 2, 256:384] = corner
        start = jnp.concatenate([after[first], after[second]], axis=1)
        finish = jnp.concatenate([before[first], before[second]], axis=1)
        columns = jnp.concatenate([start, jnp.zeros((124, tile_x), F32), finish], axis=0)
        out_ref[i, MARGIN : MARGIN + tile_x, tile_y:] = columns.T


def ocean(
    place, wide_ref, forcing_ref, s1_ref, s2_ref, out_ref, bed_ref, state, bed, cell,
):
    tile_x, tile_y = bed_ref.shape
    span = tile_y + 128
    a1, _ = unequal(place)
    below = jnp.where(a1 > 0, s2_ref[...], s1_ref[...])[0:2]
    above = jnp.where(a1 > 0, s1_ref[...], s2_ref[...])[0:2]
    force_lo = step_ocean * below
    force_hi = step_ocean * above
    height = tile_x + 2 * MARGIN
    strip = 16

    def next_of(x):
        return pltpu.roll(x, span - 1, 1)

    def previous_of(x):
        return pltpu.roll(x, 1, 1)

    bed[...] = wide_ref[3]
    bed[MARGIN : MARGIN + tile_x, :] += step_ocean * forcing_ref[...]
    bed[MARGIN - 2 : MARGIN, :] += force_lo
    bed[MARGIN + tile_x : MARGIN + tile_x + 2, :] += force_hi
    lane = iota((strip, span), 1)
    outside = ((lane == span - 1) & (place[1] == 0)) | (
        (lane == tile_y) & (place[1] == place[3] - 1)
    )

    def cells(read, at, rows):
        h, mx, my = (read(k, at, rows) for k in range(3))
        safe = jnp.maximum(h, depth_floor)
        u, v = mx / safe, my / safe
        c = jnp.sqrt(safe)
        half = 0.5 * h * h
        cell[0, at : at + rows, :] = mx * u + half
        cell[1, at : at + rows, :] = my * u
        cell[2, at : at + rows, :] = my * v + half
        cell[3, at : at + rows, :] = jnp.abs(u) + c
        cell[4, at : at + rows, :] = jnp.abs(v) + c

    def update(read, at, rows):
        here, up, down = slice(at, at + rows), slice(at + 1, at + rows + 1), slice(at - 1, at + rows - 1)

        def x_face(i, j):
            wave = 0.5 * jnp.maximum(cell[3, i, :], cell[3, j, :])
            u_i, u_j = [read(k, i) for k in range(3)], [read(k, j) for k in range(3)]
            f_i = (u_i[1], cell[0, i, :], cell[1, i, :])
            f_j = (u_j[1], cell[0, j, :], cell[1, j, :])
            return [0.5 * (f_i[k] + f_j[k]) - wave * (u_j[k] - u_i[k]) for k in range(3)]

        now = [read(k, here) for k in range(3)]
        flux = (now[2], cell[1, here, :], cell[2, here, :])
        speed = cell[4, here, :]
        wave = 0.5 * jnp.maximum(speed, next_of(speed))
        y_face = [
            0.5 * (flux[k] + next_of(flux[k])) - wave * (next_of(now[k]) - now[k]) for k in range(3)
        ]
        upper, lower = x_face(here, up), x_face(down, here)
        new = [
            now[k] - step_ocean * (upper[k] - lower[k] + y_face[k] - previous_of(y_face[k]))
            for k in range(3)
        ]
        b = bed[here, :]
        slope_x = 0.5 * (bed[up, :] - bed[down, :])
        slope_y = 0.5 * (next_of(b) - previous_of(b))
        new[1] = new[1] - step_ocean * now[0] * slope_x
        new[2] = new[2] - step_ocean * now[0] * slope_y
        return new

    for at in range(8, height - 8, 8):
        cells(lambda k, i, n: wide_ref[k, i : i + n, :], at, 8)
    for at in range(8, height - 8, strip):
        rows = min(strip, height - 8 - at)
        new = update(lambda k, i: wide_ref[k, i, :], at, rows)
        out = outside[:rows]
        row = iota((rows, span), 0) + at
        out = out | ((row < MARGIN) & (place[0] == 0))
        out = out | ((row >= MARGIN + tile_x) & (place[0] == place[2] - 1))
        for k in range(3):
            state[k, at : at + rows, :] = jnp.where(out, 0.0, new[k])
    for at in range(8, height - 8, 8):
        cells(lambda k, i, n: state[k, i : i + n, :], at, 8)
    bed[MARGIN : MARGIN + tile_x, :] += step_ocean * forcing_ref[...]
    bed[MARGIN - 2 : MARGIN, :] += force_lo
    bed[MARGIN + tile_x : MARGIN + tile_x + 2, :] += force_hi
    for at in range(MARGIN, MARGIN + tile_x, strip):
        new = update(lambda k, i: state[k, i, :], at, strip)
        for k in range(3):
            out_ref[k, at - MARGIN : at - MARGIN + strip, :] = new[k][:, :tile_y]
    bed_ref[...] = bed[MARGIN : MARGIN + tile_x, :tile_y]


def call(body, out_shape, *args, place=None, scratch=(), aliases=None):
    specs = [pl.BlockSpec(memory_space=pltpu.VMEM) for _ in args]
    if place is not None:
        specs = [pl.BlockSpec(memory_space=pltpu.SMEM)] + specs
        args = (place,) + args
    shapes = [jax.ShapeDtypeStruct(s, F32) for s in out_shape]
    return pl.pallas_call(
        body,
        out_shape=shapes,
        in_specs=specs,
        out_specs=[pl.BlockSpec(memory_space=pltpu.VMEM) for _ in shapes],
        scratch_shapes=[pltpu.VMEM(s, F32) for s in scratch],
        input_output_aliases=aliases or {},
        compiler_params=pltpu.CompilerParams(vmem_limit_bytes=VMEM_LIMIT),
    )(*args)


def swap(block, axis, parity):
    count = lax.axis_size(axis)
    pairs = []
    for i in range(parity, count - 1, 2):
        pairs += [(i, i + 1), (i + 1, i)]
    return lax.ppermute(block, axis, pairs)


def per_device(
    coefficients,
    jacobian,
    face_normals,
    wave_speed,
    star_mats,
    deriv_mats,
    stiff_mats,
    source_mat,
    trace_mats,
    lift_mats,
    face_partner,
    send_faces,
    sea_face,
    sea_row,
    sea_base,
    interp_mat,
    water_depth,
    momentum,
    bottom,
):
    basis, elements = coefficients.shape[1:]
    rows = FIELDS * basis
    tile_x, tile_y = water_depth.shape
    tiles = lax.axis_size("gy")
    place = jnp.stack(
        [lax.axis_index("gx"), lax.axis_index("gy"), lax.axis_size("gx"), tiles]
    ).astype(jnp.int32)
    speed = wave_speed.reshape(1, elements)
    spread = (FIELDS, 3 * basis, elements)
    faces = (TABLE, 4 * elements)
    buffer = (3 * HALF, 128)
    state = coefficients.reshape(rows, elements)
    edge_rows = call(
        edges_out, [(OCEAN_ROWS, 128)] * 4, water_depth, momentum, bottom, place=place
    )
    for section in range(2):
        integral, table, p1, p2, q1, q2 = call(
            front,
            [(rows, elements), faces, buffer, buffer, (HALF, 128), (HALF, 128)],
            state, jacobian, star_mats, source_mat, deriv_mats, trace_mats, send_faces,
            place=place,
            scratch=[spread, (rows, elements), (rows, elements), (rows, elements)],
        )
        own = (q1, q2)
        if section == 0:
            p1 = jnp.concatenate([p1, edge_rows[0]], axis=0)
            p2 = jnp.concatenate([p2, edge_rows[1]], axis=0)
        p1, p2 = swap(p1, "gx", 0), swap(p2, "gx", 1)
        base, outer = call(
            middle,
            [(rows, elements), faces],
            state, jacobian, star_mats, stiff_mats, integral, table, face_partner,
            scratch=[spread],
        )
        sent = []
        for n in range(2):
            at = slice((n + 1) * HALF, (n + 2) * HALF)
            pieces = [own[n], p1[at], p2[at]]
            if section == 0:
                pieces += [edge_rows[2 + n], p1[3 * HALF :], p2[3 * HALF :]]
            sent.append(jnp.concatenate(pieces, axis=0))
        q1, q2 = swap(sent[0], "gy", 0), swap(sent[1], "gy", 1)
        (state,) = call(
            back,
            [(rows, elements)],
            base, table, outer, face_partner, face_normals, speed, star_mats, lift_mats,
            p1, p2, q1, q2,
            place=place,
            scratch=[(FIELDS, 4 * FACE_PAD, elements)],
        )
        if section == 0:
            (wide,) = call(
                widened,
                [(4, tile_x + 2 * MARGIN, tile_y + 128)],
                water_depth, momentum, bottom,
                p1[3 * HALF :], p2[3 * HALF :], q1[3 * HALF :], q2[3 * HALF :],
                place=place,
            )
    corners = jnp.pad(sea_base.T.astype(F32), ((0, 6), (0, 0)))
    (outgoing,) = call(
        rates_out,
        [(tiles, 32, 128)],
        state, trace_mats, interp_mat, sea_face.reshape(1, -1), corners, sea_row,
    )
    incoming = lax.all_to_all(outgoing, "gy", split_axis=0, concat_axis=0, tiled=True)
    forcing, s1, s2 = call(
        forced,
        [(tile_x, tile_y + 128), (8, tile_y + 128), (8, tile_y + 128)],
        incoming,
        place=place,
    )
    s1, s2 = swap(s1, "gx", 0), swap(s2, "gx", 1)
    wide_shape = (tile_x + 2 * MARGIN, tile_y + 128)
    ocean_final, bed_final = call(
        ocean,
        [(3, tile_x, tile_y), (tile_x, tile_y)],
        wide, forcing, s1, s2,
        place=place,
        scratch=[(3,) + wide_shape, wide_shape, (5,) + wide_shape],
    )
    return (state.reshape(coefficients.shape), ocean_final, bed_final)


def solution(mesh):
    in_specs = (
        P(None, None, ("gx", "gy")),
        P(None, None, ("gx", "gy")),
        P(None, None, ("gx", "gy")),
        P(("gx", "gy")),
        P(),
        P(),
        P(),
        P(),
        P(),
        P(),
        P(None, ("gx", "gy")),
        P(None, ("gx", "gy")),
        P(("gx", "gy")),
        P(("gx", "gy"), None),
        P(("gx", "gy"), None),
        P(),
        P("gx", "gy"),
        P(None, "gx", "gy"),
        P("gx", "gy"),
    )
    out_specs = (P(None, None, ("gx", "gy")), P(None, "gx", "gy"), P("gx", "gy"))
    return jax.shard_map(
        per_device, mesh=mesh, in_specs=in_specs, out_specs=out_specs, check_vma=False
    )
```

profile of v0, /device:TPU:1, one launch (start us, length us, event | category | flops | bytes accessed | tf_op | source)
XLA Modules:
  0.0 103.6 jit_solution(14905906349503562717)
XLA Ops:
  0.6 0.9 copy.22.trace_ref
  1.5 0.1 pad_add_fusion.place
  1.6 1.0 %copy-done.2 = f32[2,256,256]{2,1,0:T(8,128)S(1)} copy-done((f32[2,256,256]{2,1,0:T(8,128)S(1)}, f32[2,256,256]{2,1,0:T(8,128)}, u32[]{:S(2)}) %copy-start.2) | copy-done | bytes 524312
  2.6 0.9 copy-done.4
  3.6 0.9 copy-done.6
  4.5 1.5 %shard_map.204 = (f32[16,128]{1,0:T(8,128)S(1)}, f32[16,128]{1,0:T(8,128)S(1)}, f32[16,128]{1,0:T(8,128)S(1)}, f32[16,128]{1,0:T(8,128)S(1)}) custom-call(s32[4]{0:T(128)S(1)} %pad_add_fusion.place, f32[256,256]{1,0:T(8,128)S(1)} %copy-done.4, f32[2,256,256]{2,1,0:T(8,128)S(1)} %copy-done.2, f32[256,256]{1,0:T(8,128)S(1)} %copy-done.6), custom_call_target="tpu_custom_call" | custom-call | tf_op jit(solution)/shard_map/pallas_call | solution.py:536
  6.0 0.8 copy-done.8
  6.8 0.9 copy-done.12
  7.6 0.7 copy-done.14
  8.3 0.7 copy-done.23
  9.0 0.7 copy-done.27
  9.7 6.2 %shard_map.202 = (f32[728,256]{1,0:T(8,128)S(1)}, f32[312,1024]{1,0:T(8,128)S(1)}, f32[480,128]{1,0:T(8,128)S(1)}, f32[480,128]{1,0:T(8,128)S(1)}, f32[160,128]{1,0:T(8,128)S(1)}, /*index=5*/f32[160,128]{1,0:T(8,128)S(1)}) custom-call(s32[4]{0:T(128)S(1)} %pad_add_fusion.place, f32[728,256]{1,0:T(8,128)S(1)} %bitcast.8, f32[3,3,256]{2,1,0:T(4,128)S(1)} %copy-done.14, ...), custom_call_target="tpu_custom_call" | custom-call | tf_op jit(solution)/shard_map/pallas_call | solution.py:536
  15.9 0.0 copy-start.33
  16.0 0.0 copy-start.9
  16.0 0.0 copy-start.11
  16.0 0.0 copy-start.19
  16.0 0.1 collective-permute-start
  16.2 4.5 %collective-permute-start.1 = (f32[496,128]{1,0:T(8,128)S(1)}, f32[496,128]{1,0:T(8,128)S(1)}, u32[]{:S(2)}, u32[]{:S(2)}) collective-permute-start(f32[496,128]{1,0:T(8,128)S(1)} %pad_maximum_fusion.1), channel_id=1, source_target_pairs={{8,16},{16,8},{9,17},{17,9},{10,18},{18,10},{11,19},{19,11},{12,20... | collective-permute-start | bytes 761864 | tf_op jit(solution)/shard_map/ppermute | solution.py:552
  20.7 0.7 constant_dynamic-update-slice_fusion.3
  21.4 0.7 slice_dynamic-update-slice_fusion.1
  22.0 2.6 %collective-permute-done.1.p2_ref = f32[496,128]{1,0:T(8,128)S(1)} collective-permute-done((f32[496,128]{1,0:T(8,128)S(1)}, f32[496,128]{1,0:T(8,128)S(1)}, u32[]{:S(2)}, u32[]{:S(2)}) %collective-permute-start.1) | collective-permute-done | bytes 253984 | tf_op jit(solution)/shard_map/ppermute | solution.py:552
  24.6 0.7 slice_dynamic-update-slice_fusion
  25.3 0.6 constant_dynamic-update-slice_fusion.2
  25.9 0.6 constant_dynamic-update-slice_fusion.6
  26.5 0.6 fusion.1
  27.1 0.6 fusion
  27.7 1.8 %collective-permute-start.2 = (f32[528,128]{1,0:T(8,128)}, f32[528,128]{1,0:T(8,128)}, u32[]{:S(2)}, u32[]{:S(2)}) collective-permute-start(f32[528,128]{1,0:T(8,128)} %get-tuple-element.54), channel_id=1, source_target_pairs={{0,1},{1,0},{2,3},{3,2},{4,5},{5,4},{6,7},{7,6},{8,9},{9,8},{10,11... | collective-permute-start | bytes 811016 | tf_op jit(solution)/shard_map/ppermute | solution.py:552
  29.5 1.4 %collective-permute-start.3 = (f32[528,128]{1,0:T(8,128)}, f32[528,128]{1,0:T(8,128)}, u32[]{:S(2)}, u32[]{:S(2)}) collective-permute-start(f32[528,128]{1,0:T(8,128)} %get-tuple-element.55), channel_id=1, source_target_pairs={{1,2},{2,1},{3,4},{4,3},{5,6},{6,5},{9,10},{10,9},{11,12},{12,11},... | collective-permute-start | bytes 811016 | tf_op jit(solution)/shard_map/ppermute | solution.py:552
  30.9 0.6 copy.23.normal_ref
  31.5 0.9 copy.24.lift_ref
  32.4 0.0 copy-start.15
  32.4 0.7 copy-done.15
  33.2 3.1 %shard_map.203 = (f32[728,256]{1,0:T(8,128)S(1)}, f32[312,1024]{1,0:T(8,128)S(1)}) custom-call(f32[728,256]{1,0:T(8,128)S(1)} %bitcast.9, f32[3,3,256]{2,1,0:T(4,128)S(1)} %copy-done.15, f32[3,13,13]{2,1,0:T(8,128)S(1)} %copy-done.9, f32[3,56,56]{2,1,0:T(8,128)S(1)} %copy-done.11, f32[728,256]{1,0:T(8,128)S(1)} %get-tuple-element.28.integral_ref, ...), custom_call_target="tpu_custom_call" | custom-call | tf_op jit(solution)/shard_map/pallas_call | solution.py:536
  36.3 0.7 collective-permute-done.2.q1_ref
  37.0 0.0 copy-start.13
  37.0 0.0 copy-start.24
  37.0 4.4 %shard_map.205.q_ref = f32[728,256]{1,0:T(8,128)S(1)} custom-call(s32[4]{0:T(128)S(1)} %copy-done.21, f32[728,256]{1,0:T(8,128)S(1)} %get-tuple-element.30.base_ref, f32[312,1024]{1,0:T(8,128)S(1)} %get-tuple-element.29.table_ref, f32[312,1024]{1,0:T(8,128)S(1)} %get-tuple-element.31.outer_ref, s32[4,256]{1,0:T(4,128)S(1)} %copy-done.19, ...), custom_call_target="tpu_custom_call" | custom-call | tf_op jit(solution)/shard_map/pallas_call | solution.py:536
  41.4 6.2 %shard_map.206 = (f32[728,256]{1,0:T(8,128)S(1)}, f32[312,1024]{1,0:T(8,128)S(1)}, f32[480,128]{1,0:T(8,128)S(1)}, f32[480,128]{1,0:T(8,128)S(1)}, f32[160,128]{1,0:T(8,128)S(1)}, /*index=5*/f32[160,128]{1,0:T(8,128)S(1)}) custom-call(s32[4]{0:T(128)S(1)} %copy-done.21, f32[728,256]{1,0:T(8,128)S(1)} %shard_map.205.q_ref, f32[3,3,256]{2,1,0:T(4,128)S(1)} %copy-done.15, ...), custom_call_target="tpu_custom_call" | custom-call | tf_op jit(solution)/shard_map/pallas_call | solution.py:536
  47.6 2.7 %collective-permute-start.5 = (f32[480,128]{1,0:T(8,128)S(1)}, f32[480,128]{1,0:T(8,128)S(1)}, u32[]{:S(2)}, u32[]{:S(2)}) collective-permute-start(f32[480,128]{1,0:T(8,128)S(1)} %get-tuple-element.45), channel_id=1, source_target_pairs={{8,16},{16,8},{9,17},{17,9},{10,18},{18,10},{11,19},{19,11},{12,20... | collective-permute-start | bytes 737288 | tf_op jit(solution)/shard_map/ppermute | solution.py:552
  50.3 0.1 collective-permute-start.4
  50.4 4.7 %collective-permute-done.5.p2_ref = f32[480,128]{1,0:T(8,128)S(1)} collective-permute-done((f32[480,128]{1,0:T(8,128)S(1)}, f32[480,128]{1,0:T(8,128)S(1)}, u32[]{:S(2)}, u32[]{:S(2)}) %collective-permute-start.5) | collective-permute-done | bytes 245792 | tf_op jit(solution)/shard_map/ppermute | solution.py:552
  55.2 0.7 pad_maximum_fusion.2
  55.9 2.5 %collective-permute-start.6 = (f32[480,128]{1,0:T(8,128)}, f32[480,128]{1,0:T(8,128)}, u32[]{:S(2)}, u32[]{:S(2)}) collective-permute-start(f32[480,128]{1,0:T(8,128)} %pad_maximum_fusion.2), channel_id=1, source_target_pairs={{0,1},{1,0},{2,3},{3,2},{4,5},{5,4},{6,7},{7,6},{8,9},{9,8},{10,11... | collective-permute-start | bytes 737288 | tf_op jit(solution)/shard_map/ppermute | solution.py:552
  58.5 0.7 pad_maximum_fusion.3
  59.2 1.4 %collective-permute-start.7 = (f32[480,128]{1,0:T(8,128)}, f32[480,128]{1,0:T(8,128)}, u32[]{:S(2)}, u32[]{:S(2)}) collective-permute-start(f32[480,128]{1,0:T(8,128)} %pad_maximum_fusion.3), channel_id=1, source_target_pairs={{1,2},{2,1},{3,4},{4,3},{5,6},{6,5},{9,10},{10,9},{11,12},{12,11},... | collective-permute-start | bytes 737288 | tf_op jit(solution)/shard_map/ppermute | solution.py:552
  60.5 0.8 copy.29.sea_row_ref
  61.3 0.7 convert_bitcast_fusion
  62.0 0.0 copy-start.31
  62.0 3.1 %shard_map.207 = (f32[728,256]{1,0:T(8,128)S(1)}, f32[312,1024]{1,0:T(8,128)S(1)}) custom-call(f32[728,256]{1,0:T(8,128)S(1)} %shard_map.205.q_ref, f32[3,3,256]{2,1,0:T(4,128)S(1)} %copy-done.16, f32[3,13,13]{2,1,0:T(8,128)S(1)} %copy-done.9, f32[3,56,56]{2,1,0:T(8,128)S(1)} %copy-done.11, f32[728,256]{1,0:T(8,128)S(1)} %get-tuple-element.40.integral_ref, ...), custom_call_target="tpu_custom_call" | custom-call | tf_op jit(solution)/shard_map/pallas_call | solution.py:536
  65.2 2.9 %collective-permute-done.6.q1_ref = f32[480,128]{1,0:T(8,128)} collective-permute-done((f32[480,128]{1,0:T(8,128)}, f32[480,128]{1,0:T(8,128)}, u32[]{:S(2)}, u32[]{:S(2)}) %collective-permute-start.6) | collective-permute-done | bytes 245792 | tf_op jit(solution)/shard_map/ppermute | solution.py:552
  68.1 0.0 copy-start.10
  68.1 0.0 copy-start.29
  68.1 5.3 %shard_map.208.state_ref = f32[728,256]{1,0:T(8,128)} custom-call(s32[4]{0:T(128)S(1)} %copy-done.22, f32[728,256]{1,0:T(8,128)S(1)} %get-tuple-element.42.base_ref, f32[312,1024]{1,0:T(8,128)S(1)} %get-tuple-element.41.table_ref, f32[312,1024]{1,0:T(8,128)S(1)} %get-tuple-element.43.outer_ref, s32[4,256]{1,0:T(4,128)S(1)} %copy-done.19, ...), custom_call_target="tpu_custom_call" | custom-call | tf_op jit(solution)/shard_map/pallas_call | solution.py:536
  73.4 0.0 copy-start.1
  73.4 1.1 %copy-done.1 = f32[728,256]{1,0:T(8,128)S(1)} copy-done((f32[728,256]{1,0:T(8,128)S(1)}, f32[728,256]{1,0:T(8,128)}, u32[]{:S(2)}) %copy-start.1) | copy-done | bytes 745496
  74.5 1.2 %shard_map.210 = f32[8,32,128]{2,1,0:T(8,128)S(1)} custom-call(f32[728,256]{1,0:T(8,128)S(1)} %copy-done.1, f32[4,21,56]{2,1,0:T(8,128)S(1)} %copy.22.trace_ref, f32[16,21]{1,0:T(8,128)S(1)} %copy-done.29, s32[1,256]{1,0:T(1,128)S(1)} %bitcast.13, f32[8,256]{1,0:T(8,128)S(1)} %pad.4.sea_base_ref, s32[256,1]{1,0:T(8,128)S(1)} %copy-done.10), custom_call_target="tpu_custom_call" | custom-call | tf_op jit(solution)/shard_map/pallas_call | solution.py:536
  75.7 11.8 %all_to_all.5.got_ref = f32[8,32,128]{2,1,0:T(8,128)S(1)} all-to-all(f32[8,32,128]{2,1,0:T(8,128)S(1)} %shard_map.210), channel_id=1, replica_groups=mesh['gx'=4,'gy'=8] {'gy'}, dimensions={0} | all-to-all | bytes 262144 | tf_op jit(solution)/shard_map/all_to_all | solution.py:640
  87.5 2.7 %shard_map.211 = (f32[256,384]{1,0:T(8,128)S(1)}, f32[8,384]{1,0:T(8,128)S(1)}, f32[8,384]{1,0:T(8,128)S(1)}) custom-call(s32[4]{0:T(128)S(1)} %copy-done.22, f32[8,32,128]{2,1,0:T(8,128)S(1)} %all_to_all.5.got_ref), custom_call_target="tpu_custom_call" | custom-call | tf_op jit(solution)/shard_map/pallas_call | solution.py:536
  90.2 0.1 collective-permute-start.8
  90.3 4.6 %collective-permute-start.9 = (f32[8,384]{1,0:T(8,128)S(1)}, f32[8,384]{1,0:T(8,128)S(1)}, u32[]{:S(2)}, u32[]{:S(2)}) collective-permute-start(f32[8,384]{1,0:T(8,128)S(1)} %get-tuple-element.50), channel_id=1, source_target_pairs={{8,16},{16,8},{9,17},{17,9},{10,18},{18,10},{11,19},{19,11},{12,20... | collective-permute-start | bytes 36872 | tf_op jit(solution)/shard_map/ppermute | solution.py:552
  94.9 0.7 slice.62.q1_ref
  95.7 0.7 slice.63.q2_ref
  96.5 0.8 shard_map.209.wide_ref
  97.2 6.3 %shard_map.212 = (f32[3,256,256]{2,1,0:T(8,128)}, f32[256,256]{1,0:T(8,128)}) custom-call(s32[4]{0:T(128)S(1)} %copy-done.22, f32[4,288,384]{2,1,0:T(8,128)S(1)} %shard_map.209.wide_ref, f32[256,384]{1,0:T(8,128)S(1)} %get-tuple-element.48.forcing_ref, f32[8,384]{1,0:T(8,128)S(1)} %collective-permute-done.8.s1_ref, f32[8,384]{1,0:T(8,128)S(1)} %collective-permute-done.9.s2_ref), custom_call_target="tpu_custom_call" | custom-call | tf_op jit(solution)/shard_map/pallas_call | solution.py:536
  (60 shorter events, 0.2 us)
Async XLA Ops:
  0.6 5.4 %copy-start = (f32[13,56,256]{2,1,0:T(8,128)S(1)}, f32[13,56,256]{2,1,0:T(8,128)}, u32[]{:S(2)}) copy-start(f32[13,56,256]{2,1,0:T(8,128)} %param.19) | copy-start | bytes 2236420
  1.6 1.0 %copy-start.2 = (f32[2,256,256]{2,1,0:T(8,128)S(1)}, f32[2,256,256]{2,1,0:T(8,128)}, u32[]{:S(2)}) copy-start(f32[2,256,256]{2,1,0:T(8,128)} %momentum_ref.3) | copy-start | bytes 1572868
  2.6 0.9 copy-start.4
  3.6 0.9 copy-start.6
  4.5 11.6 %copy-start.20 = (s32[4]{0:T(128)}, s32[4]{0:T(128)S(1)}, u32[]{:S(2)}) copy-start(s32[4]{0:T(128)S(1)} %pad_add_fusion.place) | copy-start | bytes 52
  6.0 0.8 copy-start.8
  6.7 0.9 copy-start.12
  7.6 0.7 copy-start.14
  8.3 0.7 copy-start.23
  9.0 0.7 copy-start.27
  15.9 15.0 %copy-start.33 = (f32[4,3,256]{2,0,1:T(4,128)S(1)}, f32[4,3,256]{2,0,1:T(4,128)}, u32[]{:S(2)}) copy-start(f32[4,3,256]{2,0,1:T(4,128)} %param.21) | copy-start | bytes 36868
  16.0 16.5 %copy-start.9 = (f32[3,13,13]{2,1,0:T(8,128)S(1)}, f32[3,13,13]{2,1,0:T(8,128)}, u32[]{:S(2)}) copy-start(f32[3,13,13]{2,1,0:T(8,128)} %star_ref.11) | copy-start | bytes 6088
  16.0 16.4 %copy-start.11 = (f32[3,56,56]{2,1,0:T(8,128)S(1)}, f32[3,56,56]{2,1,0:T(8,128)}, u32[]{:S(2)}) copy-start(f32[3,56,56]{2,1,0:T(8,128)} %stiff_ref.3) | copy-start | bytes 112900
  16.0 16.4 %copy-start.19 = (s32[4,256]{1,0:T(4,128)S(1)}, s32[4,256]{1,0:T(4,128)}, u32[]{:S(2)}) copy-start(s32[4,256]{1,0:T(4,128)} %partner_ref.7) | copy-start | bytes 12292
  16.0 5.3 %collective-permute-start = (f32[496,128]{1,0:T(8,128)S(1)}, f32[496,128]{1,0:T(8,128)S(1)}, u32[]{:S(2)}, u32[]{:S(2)}) collective-permute-start(f32[496,128]{1,0:T(8,128)S(1)} %pad_maximum_fusion), channel_id=1, source_target_pairs={{0,8},{8,0},{16,24},{24,16},{1,9},{9,1},{17,25},{25,17},{2,10},{10... | collective-permute-start | bytes 761864 | tf_op jit(solution)/shard_map/ppermute | solution.py:552
  16.2 8.5 %collective-permute-start.1 = (f32[496,128]{1,0:T(8,128)S(1)}, f32[496,128]{1,0:T(8,128)S(1)}, u32[]{:S(2)}, u32[]{:S(2)}) collective-permute-start(f32[496,128]{1,0:T(8,128)S(1)} %pad_maximum_fusion.1), channel_id=1, source_target_pairs={{8,16},{16,8},{9,17},{17,9},{10,18},{18,10},{11,19},{19,11},{12,20... | collective-permute-start | bytes 761864 | tf_op jit(solution)/shard_map/ppermute | solution.py:552
  27.7 9.3 %collective-permute-start.2 = (f32[528,128]{1,0:T(8,128)}, f32[528,128]{1,0:T(8,128)}, u32[]{:S(2)}, u32[]{:S(2)}) collective-permute-start(f32[528,128]{1,0:T(8,128)} %get-tuple-element.54), channel_id=1, source_target_pairs={{0,1},{1,0},{2,3},{3,2},{4,5},{5,4},{6,7},{7,6},{8,9},{9,8},{10,11... | collective-permute-start | bytes 811016 | tf_op jit(solution)/shard_map/ppermute | solution.py:552
  29.5 7.4 %collective-permute-start.3 = (f32[528,128]{1,0:T(8,128)}, f32[528,128]{1,0:T(8,128)}, u32[]{:S(2)}, u32[]{:S(2)}) collective-permute-start(f32[528,128]{1,0:T(8,128)} %get-tuple-element.55), channel_id=1, source_target_pairs={{1,2},{2,1},{3,4},{4,3},{5,6},{6,5},{9,10},{10,9},{11,12},{12,11},... | collective-permute-start | bytes 811016 | tf_op jit(solution)/shard_map/ppermute | solution.py:552
  32.4 0.7 copy-start.15
  33.1 3.8 %copy-start.17 = (f32[4,3,256]{2,1,0:T(4,128)S(1)}, f32[4,3,256]{2,1,0:T(4,128)}, u32[]{:S(2)}) copy-start(f32[4,3,256]{2,1,0:T(4,128)} %copy.23.normal_ref) | copy-start | bytes 36868
  33.1 3.8 %copy-start.21 = (s32[4]{0:T(128)S(1)}, s32[4]{0:T(128)}, u32[]{:S(2)}) copy-start(s32[4]{0:T(128)} %copy-done.20) | copy-start | bytes 52
  33.2 3.8 %copy-start.30 = (f32[256]{0:T(256)S(1)}, f32[256]{0:T(256)}, u32[]{:S(2)}) copy-start(f32[256]{0:T(256)} %param.22) | copy-start | bytes 3076
  37.0 4.4 %copy-start.13 = (f32[3,56,56]{2,1,0:T(8,128)S(1)}, f32[3,56,56]{2,1,0:T(8,128)}, u32[]{:S(2)}) copy-start(f32[3,56,56]{2,1,0:T(8,128)} %deriv_ref.3) | copy-start | bytes 112900
  37.0 4.4 %copy-start.24 = (f32[13,13]{1,0:T(8,128)S(1)}, f32[13,13]{1,0:T(8,128)}, u32[]{:S(2)}) copy-start(f32[13,13]{1,0:T(8,128)} %source_ref.3) | copy-start | bytes 2032
  37.0 4.4 %copy-start.28 = (s32[8,64]{1,0:T(8,128)S(1)}, s32[8,64]{1,0:T(8,128)}, u32[]{:S(2)}) copy-start(s32[8,64]{1,0:T(8,128)} %send_ref.3) | copy-start | bytes 6148
  41.4 19.1 %copy-start.34 = (s32[256,1]{0,1:T(1,128)S(1)}, s32[256,1]{0,1:T(1,128)}, u32[]{:S(2)}) copy-start(s32[256,1]{0,1:T(1,128)} %param.32) | copy-start | bytes 3076
  41.4 20.6 %copy-start.16 = (f32[3,3,256]{2,1,0:T(4,128)S(1)}, f32[3,3,256]{2,1,0:T(4,128)}, u32[]{:S(2)}) copy-start(f32[3,3,256]{2,1,0:T(4,128)} %jac_ref.7) | copy-start | bytes 27652
  47.6 7.5 %collective-permute-start.5 = (f32[480,128]{1,0:T(8,128)S(1)}, f32[480,128]{1,0:T(8,128)S(1)}, u32[]{:S(2)}, u32[]{:S(2)}) collective-permute-start(f32[480,128]{1,0:T(8,128)S(1)} %get-tuple-element.45), channel_id=1, source_target_pairs={{8,16},{16,8},{9,17},{17,9},{10,18},{18,10},{11,19},{19,11},{12,20... | collective-permute-start | bytes 737288 | tf_op jit(solution)/shard_map/ppermute | solution.py:552
  50.3 4.8 %collective-permute-start.4 = (f32[480,128]{1,0:T(8,128)S(1)}, f32[480,128]{1,0:T(8,128)S(1)}, u32[]{:S(2)}, u32[]{:S(2)}) collective-permute-start(f32[480,128]{1,0:T(8,128)S(1)} %get-tuple-element.44), channel_id=1, source_target_pairs={{0,8},{8,0},{16,24},{24,16},{1,9},{9,1},{17,25},{25,17},{2,10},{10... | collective-permute-start | bytes 737288 | tf_op jit(solution)/shard_map/ppermute | solution.py:552
  55.9 12.2 %collective-permute-start.6 = (f32[480,128]{1,0:T(8,128)}, f32[480,128]{1,0:T(8,128)}, u32[]{:S(2)}, u32[]{:S(2)}) collective-permute-start(f32[480,128]{1,0:T(8,128)} %pad_maximum_fusion.2), channel_id=1, source_target_pairs={{0,1},{1,0},{2,3},{3,2},{4,5},{5,4},{6,7},{7,6},{8,9},{9,8},{10,11... | collective-permute-start | bytes 737288 | tf_op jit(solution)/shard_map/ppermute | solution.py:552
  59.2 8.9 %collective-permute-start.7 = (f32[480,128]{1,0:T(8,128)}, f32[480,128]{1,0:T(8,128)}, u32[]{:S(2)}, u32[]{:S(2)}) collective-permute-start(f32[480,128]{1,0:T(8,128)} %pad_maximum_fusion.3), channel_id=1, source_target_pairs={{1,2},{2,1},{3,4},{4,3},{5,6},{6,5},{9,10},{10,9},{11,12},{12,11},... | collective-permute-start | bytes 737288 | tf_op jit(solution)/shard_map/ppermute | solution.py:552
  62.0 6.1 %copy-start.18 = (f32[4,3,256]{2,1,0:T(4,128)S(1)}, f32[4,3,256]{2,1,0:T(4,128)}, u32[]{:S(2)}) copy-start(f32[4,3,256]{2,1,0:T(4,128)} %copy.23.normal_ref) | copy-start | bytes 36868
  62.0 6.1 %copy-start.22 = (s32[4]{0:T(128)S(1)}, s32[4]{0:T(128)}, u32[]{:S(2)}) copy-start(s32[4]{0:T(128)} %copy-done.20) | copy-start | bytes 52
  62.0 6.0 %copy-start.31 = (f32[256]{0:T(256)S(1)}, f32[256]{0:T(256)}, u32[]{:S(2)}) copy-start(f32[256]{0:T(256)} %param.22) | copy-start | bytes 3076
  68.1 5.3 %copy-start.10 = (s32[256,1]{1,0:T(8,128)S(1)}, s32[256,1]{1,0:T(8,128)}, u32[]{:S(2)}) copy-start(s32[256,1]{1,0:T(8,128)} %copy.29.sea_row_ref) | copy-start | bytes 3076
  68.1 5.3 %copy-start.29 = (f32[16,21]{1,0:T(8,128)S(1)}, f32[16,21]{1,0:T(8,128)}, u32[]{:S(2)}) copy-start(f32[16,21]{1,0:T(8,128)} %interp_ref.1) | copy-start | bytes 4036
  68.1 5.3 %copy-start.32 = (s32[256]{0:T(256)S(1)}, s32[256]{0:T(256)}, u32[]{:S(2)}) copy-start(s32[256]{0:T(256)} %param.31) | copy-start | bytes 3076
  73.4 1.1 %copy-start.1 = (f32[728,256]{1,0:T(8,128)S(1)}, f32[728,256]{1,0:T(8,128)}, u32[]{:S(2)}) copy-start(f32[728,256]{1,0:T(8,128)} %shard_map.208.state_ref) | copy-start | bytes 2236420
  74.5 21.9 %copy-start.3 = (f32[2,256,256]{2,1,0:T(8,128)S(1)}, f32[2,256,256]{2,1,0:T(8,128)}, u32[]{:S(2)}) copy-start(f32[2,256,256]{2,1,0:T(8,128)} %momentum_ref.3) | copy-start | bytes 1572868
  74.5 21.9 %copy-start.5 = (f32[256,256]{1,0:T(8,128)S(1)}, f32[256,256]{1,0:T(8,128)}, u32[]{:S(2)}) copy-start(f32[256,256]{1,0:T(8,128)} %depth_ref.3) | copy-start | bytes 786436
  74.5 21.9 %copy-start.7 = (f32[256,256]{1,0:T(8,128)S(1)}, f32[256,256]{1,0:T(8,128)}, u32[]{:S(2)}) copy-start(f32[256,256]{1,0:T(8,128)} %bottom_ref.3) | copy-start | bytes 786436
  74.5 21.9 %copy-start.25 = (f32[16,128]{1,0:T(8,128)S(1)}, f32[16,128]{1,0:T(8,128)}, u32[]{:S(2)}) copy-start(f32[16,128]{1,0:T(8,128)} %get-tuple-element.56.p1_ref) | copy-start | bytes 24580
  74.5 21.9 %copy-start.26 = (f32[16,128]{1,0:T(8,128)S(1)}, f32[16,128]{1,0:T(8,128)}, u32[]{:S(2)}) copy-start(f32[16,128]{1,0:T(8,128)} %get-tuple-element.53.p2_ref) | copy-start | bytes 24580
  90.2 7.0 %collective-permute-start.8 = (f32[8,384]{1,0:T(8,128)S(1)}, f32[8,384]{1,0:T(8,128)S(1)}, u32[]{:S(2)}, u32[]{:S(2)}) collective-permute-start(f32[8,384]{1,0:T(8,128)S(1)} %get-tuple-element.49), channel_id=1, source_target_pairs={{0,8},{8,0},{16,24},{24,16},{1,9},{9,1},{17,25},{25,17},{2,10},{10... | collective-permute-start | bytes 36872 | tf_op jit(solution)/shard_map/ppermute | solution.py:552
  90.3 6.9 %collective-permute-start.9 = (f32[8,384]{1,0:T(8,128)S(1)}, f32[8,384]{1,0:T(8,128)S(1)}, u32[]{:S(2)}, u32[]{:S(2)}) collective-permute-start(f32[8,384]{1,0:T(8,128)S(1)} %get-tuple-element.50), channel_id=1, source_target_pairs={{8,16},{16,8},{9,17},{17,9},{10,18},{18,10},{11,19},{19,11},{12,20... | collective-permute-start | bytes 36872 | tf_op jit(solution)/shard_map/ppermute | solution.py:552
where the time goes:
time: 104 us
  Pallas kernels  40.8 us (39%)
  starting transfers between devices  19.2 us (18%)
  local copies, waits for them, and re-layouts  17.7 us (17%)
  blocking collectives  11.8 us (11%)
  waiting for transfers between devices  10.9 us (10%)
  other arithmetic  2.22 us (2%)
  between operations  1.04 us (1%)
    pallas_call x11, Pallas kernels, call(): pl.pallas_call(body, out_shape=shapes, in_specs=specs, out_specs=[pl.Bloc...  40.8 us
    ppermute x10, starting transfers between devices, swap(): return lax.ppermute(block, axis, pairs)  19.2 us
    unnamed x79, local copies, waits for them, and re-layouts  15 us
    all_to_all x1, blocking collectives, per_device(): lax.all_to_all(outgoing, 'gy', split_axis=0, concat_axis=0, tiled=True)  11.8 us
    ppermute x10, waiting for transfers between devices, swap(): return lax.ppermute(block, axis, pairs)  10.9 us
  transfers between devices with their start and end apart: 10, of which 4 were waited for; matrix products, arithmetic and copies ran while one was open for 6% of the time, Pallas kernels for 7%

commit v1 on v0

--- a/solution.py
+++ b/solution.py
@@ -1,5 +1,3 @@
-import functools
-
 import jax
 import jax.numpy as jnp
 from jax import lax
@@ -30,6 +28,7 @@
 BF16 = jnp.bfloat16
 NT = (((1,), (1,)), ((), ()))
 VMEM_LIMIT = 48 * 1024 * 1024
+START_LIMIT = 62 * 1024 * 1024
 
 
 def iota(shape, dim):
@@ -98,11 +97,10 @@
 
 
 def stacked_traces(trace_ref):
-    basis = trace_ref.shape[2]
     place = (
         iota((FACE_PAD, FACE_BASIS), 0) == iota((FACE_PAD, FACE_BASIS), 1)
     ).astype(F32)
-    return jnp.concatenate([exact_dot(place, trace_ref[f]) for f in range(4)], axis=0)
+    return jnp.concatenate([exact_dot(place, trace_ref[:, f, :]) for f in range(4)], axis=0)
 
 
 def spread_out(source, jac_ref, star, target, extra=None):
@@ -195,6 +193,29 @@
         ref[at : at + HALF, :] = jnp.where(left, pltpu.roll(low, CAP, 1), high)
 
 
+def start(place, *refs):
+    sources, water, refs = refs[:7], refs[7:10], refs[10:]
+    outs, refs = refs[:6], refs[6:]
+    held, (sems, heads, tails, *scratch) = refs[:7], refs[7:]
+    depth, momentum, bottom = water
+    last = depth.shape[0] - 8
+    pairs = [(sources[i], held[i]) for i in range(7)]
+    for rows, target in ((pl.ds(0, 8), heads), (pl.ds(last, 8), tails)):
+        pairs += [
+            (depth.at[rows], target.at[0]),
+            (momentum.at[0, rows], target.at[1]),
+            (momentum.at[1, rows], target.at[2]),
+            (bottom.at[rows], target.at[3]),
+        ]
+    copies = [pltpu.make_async_copy(a, b, sems.at[i]) for i, (a, b) in enumerate(pairs)]
+    for copy in copies:
+        copy.start()
+    for copy in copies:
+        copy.wait()
+    edge_rows(place, heads, tails, *outs[2:4])
+    front(place, *held, *outs, *scratch)
+
+
 def table_parts(table_ref):
     pad = jnp.zeros((WIDE - TABLE, table_ref.shape[1]), BF16)
     high, low = parts(table_ref[...])
@@ -202,18 +223,32 @@
     return jnp.concatenate(both, axis=0).astype(BF16)
 
 
-def middle(
-    q_ref, jac_ref, star_ref, stiff_ref, integral_ref, table_ref, partner_ref,
-    base_ref, outer_ref, spread_ref,
-):
+def volume(q_ref, jac_ref, star_ref, stiff_ref, integral_ref, base_ref, spread_ref):
     basis = stiff_ref.shape[1]
-    elements = q_ref.shape[1]
     star = star_weights([star_ref[0], star_ref[1], star_ref[2]])
     basis_weights = weights(side_by_side([stiff_ref[d] for d in range(3)]))
     spread_out(integral_ref, jac_ref, star, spread_ref)
     for g in range(FIELDS):
         rows = slice(g * basis, (g + 1) * basis)
         base_ref[rows, :] = q_ref[rows, :] + weighted(*basis_weights, spread_ref[g])
+
+
+def forward(p1_ref, p2_ref, *refs):
+    outs = refs[-2:]
+    for n, out in enumerate(outs):
+        at = slice((n + 1) * HALF, (n + 2) * HALF)
+        out[0:HALF, :] = refs[n][...]
+        out[HALF : 2 * HALF, :] = p1_ref[at, :]
+        out[2 * HALF : 3 * HALF, :] = p2_ref[at, :]
+        if len(refs) > 4:
+            at = 3 * HALF
+            for piece in (refs[2 + n][...], p1_ref[3 * HALF :, :], p2_ref[3 * HALF :, :]):
+                out[at : at + OCEAN_ROWS, :] = piece
+                at += OCEAN_ROWS
+
+
+def local_faces(table_ref, partner_ref, outer_ref):
+    elements = partner_ref.shape[1]
     stack = table_parts(table_ref)
     codes = iota((4 * elements, elements), 0)
     for f in range(4):
@@ -225,7 +260,7 @@
     place, base_ref, table_ref, outer_ref, partner_ref, normal_ref, speed_ref, star_ref, lift_ref,
     p1_ref, p2_ref, q1_ref, q2_ref, state_ref, flux_ref,
 ):
-    basis = lift_ref.shape[1]
+    basis = lift_ref.shape[2]
     elements = base_ref.shape[1]
     a1, c1 = unequal(place)
     blocks = [
@@ -268,15 +303,20 @@
             y = folded(dot(star, both_parts(inner + outer)))
             flux = 0.5 * speed_ref[...] * (inner - outer)
             for c in range(3):
-                flux = flux + 0.5 * normal_ref[f, c : c + 1, :] * y[c * size : (c + 1) * size]
+                flux = flux + 0.5 * normal_ref[c, f : f + 1, :] * y[c * size : (c + 1) * size]
             for g in range(FIELDS):
                 flux_ref[g, f * FACE_PAD + 8 * part : f * FACE_PAD + 8 * part + 8, :] = flux[
                     8 * g : 8 * g + 8
                 ]
-    place_lift = [
-        exact_dot(lift_ref[f], selector(FACE_BASIS, 4 * FACE_PAD, f * FACE_PAD)) for f in range(4)
-    ]
-    lift = weights(sum(place_lift))
+    lift = weights(
+        lax.dot_general(
+            selector(basis, basis, 0),
+            stacked_traces(lift_ref),
+            NT,
+            preferred_element_type=F32,
+            precision=lax.Precision.HIGHEST,
+        )
+    )
     for g in range(FIELDS):
         rows = slice(g * basis, (g + 1) * basis)
         state_ref[rows, :] = base_ref[rows, :] - weighted(*lift, flux_ref[g])
@@ -293,27 +333,36 @@
     hot = (iota((4 * elements, faces), 0) == sea_face_ref[...]).astype(F32).astype(BF16)
     coeffs = folded(dot(both_parts(sea), hot))[:FACE_BASIS]
     rates = exact_dot(interp_ref[...], coeffs)
-    sent = both_parts(jnp.concatenate([rates, sea_base_ref[...]], axis=0))
+    corners = jnp.where(
+        iota((8, faces), 0) == 0, sea_base_ref[0:1, :], sea_base_ref[1:2, :]
+    ).astype(F32)
+    sent = both_parts(jnp.concatenate([rates, corners], axis=0))
     row = sea_row_ref[...]
-    hits = (iota((faces, 128), 1) == row).astype(F32)
-    before = (iota((faces, faces), 1) < iota((faces, faces), 0)).astype(F32)
-    count = dot(before.astype(BF16), hits.astype(BF16))
-    slot = jnp.sum(count * hits, axis=1, keepdims=True).astype(jnp.int32)
-    lane = iota((faces, 2 * CAP), 1)
+    hits = (iota((tiles, faces), 0) == row).astype(F32)
+    before = (iota((faces, faces), 0) < iota((faces, faces), 1)).astype(F32)
+    count = dot(hits.astype(BF16), before.astype(BF16))
+    slot = jnp.sum(count * hits, axis=0, keepdims=True).astype(jnp.int32)
+    lane = iota((2 * CAP, faces), 0)
     mine = slot == lane % CAP
     left = iota((POINTS // 2, 2 * CAP), 1) < CAP
     left_1 = iota((1, 2 * CAP), 1) < CAP
     for j in range(tiles):
         edges = mine & (row == jnp.where(lane < CAP, j - 1, j + 1))
         inside = mine & (row == j)
-        hot = jnp.concatenate([edges.astype(F32), inside.astype(F32)], axis=1).astype(BF16)
-        got = folded(dot(sent, hot))
+        hot = jnp.concatenate([edges.astype(F32), inside.astype(F32)], axis=0).astype(BF16)
+        got = folded(lax.dot_general(sent, hot, NT, preferred_element_type=F32))
         near, own = got[:, : 2 * CAP], got[:, 2 * CAP :]
         out_ref[j, 0:POINTS, :] = near[:POINTS]
         out_ref[j, 16:24, :] = jnp.where(left, own[0:8], own[8:16])
         out_ref[j, 24:26, :] = near[POINTS : POINTS + 2]
         out_ref[j, 26:27, :] = jnp.where(left_1, own[16:17], own[17:18])
         out_ref[j, 27:32, :] = jnp.zeros((5, 2 * CAP), F32)
+
+
+def finish(*refs):
+    solid, sea, (state_ref, out_ref, flux_ref) = refs[:13], refs[13:18], refs[18:]
+    back(*solid, state_ref, flux_ref)
+    rates_out(state_ref, *sea, out_ref)
 
 
 def forced(place, got_ref, forcing_ref, s1_ref, s2_ref):
@@ -374,36 +423,51 @@
     s2_ref[...] = jnp.where(a1 > 0, head, tail)
 
 
-def edges_out(place, depth_ref, momentum_ref, bottom_ref, p1_ref, p2_ref, q1_ref, q2_ref):
+def edge_rows(place, heads, tails, p1_ref, p2_ref):
+    a1, _ = unequal(place)
+    for i in range(4):
+        head, tail = heads[i, 0:2, :], tails[i, 6:8, :]
+        one = jnp.where(a1 > 0, tail, head)
+        two = jnp.where(a1 > 0, head, tail)
+        for h in range(2):
+            at = slice(3 * HALF + 4 * i + 2 * h, 3 * HALF + 4 * i + 2 * h + 2)
+            lanes = slice(128 * h, 128 * (h + 1))
+            p1_ref[at, :] = one[:, lanes]
+            p2_ref[at, :] = two[:, lanes]
+
+
+def edge_columns(place, depth_ref, momentum_ref, bottom_ref, one_ref, two_ref):
     arrays = [depth_ref[...], momentum_ref[0], momentum_ref[1], bottom_ref[...]]
-    a1, c1 = unequal(place)
-    tile_x, tile_y = depth_ref.shape
+    _, c1 = unequal(place)
+    tile_y = depth_ref.shape[1]
     row = iota((8, tile_y), 0)
     up = jnp.where(row < 2, row + (tile_y - 2), row - 2)
     down = jnp.where(row < 2, row, row + (tile_y - 4))
     wanted = jnp.where(c1 > 0, up, down)
     hot = ((row < 4) & (wanted == iota((8, tile_y), 1))).astype(F32)
     for i, array in enumerate(arrays):
-        head, tail = array[0:2], array[tile_x - 2 : tile_x]
-        one = jnp.where(a1 > 0, tail, head)
-        two = jnp.where(a1 > 0, head, tail)
         columns = lax.dot_general(
             hot, array, NT, preferred_element_type=F32, precision=lax.Precision.HIGHEST
         )
         for h in range(2):
             at = slice(4 * i + 2 * h, 4 * i + 2 * h + 2)
             lanes = slice(128 * h, 128 * (h + 1))
-            p1_ref[at, :] = one[:, lanes]
-            p2_ref[at, :] = two[:, lanes]
-            q1_ref[at, :] = columns[0:2, lanes]
-            q2_ref[at, :] = columns[2:4, lanes]
+            one_ref[at, :] = columns[0:2, lanes]
+            two_ref[at, :] = columns[2:4, lanes]
+
+
+def volume_and_columns(place, *refs):
+    solid, water, (base_ref, one_ref, two_ref, spread_ref) = refs[:5], refs[5:8], refs[8:]
+    volume(*solid, base_ref, spread_ref)
+    edge_columns(place, *water, one_ref, two_ref)
 
 
 def widened(place, depth_ref, momentum_ref, bottom_ref, p1_ref, p2_ref, q1_ref, q2_ref, out_ref):
     tile_x, tile_y = depth_ref.shape
     a1, c1 = unequal(place)
     arrays = [depth_ref[...], momentum_ref[0], momentum_ref[1], bottom_ref[...]]
-    p1, p2, q1, q2 = p1_ref[...], p2_ref[...], q1_ref[...], q2_ref[...]
+    at = 3 * HALF
+    p1, p2, q1, q2 = p1_ref[at:, :], p2_ref[at:, :], q1_ref[at:, :], q2_ref[at:, :]
     below, above = jnp.where(a1 > 0, p2, p1), jnp.where(a1 > 0, p1, p2)
     before, after = jnp.where(c1 > 0, q2, q1), jnp.where(c1 > 0, q1, q2)
     n = OCEAN_ROWS
@@ -435,112 +499,145 @@
         out_ref[i, MARGIN : MARGIN + tile_x, tile_y:] = columns.T
 
 
-def ocean(
-    place, wide_ref, forcing_ref, s1_ref, s2_ref, out_ref, bed_ref, state, bed, cell,
+STRIP = 16
+
+
+def next_of(x):
+    return pltpu.roll(x, x.shape[1] - 1, 1)
+
+
+def previous_of(x):
+    return pltpu.roll(x, 1, 1)
+
+
+def cells(state, cell):
+    for at in range(8, cell.shape[1] - 8, 8):
+        here = slice(at, at + 8)
+        h, mx, my = state[0, here, :], state[1, here, :], state[2, here, :]
+        safe = jnp.maximum(h, depth_floor)
+        root = lax.rsqrt(safe)
+        inverse = root * root
+        c = safe * root
+        u, v = mx * inverse, my * inverse
+        half = 0.5 * h * h
+        cell[0, here, :] = mx * u + half
+        cell[1, here, :] = my * u
+        cell[2, here, :] = my * v + half
+        cell[3, here, :] = 0.5 * (jnp.abs(u) + c)
+        cell[4, here, :] = 0.5 * (jnp.abs(v) + c)
+
+
+def moved(state, cell, at, rows):
+    here, up, down = slice(at, at + rows), slice(at + 1, at + rows + 1), slice(at - 1, at + rows - 1)
+
+    def x_face(i, j):
+        wave = jnp.maximum(cell[3, i, :], cell[3, j, :])
+        u_i, u_j = [state[k, i, :] for k in range(3)], [state[k, j, :] for k in range(3)]
+        f_i = (u_i[1], cell[0, i, :], cell[1, i, :])
+        f_j = (u_j[1], cell[0, j, :], cell[1, j, :])
+        return [0.5 * (f_i[k] + f_j[k]) - wave * (u_j[k] - u_i[k]) for k in range(3)]
+
+    now = [state[k, here, :] for k in range(3)]
+    flux = (now[2], cell[1, here, :], cell[2, here, :])
+    speed = cell[4, here, :]
+    wave = jnp.maximum(speed, next_of(speed))
+    y_face = [
+        0.5 * (flux[k] + next_of(flux[k])) - wave * (next_of(now[k]) - now[k]) for k in range(3)
+    ]
+    upper, lower = x_face(here, up), x_face(down, here)
+    return [
+        now[k] - step_ocean * (upper[k] - lower[k] + y_face[k] - previous_of(y_face[k]))
+        for k in range(3)
+    ]
+
+
+def sloped(height, bed, at, rows):
+    b = bed[at : at + rows, :]
+    slope_x = 0.5 * (bed[at + 1 : at + rows + 1, :] - bed[at - 1 : at + rows - 1, :])
+    slope_y = 0.5 * (next_of(b) - previous_of(b))
+    scale = step_ocean * height
+    return scale * slope_x, scale * slope_y
+
+
+def ocean_first(
+    place, depth_ref, momentum_ref, bottom_ref, p1_ref, p2_ref, q1_ref, q2_ref, wide, state, cell
 ):
-    tile_x, tile_y = bed_ref.shape
-    span = tile_y + 128
-    a1, _ = unequal(place)
-    below = jnp.where(a1 > 0, s2_ref[...], s1_ref[...])[0:2]
-    above = jnp.where(a1 > 0, s1_ref[...], s2_ref[...])[0:2]
-    force_lo = step_ocean * below
-    force_hi = step_ocean * above
-    height = tile_x + 2 * MARGIN
-    strip = 16
-
-    def next_of(x):
-        return pltpu.roll(x, span - 1, 1)
-
-    def previous_of(x):
-        return pltpu.roll(x, 1, 1)
-
-    bed[...] = wide_ref[3]
-    bed[MARGIN : MARGIN + tile_x, :] += step_ocean * forcing_ref[...]
-    bed[MARGIN - 2 : MARGIN, :] += force_lo
-    bed[MARGIN + tile_x : MARGIN + tile_x + 2, :] += force_hi
-    lane = iota((strip, span), 1)
+    tile_x, tile_y = depth_ref.shape
+    widened(place, depth_ref, momentum_ref, bottom_ref, p1_ref, p2_ref, q1_ref, q2_ref, wide)
+    cells(wide, cell)
+    height, span = wide.shape[1:]
+    lane = iota((STRIP, span), 1)
     outside = ((lane == span - 1) & (place[1] == 0)) | (
         (lane == tile_y) & (place[1] == place[3] - 1)
     )
-
-    def cells(read, at, rows):
-        h, mx, my = (read(k, at, rows) for k in range(3))
-        safe = jnp.maximum(h, depth_floor)
-        u, v = mx / safe, my / safe
-        c = jnp.sqrt(safe)
-        half = 0.5 * h * h
-        cell[0, at : at + rows, :] = mx * u + half
-        cell[1, at : at + rows, :] = my * u
-        cell[2, at : at + rows, :] = my * v + half
-        cell[3, at : at + rows, :] = jnp.abs(u) + c
-        cell[4, at : at + rows, :] = jnp.abs(v) + c
-
-    def update(read, at, rows):
-        here, up, down = slice(at, at + rows), slice(at + 1, at + rows + 1), slice(at - 1, at + rows - 1)
-
-        def x_face(i, j):
-            wave = 0.5 * jnp.maximum(cell[3, i, :], cell[3, j, :])
-            u_i, u_j = [read(k, i) for k in range(3)], [read(k, j) for k in range(3)]
-            f_i = (u_i[1], cell[0, i, :], cell[1, i, :])
-            f_j = (u_j[1], cell[0, j, :], cell[1, j, :])
-            return [0.5 * (f_i[k] + f_j[k]) - wave * (u_j[k] - u_i[k]) for k in range(3)]
-
-        now = [read(k, here) for k in range(3)]
-        flux = (now[2], cell[1, here, :], cell[2, here, :])
-        speed = cell[4, here, :]
-        wave = 0.5 * jnp.maximum(speed, next_of(speed))
-        y_face = [
-            0.5 * (flux[k] + next_of(flux[k])) - wave * (next_of(now[k]) - now[k]) for k in range(3)
-        ]
-        upper, lower = x_face(here, up), x_face(down, here)
-        new = [
-            now[k] - step_ocean * (upper[k] - lower[k] + y_face[k] - previous_of(y_face[k]))
-            for k in range(3)
-        ]
-        b = bed[here, :]
-        slope_x = 0.5 * (bed[up, :] - bed[down, :])
-        slope_y = 0.5 * (next_of(b) - previous_of(b))
-        new[1] = new[1] - step_ocean * now[0] * slope_x
-        new[2] = new[2] - step_ocean * now[0] * slope_y
-        return new
-
-    for at in range(8, height - 8, 8):
-        cells(lambda k, i, n: wide_ref[k, i : i + n, :], at, 8)
-    for at in range(8, height - 8, strip):
-        rows = min(strip, height - 8 - at)
-        new = update(lambda k, i: wide_ref[k, i, :], at, rows)
-        out = outside[:rows]
-        row = iota((rows, span), 0) + at
-        out = out | ((row < MARGIN) & (place[0] == 0))
+    state[:, 0:8, :] = jnp.zeros((3, 8, span), F32)
+    state[:, height - 8 :, :] = jnp.zeros((3, 8, span), F32)
+    for at in range(8, height - 8, STRIP):
+        new = moved(wide, cell, at, STRIP)
+        row = iota((STRIP, span), 0) + at
+        out = outside | ((row < MARGIN) & (place[0] == 0))
         out = out | ((row >= MARGIN + tile_x) & (place[0] == place[2] - 1))
         for k in range(3):
-            state[k, at : at + rows, :] = jnp.where(out, 0.0, new[k])
-    for at in range(8, height - 8, 8):
-        cells(lambda k, i, n: state[k, i : i + n, :], at, 8)
-    bed[MARGIN : MARGIN + tile_x, :] += step_ocean * forcing_ref[...]
-    bed[MARGIN - 2 : MARGIN, :] += force_lo
-    bed[MARGIN + tile_x : MARGIN + tile_x + 2, :] += force_hi
-    for at in range(MARGIN, MARGIN + tile_x, strip):
-        new = update(lambda k, i: state[k, i, :], at, strip)
+            state[k, at : at + STRIP, :] = jnp.where(out, 0.0, new[k])
+
+
+def ocean_last(place, wide, first, forcing_ref, s1_ref, s2_ref, out_ref, bed_ref, state, bed, cell):
+    tile_x, tile_y = bed_ref.shape
+    height = wide.shape[1]
+    a1, _ = unequal(place)
+    force_lo = step_ocean * jnp.where(a1 > 0, s2_ref[...], s1_ref[...])[0:2]
+    force_hi = step_ocean * jnp.where(a1 > 0, s1_ref[...], s2_ref[...])[0:2]
+    inner = slice(MARGIN, MARGIN + tile_x)
+
+    def raised(source):
+        bed[inner, :] = source[inner, :] + step_ocean * forcing_ref[...]
+        bed[MARGIN - 2 : MARGIN, :] = source[MARGIN - 2 : MARGIN, :] + force_lo
+        above = slice(MARGIN + tile_x, MARGIN + tile_x + 2)
+        bed[above, :] = source[above, :] + force_hi
+
+    bed[0:MARGIN, :] = wide[3, 0:MARGIN, :]
+    bed[MARGIN + tile_x :, :] = wide[3, MARGIN + tile_x :, :]
+    raised(wide.at[3])
+    for at in range(8, height - 8, STRIP):
+        here = slice(at, at + STRIP)
+        change_x, change_y = sloped(wide[0, here, :], bed, at, STRIP)
+        state[0, here, :] = first[0, here, :]
+        state[1, here, :] = first[1, here, :] - change_x
+        state[2, here, :] = first[2, here, :] - change_y
+    cells(state, cell)
+    raised(bed)
+    for at in range(MARGIN, MARGIN + tile_x, STRIP):
+        new = moved(state, cell, at, STRIP)
+        change_x, change_y = sloped(state[0, at : at + STRIP, :], bed, at, STRIP)
+        new[1] -= change_x
+        new[2] -= change_y
         for k in range(3):
-            out_ref[k, at - MARGIN : at - MARGIN + strip, :] = new[k][:, :tile_y]
-    bed_ref[...] = bed[MARGIN : MARGIN + tile_x, :tile_y]
-
-
-def call(body, out_shape, *args, place=None, scratch=(), aliases=None):
-    specs = [pl.BlockSpec(memory_space=pltpu.VMEM) for _ in args]
+            out_ref[k, at - MARGIN : at - MARGIN + STRIP, :] = new[k][:, :tile_y]
+    bed_ref[...] = bed[inner, :tile_y]
+
+
+def call(body, out_shape, *args, place=None, scratch=(), held=0, copies=0, limit=VMEM_LIMIT):
+    space = pltpu.HBM if held else pltpu.VMEM
+    specs = [pl.BlockSpec(memory_space=space) for _ in args]
+    scratch = [pltpu.VMEM(s, F32) for s in scratch]
+    if held:
+        sems = pltpu.SemaphoreType.DMA((copies,))
+        scratch = [pltpu.VMEM(x.shape, x.dtype) for x in args[:held]] + [sems] + scratch
     if place is not None:
-        specs = [pl.BlockSpec(memory_space=pltpu.SMEM)] + specs
-        args = (place,) + args
+        sizes, inner = place, body
+
+        def body(*refs):
+            here = (lax.axis_index("gx"), lax.axis_index("gy"))
+            inner(here + sizes, *refs)
+
     shapes = [jax.ShapeDtypeStruct(s, F32) for s in out_shape]
     return pl.pallas_call(
         body,
         out_shape=shapes,
         in_specs=specs,
         out_specs=[pl.BlockSpec(memory_space=pltpu.VMEM) for _ in shapes],
-        scratch_shapes=[pltpu.VMEM(s, F32) for s in scratch],
-        input_output_aliases=aliases or {},
-        compiler_params=pltpu.CompilerParams(vmem_limit_bytes=VMEM_LIMIT),
+        scratch_shapes=scratch,
+        compiler_params=pltpu.CompilerParams(vmem_limit_bytes=limit),
     )(*args)
 
 
@@ -577,66 +674,73 @@
     rows = FIELDS * basis
     tile_x, tile_y = water_depth.shape
     tiles = lax.axis_size("gy")
-    place = jnp.stack(
-        [lax.axis_index("gx"), lax.axis_index("gy"), lax.axis_size("gx"), tiles]
-    ).astype(jnp.int32)
+    place = (lax.axis_size("gx"), tiles)
     speed = wave_speed.reshape(1, elements)
+    traces = trace_mats.transpose(1, 0, 2)
+    normals = face_normals.transpose(1, 0, 2)
+    lifts = lift_mats.transpose(2, 0, 1)
     spread = (FIELDS, 3 * basis, elements)
     faces = (TABLE, 4 * elements)
-    buffer = (3 * HALF, 128)
-    state = coefficients.reshape(rows, elements)
-    edge_rows = call(
-        edges_out, [(OCEAN_ROWS, 128)] * 4, water_depth, momentum, bottom, place=place
-    )
+    solid = (rows, elements)
+    wide_shape = (tile_x + 2 * MARGIN, tile_y + 128)
+    state = coefficients.reshape(solid)
     for section in range(2):
-        integral, table, p1, p2, q1, q2 = call(
-            front,
-            [(rows, elements), faces, buffer, buffer, (HALF, 128), (HALF, 128)],
-            state, jacobian, star_mats, source_mat, deriv_mats, trace_mats, send_faces,
-            place=place,
-            scratch=[spread, (rows, elements), (rows, elements), (rows, elements)],
+        fixed = (state, jacobian, star_mats, source_mat, deriv_mats, traces, send_faces)
+        scratch = [spread, solid, solid, solid]
+        if section == 0:
+            extra = OCEAN_ROWS
+            buffers = [(3 * HALF + extra, 128)] * 2 + [(HALF, 128)] * 2
+            integral, table, p1, p2, own1, own2 = call(
+                start, [solid, faces] + buffers, *fixed, water_depth, momentum, bottom,
+                place=place, scratch=[(4, 8, tile_y)] * 2 + scratch, held=len(fixed), copies=len(fixed) + 8,
+                limit=START_LIMIT,
+            )
+        else:
+            extra = 0
+            buffers = [(3 * HALF, 128)] * 2 + [(HALF, 128)] * 2
+            integral, table, p1, p2, own1, own2 = call(
+                front, [solid, faces] + buffers, *fixed, place=place, scratch=scratch
+            )
+        p2, p1 = swap(p2, "gx", 1), swap(p1, "gx", 0)
+        inside = (state, jacobian, star_mats, stiff_mats, integral)
+        own = (own1, own2)
+        if section == 0:
+            base, *columns = call(
+                volume_and_columns, [solid] + [(OCEAN_ROWS, 128)] * 2,
+                *inside, water_depth, momentum, bottom,
+                place=place, scratch=[spread],
+            )
+            own += tuple(columns)
+        else:
+            (base,) = call(volume, [solid], *inside, scratch=[spread])
+        p1, p2, base = lax.optimization_barrier((p1, p2, base))
+        q1, q2 = call(forward, [(3 * HALF + 3 * extra, 128)] * 2, p1, p2, *own)
+        q2, q1 = swap(q2, "gy", 1), swap(q1, "gy", 0)
+        (outer,) = call(local_faces, [faces], table, face_partner)
+        if section == 1:
+            wide, first = call(
+                ocean_first,
+                [(4,) + wide_shape, (3,) + wide_shape],
+                water_depth, momentum, bottom, *halos,
+                place=place, scratch=[(5,) + wide_shape],
+            )
+            q1, q2, outer, wide, first = lax.optimization_barrier((q1, q2, outer, wide, first))
+        else:
+            q1, q2, outer = lax.optimization_barrier((q1, q2, outer))
+        last = (
+            base, table, outer, face_partner, normals, speed, star_mats, lifts, p1, p2, q1, q2,
         )
-        own = (q1, q2)
+        flux = [(FIELDS, 4 * FACE_PAD, elements)]
         if section == 0:
-            p1 = jnp.concatenate([p1, edge_rows[0]], axis=0)
-            p2 = jnp.concatenate([p2, edge_rows[1]], axis=0)
-        p1, p2 = swap(p1, "gx", 0), swap(p2, "gx", 1)
-        base, outer = call(
-            middle,
-            [(rows, elements), faces],
-            state, jacobian, star_mats, stiff_mats, integral, table, face_partner,
-            scratch=[spread],
-        )
-        sent = []
-        for n in range(2):
-            at = slice((n + 1) * HALF, (n + 2) * HALF)
-            pieces = [own[n], p1[at], p2[at]]
-            if section == 0:
-                pieces += [edge_rows[2 + n], p1[3 * HALF :], p2[3 * HALF :]]
-            sent.append(jnp.concatenate(pieces, axis=0))
-        q1, q2 = swap(sent[0], "gy", 0), swap(sent[1], "gy", 1)
-        (state,) = call(
-            back,
-            [(rows, elements)],
-            base, table, outer, face_partner, face_normals, speed, star_mats, lift_mats,
-            p1, p2, q1, q2,
-            place=place,
-            scratch=[(FIELDS, 4 * FACE_PAD, elements)],
-        )
-        if section == 0:
-            (wide,) = call(
-                widened,
-                [(4, tile_x + 2 * MARGIN, tile_y + 128)],
-                water_depth, momentum, bottom,
-                p1[3 * HALF :], p2[3 * HALF :], q1[3 * HALF :], q2[3 * HALF :],
-                place=place,
+            (state,) = call(back, [solid], *last, place=place, scratch=flux)
+            halos = (p1, p2, q1, q2)
+        else:
+            state, outgoing = call(
+                finish,
+                [solid, (tiles, 32, 128)],
+                *last, traces, interp_mat, sea_face.reshape(1, -1), sea_base.T, sea_row.T,
+                place=place, scratch=flux,
             )
-    corners = jnp.pad(sea_base.T.astype(F32), ((0, 6), (0, 0)))
-    (outgoing,) = call(
-        rates_out,
-        [(tiles, 32, 128)],
-        state, trace_mats, interp_mat, sea_face.reshape(1, -1), corners, sea_row,
-    )
     incoming = lax.all_to_all(outgoing, "gy", split_axis=0, concat_axis=0, tiled=True)
     forcing, s1, s2 = call(
         forced,
@@ -644,12 +748,11 @@
         incoming,
         place=place,
     )
-    s1, s2 = swap(s1, "gx", 0), swap(s2, "gx", 1)
-    wide_shape = (tile_x + 2 * MARGIN, tile_y + 128)
+    s2, s1 = swap(s2, "gx", 1), swap(s1, "gx", 0)
     ocean_final, bed_final = call(
-        ocean,
+        ocean_last,
         [(3, tile_x, tile_y), (tile_x, tile_y)],
-        wide, forcing, s1, s2,
+        wide, first, forcing, s1, s2,
         place=place,
         scratch=[(3,) + wide_shape, wide_shape, (5,) + wide_shape],
     )

time: 104 us -> 83.2 us (0.80)
  local copies, waits for them, and re-layouts: 17.7 us -> 1.23 us
  Pallas kernels: 40.8 us -> 36.4 us
  waiting for transfers between devices: 10.9 us -> 13.9 us
  other arithmetic: 2.22 us -> 0 us
    unnamed x79 -> x46, local copies, waits for them, and re-layouts: 15 us -> 1.23 us
    pallas_call x11 -> x13, Pallas kernels: 40.8 us -> 36.4 us  [call(): pl.pallas_call(body, out_shape=shapes, in_specs=specs, out_specs=[pl.Bloc...]
    ppermute x10, waiting for transfers between devices: 10.9 us -> 13.9 us  [swap(): return lax.ppermute(block, axis, pairs)]
    slice x6 -> x0, local copies, waits for them, and re-layouts: 2.72 us -> none  [the longest x2 1.22 us: per_device(): pieces += [edge_rows[2 + n], p1[3 * HALF:], p2[3 * HALF:]]]
    concatenate x4 -> x0, other arithmetic: 1.46 us -> none  [the longest x2 1.42 us: per_device(): sent.append(jnp.concatenate(pieces, axis=0))]
  transfers between devices with their start and end apart: 10 -> 10, of which waited for: 4 -> 5; matrix products, arithmetic and copies ran while one was open for 6% -> 0% of each run, Pallas kernels for 7% -> 12%
where the time goes in v1:
time: 83.2 us; the launch traced here: 82.9 us
  Pallas kernels  36.4 us (44%)
  starting transfers between devices  18.7 us (22%)
  waiting for transfers between devices  13.9 us (17%)
  blocking collectives  11.7 us (14%)
  local copies, waits for them, and re-layouts  1.23 us (1%)
  between operations  1.06 us (1%)
    pallas_call x13, Pallas kernels, call(): pl.pallas_call(body, out_shape=shapes, in_specs=specs, out_specs=[pl.Bloc...  36.4 us
    ppermute x10, starting transfers between devices, swap(): return lax.ppermute(block, axis, pairs)  18.7 us
    ppermute x10, waiting for transfers between devices, swap(): return lax.ppermute(block, axis, pairs)  13.9 us
    all_to_all x1, blocking collectives, per_device(): lax.all_to_all(outgoing, 'gy', split_axis=0, concat_axis=0, tiled=True)  11.7 us
  transfers between devices with their start and end apart: 10, of which 5 were waited for; matrix products, arithmetic and copies ran while one was open for 0% of the time, Pallas kernels for 12%

profile of v1, /device:TPU:1, one launch (start us, length us, event | category | flops | bytes accessed | tf_op | source)
XLA Modules:
  0.0 82.9 jit_solution(6159075689506964468)
XLA Ops:
  0.6 0.0 copy-start.5
  0.6 0.0 copy-start.10
  0.7 0.0 copy-start.4
  0.7 0.0 copy-start.1
  0.7 0.0 copy-start.3
  0.7 0.0 copy-start.2
  0.7 0.0 copy-start.9
  0.7 7.9 %shard_map.202 = (f32[728,256]{1,0:T(8,128)}, f32[312,1024]{1,0:T(8,128)}, f32[496,128]{1,0:T(8,128)}, f32[496,128]{1,0:T(8,128)}, f32[160,128]{1,0:T(8,128)}, /*index=5*/f32[160,128]{1,0:T(8,128)}) custom-call(f32[728,256]{1,0:T(8,128)} %bitcast.9, f32[3,3,256]{2,1,0:T(4,128)} %jac_ref.1, f32[3,13,13]{2,1,0:T(8,128)} %refs_6_.9, f32[13,13]{1,0:T(8,128)} %refs_3_.8, ...), custom_call_target="tpu_custom_call" | custom-call | tf_op jit(solution)/shard_map/pallas_call | solution.py:634
  8.6 0.1 collective-permute-start
  8.8 4.5 %collective-permute-start.1 = (f32[496,128]{1,0:T(8,128)}, f32[496,128]{1,0:T(8,128)S(1)}, u32[]{:S(2)}, u32[]{:S(2)}) collective-permute-start(f32[496,128]{1,0:T(8,128)} %get-tuple-element.46), channel_id=1, source_target_pairs={{8,16},{16,8},{9,17},{17,9},{10,18},{18,10},{11,19},{19,11},{12,20... | collective-permute-start | bytes 761864 | tf_op jit(solution)/shard_map/ppermute | solution.py:649
  13.3 0.0 copy-done.5
  13.3 0.0 copy-done.10
  13.3 0.0 copy-done.4
  13.3 0.0 copy-done.1
  13.3 0.0 copy-done.3
  13.3 0.0 copy-done.2
  13.3 0.0 copy-done.9
  13.3 0.0 copy-start.6
  13.3 1.1 %copy-done.6 = f32[728,256]{1,0:T(8,128)S(1)} copy-done((f32[728,256]{1,0:T(8,128)S(1)}, f32[728,256]{1,0:T(8,128)}, u32[]{:S(2)}) %copy-start.6) | copy-done | bytes 745496
  14.5 2.5 %shard_map.203 = (f32[728,256]{1,0:T(8,128)S(1)}, f32[16,128]{1,0:T(8,128)S(1)}, f32[16,128]{1,0:T(8,128)S(1)}) custom-call(f32[728,256]{1,0:T(8,128)S(1)} %bitcast.10, f32[3,3,256]{2,1,0:T(4,128)S(1)} %copy-done.10, f32[3,13,13]{2,1,0:T(8,128)S(1)} %copy-done.5, f32[3,56,56]{2,1,0:T(8,128)S(1)} %copy-done.9, f32[728,256]{1,0:T(8,128)S(1)} %copy-done.6, ...), custom_call_target="tpu_custom_call" | custom-call | tf_op jit(solution)/shard_map/pallas_call | solution.py:634
  17.0 0.0 collective-permute-done.p1_ref.refs_8_.refs_3_
  17.0 0.7 collective-permute-done.1.p2_ref.refs_9_.refs_4_
  17.7 0.0 copy-done.12
  17.7 0.0 copy-done.13
  17.8 1.9 %collective-permute-start.2 = (f32[528,128]{1,0:T(8,128)S(1)}, f32[528,128]{1,0:T(8,128)S(1)}, u32[]{:S(2)}, u32[]{:S(2)}) collective-permute-start(f32[528,128]{1,0:T(8,128)S(1)} %get-tuple-element.57), channel_id=1, source_target_pairs={{0,1},{1,0},{2,3},{3,2},{4,5},{5,4},{6,7},{7,6},{8,9},{9,8},{10,11... | collective-permute-start | bytes 811016 | tf_op jit(solution)/shard_map/ppermute | solution.py:649
  19.6 0.8 %collective-permute-start.3 = (f32[528,128]{1,0:T(8,128)S(1)}, f32[528,128]{1,0:T(8,128)S(1)}, u32[]{:S(2)}, u32[]{:S(2)}) collective-permute-start(f32[528,128]{1,0:T(8,128)S(1)} %get-tuple-element.58), channel_id=1, source_target_pairs={{1,2},{2,1},{3,4},{4,3},{5,6},{6,5},{9,10},{10,9},{11,12},{12,11},... | collective-permute-start | bytes 811016 | tf_op jit(solution)/shard_map/ppermute | solution.py:649
  20.5 0.0 copy-done
  20.5 0.0 copy-start.11
  20.5 0.0 copy-start.15
  20.5 0.0 copy-start.19
  20.5 1.5 %shard_map.205.refs_2_ = f32[312,1024]{1,0:T(8,128)S(1)} custom-call(f32[312,1024]{1,0:T(8,128)S(1)} %copy-done, s32[4,256]{1,0:T(4,128)S(1)} %copy-done.14), custom_call_target="tpu_custom_call" | custom-call | tf_op jit(solution)/shard_map/pallas_call | solution.py:634
  22.1 6.5 %collective-permute-done.2.refs_10_.refs_5_ = f32[528,128]{1,0:T(8,128)S(1)} collective-permute-done((f32[528,128]{1,0:T(8,128)S(1)}, f32[528,128]{1,0:T(8,128)S(1)}, u32[]{:S(2)}, u32[]{:S(2)}) %collective-permute-start.2) | collective-permute-done | bytes 270368 | tf_op jit(solution)/shard_map/ppermute | solution.py:649
  28.6 0.0 collective-permute-done.3.refs_11_.refs_6_
  28.6 0.0 copy-done.11
  28.6 0.0 copy-start.7
  28.6 0.0 copy-start.8
  28.6 0.0 copy-start.16
  28.7 0.0 copy-start.17
  28.7 3.2 %shard_map.206.refs_0_.q_ref = f32[728,256]{1,0:T(8,128)S(1)} custom-call(f32[728,256]{1,0:T(8,128)S(1)} %get-tuple-element.49.refs_0_, f32[312,1024]{1,0:T(8,128)S(1)} %copy-done, f32[312,1024]{1,0:T(8,128)S(1)} %shard_map.205.refs_2_, s32[4,256]{1,0:T(4,128)S(1)} %copy-done.14, f32[3,4,256]{2,1,0:T(4,128)S(1)} %bitcast.16, f32[1,256]{1,0:T(1,128)S(1)} %bitcast.18, ...), custom_call_target="tpu_custom_call" | custom-call | tf_op jit(solution)/shard_map/pallas_call | solution.py:634
  31.9 5.7 %shard_map.207 = (f32[728,256]{1,0:T(8,128)S(1)}, f32[312,1024]{1,0:T(8,128)S(1)}, f32[480,128]{1,0:T(8,128)S(1)}, f32[480,128]{1,0:T(8,128)S(1)}, f32[160,128]{1,0:T(8,128)S(1)}, /*index=5*/f32[160,128]{1,0:T(8,128)S(1)}) custom-call(f32[728,256]{1,0:T(8,128)S(1)} %shard_map.206.refs_0_.q_ref, f32[3,3,256]{2,1,0:T(4,128)S(1)} %copy-done.10, ...), custom_call_target="tpu_custom_call" | custom-call | tf_op jit(solution)/shard_map/pallas_call | solution.py:634
  37.6 0.1 collective-permute-start.4
  37.7 3.1 %collective-permute-start.5 = (f32[480,128]{1,0:T(8,128)S(1)}, f32[480,128]{1,0:T(8,128)S(1)}, u32[]{:S(2)}, u32[]{:S(2)}) collective-permute-start(f32[480,128]{1,0:T(8,128)S(1)} %get-tuple-element.63), channel_id=1, source_target_pairs={{8,16},{16,8},{9,17},{17,9},{10,18},{18,10},{11,19},{19,11},{12,20... | collective-permute-start | bytes 737288 | tf_op jit(solution)/shard_map/ppermute | solution.py:649
  40.8 1.7 %shard_map.208.refs_0_ = f32[728,256]{1,0:T(8,128)S(1)} custom-call(f32[728,256]{1,0:T(8,128)S(1)} %shard_map.206.refs_0_.q_ref, f32[3,3,256]{2,1,0:T(4,128)S(1)} %copy-done.10, f32[3,13,13]{2,1,0:T(8,128)S(1)} %copy-done.5, f32[3,56,56]{2,1,0:T(8,128)S(1)} %copy-done.9, f32[728,256]{1,0:T(8,128)S(1)} %get-tuple-element.64.integral_ref), custom_call_target="tpu_custom_call" | custom-call | tf_op jit(solution)/shard_map/pallas_call | solution.py:634
  42.5 0.0 collective-permute-done.4.p1_ref.refs_8_
  42.5 3.0 %collective-permute-done.5.p2_ref.refs_9_ = f32[480,128]{1,0:T(8,128)S(1)} collective-permute-done((f32[480,128]{1,0:T(8,128)S(1)}, f32[480,128]{1,0:T(8,128)S(1)}, u32[]{:S(2)}, u32[]{:S(2)}) %collective-permute-start.5) | collective-permute-done | bytes 245792 | tf_op jit(solution)/shard_map/ppermute | solution.py:649
  45.5 2.0 %collective-permute-start.6 = (f32[480,128]{1,0:T(8,128)S(1)}, f32[480,128]{1,0:T(8,128)S(1)}, u32[]{:S(2)}, u32[]{:S(2)}) collective-permute-start(f32[480,128]{1,0:T(8,128)S(1)} %get-tuple-element.71), channel_id=1, source_target_pairs={{0,1},{1,0},{2,3},{3,2},{4,5},{5,4},{6,7},{7,6},{8,9},{9,8},{10,11... | collective-permute-start | bytes 737288 | tf_op jit(solution)/shard_map/ppermute | solution.py:649
  47.5 0.9 %collective-permute-start.7 = (f32[480,128]{1,0:T(8,128)S(1)}, f32[480,128]{1,0:T(8,128)S(1)}, u32[]{:S(2)}, u32[]{:S(2)}) collective-permute-start(f32[480,128]{1,0:T(8,128)S(1)} %get-tuple-element.72), channel_id=1, source_target_pairs={{1,2},{2,1},{3,4},{4,3},{5,6},{6,5},{9,10},{10,9},{11,12},{12,11},... | collective-permute-start | bytes 737288 | tf_op jit(solution)/shard_map/ppermute | solution.py:649
  48.4 2.4 %shard_map.211 = (f32[4,288,384]{2,1,0:T(8,128)S(1)}, f32[3,288,384]{2,1,0:T(8,128)S(1)}) custom-call(f32[256,256]{1,0:T(8,128)S(1)} %copy-done.3, f32[2,256,256]{2,1,0:T(8,128)S(1)} %copy-done.1, f32[256,256]{1,0:T(8,128)S(1)} %copy-done.4, f32[496,128]{1,0:T(8,128)S(1)} %collective-permute-done.p1_ref.refs_8_.refs_3_, ...), custom_call_target="tpu_custom_call" | custom-call | tf_op jit(solution)/shard_map/pallas_call | solution.py:634
  50.8 0.0 copy-start.18
  50.8 0.0 copy-start.20
  50.8 0.0 copy-start.21
  50.8 0.0 copy-start.22
  50.9 1.5 %shard_map.210.refs_2_ = f32[312,1024]{1,0:T(8,128)S(1)} custom-call(f32[312,1024]{1,0:T(8,128)S(1)} %get-tuple-element.66.table_ref.refs_1_, s32[4,256]{1,0:T(4,128)S(1)} %copy-done.14), custom_call_target="tpu_custom_call" | custom-call | tf_op jit(solution)/shard_map/pallas_call | solution.py:634
  52.4 2.3 %collective-permute-done.6.refs_10_ = f32[480,128]{1,0:T(8,128)S(1)} collective-permute-done((f32[480,128]{1,0:T(8,128)S(1)}, f32[480,128]{1,0:T(8,128)S(1)}, u32[]{:S(2)}, u32[]{:S(2)}) %collective-permute-start.6) | collective-permute-done | bytes 245792 | tf_op jit(solution)/shard_map/ppermute | solution.py:649
  54.7 0.0 collective-permute-done.7.refs_11_
  54.7 0.0 copy-done.21
  54.7 4.2 %shard_map.212 = (f32[728,256]{1,0:T(8,128)}, f32[8,32,128]{2,1,0:T(8,128)S(1)}) custom-call(f32[728,256]{1,0:T(8,128)S(1)} %shard_map.208.refs_0_, f32[312,1024]{1,0:T(8,128)S(1)} %get-tuple-element.66.table_ref.refs_1_, f32[312,1024]{1,0:T(8,128)S(1)} %shard_map.210.refs_2_, s32[4,256]{1,0:T(4,128)S(1)} %copy-done.14, f32[3,4,256]{2,1,0:T(4,128)S(1)} %bitcast.17, ...), custom_call_target="tpu_custom_call" | custom-call | tf_op jit(solution)/shard_map/pallas_call | solution.py:634
  59.0 11.7 %all_to_all.5.refs_0_ = f32[8,32,128]{2,1,0:T(8,128)S(1)} all-to-all(f32[8,32,128]{2,1,0:T(8,128)S(1)} %get-tuple-element.81), channel_id=1, replica_groups=mesh['gx'=4,'gy'=8] {'gy'}, dimensions={0} | all-to-all | bytes 262144 | tf_op jit(solution)/shard_map/all_to_all | solution.py:744
  70.6 2.2 %shard_map.213 = (f32[256,384]{1,0:T(8,128)S(1)}, f32[8,384]{1,0:T(8,128)S(1)}, f32[8,384]{1,0:T(8,128)S(1)}) custom-call(f32[8,32,128]{2,1,0:T(8,128)S(1)} %all_to_all.5.refs_0_), custom_call_target="tpu_custom_call" | custom-call | tf_op jit(solution)/shard_map/pallas_call | solution.py:634
  72.8 0.1 collective-permute-start.8
  72.9 5.3 %collective-permute-start.9 = (f32[8,384]{1,0:T(8,128)S(1)}, f32[8,384]{1,0:T(8,128)S(1)}, u32[]{:S(2)}, u32[]{:S(2)}) collective-permute-start(f32[8,384]{1,0:T(8,128)S(1)} %get-tuple-element.84), channel_id=1, source_target_pairs={{8,16},{16,8},{9,17},{17,9},{10,18},{18,10},{11,19},{19,11},{12,20... | collective-permute-start | bytes 36872 | tf_op jit(solution)/shard_map/ppermute | solution.py:649
  78.2 0.0 collective-permute-done.8.refs_3_
  78.2 1.4 %collective-permute-done.9.refs_4_ = f32[8,384]{1,0:T(8,128)S(1)} collective-permute-done((f32[8,384]{1,0:T(8,128)S(1)}, f32[8,384]{1,0:T(8,128)S(1)}, u32[]{:S(2)}, u32[]{:S(2)}) %collective-permute-start.9) | collective-permute-done | bytes 12320 | tf_op jit(solution)/shard_map/ppermute | solution.py:649
  79.5 3.4 %shard_map.214 = (f32[3,256,256]{2,1,0:T(8,128)}, f32[256,256]{1,0:T(8,128)}) custom-call(f32[4,288,384]{2,1,0:T(8,128)S(1)} %get-tuple-element.79.refs_0_, f32[3,288,384]{2,1,0:T(8,128)S(1)} %get-tuple-element.80.refs_1_, f32[256,384]{1,0:T(8,128)S(1)} %get-tuple-element.82.refs_2_, f32[8,384]{1,0:T(8,128)S(1)} %collective-permute-done.8.refs_3_, ...), custom_call_target="tpu_custom_call" | custom-call | tf_op jit(solution)/shard_map/pallas_call | solution.py:634
  (16 shorter events, 0.1 us)
Async XLA Ops:
  0.6 12.6 %copy-start.5 = (f32[3,13,13]{2,1,0:T(8,128)S(1)}, f32[3,13,13]{2,1,0:T(8,128)}, u32[]{:S(2)}) copy-start(f32[3,13,13]{2,1,0:T(8,128)} %refs_6_.9) | copy-start | bytes 6088
  0.6 12.6 %copy-start.10 = (f32[3,3,256]{2,1,0:T(4,128)S(1)}, f32[3,3,256]{2,1,0:T(4,128)}, u32[]{:S(2)}) copy-start(f32[3,3,256]{2,1,0:T(4,128)} %jac_ref.1) | copy-start | bytes 27652
  0.7 12.6 %copy-start.4 = (f32[256,256]{1,0:T(8,128)S(1)}, f32[256,256]{1,0:T(8,128)}, u32[]{:S(2)}) copy-start(f32[256,256]{1,0:T(8,128)} %refs_2_.7) | copy-start | bytes 786436
  0.7 12.6 %copy-start.1 = (f32[2,256,256]{2,1,0:T(8,128)S(1)}, f32[2,256,256]{2,1,0:T(8,128)}, u32[]{:S(2)}) copy-start(f32[2,256,256]{2,1,0:T(8,128)} %refs_1_.7) | copy-start | bytes 1572868
  0.7 12.6 %copy-start.3 = (f32[256,256]{1,0:T(8,128)S(1)}, f32[256,256]{1,0:T(8,128)}, u32[]{:S(2)}) copy-start(f32[256,256]{1,0:T(8,128)} %refs_0_.1) | copy-start | bytes 786436
  0.7 12.6 %copy-start.2 = (f32[13,56,256]{2,1,0:T(8,128)S(1)}, f32[13,56,256]{2,1,0:T(8,128)}, u32[]{:S(2)}) copy-start(f32[13,56,256]{2,1,0:T(8,128)} %param.19) | copy-start | bytes 2236420
  0.7 12.6 %copy-start.9 = (f32[3,56,56]{2,1,0:T(8,128)S(1)}, f32[3,56,56]{2,1,0:T(8,128)}, u32[]{:S(2)}) copy-start(f32[3,56,56]{2,1,0:T(8,128)} %stiff_ref.1) | copy-start | bytes 112900
  8.6 8.4 %collective-permute-start = (f32[496,128]{1,0:T(8,128)}, f32[496,128]{1,0:T(8,128)S(1)}, u32[]{:S(2)}, u32[]{:S(2)}) collective-permute-start(f32[496,128]{1,0:T(8,128)} %get-tuple-element.45), channel_id=1, source_target_pairs={{0,8},{8,0},{16,24},{24,16},{1,9},{9,1},{17,25},{25,17},{2,10},{10... | collective-permute-start | bytes 761864 | tf_op jit(solution)/shard_map/ppermute | solution.py:649
  8.8 9.0 %collective-permute-start.1 = (f32[496,128]{1,0:T(8,128)}, f32[496,128]{1,0:T(8,128)S(1)}, u32[]{:S(2)}, u32[]{:S(2)}) collective-permute-start(f32[496,128]{1,0:T(8,128)} %get-tuple-element.46), channel_id=1, source_target_pairs={{8,16},{16,8},{9,17},{17,9},{10,18},{18,10},{11,19},{19,11},{12,20... | collective-permute-start | bytes 761864 | tf_op jit(solution)/shard_map/ppermute | solution.py:649
  13.3 1.1 %copy-start.6 = (f32[728,256]{1,0:T(8,128)S(1)}, f32[728,256]{1,0:T(8,128)}, u32[]{:S(2)}) copy-start(f32[728,256]{1,0:T(8,128)} %get-tuple-element.47.refs_4_) | copy-start | bytes 2236420
  14.5 3.3 %copy-start.12 = (f32[160,128]{1,0:T(8,128)S(1)}, f32[160,128]{1,0:T(8,128)}, u32[]{:S(2)}) copy-start(f32[160,128]{1,0:T(8,128)} %get-tuple-element.53.refs_0_) | copy-start | bytes 245764
  14.5 3.3 %copy-start.13 = (f32[160,128]{1,0:T(8,128)S(1)}, f32[160,128]{1,0:T(8,128)}, u32[]{:S(2)}) copy-start(f32[160,128]{1,0:T(8,128)} %get-tuple-element.54.refs_1_) | copy-start | bytes 245764
  14.5 6.0 %copy-start = (f32[312,1024]{1,0:T(8,128)S(1)}, f32[312,1024]{1,0:T(8,128)}, u32[]{:S(2)}) copy-start(f32[312,1024]{1,0:T(8,128)} %get-tuple-element.50.table_ref.refs_1_) | copy-start | bytes 3833860
  14.5 6.0 %copy-start.14 = (s32[4,256]{1,0:T(4,128)S(1)}, s32[4,256]{1,0:T(4,128)}, u32[]{:S(2)}) copy-start(s32[4,256]{1,0:T(4,128)} %refs_3_.9) | copy-start | bytes 12292
  17.8 10.8 %collective-permute-start.2 = (f32[528,128]{1,0:T(8,128)S(1)}, f32[528,128]{1,0:T(8,128)S(1)}, u32[]{:S(2)}, u32[]{:S(2)}) collective-permute-start(f32[528,128]{1,0:T(8,128)S(1)} %get-tuple-element.57), channel_id=1, source_target_pairs={{0,1},{1,0},{2,3},{3,2},{4,5},{5,4},{6,7},{7,6},{8,9},{9,8},{10,11... | collective-permute-start | bytes 811016 | tf_op jit(solution)/shard_map/ppermute | solution.py:649
  19.6 9.0 %collective-permute-start.3 = (f32[528,128]{1,0:T(8,128)S(1)}, f32[528,128]{1,0:T(8,128)S(1)}, u32[]{:S(2)}, u32[]{:S(2)}) collective-permute-start(f32[528,128]{1,0:T(8,128)S(1)} %get-tuple-element.58), channel_id=1, source_target_pairs={{1,2},{2,1},{3,4},{4,3},{5,6},{6,5},{9,10},{10,9},{11,12},{12,11},... | collective-permute-start | bytes 811016 | tf_op jit(solution)/shard_map/ppermute | solution.py:649
  20.5 8.1 %copy-start.11 = (f32[4,56,21]{1,0,2:T(4,128)S(1)}, f32[4,56,21]{1,0,2:T(4,128)}, u32[]{:S(2)}) copy-start(f32[4,56,21]{1,0,2:T(4,128)} %param.28) | copy-start | bytes 56452
  20.5 8.1 %copy-start.15 = (f32[4,3,256]{2,0,1:T(4,128)S(1)}, f32[4,3,256]{2,0,1:T(4,128)}, u32[]{:S(2)}) copy-start(f32[4,3,256]{2,0,1:T(4,128)} %param.21) | copy-start | bytes 36868
  20.5 8.1 %copy-start.19 = (f32[256]{0:T(256)S(1)}, f32[256]{0:T(256)}, u32[]{:S(2)}) copy-start(f32[256]{0:T(256)} %param.22) | copy-start | bytes 3076
  28.6 3.3 %copy-start.7 = (f32[4,21,56]{2,0,1:T(4,128)S(1)}, f32[4,21,56]{2,0,1:T(4,128)}, u32[]{:S(2)}) copy-start(f32[4,21,56]{2,0,1:T(4,128)} %param.27) | copy-start | bytes 56452
  28.6 3.3 %copy-start.8 = (f32[3,56,56]{2,1,0:T(8,128)S(1)}, f32[3,56,56]{2,1,0:T(8,128)}, u32[]{:S(2)}) copy-start(f32[3,56,56]{2,1,0:T(8,128)} %refs_4_.3) | copy-start | bytes 112900
  28.6 3.3 %copy-start.16 = (f32[13,13]{1,0:T(8,128)S(1)}, f32[13,13]{1,0:T(8,128)}, u32[]{:S(2)}) copy-start(f32[13,13]{1,0:T(8,128)} %refs_3_.8) | copy-start | bytes 2032
  28.7 3.3 %copy-start.17 = (s32[8,64]{1,0:T(8,128)S(1)}, s32[8,64]{1,0:T(8,128)}, u32[]{:S(2)}) copy-start(s32[8,64]{1,0:T(8,128)} %refs_6_.8) | copy-start | bytes 6148
  37.6 4.9 %collective-permute-start.4 = (f32[480,128]{1,0:T(8,128)S(1)}, f32[480,128]{1,0:T(8,128)S(1)}, u32[]{:S(2)}, u32[]{:S(2)}) collective-permute-start(f32[480,128]{1,0:T(8,128)S(1)} %get-tuple-element.62), channel_id=1, source_target_pairs={{0,8},{8,0},{16,24},{24,16},{1,9},{9,1},{17,25},{25,17},{2,10},{10... | collective-permute-start | bytes 737288 | tf_op jit(solution)/shard_map/ppermute | solution.py:649
  37.7 7.8 %collective-permute-start.5 = (f32[480,128]{1,0:T(8,128)S(1)}, f32[480,128]{1,0:T(8,128)S(1)}, u32[]{:S(2)}, u32[]{:S(2)}) collective-permute-start(f32[480,128]{1,0:T(8,128)S(1)} %get-tuple-element.63), channel_id=1, source_target_pairs={{8,16},{16,8},{9,17},{17,9},{10,18},{18,10},{11,19},{19,11},{12,20... | collective-permute-start | bytes 737288 | tf_op jit(solution)/shard_map/ppermute | solution.py:649
  45.5 9.1 %collective-permute-start.6 = (f32[480,128]{1,0:T(8,128)S(1)}, f32[480,128]{1,0:T(8,128)S(1)}, u32[]{:S(2)}, u32[]{:S(2)}) collective-permute-start(f32[480,128]{1,0:T(8,128)S(1)} %get-tuple-element.71), channel_id=1, source_target_pairs={{0,1},{1,0},{2,3},{3,2},{4,5},{5,4},{6,7},{7,6},{8,9},{9,8},{10,11... | collective-permute-start | bytes 737288 | tf_op jit(solution)/shard_map/ppermute | solution.py:649
  47.5 7.1 %collective-permute-start.7 = (f32[480,128]{1,0:T(8,128)S(1)}, f32[480,128]{1,0:T(8,128)S(1)}, u32[]{:S(2)}, u32[]{:S(2)}) collective-permute-start(f32[480,128]{1,0:T(8,128)S(1)} %get-tuple-element.72), channel_id=1, source_target_pairs={{1,2},{2,1},{3,4},{4,3},{5,6},{6,5},{9,10},{10,9},{11,12},{12,11},... | collective-permute-start | bytes 737288 | tf_op jit(solution)/shard_map/ppermute | solution.py:649
  50.8 3.9 %copy-start.18 = (f32[16,21]{1,0:T(8,128)S(1)}, f32[16,21]{1,0:T(8,128)}, u32[]{:S(2)}) copy-start(f32[16,21]{1,0:T(8,128)} %refs_13_.1) | copy-start | bytes 4036
  50.8 3.9 %copy-start.20 = (s32[256,2]{0,1:T(2,128)S(1)}, s32[256,2]{0,1:T(2,128)}, u32[]{:S(2)}) copy-start(s32[256,2]{0,1:T(2,128)} %param.33) | copy-start | bytes 6148
  50.8 3.9 %copy-start.21 = (s32[256]{0:T(256)S(1)}, s32[256]{0:T(256)}, u32[]{:S(2)}) copy-start(s32[256]{0:T(256)} %param.31) | copy-start | bytes 3076
  50.8 3.9 %copy-start.22 = (s32[256,1]{0,1:T(1,128)S(1)}, s32[256,1]{0,1:T(1,128)}, u32[]{:S(2)}) copy-start(s32[256,1]{0,1:T(1,128)} %param.32) | copy-start | bytes 3076
  72.8 5.4 %collective-permute-start.8 = (f32[8,384]{1,0:T(8,128)S(1)}, f32[8,384]{1,0:T(8,128)S(1)}, u32[]{:S(2)}, u32[]{:S(2)}) collective-permute-start(f32[8,384]{1,0:T(8,128)S(1)} %get-tuple-element.83), channel_id=1, source_target_pairs={{0,8},{8,0},{16,24},{24,16},{1,9},{9,1},{17,25},{25,17},{2,10},{10... | collective-permute-start | bytes 36872 | tf_op jit(solution)/shard_map/ppermute | solution.py:649
  72.9 6.7 %collective-permute-start.9 = (f32[8,384]{1,0:T(8,128)S(1)}, f32[8,384]{1,0:T(8,128)S(1)}, u32[]{:S(2)}, u32[]{:S(2)}) collective-permute-start(f32[8,384]{1,0:T(8,128)S(1)} %get-tuple-element.84), channel_id=1, source_target_pairs={{8,16},{16,8},{9,17},{17,9},{10,18},{18,10},{11,19},{19,11},{12,20... | collective-permute-start | bytes 36872 | tf_op jit(solution)/shard_map/ppermute | solution.py:649

commit v2 on v1

--- a/solution.py
+++ b/solution.py
@@ -13,8 +13,8 @@
 STEPS_OCEAN = 2
 CAP = 64
 TABLE = FIELDS * FACE_PAD
-HALF = 160
-WIDE = 2 * HALF
+WIDE = 320
+HALF = 144
 OCEAN_ROWS = 16
 MARGIN = 16
 
@@ -146,18 +146,22 @@
 
 def front(
     place, q_ref, jac_ref, star_ref, source_ref, deriv_ref, trace_ref, send_ref,
-    integral_ref, table_ref, p1_ref, p2_ref, q1_ref, q2_ref, spread_ref, relaxed_ref, d1_ref, d2_ref,
+    integral_ref, table_ref, p1_ref, p2_ref, own1_ref, own2_ref,
+    spread_ref, relaxed_ref, d1_ref, d2_ref, packed_ref, ready=lambda *numbers: None, made=lambda *numbers: None,
 ):
+    elements = q_ref.shape[1]
+    ready(2, 3)
+    star = star_weights([star_ref[0], star_ref[1], star_ref[2], source_ref[...]])
+    ready(4, 5)
     basis = deriv_ref.shape[1]
-    elements = q_ref.shape[1]
-    star = star_weights([star_ref[0], star_ref[1], star_ref[2], source_ref[...]])
     basis_weights = weights(side_by_side([deriv_ref[d] for d in range(3)]))
+    trace = weights(stacked_traces(trace_ref))
+    ready(0, 1)
     derivative(q_ref, d1_ref, jac_ref, star, basis_weights, spread_ref, relaxed_ref)
     derivative(d1_ref, d2_ref, jac_ref, star, basis_weights, spread_ref, relaxed_ref)
     first = step_solid
     second = first * step_solid / 2
     third = second * step_solid / 3
-    trace = weights(stacked_traces(trace_ref))
     for g in range(FIELDS):
         rows = slice(g * basis, (g + 1) * basis)
         whole = first * q_ref[rows, :] + second * d1_ref[rows, :] + third * d2_ref[rows, :]
@@ -167,6 +171,8 @@
             table_ref[g * FACE_PAD : (g + 1) * FACE_PAD, f * elements : (f + 1) * elements] = faces[
                 f * FACE_PAD : (f + 1) * FACE_PAD
             ]
+    made(0, 1)
+    ready(6)
     a1, c1 = unequal(place)
     picks = [
         (p1_ref, 0, column_block(a1)),
@@ -175,28 +181,49 @@
         (p1_ref, 2 * HALF, column_block(a1) - c1),
         (p2_ref, HALF, column_block(-a1) + c1),
         (p2_ref, 2 * HALF, column_block(-a1) - c1),
-        (q1_ref, 0, row_block(c1)),
-        (q2_ref, 0, row_block(-c1)),
+        (own1_ref, 0, row_block(c1)),
+        (own2_ref, 0, row_block(-c1)),
     ]
     stack = table_parts(table_ref)
     left = iota((HALF, 2 * CAP), 1) < CAP
-    codes = iota((4 * elements, 2 * CAP), 0)
-    for n in range(0, 8, 2):
-        wanted = jnp.concatenate(
-            [send_ref[pl.ds(picks[n][2], 1), :], send_ref[pl.ds(picks[n + 1][2], 1), :]], axis=1
-        )
+    codes = iota((4 * elements, 4 * CAP), 0)
+    packed_ref[FIELDS * FACE_BASIS :, :] = jnp.zeros((2 * HALF - FIELDS * FACE_BASIS, 4 * CAP), F32)
+    for n in range(0, 8, 4):
+        wanted = jnp.concatenate([send_ref[pl.ds(pick[2], 1), :] for pick in picks[n : n + 4]], axis=1)
         got = folded(dot(stack, (codes == wanted).astype(F32).astype(BF16)))
-        low, high = got[:HALF], got[HALF:]
-        ref, at, _ = picks[n]
-        ref[at : at + HALF, :] = jnp.where(left, low, pltpu.roll(high, CAP, 1))
-        ref, at, _ = picks[n + 1]
-        ref[at : at + HALF, :] = jnp.where(left, pltpu.roll(low, CAP, 1), high)
+        pack(got, packed_ref)
+        for pair in range(2):
+            lanes = slice(pair * 2 * CAP, (pair + 1) * 2 * CAP)
+            low, high = packed_ref[0:HALF, lanes], packed_ref[HALF:, lanes]
+            ref, at, _ = picks[n + 2 * pair]
+            ref[at : at + HALF, :] = jnp.where(left, low, pltpu.roll(high, CAP, 1))
+            ref, at, _ = picks[n + 2 * pair + 1]
+            ref[at : at + HALF, :] = jnp.where(left, pltpu.roll(low, CAP, 1), high)
+
+
+def pack(table, packed_ref):
+    rest = FACE_BASIS - 16
+    for g in range(FIELDS):
+        packed_ref[16 * g : 16 * (g + 1), :] = table[FACE_PAD * g : FACE_PAD * g + 16]
+        at = 16 * FIELDS + rest * g
+        packed_ref[at : at + rest, :] = table[FACE_PAD * g + 16 : FACE_PAD * g + FACE_BASIS]
+
+
+def unpack(packed_ref, table_ref):
+    rest = FACE_BASIS - 16
+    for g in range(FIELDS):
+        table_ref[FACE_PAD * g : FACE_PAD * g + 16, :] = packed_ref[16 * g : 16 * (g + 1), :]
+        at = 16 * FIELDS + rest * g
+        last = FACE_PAD * g + 16
+        table_ref[last : last + 8, :] = jnp.zeros((8, table_ref.shape[1]), F32)
+        table_ref[last : last + rest, :] = packed_ref[at : at + rest, :]
 
 
 def start(place, *refs):
     sources, water, refs = refs[:7], refs[7:10], refs[10:]
-    outs, refs = refs[:6], refs[6:]
-    held, (sems, heads, tails, *scratch) = refs[:7], refs[7:]
+    targets, refs = refs[:6], refs[6:]
+    held, (sems, heads, tails), refs = refs[:7], refs[7:10], refs[10:]
+    outs, scratch = refs[:6], refs[6:]
     depth, momentum, bottom = water
     last = depth.shape[0] - 8
     pairs = [(sources[i], held[i]) for i in range(7)]
@@ -207,13 +234,25 @@
             (momentum.at[1, rows], target.at[2]),
             (bottom.at[rows], target.at[3]),
         ]
+    first_out = len(pairs)
+    pairs += list(zip(outs, targets))
     copies = [pltpu.make_async_copy(a, b, sems.at[i]) for i, (a, b) in enumerate(pairs)]
-    for copy in copies:
+    for copy in copies[:first_out]:
         copy.start()
-    for copy in copies:
-        copy.wait()
+
+    def ready(*numbers):
+        for i in numbers:
+            copies[i].wait()
+
+    def made(*numbers):
+        for i in numbers:
+            copies[first_out + i].start()
+
+    front(place, *held, *outs, *scratch, ready=ready, made=made)
+    ready(*range(7, first_out))
     edge_rows(place, heads, tails, *outs[2:4])
-    front(place, *held, *outs, *scratch)
+    made(2, 3, 4, 5)
+    ready(*range(first_out, len(copies)))
 
 
 def table_parts(table_ref):
@@ -233,18 +272,24 @@
         base_ref[rows, :] = q_ref[rows, :] + weighted(*basis_weights, spread_ref[g])
 
 
-def forward(p1_ref, p2_ref, *refs):
+def forward(place, p1_ref, p2_ref, *refs):
     outs = refs[-2:]
+    _, c1 = unequal(place)
     for n, out in enumerate(outs):
         at = slice((n + 1) * HALF, (n + 2) * HALF)
-        out[0:HALF, :] = refs[n][...]
-        out[HALF : 2 * HALF, :] = p1_ref[at, :]
-        out[2 * HALF : 3 * HALF, :] = p2_ref[at, :]
+        out[0:HALF, :] = p1_ref[at, :]
+        out[HALF : 2 * HALF, :] = p2_ref[at, :]
+        out[2 * HALF : 3 * HALF, :] = refs[n][...]
         if len(refs) > 4:
-            at = 3 * HALF
-            for piece in (refs[2 + n][...], p1_ref[3 * HALF :, :], p2_ref[3 * HALF :, :]):
-                out[at : at + OCEAN_ROWS, :] = piece
-                at += OCEAN_ROWS
+            at = 3 * HALF + OCEAN_ROWS
+            out[3 * HALF : at, :] = refs[2 + n][...]
+            for p_ref in (p1_ref, p2_ref):
+                rows = p_ref[3 * HALF :, :]
+                for i in range(4):
+                    low, high = rows[4 * i : 4 * i + 2], rows[4 * i + 2 : 4 * i + 4]
+                    ends = (high, low) if n == 0 else (low, high)
+                    out[at : at + 2, :] = jnp.where(c1 > 0, *ends)
+                    at += 2
 
 
 def local_faces(table_ref, partner_ref, outer_ref):
@@ -256,34 +301,29 @@
         outer_ref[:, f * elements : (f + 1) * elements] = folded(dot(stack, hot))[:TABLE]
 
 
-def back(
-    place, base_ref, table_ref, outer_ref, partner_ref, normal_ref, speed_ref, star_ref, lift_ref,
-    p1_ref, p2_ref, q1_ref, q2_ref, state_ref, flux_ref,
-):
-    basis = lift_ref.shape[2]
-    elements = base_ref.shape[1]
+def remote_faces(place, outer_ref, partner_ref, table_refs, packed_ref, table_ref):
+    p1_ref, p2_ref, q1_ref, q2_ref = table_refs
+    elements = partner_ref.shape[1]
     a1, c1 = unequal(place)
     blocks = [
         (p1_ref, 0, column_block(a1)),
         (p2_ref, 0, column_block(-a1)),
-        (q1_ref, 0, row_block(c1)),
-        (q1_ref, HALF, column_block(a1) + c1),
-        (q1_ref, 2 * HALF, column_block(-a1) + c1),
-        (q2_ref, 0, row_block(-c1)),
-        (q2_ref, HALF, column_block(a1) - c1),
-        (q2_ref, 2 * HALF, column_block(-a1) - c1),
+        (q1_ref, 2 * HALF, row_block(c1)),
+        (q2_ref, 2 * HALF, row_block(-c1)),
+        (q1_ref, 0, column_block(a1) + c1),
+        (q1_ref, HALF, column_block(-a1) + c1),
+        (q2_ref, 0, column_block(a1) - c1),
+        (q2_ref, HALF, column_block(-a1) - c1),
     ]
     left = iota((HALF, 2 * CAP), 1) < CAP
-    tops, bottoms = [], []
     for n in range(0, 8, 2):
         one = blocks[n][0][blocks[n][1] : blocks[n][1] + HALF, :]
         two = blocks[n + 1][0][blocks[n + 1][1] : blocks[n + 1][1] + HALF, :]
-        tops.append(jnp.where(left, one, pltpu.roll(two, CAP, 1)))
-        bottoms.append(jnp.where(left, pltpu.roll(one, CAP, 1), two))
-    remote = jnp.concatenate(
-        [jnp.concatenate(tops, axis=1), jnp.concatenate(bottoms, axis=1)], axis=0
-    )
-    remote = both_parts(remote)
+        lanes = slice(n * CAP, (n + 2) * CAP)
+        packed_ref[0:HALF, lanes] = jnp.where(left, one, pltpu.roll(two, CAP, 1))
+        packed_ref[HALF:, lanes] = jnp.where(left, pltpu.roll(one, CAP, 1), two)
+    unpack(packed_ref, table_ref)
+    remote = table_parts(table_ref)
     slot = iota((CAP, elements), 0)
     for f in range(4):
         wanted = partner_ref[f : f + 1, :] - 4 * elements
@@ -292,6 +332,24 @@
         ).astype(BF16)
         columns = slice(f * elements, (f + 1) * elements)
         outer_ref[:, columns] += folded(dot(remote, hot))[:TABLE]
+
+
+def lift_weights(lift_ref):
+    basis = lift_ref.shape[2]
+    return weights(
+        lax.dot_general(
+            selector(basis, basis, 0),
+            stacked_traces(lift_ref),
+            NT,
+            preferred_element_type=F32,
+            precision=lax.Precision.HIGHEST,
+        )
+    )
+
+
+def lifted(base_ref, table_ref, outer_ref, normal_ref, speed_ref, star_ref, lift_ref, state_ref, flux_ref):
+    basis = lift_ref.shape[2]
+    elements = base_ref.shape[1]
     star = star_weights([star_ref[0], star_ref[1], star_ref[2]])
     size = FIELDS * 8
     for part in range(FACE_PAD // 8):
@@ -308,26 +366,26 @@
                 flux_ref[g, f * FACE_PAD + 8 * part : f * FACE_PAD + 8 * part + 8, :] = flux[
                     8 * g : 8 * g + 8
                 ]
-    lift = weights(
-        lax.dot_general(
-            selector(basis, basis, 0),
-            stacked_traces(lift_ref),
-            NT,
-            preferred_element_type=F32,
-            precision=lax.Precision.HIGHEST,
-        )
-    )
+    lift = lift_weights(lift_ref)
     for g in range(FIELDS):
         rows = slice(g * basis, (g + 1) * basis)
         state_ref[rows, :] = base_ref[rows, :] - weighted(*lift, flux_ref[g])
 
 
-def rates_out(state_ref, trace_ref, interp_ref, sea_face_ref, sea_base_ref, sea_row_ref, out_ref):
-    basis = trace_ref.shape[2]
-    elements = state_ref.shape[1]
+def back(
+    place, base_ref, table_ref, outer_ref, partner_ref, normal_ref, speed_ref, star_ref, lift_ref,
+    p1_ref, p2_ref, q1_ref, q2_ref,
+    state_ref, flux_ref, packed_ref, remote_ref,
+):
+    arrived = (p1_ref, p2_ref, q1_ref, q2_ref)
+    remote_faces(place, outer_ref, partner_ref, arrived, packed_ref, remote_ref)
+    lifted(base_ref, table_ref, outer_ref, normal_ref, speed_ref, star_ref, lift_ref, state_ref, flux_ref)
+
+
+def rates_out(vertical, trace_ref, interp_ref, sea_face_ref, sea_base_ref, sea_row_ref, out_ref):
+    elements = vertical.shape[1]
     faces = sea_face_ref.shape[1]
     tiles = out_ref.shape[0]
-    vertical = state_ref[vertical_field * basis : (vertical_field + 1) * basis, :]
     sea = weighted(*weights(stacked_traces(trace_ref)), vertical)
     sea = jnp.concatenate([sea[f * FACE_PAD : (f + 1) * FACE_PAD] for f in range(4)], axis=1)
     hot = (iota((4 * elements, faces), 0) == sea_face_ref[...]).astype(F32).astype(BF16)
@@ -360,9 +418,11 @@
 
 
 def finish(*refs):
-    solid, sea, (state_ref, out_ref, flux_ref) = refs[:13], refs[13:18], refs[18:]
-    back(*solid, state_ref, flux_ref)
-    rates_out(state_ref, *sea, out_ref)
+    solid, sea, (state_ref, out_ref, *scratch) = refs[:13], refs[13:18], refs[18:]
+    back(*solid, state_ref, *scratch)
+    basis = sea[0].shape[2]
+    vertical = state_ref[vertical_field * basis : (vertical_field + 1) * basis, :]
+    rates_out(vertical, *sea, out_ref)
 
 
 def forced(place, got_ref, forcing_ref, s1_ref, s2_ref):
@@ -466,15 +526,21 @@
     tile_x, tile_y = depth_ref.shape
     a1, c1 = unequal(place)
     arrays = [depth_ref[...], momentum_ref[0], momentum_ref[1], bottom_ref[...]]
-    at = 3 * HALF
-    p1, p2, q1, q2 = p1_ref[at:, :], p2_ref[at:, :], q1_ref[at:, :], q2_ref[at:, :]
-    below, above = jnp.where(a1 > 0, p2, p1), jnp.where(a1 > 0, p1, p2)
-    before, after = jnp.where(c1 > 0, q2, q1), jnp.where(c1 > 0, q1, q2)
+    p1, p2 = p1_ref[3 * HALF :, :], p2_ref[3 * HALF :, :]
+    q1, q2 = q1_ref[3 * HALF :, :], q2_ref[3 * HALF :, :]
+    is_below, is_above = place[0] > 0, place[0] < place[2] - 1
+    below = jnp.where(is_below, jnp.where(a1 > 0, p2, p1), 0.0)
+    above = jnp.where(is_above, jnp.where(a1 > 0, p1, p2), 0.0)
+    before = jnp.where(place[1] > 0, jnp.where(c1 > 0, q2, q1), 0.0)
+    after = jnp.where(place[1] < place[3] - 1, jnp.where(c1 > 0, q1, q2), 0.0)
     n = OCEAN_ROWS
 
     def ends(rows):
-        one, two = rows[n : 2 * n], rows[2 * n :]
-        return jnp.where(a1 > 0, two, one), jnp.where(a1 > 0, one, two)
+        one, two = rows[n : n + 8], rows[n + 8 :]
+        return (
+            jnp.where(is_below, jnp.where(a1 > 0, two, one), 0.0),
+            jnp.where(is_above, jnp.where(a1 > 0, one, two), 0.0),
+        )
 
     before_below, before_above = ends(before)
     after_below, after_above = ends(after)
@@ -491,7 +557,8 @@
         ):
             out_ref[i, at : at + 2, 0:128] = rows[first]
             out_ref[i, at : at + 2, 128:256] = rows[second]
-            corner = jnp.where(low, right[first], jnp.where(high, left[second], 0.0))
+            end = slice(2 * i, 2 * i + 2)
+            corner = jnp.where(low, right[end], jnp.where(high, left[end], 0.0))
             out_ref[i, at : at + 2, 256:384] = corner
         start = jnp.concatenate([after[first], after[second]], axis=1)
         finish = jnp.concatenate([before[first], before[second]], axis=1)
@@ -586,7 +653,9 @@
     height = wide.shape[1]
     a1, _ = unequal(place)
     force_lo = step_ocean * jnp.where(a1 > 0, s2_ref[...], s1_ref[...])[0:2]
+    force_lo = jnp.where(place[0] > 0, force_lo, 0.0)
     force_hi = step_ocean * jnp.where(a1 > 0, s1_ref[...], s2_ref[...])[0:2]
+    force_hi = jnp.where(place[0] < place[2] - 1, force_hi, 0.0)
     inner = slice(MARGIN, MARGIN + tile_x)
 
     def raised(source):
@@ -620,6 +689,7 @@
     space = pltpu.HBM if held else pltpu.VMEM
     specs = [pl.BlockSpec(memory_space=space) for _ in args]
     scratch = [pltpu.VMEM(s, F32) for s in scratch]
+    outer_space = pltpu.HBM if held else pltpu.VMEM
     if held:
         sems = pltpu.SemaphoreType.DMA((copies,))
         scratch = [pltpu.VMEM(x.shape, x.dtype) for x in args[:held]] + [sems] + scratch
@@ -635,17 +705,20 @@
         body,
         out_shape=shapes,
         in_specs=specs,
-        out_specs=[pl.BlockSpec(memory_space=pltpu.VMEM) for _ in shapes],
+        out_specs=[pl.BlockSpec(memory_space=outer_space) for _ in shapes],
         scratch_shapes=scratch,
         compiler_params=pltpu.CompilerParams(vmem_limit_bytes=limit),
     )(*args)
 
 
-def swap(block, axis, parity):
+def swap(block, axis, parity, wrap=False):
     count = lax.axis_size(axis)
+    last = count + parity - 1 if wrap else count - 1
     pairs = []
-    for i in range(parity, count - 1, 2):
-        pairs += [(i, i + 1), (i + 1, i)]
+    for i in range(parity, last, 2):
+        pairs += [(i, (i + 1) % count), ((i + 1) % count, i)]
+    taken = {source for source, _ in pairs}
+    pairs += [(i, i) for i in range(count) if i not in taken]
     return lax.ppermute(block, axis, pairs)
 
 
@@ -684,37 +757,36 @@
     solid = (rows, elements)
     wide_shape = (tile_x + 2 * MARGIN, tile_y + 128)
     state = coefficients.reshape(solid)
+    packed = (2 * HALF, 8 * CAP)
     for section in range(2):
         fixed = (state, jacobian, star_mats, source_mat, deriv_mats, traces, send_faces)
-        scratch = [spread, solid, solid, solid]
+        scratch = [spread, solid, solid, solid, (2 * HALF, 4 * CAP)]
         if section == 0:
-            extra = OCEAN_ROWS
-            buffers = [(3 * HALF + extra, 128)] * 2 + [(HALF, 128)] * 2
+            buffers = [(3 * HALF + OCEAN_ROWS, 128)] * 2 + [(HALF, 128)] * 2
             integral, table, p1, p2, own1, own2 = call(
                 start, [solid, faces] + buffers, *fixed, water_depth, momentum, bottom,
-                place=place, scratch=[(4, 8, tile_y)] * 2 + scratch, held=len(fixed), copies=len(fixed) + 8,
-                limit=START_LIMIT,
+                place=place, scratch=[(4, 8, tile_y)] * 2 + [solid, faces] + buffers + scratch,
+                held=len(fixed), copies=len(fixed) + 14, limit=START_LIMIT,
             )
         else:
-            extra = 0
             buffers = [(3 * HALF, 128)] * 2 + [(HALF, 128)] * 2
             integral, table, p1, p2, own1, own2 = call(
                 front, [solid, faces] + buffers, *fixed, place=place, scratch=scratch
             )
         p2, p1 = swap(p2, "gx", 1), swap(p1, "gx", 0)
         inside = (state, jacobian, star_mats, stiff_mats, integral)
-        own = (own1, own2)
         if section == 0:
             base, *columns = call(
                 volume_and_columns, [solid] + [(OCEAN_ROWS, 128)] * 2,
                 *inside, water_depth, momentum, bottom,
                 place=place, scratch=[spread],
             )
-            own += tuple(columns)
+            size = 3 * HALF + 2 * OCEAN_ROWS
         else:
             (base,) = call(volume, [solid], *inside, scratch=[spread])
+            columns, size = [], 3 * HALF
         p1, p2, base = lax.optimization_barrier((p1, p2, base))
-        q1, q2 = call(forward, [(3 * HALF + 3 * extra, 128)] * 2, p1, p2, *own)
+        q1, q2 = call(forward, [(size, 128)] * 2, p1, p2, own1, own2, *columns, place=place)
         q2, q1 = swap(q2, "gy", 1), swap(q1, "gy", 0)
         (outer,) = call(local_faces, [faces], table, face_partner)
         if section == 1:
@@ -727,19 +799,23 @@
             q1, q2, outer, wide, first = lax.optimization_barrier((q1, q2, outer, wide, first))
         else:
             q1, q2, outer = lax.optimization_barrier((q1, q2, outer))
-        last = (
-            base, table, outer, face_partner, normals, speed, star_mats, lifts, p1, p2, q1, q2,
-        )
-        flux = [(FIELDS, 4 * FACE_PAD, elements)]
+        fixed = (normals, speed, star_mats, lifts)
+        arrived = (p1, p2, q1, q2)
+        flux = (FIELDS, 4 * FACE_PAD, elements)
+        remote = (TABLE, 8 * CAP)
         if section == 0:
-            (state,) = call(back, [solid], *last, place=place, scratch=flux)
+            (state,) = call(
+                back, [solid], base, table, outer, face_partner, *fixed, *arrived,
+                place=place, scratch=[flux, packed, remote],
+            )
             halos = (p1, p2, q1, q2)
         else:
             state, outgoing = call(
                 finish,
                 [solid, (tiles, 32, 128)],
-                *last, traces, interp_mat, sea_face.reshape(1, -1), sea_base.T, sea_row.T,
-                place=place, scratch=flux,
+                base, table, outer, face_partner, *fixed, *arrived,
+                traces, interp_mat, sea_face.reshape(1, -1), sea_base.T, sea_row.T,
+                place=place, scratch=[flux, packed, remote],
             )
     incoming = lax.all_to_all(outgoing, "gy", split_axis=0, concat_axis=0, tiled=True)
     forcing, s1, s2 = call(
@@ -748,7 +824,7 @@
         incoming,
         place=place,
     )
-    s2, s1 = swap(s2, "gx", 1), swap(s1, "gx", 0)
+    s2, s1 = swap(s2, "gx", 1, wrap=True), swap(s1, "gx", 0)
     ocean_final, bed_final = call(
         ocean_last,
         [(3, tile_x, tile_y), (tile_x, tile_y)],

time: 83.2 us -> 79.4 us (0.954)
  starting transfers between devices: 18.7 us -> 16.6 us
  waiting for transfers between devices: 13.9 us -> 12.4 us
    ppermute x10, starting transfers between devices: 18.7 us -> 16.6 us  [swap(): return lax.ppermute(block, axis, pairs)]
    ppermute x10, waiting for transfers between devices: 13.9 us -> 12.4 us  [swap(): return lax.ppermute(block, axis, pairs)]
where the time goes in v2:
time: 79.4 us; the launch traced here: 78.7 us
  Pallas kernels  35.8 us (45%)
  starting transfers between devices  16.6 us (21%)
  waiting for transfers between devices  12.4 us (16%)
  blocking collectives  11.6 us (15%)
  local copies, waits for them, and re-layouts  1.23 us (2%)
  between operations  1.05 us (1%)
    pallas_call x13, Pallas kernels, call(): pl.pallas_call(body, out_shape=shapes, in_specs=specs, out_specs=[pl.Bloc...  35.8 us
    ppermute x10, starting transfers between devices, swap(): return lax.ppermute(block, axis, pairs)  16.6 us
    ppermute x10, waiting for transfers between devices, swap(): return lax.ppermute(block, axis, pairs)  12.4 us
    all_to_all x1, blocking collectives, per_device(): lax.all_to_all(outgoing, 'gy', split_axis=0, concat_axis=0, tiled=True)  11.6 us
  transfers between devices with their start and end apart: 10, of which 5 were waited for; matrix products, arithmetic and copies ran while one was open for 0% of the time, Pallas kernels for 12%

profile of v2, /device:TPU:1, one launch (start us, length us, event | category | flops | bytes accessed | tf_op | source)
XLA Modules:
  0.0 78.7 jit_solution(9292316652972868307)
XLA Ops:
  0.6 0.0 copy-start.5
  0.6 0.0 copy-start.10
  0.7 0.0 copy-start.4
  0.7 0.0 copy-start.1
  0.7 0.0 copy-start.3
  0.7 0.0 copy-start.2
  0.7 0.0 copy-start.9
  0.7 7.8 %shard_map.202 = (f32[728,256]{1,0:T(8,128)}, f32[312,1024]{1,0:T(8,128)}, f32[448,128]{1,0:T(8,128)}, f32[448,128]{1,0:T(8,128)}, f32[144,128]{1,0:T(8,128)}, /*index=5*/f32[144,128]{1,0:T(8,128)}) custom-call(f32[728,256]{1,0:T(8,128)} %bitcast.9, f32[3,3,256]{2,1,0:T(4,128)} %jac_ref.1, f32[3,13,13]{2,1,0:T(8,128)} %refs_6_.9, f32[13,13]{1,0:T(8,128)} %refs_3_.8, ...), custom_call_target="tpu_custom_call" | custom-call | tf_op jit(solution)/shard_map/pallas_call | solution.py:704
  8.5 0.1 collective-permute-start
  8.6 4.5 %collective-permute-start.1 = (f32[448,128]{1,0:T(8,128)}, f32[448,128]{1,0:T(8,128)S(1)}, u32[]{:S(2)}, u32[]{:S(2)}) collective-permute-start(f32[448,128]{1,0:T(8,128)} %get-tuple-element.46), channel_id=1, source_target_pairs={{8,16},{16,8},{0,0},{24,24},{9,17},{17,9},{1,1},{25,25},{10,18},{1... | collective-permute-start | bytes 688136 | tf_op jit(solution)/shard_map/ppermute | solution.py:722
  13.1 0.0 copy-done.5
  13.1 0.0 copy-done.10
  13.2 0.0 copy-done.4
  13.2 0.0 copy-done.1
  13.2 0.0 copy-done.3
  13.2 0.0 copy-done.2
  13.2 0.0 copy-done.9
  13.2 0.0 copy-start.6
  13.2 1.1 %copy-done.6 = f32[728,256]{1,0:T(8,128)S(1)} copy-done((f32[728,256]{1,0:T(8,128)S(1)}, f32[728,256]{1,0:T(8,128)}, u32[]{:S(2)}) %copy-start.6) | copy-done | bytes 745496
  14.3 2.5 %shard_map.203 = (f32[728,256]{1,0:T(8,128)S(1)}, f32[16,128]{1,0:T(8,128)S(1)}, f32[16,128]{1,0:T(8,128)S(1)}) custom-call(f32[728,256]{1,0:T(8,128)S(1)} %bitcast.10, f32[3,3,256]{2,1,0:T(4,128)S(1)} %copy-done.10, f32[3,13,13]{2,1,0:T(8,128)S(1)} %copy-done.5, f32[3,56,56]{2,1,0:T(8,128)S(1)} %copy-done.9, f32[728,256]{1,0:T(8,128)S(1)} %copy-done.6, ...), custom_call_target="tpu_custom_call" | custom-call | tf_op jit(solution)/shard_map/pallas_call | solution.py:704
  16.9 0.0 collective-permute-done.refs_0_.refs_8_.refs_3_
  16.9 0.2 collective-permute-done.1.refs_1_.refs_9_.refs_4_
  17.0 0.0 copy-done.12
  17.1 1.9 %collective-permute-start.2 = (f32[464,128]{1,0:T(8,128)S(1)}, f32[464,128]{1,0:T(8,128)S(1)}, u32[]{:S(2)}, u32[]{:S(2)}) collective-permute-start(f32[464,128]{1,0:T(8,128)S(1)} %get-tuple-element.57), channel_id=1, source_target_pairs={{0,1},{1,0},{2,3},{3,2},{4,5},{5,4},{6,7},{7,6},{8,9},{9,8},{10,11... | collective-permute-start | bytes 712712 | tf_op jit(solution)/shard_map/ppermute | solution.py:722
  18.9 0.8 %collective-permute-start.3 = (f32[464,128]{1,0:T(8,128)S(1)}, f32[464,128]{1,0:T(8,128)S(1)}, u32[]{:S(2)}, u32[]{:S(2)}) collective-permute-start(f32[464,128]{1,0:T(8,128)S(1)} %get-tuple-element.58), channel_id=1, source_target_pairs={{1,2},{2,1},{3,4},{4,3},{5,6},{6,5},{0,0},{7,7},{9,10},{10,9},{11,... | collective-permute-start | bytes 712712 | tf_op jit(solution)/shard_map/ppermute | solution.py:722
  19.8 0.0 copy-done
  19.8 0.0 copy-done.14
  19.8 0.0 copy-start.11
  19.8 0.0 copy-start.15
  19.8 0.0 copy-start.19
  19.8 1.5 %shard_map.205.refs_2_ = f32[312,1024]{1,0:T(8,128)S(1)} custom-call(f32[312,1024]{1,0:T(8,128)S(1)} %copy-done, s32[4,256]{1,0:T(4,128)S(1)} %copy-done.14), custom_call_target="tpu_custom_call" | custom-call | tf_op jit(solution)/shard_map/pallas_call | solution.py:704
  21.4 6.6 %collective-permute-done.2.refs_10_.refs_5_ = f32[464,128]{1,0:T(8,128)S(1)} collective-permute-done((f32[464,128]{1,0:T(8,128)S(1)}, f32[464,128]{1,0:T(8,128)S(1)}, u32[]{:S(2)}, u32[]{:S(2)}) %collective-permute-start.2) | collective-permute-done | bytes 237600 | tf_op jit(solution)/shard_map/ppermute | solution.py:722
  27.9 0.0 collective-permute-done.3.refs_11_.refs_6_
  27.9 0.0 copy-done.11
  28.0 0.0 copy-start.7
  28.0 0.0 copy-start.8
  28.0 0.0 copy-start.16
  28.0 0.0 copy-start.17
  28.0 3.3 %shard_map.206.refs_0_.q_ref = f32[728,256]{1,0:T(8,128)S(1)} custom-call(f32[728,256]{1,0:T(8,128)S(1)} %get-tuple-element.49.refs_0_, f32[312,1024]{1,0:T(8,128)S(1)} %copy-done, f32[312,1024]{1,0:T(8,128)S(1)} %shard_map.205.refs_2_, s32[4,256]{1,0:T(4,128)S(1)} %copy-done.14, f32[3,4,256]{2,1,0:T(4,128)S(1)} %bitcast.16, f32[1,256]{1,0:T(1,128)S(1)} %bitcast.18, ...), custom_call_target="tpu_custom_call" | custom-call | tf_op jit(solution)/shard_map/pallas_call | solution.py:704
  31.3 5.2 %shard_map.207 = (f32[728,256]{1,0:T(8,128)S(1)}, f32[312,1024]{1,0:T(8,128)S(1)}, f32[432,128]{1,0:T(8,128)S(1)}, f32[432,128]{1,0:T(8,128)S(1)}, f32[144,128]{1,0:T(8,128)S(1)}, /*index=5*/f32[144,128]{1,0:T(8,128)S(1)}) custom-call(f32[728,256]{1,0:T(8,128)S(1)} %shard_map.206.refs_0_.q_ref, f32[3,3,256]{2,1,0:T(4,128)S(1)} %copy-done.10, ...), custom_call_target="tpu_custom_call" | custom-call | tf_op jit(solution)/shard_map/pallas_call | solution.py:704
  36.5 0.1 collective-permute-start.4
  36.6 3.1 %collective-permute-start.5 = (f32[432,128]{1,0:T(8,128)S(1)}, f32[432,128]{1,0:T(8,128)S(1)}, u32[]{:S(2)}, u32[]{:S(2)}) collective-permute-start(f32[432,128]{1,0:T(8,128)S(1)} %get-tuple-element.63), channel_id=1, source_target_pairs={{8,16},{16,8},{0,0},{24,24},{9,17},{17,9},{1,1},{25,25},{10,18},{1... | collective-permute-start | bytes 663560 | tf_op jit(solution)/shard_map/ppermute | solution.py:722
  39.6 1.7 %shard_map.208.refs_0_ = f32[728,256]{1,0:T(8,128)S(1)} custom-call(f32[728,256]{1,0:T(8,128)S(1)} %shard_map.206.refs_0_.q_ref, f32[3,3,256]{2,1,0:T(4,128)S(1)} %copy-done.10, f32[3,13,13]{2,1,0:T(8,128)S(1)} %copy-done.5, f32[3,56,56]{2,1,0:T(8,128)S(1)} %copy-done.9, f32[728,256]{1,0:T(8,128)S(1)} %get-tuple-element.64.integral_ref), custom_call_target="tpu_custom_call" | custom-call | tf_op jit(solution)/shard_map/pallas_call | solution.py:704
  41.4 0.0 collective-permute-done.4.refs_0_.refs_8_
  41.4 2.7 %collective-permute-done.5.refs_1_.refs_9_ = f32[432,128]{1,0:T(8,128)S(1)} collective-permute-done((f32[432,128]{1,0:T(8,128)S(1)}, f32[432,128]{1,0:T(8,128)S(1)}, u32[]{:S(2)}, u32[]{:S(2)}) %collective-permute-start.5) | collective-permute-done | bytes 221216 | tf_op jit(solution)/shard_map/ppermute | solution.py:722
  44.1 2.0 %collective-permute-start.6 = (f32[432,128]{1,0:T(8,128)S(1)}, f32[432,128]{1,0:T(8,128)S(1)}, u32[]{:S(2)}, u32[]{:S(2)}) collective-permute-start(f32[432,128]{1,0:T(8,128)S(1)} %get-tuple-element.71), channel_id=1, source_target_pairs={{0,1},{1,0},{2,3},{3,2},{4,5},{5,4},{6,7},{7,6},{8,9},{9,8},{10,11... | collective-permute-start | bytes 663560 | tf_op jit(solution)/shard_map/ppermute | solution.py:722
  46.1 0.9 %collective-permute-start.7 = (f32[432,128]{1,0:T(8,128)S(1)}, f32[432,128]{1,0:T(8,128)S(1)}, u32[]{:S(2)}, u32[]{:S(2)}) collective-permute-start(f32[432,128]{1,0:T(8,128)S(1)} %get-tuple-element.72), channel_id=1, source_target_pairs={{1,2},{2,1},{3,4},{4,3},{5,6},{6,5},{0,0},{7,7},{9,10},{10,9},{11,... | collective-permute-start | bytes 663560 | tf_op jit(solution)/shard_map/ppermute | solution.py:722
  47.0 2.3 %shard_map.211 = (f32[4,288,384]{2,1,0:T(8,128)S(1)}, f32[3,288,384]{2,1,0:T(8,128)S(1)}) custom-call(f32[256,256]{1,0:T(8,128)S(1)} %copy-done.3, f32[2,256,256]{2,1,0:T(8,128)S(1)} %copy-done.1, f32[256,256]{1,0:T(8,128)S(1)} %copy-done.4, f32[448,128]{1,0:T(8,128)S(1)} %collective-permute-done.refs_0_.refs_8_.refs_3_, ...), custom_call_target="tpu_custom_call" | custom-call | tf_op jit(solution)/shard_map/pallas_call | solution.py:704
  49.4 0.0 copy-start.18
  49.4 0.0 copy-start.20
  49.4 0.0 copy-start.21
  49.4 0.0 copy-start.22
  49.4 1.5 %shard_map.210.refs_2_ = f32[312,1024]{1,0:T(8,128)S(1)} custom-call(f32[312,1024]{1,0:T(8,128)S(1)} %get-tuple-element.66.table_ref.refs_1_, s32[4,256]{1,0:T(4,128)S(1)} %copy-done.14), custom_call_target="tpu_custom_call" | custom-call | tf_op jit(solution)/shard_map/pallas_call | solution.py:704
  50.9 1.6 %collective-permute-done.6.refs_10_ = f32[432,128]{1,0:T(8,128)S(1)} collective-permute-done((f32[432,128]{1,0:T(8,128)S(1)}, f32[432,128]{1,0:T(8,128)S(1)}, u32[]{:S(2)}, u32[]{:S(2)}) %collective-permute-start.6) | collective-permute-done | bytes 221216 | tf_op jit(solution)/shard_map/ppermute | solution.py:722
  52.5 0.0 collective-permute-done.7.refs_11_
  52.5 0.0 copy-done.18
  52.5 4.3 %shard_map.212 = (f32[728,256]{1,0:T(8,128)}, f32[8,32,128]{2,1,0:T(8,128)S(1)}) custom-call(f32[728,256]{1,0:T(8,128)S(1)} %shard_map.208.refs_0_, f32[312,1024]{1,0:T(8,128)S(1)} %get-tuple-element.66.table_ref.refs_1_, f32[312,1024]{1,0:T(8,128)S(1)} %shard_map.210.refs_2_, s32[4,256]{1,0:T(4,128)S(1)} %copy-done.14, f32[3,4,256]{2,1,0:T(4,128)S(1)} %bitcast.17, ...), custom_call_target="tpu_custom_call" | custom-call | tf_op jit(solution)/shard_map/pallas_call | solution.py:704
  56.9 11.6 %all_to_all.5.refs_0_ = f32[8,32,128]{2,1,0:T(8,128)S(1)} all-to-all(f32[8,32,128]{2,1,0:T(8,128)S(1)} %get-tuple-element.81), channel_id=1, replica_groups=mesh['gx'=4,'gy'=8] {'gy'}, dimensions={0} | all-to-all | bytes 262144 | tf_op jit(solution)/shard_map/all_to_all | solution.py:820
  68.5 2.2 %shard_map.213 = (f32[256,384]{1,0:T(8,128)S(1)}, f32[8,384]{1,0:T(8,128)S(1)}, f32[8,384]{1,0:T(8,128)S(1)}) custom-call(f32[8,32,128]{2,1,0:T(8,128)S(1)} %all_to_all.5.refs_0_), custom_call_target="tpu_custom_call" | custom-call | tf_op jit(solution)/shard_map/pallas_call | solution.py:704
  70.6 0.1 collective-permute-start.8
  70.7 3.2 %collective-permute-start.9 = (f32[8,384]{1,0:T(8,128)S(1)}, f32[8,384]{1,0:T(8,128)S(1)}, u32[]{:S(2)}, u32[]{:S(2)}) collective-permute-start(f32[8,384]{1,0:T(8,128)S(1)} %get-tuple-element.84), channel_id=1, source_target_pairs={{8,16},{16,8},{24,0},{0,24},{9,17},{17,9},{25,1},{1,25},{10,18},{1... | collective-permute-start | bytes 36872 | tf_op jit(solution)/shard_map/ppermute | solution.py:722
  73.9 0.0 collective-permute-done.8.refs_3_
  73.9 1.4 %collective-permute-done.9.refs_4_ = f32[8,384]{1,0:T(8,128)S(1)} collective-permute-done((f32[8,384]{1,0:T(8,128)S(1)}, f32[8,384]{1,0:T(8,128)S(1)}, u32[]{:S(2)}, u32[]{:S(2)}) %collective-permute-start.9) | collective-permute-done | bytes 12320 | tf_op jit(solution)/shard_map/ppermute | solution.py:722
  75.3 3.4 %shard_map.214 = (f32[3,256,256]{2,1,0:T(8,128)}, f32[256,256]{1,0:T(8,128)}) custom-call(f32[4,288,384]{2,1,0:T(8,128)S(1)} %get-tuple-element.79.refs_0_, f32[3,288,384]{2,1,0:T(8,128)S(1)} %get-tuple-element.80.refs_1_, f32[256,384]{1,0:T(8,128)S(1)} %get-tuple-element.82.refs_2_, f32[8,384]{1,0:T(8,128)S(1)} %collective-permute-done.8.refs_3_, ...), custom_call_target="tpu_custom_call" | custom-call | tf_op jit(solution)/shard_map/pallas_call | solution.py:704
  (16 shorter events, 0.1 us)
Async XLA Ops:
  0.6 12.5 %copy-start.5 = (f32[3,13,13]{2,1,0:T(8,128)S(1)}, f32[3,13,13]{2,1,0:T(8,128)}, u32[]{:S(2)}) copy-start(f32[3,13,13]{2,1,0:T(8,128)} %refs_6_.9) | copy-start | bytes 6088
  0.6 12.5 %copy-start.10 = (f32[3,3,256]{2,1,0:T(4,128)S(1)}, f32[3,3,256]{2,1,0:T(4,128)}, u32[]{:S(2)}) copy-start(f32[3,3,256]{2,1,0:T(4,128)} %jac_ref.1) | copy-start | bytes 27652
  0.7 12.5 %copy-start.4 = (f32[256,256]{1,0:T(8,128)S(1)}, f32[256,256]{1,0:T(8,128)}, u32[]{:S(2)}) copy-start(f32[256,256]{1,0:T(8,128)} %refs_2_.7) | copy-start | bytes 786436
  0.7 12.5 %copy-start.1 = (f32[2,256,256]{2,1,0:T(8,128)S(1)}, f32[2,256,256]{2,1,0:T(8,128)}, u32[]{:S(2)}) copy-start(f32[2,256,256]{2,1,0:T(8,128)} %refs_1_.7) | copy-start | bytes 1572868
  0.7 12.5 %copy-start.3 = (f32[256,256]{1,0:T(8,128)S(1)}, f32[256,256]{1,0:T(8,128)}, u32[]{:S(2)}) copy-start(f32[256,256]{1,0:T(8,128)} %refs_0_.1) | copy-start | bytes 786436
  0.7 12.5 %copy-start.2 = (f32[13,56,256]{2,1,0:T(8,128)S(1)}, f32[13,56,256]{2,1,0:T(8,128)}, u32[]{:S(2)}) copy-start(f32[13,56,256]{2,1,0:T(8,128)} %param.19) | copy-start | bytes 2236420
  0.7 12.5 %copy-start.9 = (f32[3,56,56]{2,1,0:T(8,128)S(1)}, f32[3,56,56]{2,1,0:T(8,128)}, u32[]{:S(2)}) copy-start(f32[3,56,56]{2,1,0:T(8,128)} %stiff_ref.1) | copy-start | bytes 112900
  8.5 8.4 %collective-permute-start = (f32[448,128]{1,0:T(8,128)}, f32[448,128]{1,0:T(8,128)S(1)}, u32[]{:S(2)}, u32[]{:S(2)}) collective-permute-start(f32[448,128]{1,0:T(8,128)} %get-tuple-element.45), channel_id=1, source_target_pairs={{0,8},{8,0},{16,24},{24,16},{1,9},{9,1},{17,25},{25,17},{2,10},{10... | collective-permute-start | bytes 688136 | tf_op jit(solution)/shard_map/ppermute | solution.py:722
  8.6 8.4 %collective-permute-start.1 = (f32[448,128]{1,0:T(8,128)}, f32[448,128]{1,0:T(8,128)S(1)}, u32[]{:S(2)}, u32[]{:S(2)}) collective-permute-start(f32[448,128]{1,0:T(8,128)} %get-tuple-element.46), channel_id=1, source_target_pairs={{8,16},{16,8},{0,0},{24,24},{9,17},{17,9},{1,1},{25,25},{10,18},{1... | collective-permute-start | bytes 688136 | tf_op jit(solution)/shard_map/ppermute | solution.py:722
  13.2 1.1 %copy-start.6 = (f32[728,256]{1,0:T(8,128)S(1)}, f32[728,256]{1,0:T(8,128)}, u32[]{:S(2)}) copy-start(f32[728,256]{1,0:T(8,128)} %get-tuple-element.47.refs_4_) | copy-start | bytes 2236420
  14.3 2.7 %copy-start.12 = (f32[144,128]{1,0:T(8,128)S(1)}, f32[144,128]{1,0:T(8,128)}, u32[]{:S(2)}) copy-start(f32[144,128]{1,0:T(8,128)} %get-tuple-element.53.refs_2_) | copy-start | bytes 221188
  14.3 2.7 %copy-start.13 = (f32[144,128]{1,0:T(8,128)S(1)}, f32[144,128]{1,0:T(8,128)}, u32[]{:S(2)}) copy-start(f32[144,128]{1,0:T(8,128)} %get-tuple-element.54.refs_3_) | copy-start | bytes 221188
  14.3 5.5 %copy-start = (f32[312,1024]{1,0:T(8,128)S(1)}, f32[312,1024]{1,0:T(8,128)}, u32[]{:S(2)}) copy-start(f32[312,1024]{1,0:T(8,128)} %get-tuple-element.50.table_ref.refs_1_) | copy-start | bytes 3833860
  14.3 5.5 %copy-start.14 = (s32[4,256]{1,0:T(4,128)S(1)}, s32[4,256]{1,0:T(4,128)}, u32[]{:S(2)}) copy-start(s32[4,256]{1,0:T(4,128)} %refs_3_.9) | copy-start | bytes 12292
  17.1 10.9 %collective-permute-start.2 = (f32[464,128]{1,0:T(8,128)S(1)}, f32[464,128]{1,0:T(8,128)S(1)}, u32[]{:S(2)}, u32[]{:S(2)}) collective-permute-start(f32[464,128]{1,0:T(8,128)S(1)} %get-tuple-element.57), channel_id=1, source_target_pairs={{0,1},{1,0},{2,3},{3,2},{4,5},{5,4},{6,7},{7,6},{8,9},{9,8},{10,11... | collective-permute-start | bytes 712712 | tf_op jit(solution)/shard_map/ppermute | solution.py:722
  18.9 9.0 %collective-permute-start.3 = (f32[464,128]{1,0:T(8,128)S(1)}, f32[464,128]{1,0:T(8,128)S(1)}, u32[]{:S(2)}, u32[]{:S(2)}) collective-permute-start(f32[464,128]{1,0:T(8,128)S(1)} %get-tuple-element.58), channel_id=1, source_target_pairs={{1,2},{2,1},{3,4},{4,3},{5,6},{6,5},{0,0},{7,7},{9,10},{10,9},{11,... | collective-permute-start | bytes 712712 | tf_op jit(solution)/shard_map/ppermute | solution.py:722
  19.8 8.1 %copy-start.11 = (f32[4,56,21]{1,0,2:T(4,128)S(1)}, f32[4,56,21]{1,0,2:T(4,128)}, u32[]{:S(2)}) copy-start(f32[4,56,21]{1,0,2:T(4,128)} %param.28) | copy-start | bytes 56452
  19.8 8.1 %copy-start.15 = (f32[4,3,256]{2,0,1:T(4,128)S(1)}, f32[4,3,256]{2,0,1:T(4,128)}, u32[]{:S(2)}) copy-start(f32[4,3,256]{2,0,1:T(4,128)} %param.21) | copy-start | bytes 36868
  19.8 8.1 %copy-start.19 = (f32[256]{0:T(256)S(1)}, f32[256]{0:T(256)}, u32[]{:S(2)}) copy-start(f32[256]{0:T(256)} %param.22) | copy-start | bytes 3076
  28.0 3.3 %copy-start.7 = (f32[4,21,56]{2,0,1:T(4,128)S(1)}, f32[4,21,56]{2,0,1:T(4,128)}, u32[]{:S(2)}) copy-start(f32[4,21,56]{2,0,1:T(4,128)} %param.27) | copy-start | bytes 56452
  28.0 3.3 %copy-start.8 = (f32[3,56,56]{2,1,0:T(8,128)S(1)}, f32[3,56,56]{2,1,0:T(8,128)}, u32[]{:S(2)}) copy-start(f32[3,56,56]{2,1,0:T(8,128)} %refs_4_.3) | copy-start | bytes 112900
  28.0 3.3 %copy-start.16 = (f32[13,13]{1,0:T(8,128)S(1)}, f32[13,13]{1,0:T(8,128)}, u32[]{:S(2)}) copy-start(f32[13,13]{1,0:T(8,128)} %refs_3_.8) | copy-start | bytes 2032
  28.0 3.3 %copy-start.17 = (s32[8,64]{1,0:T(8,128)S(1)}, s32[8,64]{1,0:T(8,128)}, u32[]{:S(2)}) copy-start(s32[8,64]{1,0:T(8,128)} %refs_6_.8) | copy-start | bytes 6148
  36.5 4.9 %collective-permute-start.4 = (f32[432,128]{1,0:T(8,128)S(1)}, f32[432,128]{1,0:T(8,128)S(1)}, u32[]{:S(2)}, u32[]{:S(2)}) collective-permute-start(f32[432,128]{1,0:T(8,128)S(1)} %get-tuple-element.62), channel_id=1, source_target_pairs={{0,8},{8,0},{16,24},{24,16},{1,9},{9,1},{17,25},{25,17},{2,10},{10... | collective-permute-start | bytes 663560 | tf_op jit(solution)/shard_map/ppermute | solution.py:722
  36.6 7.5 %collective-permute-start.5 = (f32[432,128]{1,0:T(8,128)S(1)}, f32[432,128]{1,0:T(8,128)S(1)}, u32[]{:S(2)}, u32[]{:S(2)}) collective-permute-start(f32[432,128]{1,0:T(8,128)S(1)} %get-tuple-element.63), channel_id=1, source_target_pairs={{8,16},{16,8},{0,0},{24,24},{9,17},{17,9},{1,1},{25,25},{10,18},{1... | collective-permute-start | bytes 663560 | tf_op jit(solution)/shard_map/ppermute | solution.py:722
  44.1 8.4 %collective-permute-start.6 = (f32[432,128]{1,0:T(8,128)S(1)}, f32[432,128]{1,0:T(8,128)S(1)}, u32[]{:S(2)}, u32[]{:S(2)}) collective-permute-start(f32[432,128]{1,0:T(8,128)S(1)} %get-tuple-element.71), channel_id=1, source_target_pairs={{0,1},{1,0},{2,3},{3,2},{4,5},{5,4},{6,7},{7,6},{8,9},{9,8},{10,11... | collective-permute-start | bytes 663560 | tf_op jit(solution)/shard_map/ppermute | solution.py:722
  46.1 6.4 %collective-permute-start.7 = (f32[432,128]{1,0:T(8,128)S(1)}, f32[432,128]{1,0:T(8,128)S(1)}, u32[]{:S(2)}, u32[]{:S(2)}) collective-permute-start(f32[432,128]{1,0:T(8,128)S(1)} %get-tuple-element.72), channel_id=1, source_target_pairs={{1,2},{2,1},{3,4},{4,3},{5,6},{6,5},{0,0},{7,7},{9,10},{10,9},{11,... | collective-permute-start | bytes 663560 | tf_op jit(solution)/shard_map/ppermute | solution.py:722
  49.4 3.1 %copy-start.18 = (f32[16,21]{1,0:T(8,128)S(1)}, f32[16,21]{1,0:T(8,128)}, u32[]{:S(2)}) copy-start(f32[16,21]{1,0:T(8,128)} %refs_13_.1) | copy-start | bytes 4036
  49.4 3.1 %copy-start.20 = (s32[256,2]{0,1:T(2,128)S(1)}, s32[256,2]{0,1:T(2,128)}, u32[]{:S(2)}) copy-start(s32[256,2]{0,1:T(2,128)} %param.33) | copy-start | bytes 6148
  49.4 3.1 %copy-start.21 = (s32[256]{0:T(256)S(1)}, s32[256]{0:T(256)}, u32[]{:S(2)}) copy-start(s32[256]{0:T(256)} %param.31) | copy-start | bytes 3076
  49.4 3.1 %copy-start.22 = (s32[256,1]{0,1:T(1,128)S(1)}, s32[256,1]{0,1:T(1,128)}, u32[]{:S(2)}) copy-start(s32[256,1]{0,1:T(1,128)} %param.32) | copy-start | bytes 3076
  70.6 3.3 %collective-permute-start.8 = (f32[8,384]{1,0:T(8,128)S(1)}, f32[8,384]{1,0:T(8,128)S(1)}, u32[]{:S(2)}, u32[]{:S(2)}) collective-permute-start(f32[8,384]{1,0:T(8,128)S(1)} %get-tuple-element.83), channel_id=1, source_target_pairs={{0,8},{8,0},{16,24},{24,16},{1,9},{9,1},{17,25},{25,17},{2,10},{10... | collective-permute-start | bytes 36872 | tf_op jit(solution)/shard_map/ppermute | solution.py:722
  70.7 4.6 %collective-permute-start.9 = (f32[8,384]{1,0:T(8,128)S(1)}, f32[8,384]{1,0:T(8,128)S(1)}, u32[]{:S(2)}, u32[]{:S(2)}) collective-permute-start(f32[8,384]{1,0:T(8,128)S(1)} %get-tuple-element.84), channel_id=1, source_target_pairs={{8,16},{16,8},{24,0},{0,24},{9,17},{17,9},{25,1},{1,25},{10,18},{1... | collective-permute-start | bytes 36872 | tf_op jit(solution)/shard_map/ppermute | solution.py:722

commit v3 on v2

--- a/solution.py
+++ b/solution.py
@@ -27,7 +27,7 @@
 F32 = jnp.float32
 BF16 = jnp.bfloat16
 NT = (((1,), (1,)), ((), ()))
-VMEM_LIMIT = 48 * 1024 * 1024
+VMEM_LIMIT = 24 * 1024 * 1024
 START_LIMIT = 62 * 1024 * 1024
 
 
@@ -144,18 +144,27 @@
     return jnp.where(c > 0, 4, 3)
 
 
+def front_weights(star_ref, source_ref, deriv_ref, trace_ref, ready=lambda *numbers: None):
+    ready(2, 3)
+    star = star_weights([star_ref[0], star_ref[1], star_ref[2], source_ref[...]])
+    ready(4, 5)
+    basis_weights = weights(side_by_side([deriv_ref[d] for d in range(3)]))
+    return star, basis_weights, weights(stacked_traces(trace_ref))
+
+
+def front_again(place, q_ref, jac_ref, star_ref, b1_ref, b2_ref, t1_ref, t2_ref, *refs):
+    held = star_ref[...], (b1_ref[...], b2_ref[...]), (t1_ref[...], t2_ref[...])
+    front(place, held, q_ref, jac_ref, *refs)
+
+
 def front(
-    place, q_ref, jac_ref, star_ref, source_ref, deriv_ref, trace_ref, send_ref,
+    place, held, q_ref, jac_ref, send_ref,
     integral_ref, table_ref, p1_ref, p2_ref, own1_ref, own2_ref,
     spread_ref, relaxed_ref, d1_ref, d2_ref, packed_ref, ready=lambda *numbers: None, made=lambda *numbers: None,
 ):
     elements = q_ref.shape[1]
-    ready(2, 3)
-    star = star_weights([star_ref[0], star_ref[1], star_ref[2], source_ref[...]])
-    ready(4, 5)
-    basis = deriv_ref.shape[1]
-    basis_weights = weights(side_by_side([deriv_ref[d] for d in range(3)]))
-    trace = weights(stacked_traces(trace_ref))
+    basis = q_ref.shape[0] // FIELDS
+    star, basis_weights, trace = held
     ready(0, 1)
     derivative(q_ref, d1_ref, jac_ref, star, basis_weights, spread_ref, relaxed_ref)
     derivative(d1_ref, d2_ref, jac_ref, star, basis_weights, spread_ref, relaxed_ref)
@@ -222,8 +231,7 @@
 def start(place, *refs):
     sources, water, refs = refs[:7], refs[7:10], refs[10:]
     targets, refs = refs[:6], refs[6:]
-    held, (sems, heads, tails), refs = refs[:7], refs[7:10], refs[10:]
-    outs, scratch = refs[:6], refs[6:]
+    held, outs, (sems, heads, tails, *scratch) = refs[:7], refs[7:13], refs[13:]
     depth, momentum, bottom = water
     last = depth.shape[0] - 8
     pairs = [(sources[i], held[i]) for i in range(7)]
@@ -248,7 +256,8 @@
         for i in numbers:
             copies[first_out + i].start()
 
-    front(place, *held, *outs, *scratch, ready=ready, made=made)
+    ready_weights = front_weights(*held[2:6], ready=ready)
+    front(place, ready_weights, *held[:2], held[6], *outs, *scratch, ready=ready, made=made)
     ready(*range(7, first_out))
     edge_rows(place, heads, tails, *outs[2:4])
     made(2, 3, 4, 5)
@@ -301,20 +310,58 @@
         outer_ref[:, f * elements : (f + 1) * elements] = folded(dot(stack, hot))[:TABLE]
 
 
-def remote_faces(place, outer_ref, partner_ref, table_refs, packed_ref, table_ref):
-    p1_ref, p2_ref, q1_ref, q2_ref = table_refs
+def remote_blocks(place, p1, p2, q1, q2):
+    a1, c1 = unequal(place)
+    return [
+        (p1, 0, column_block(a1)),
+        (p2, 0, column_block(-a1)),
+        (q1, 2 * HALF, row_block(c1)),
+        (q2, 2 * HALF, row_block(-c1)),
+        (q1, 0, column_block(a1) + c1),
+        (q1, HALF, column_block(-a1) + c1),
+        (q2, 0, column_block(a1) - c1),
+        (q2, HALF, column_block(-a1) - c1),
+    ]
+
+
+def prepared(
+    place, star_ref, source_ref, deriv_ref, trace_ref, lift_ref, partner_ref,
+    sea_face_ref, sea_row_ref,
+    star4_ref, star3_ref, b1_ref, b2_ref, t1_ref, t2_ref, l1_ref, l2_ref, hot_ref, sea_ref, slot_ref,
+):
+    star, (b1_ref[...], b2_ref[...]), (t1_ref[...], t2_ref[...]) = front_weights(
+        star_ref, source_ref, deriv_ref, trace_ref
+    )
+    star4_ref[...] = star
+    star3_ref[...] = star_weights([star_ref[0], star_ref[1], star_ref[2]])
+    l1_ref[...], l2_ref[...] = lift_weights(lift_ref)
     elements = partner_ref.shape[1]
-    a1, c1 = unequal(place)
-    blocks = [
-        (p1_ref, 0, column_block(a1)),
-        (p2_ref, 0, column_block(-a1)),
-        (q1_ref, 2 * HALF, row_block(c1)),
-        (q2_ref, 2 * HALF, row_block(-c1)),
-        (q1_ref, 0, column_block(a1) + c1),
-        (q1_ref, HALF, column_block(-a1) + c1),
-        (q2_ref, 0, column_block(a1) - c1),
-        (q2_ref, HALF, column_block(-a1) - c1),
-    ]
+    blocks = remote_blocks(place, None, None, None, None)
+    slot = iota((CAP, elements), 0)
+    for f in range(4):
+        wanted = partner_ref[f : f + 1, :] - 4 * elements
+        hot_ref[:, f * elements : (f + 1) * elements] = jnp.concatenate(
+            [(slot + CAP * block[2] == wanted).astype(F32) for block in blocks], axis=0
+        ).astype(BF16)
+    faces = sea_face_ref.shape[1]
+    sea_ref[...] = (iota((4 * elements, faces), 0) == sea_face_ref[...]).astype(F32).astype(BF16)
+    row = sea_row_ref[...]
+    tiles = slot_ref.shape[0]
+    hits = (iota((tiles, faces), 0) == row).astype(F32)
+    before = (iota((faces, faces), 0) < iota((faces, faces), 1)).astype(F32)
+    count = dot(hits.astype(BF16), before.astype(BF16))
+    mine = jnp.sum(count * hits, axis=0, keepdims=True).astype(jnp.int32)
+    lane = iota((2 * CAP, faces), 0)
+    mine = mine == lane % CAP
+    for j in range(tiles):
+        edges = mine & (row == jnp.where(lane < CAP, j - 1, j + 1))
+        inside = mine & (row == j)
+        slot_ref[j] = jnp.concatenate([edges.astype(F32), inside.astype(F32)], axis=0).astype(BF16)
+
+
+def remote_faces(place, outer_ref, hot_ref, table_refs, packed_ref, table_ref):
+    elements = hot_ref.shape[1] // 4
+    blocks = remote_blocks(place, *table_refs)
     left = iota((HALF, 2 * CAP), 1) < CAP
     for n in range(0, 8, 2):
         one = blocks[n][0][blocks[n][1] : blocks[n][1] + HALF, :]
@@ -324,14 +371,9 @@
         packed_ref[HALF:, lanes] = jnp.where(left, pltpu.roll(one, CAP, 1), two)
     unpack(packed_ref, table_ref)
     remote = table_parts(table_ref)
-    slot = iota((CAP, elements), 0)
     for f in range(4):
-        wanted = partner_ref[f : f + 1, :] - 4 * elements
-        hot = jnp.concatenate(
-            [(slot + CAP * block[2] == wanted).astype(F32) for block in blocks], axis=0
-        ).astype(BF16)
         columns = slice(f * elements, (f + 1) * elements)
-        outer_ref[:, columns] += folded(dot(remote, hot))[:TABLE]
+        outer_ref[:, columns] += folded(dot(remote, hot_ref[:, columns]))[:TABLE]
 
 
 def lift_weights(lift_ref):
@@ -347,10 +389,9 @@
     )
 
 
-def lifted(base_ref, table_ref, outer_ref, normal_ref, speed_ref, star_ref, lift_ref, state_ref, flux_ref):
-    basis = lift_ref.shape[2]
+def lifted(base_ref, table_ref, outer_ref, normal_ref, speed_ref, star, lift, state_ref, flux_ref):
     elements = base_ref.shape[1]
-    star = star_weights([star_ref[0], star_ref[1], star_ref[2]])
+    basis = base_ref.shape[0] // FIELDS
     size = FIELDS * 8
     for part in range(FACE_PAD // 8):
         at = [slice(g * FACE_PAD + 8 * part, g * FACE_PAD + 8 * part + 8) for g in range(FIELDS)]
@@ -366,49 +407,38 @@
                 flux_ref[g, f * FACE_PAD + 8 * part : f * FACE_PAD + 8 * part + 8, :] = flux[
                     8 * g : 8 * g + 8
                 ]
-    lift = lift_weights(lift_ref)
     for g in range(FIELDS):
         rows = slice(g * basis, (g + 1) * basis)
         state_ref[rows, :] = base_ref[rows, :] - weighted(*lift, flux_ref[g])
 
 
 def back(
-    place, base_ref, table_ref, outer_ref, partner_ref, normal_ref, speed_ref, star_ref, lift_ref,
+    place, base_ref, table_ref, outer_ref, normal_ref, speed_ref, star_ref, l1_ref, l2_ref, hot_ref,
     p1_ref, p2_ref, q1_ref, q2_ref,
     state_ref, flux_ref, packed_ref, remote_ref,
 ):
     arrived = (p1_ref, p2_ref, q1_ref, q2_ref)
-    remote_faces(place, outer_ref, partner_ref, arrived, packed_ref, remote_ref)
-    lifted(base_ref, table_ref, outer_ref, normal_ref, speed_ref, star_ref, lift_ref, state_ref, flux_ref)
-
-
-def rates_out(vertical, trace_ref, interp_ref, sea_face_ref, sea_base_ref, sea_row_ref, out_ref):
-    elements = vertical.shape[1]
-    faces = sea_face_ref.shape[1]
-    tiles = out_ref.shape[0]
-    sea = weighted(*weights(stacked_traces(trace_ref)), vertical)
+    remote_faces(place, outer_ref, hot_ref, arrived, packed_ref, remote_ref)
+    lift = l1_ref[...], l2_ref[...]
+    lifted(
+        base_ref, table_ref, outer_ref, normal_ref, speed_ref, star_ref[...], lift, state_ref, flux_ref
+    )
+
+
+def rates_out(vertical, t1_ref, t2_ref, interp_ref, sea_base_ref, sea_ref, slot_ref, out_ref):
+    tiles, _, faces = slot_ref.shape
+    sea = weighted(t1_ref[...], t2_ref[...], vertical)
     sea = jnp.concatenate([sea[f * FACE_PAD : (f + 1) * FACE_PAD] for f in range(4)], axis=1)
-    hot = (iota((4 * elements, faces), 0) == sea_face_ref[...]).astype(F32).astype(BF16)
-    coeffs = folded(dot(both_parts(sea), hot))[:FACE_BASIS]
+    coeffs = folded(dot(both_parts(sea), sea_ref[...]))[:FACE_BASIS]
     rates = exact_dot(interp_ref[...], coeffs)
     corners = jnp.where(
         iota((8, faces), 0) == 0, sea_base_ref[0:1, :], sea_base_ref[1:2, :]
     ).astype(F32)
     sent = both_parts(jnp.concatenate([rates, corners], axis=0))
-    row = sea_row_ref[...]
-    hits = (iota((tiles, faces), 0) == row).astype(F32)
-    before = (iota((faces, faces), 0) < iota((faces, faces), 1)).astype(F32)
-    count = dot(hits.astype(BF16), before.astype(BF16))
-    slot = jnp.sum(count * hits, axis=0, keepdims=True).astype(jnp.int32)
-    lane = iota((2 * CAP, faces), 0)
-    mine = slot == lane % CAP
     left = iota((POINTS // 2, 2 * CAP), 1) < CAP
     left_1 = iota((1, 2 * CAP), 1) < CAP
     for j in range(tiles):
-        edges = mine & (row == jnp.where(lane < CAP, j - 1, j + 1))
-        inside = mine & (row == j)
-        hot = jnp.concatenate([edges.astype(F32), inside.astype(F32)], axis=0).astype(BF16)
-        got = folded(lax.dot_general(sent, hot, NT, preferred_element_type=F32))
+        got = folded(lax.dot_general(sent, slot_ref[j], NT, preferred_element_type=F32))
         near, own = got[:, : 2 * CAP], got[:, 2 * CAP :]
         out_ref[j, 0:POINTS, :] = near[:POINTS]
         out_ref[j, 16:24, :] = jnp.where(left, own[0:8], own[8:16])
@@ -418,11 +448,15 @@
 
 
 def finish(*refs):
-    solid, sea, (state_ref, out_ref, *scratch) = refs[:13], refs[13:18], refs[18:]
+    solid, sea, refs = refs[:14], refs[14:20], refs[20:]
+    state_out, out_ref, state_ref, sems, *scratch = refs
     back(*solid, state_ref, *scratch)
-    basis = sea[0].shape[2]
+    copy = pltpu.make_async_copy(state_ref, state_out, sems.at[0])
+    copy.start()
+    basis = state_ref.shape[0] // FIELDS
     vertical = state_ref[vertical_field * basis : (vertical_field + 1) * basis, :]
     rates_out(vertical, *sea, out_ref)
+    copy.wait()
 
 
 def forced(place, got_ref, forcing_ref, s1_ref, s2_ref):
@@ -442,7 +476,7 @@
     lower, upper = jnp.concatenate(tops, axis=1), jnp.concatenate(bottoms, axis=1)
     x0, y0 = jnp.concatenate(xs, axis=1), jnp.concatenate(ys, axis=1)
     arrived = x0.shape[1]
-    from_x = iota((tile_x, arrived), 0).astype(F32) - x0
+    hot = (iota((tile_x, arrived), 0).astype(F32) == x0).astype(F32).astype(BF16)
     from_y = iota((tile_y, arrived), 0).astype(F32) - y0
     total = jnp.zeros((tile_x, tile_y), F32)
     for pr in range(patch_side):
@@ -451,30 +485,37 @@
         for pc in range(patch_side):
             at = (pr * patch_side + pc) % 8
             value = jnp.where(from_y == pc, source[at : at + 1], value)
-        hot = (from_x == pr).astype(F32).astype(BF16)
-        for value in parts(value):
-            total += lax.dot_general(hot, value, NT, preferred_element_type=F32)
+        got = sum(
+            lax.dot_general(hot, part, NT, preferred_element_type=F32) for part in parts(value)
+        )
+        total += got if pr == 0 else pltpu.roll(got, pr, 0)
     forcing_ref[:, :tile_y] = total
     near = jnp.concatenate([got_ref[s, 0:POINTS, :] for s in range(tiles)], axis=1)
     x0 = jnp.concatenate([got_ref[s, 24:25, :] for s in range(tiles)], axis=1)
     y0 = jnp.concatenate([got_ref[s, 25:26, :] for s in range(tiles)], axis=1)
     arrived = x0.shape[1]
-    from_x = iota((tile_x, arrived), 0).astype(F32) - x0
+    hot = (iota((tile_x, arrived), 0).astype(F32) == x0).astype(F32).astype(BF16)
     rows = iota((8, arrived), 0)
     before = iota((8, arrived), 1) % (2 * CAP) < CAP
     high_y = jnp.where(before & (rows >= 6), (rows + (tile_y - 8)).astype(F32) - y0, -1.0)
     low_y = jnp.where(before | (rows >= 2), -1.0, rows.astype(F32) - y0)
-    total = jnp.zeros((tile_x, 128), F32)
-    blank = jnp.zeros((128 - 16, arrived), F32)
+    chunks = [None] * 16
     for pr in range(patch_side):
         high, low = jnp.zeros((8, arrived), F32), jnp.zeros((8, arrived), F32)
         for pc in range(patch_side):
             at = pr * patch_side + pc
             high = jnp.where(high_y == pc, near[at : at + 1], high)
             low = jnp.where(low_y == pc, near[at : at + 1], low)
-        hot = (from_x == pr).astype(F32).astype(BF16)
-        for value in parts(jnp.concatenate([low, blank, high], axis=0)):
-            total += lax.dot_general(hot, value, NT, preferred_element_type=F32)
+        chunks[(4 * pr - 1) % 16], chunks[4 * pr] = high, low
+    blank = jnp.zeros((8, arrived), F32)
+    value = jnp.concatenate([blank if c is None else c for c in chunks], axis=0)
+    got = sum(lax.dot_general(hot, part, NT, preferred_element_type=F32) for part in parts(value))
+    lane = iota((tile_x, 128), 1)
+    used = (lane < 2) | (lane >= 126)
+    total = jnp.where(used, got, 0.0)
+    for pr in range(1, patch_side):
+        moved_back = pltpu.roll(pltpu.roll(got, 128 - 32 * pr, 1), pr, 0)
+        total += jnp.where(used, moved_back, 0.0)
     forcing_ref[:, tile_y:] = total
     a1, _ = unequal(place)
     head, tail = forcing_ref[0:8, :], forcing_ref[tile_x - 8 : tile_x, :]
@@ -577,8 +618,8 @@
     return pltpu.roll(x, 1, 1)
 
 
-def cells(state, cell):
-    for at in range(8, cell.shape[1] - 8, 8):
+def cells(state, cell, low, high):
+    for at in range(low, high, 8):
         here = slice(at, at + 8)
         h, mx, my = state[0, here, :], state[1, here, :], state[2, here, :]
         safe = jnp.maximum(h, depth_floor)
@@ -594,26 +635,29 @@
         cell[4, here, :] = 0.5 * (jnp.abs(v) + c)
 
 
-def moved(state, cell, at, rows):
-    here, up, down = slice(at, at + rows), slice(at + 1, at + rows + 1), slice(at - 1, at + rows - 1)
-
-    def x_face(i, j):
-        wave = jnp.maximum(cell[3, i, :], cell[3, j, :])
-        u_i, u_j = [state[k, i, :] for k in range(3)], [state[k, j, :] for k in range(3)]
-        f_i = (u_i[1], cell[0, i, :], cell[1, i, :])
-        f_j = (u_j[1], cell[0, j, :], cell[1, j, :])
-        return [0.5 * (f_i[k] + f_j[k]) - wave * (u_j[k] - u_i[k]) for k in range(3)]
-
+def moved(state, cell, face, at, rows):
+    here, up = slice(at, at + rows), slice(at + 1, at + rows + 1)
+    below = slice(at - 1, at + rows - 1)
     now = [state[k, here, :] for k in range(3)]
-    flux = (now[2], cell[1, here, :], cell[2, here, :])
+    cross = cell[1, here, :]
+    next_now = [state[k, up, :] for k in range(3)]
+    wave = jnp.maximum(cell[3, here, :], cell[3, up, :])
+    pairs = ((now[1], next_now[1]), (cell[0, here, :], cell[0, up, :]), (cross, cell[1, up, :]))
+    upper = [
+        0.5 * (pairs[k][0] + pairs[k][1]) - wave * (next_now[k] - now[k]) for k in range(3)
+    ]
+    for k in range(3):
+        face[k, here, :] = upper[k]
+    flux = (now[2], cross, cell[2, here, :])
     speed = cell[4, here, :]
     wave = jnp.maximum(speed, next_of(speed))
+    next_now = [next_of(x) for x in now]
+    next_flux = (next_now[2], next_of(flux[1]), next_of(flux[2]))
     y_face = [
-        0.5 * (flux[k] + next_of(flux[k])) - wave * (next_of(now[k]) - now[k]) for k in range(3)
+        0.5 * (flux[k] + next_flux[k]) - wave * (next_now[k] - now[k]) for k in range(3)
     ]
-    upper, lower = x_face(here, up), x_face(down, here)
     return [
-        now[k] - step_ocean * (upper[k] - lower[k] + y_face[k] - previous_of(y_face[k]))
+        now[k] - step_ocean * (upper[k] - face[k, below, :] + y_face[k] - previous_of(y_face[k]))
         for k in range(3)
     ]
 
@@ -627,11 +671,11 @@
 
 
 def ocean_first(
-    place, depth_ref, momentum_ref, bottom_ref, p1_ref, p2_ref, q1_ref, q2_ref, wide, state, cell
+    place, depth_ref, momentum_ref, bottom_ref, p1_ref, p2_ref, q1_ref, q2_ref, wide, state, cell, face
 ):
     tile_x, tile_y = depth_ref.shape
     widened(place, depth_ref, momentum_ref, bottom_ref, p1_ref, p2_ref, q1_ref, q2_ref, wide)
-    cells(wide, cell)
+    cells(wide, cell, 8, cell.shape[1] - 8)
     height, span = wide.shape[1:]
     lane = iota((STRIP, span), 1)
     outside = ((lane == span - 1) & (place[1] == 0)) | (
@@ -639,8 +683,9 @@
     )
     state[:, 0:8, :] = jnp.zeros((3, 8, span), F32)
     state[:, height - 8 :, :] = jnp.zeros((3, 8, span), F32)
+    face[:, 0:8, :] = jnp.zeros((3, 8, span), F32)
     for at in range(8, height - 8, STRIP):
-        new = moved(wide, cell, at, STRIP)
+        new = moved(wide, cell, face, at, STRIP)
         row = iota((STRIP, span), 0) + at
         out = outside | ((row < MARGIN) & (place[0] == 0))
         out = out | ((row >= MARGIN + tile_x) & (place[0] == place[2] - 1))
@@ -648,51 +693,100 @@
             state[k, at : at + STRIP, :] = jnp.where(out, 0.0, new[k])
 
 
-def ocean_last(place, wide, first, forcing_ref, s1_ref, s2_ref, out_ref, bed_ref, state, bed, cell):
+def second_step(wide, first, bed, state, cell, face, rows, put, raise_bed):
+    low, high = rows.start - 8, rows.stop + 8
+    raise_bed(wide.at[3])
+    for at in range(low, high, STRIP):
+        here = slice(at, at + STRIP)
+        change_x, change_y = sloped(wide[0, here, :], bed, at, STRIP)
+        state[0, here, :] = first[0, here, :]
+        state[1, here, :] = first[1, here, :] - change_x
+        state[2, here, :] = first[2, here, :] - change_y
+    cells(state, cell, low, high)
+    raise_bed(bed)
+    moved(state, cell, face, low, 8)
+    for at in range(rows.start, rows.stop, STRIP):
+        new = moved(state, cell, face, at, STRIP)
+        change_x, change_y = sloped(state[0, at : at + STRIP, :], bed, at, STRIP)
+        new[1] -= change_x
+        new[2] -= change_y
+        put(at, new)
+
+
+def ocean_inner(wide, first, forcing_ref, out_ref, bed_ref, state, bed, cell, face):
     tile_x, tile_y = bed_ref.shape
-    height = wide.shape[1]
+    inner = slice(MARGIN, MARGIN + tile_x)
+    bed[...] = wide[3]
+
+    def raise_bed(source):
+        bed[inner, :] = source[inner, :] + step_ocean * forcing_ref[...]
+
+    def put(at, new):
+        for k in range(3):
+            out_ref[k, at - MARGIN : at - MARGIN + STRIP, :] = new[k][:, :tile_y]
+
+    rows = slice(MARGIN + STRIP, MARGIN + tile_x - STRIP)
+    second_step(wide, first, bed, state, cell, face, rows, put, raise_bed)
+    bed_ref[...] = bed[inner, :tile_y]
+
+
+def ocean_ends(
+    place, wide, first, forcing_ref, s1_ref, s2_ref, inner_ref, raised_ref, out_hbm, bed_hbm,
+    out_ref, bed_ref, sems, state, bed, cell, face,
+):
+    tile_x, tile_y = raised_ref.shape
+    last = tile_x - STRIP
+    middle = pl.ds(STRIP, tile_x - 2 * STRIP)
+    copies = [
+        pltpu.make_async_copy(raised_ref, bed_hbm, sems.at[0]),
+        pltpu.make_async_copy(inner_ref.at[:, middle], out_hbm.at[:, middle], sems.at[1]),
+    ]
+    for copy in copies:
+        copy.start()
     a1, _ = unequal(place)
     force_lo = step_ocean * jnp.where(a1 > 0, s2_ref[...], s1_ref[...])[0:2]
     force_lo = jnp.where(place[0] > 0, force_lo, 0.0)
     force_hi = step_ocean * jnp.where(a1 > 0, s1_ref[...], s2_ref[...])[0:2]
     force_hi = jnp.where(place[0] < place[2] - 1, force_hi, 0.0)
-    inner = slice(MARGIN, MARGIN + tile_x)
-
-    def raised(source):
-        bed[inner, :] = source[inner, :] + step_ocean * forcing_ref[...]
-        bed[MARGIN - 2 : MARGIN, :] = source[MARGIN - 2 : MARGIN, :] + force_lo
-        above = slice(MARGIN + tile_x, MARGIN + tile_x + 2)
-        bed[above, :] = source[above, :] + force_hi
-
-    bed[0:MARGIN, :] = wide[3, 0:MARGIN, :]
-    bed[MARGIN + tile_x :, :] = wide[3, MARGIN + tile_x :, :]
-    raised(wide.at[3])
-    for at in range(8, height - 8, STRIP):
-        here = slice(at, at + STRIP)
-        change_x, change_y = sloped(wide[0, here, :], bed, at, STRIP)
-        state[0, here, :] = first[0, here, :]
-        state[1, here, :] = first[1, here, :] - change_x
-        state[2, here, :] = first[2, here, :] - change_y
-    cells(state, cell)
-    raised(bed)
-    for at in range(MARGIN, MARGIN + tile_x, STRIP):
-        new = moved(state, cell, at, STRIP)
-        change_x, change_y = sloped(state[0, at : at + STRIP, :], bed, at, STRIP)
-        new[1] -= change_x
-        new[2] -= change_y
+
+    def put(at, new):
         for k in range(3):
             out_ref[k, at - MARGIN : at - MARGIN + STRIP, :] = new[k][:, :tile_y]
-    bed_ref[...] = bed[inner, :tile_y]
-
-
-def call(body, out_shape, *args, place=None, scratch=(), held=0, copies=0, limit=VMEM_LIMIT):
-    space = pltpu.HBM if held else pltpu.VMEM
-    specs = [pl.BlockSpec(memory_space=space) for _ in args]
+
+    for n, start in enumerate((MARGIN, MARGIN + last)):
+        outer = slice(start - 16, start) if n == 0 else slice(start + STRIP, start + STRIP + 16)
+        edge = slice(MARGIN - 2, MARGIN) if n == 0 else slice(MARGIN + tile_x, MARGIN + tile_x + 2)
+        force = force_lo if n == 0 else force_hi
+        own = slice(start, start + 32) if n == 0 else slice(start - 16, start + 16)
+        forcing = forcing_ref[own.start - MARGIN : own.stop - MARGIN, :]
+        bed[outer, :] = wide[3, outer, :]
+
+        def raise_bed(source):
+            bed[own, :] = source[own, :] + step_ocean * forcing
+            bed[edge, :] = source[edge, :] + force
+
+        second_step(
+            wide, first, bed, state, cell, face, slice(start, start + STRIP), put, raise_bed
+        )
+        at = pl.ds(start - MARGIN, STRIP)
+        copies.append(pltpu.make_async_copy(out_ref.at[:, at], out_hbm.at[:, at], sems.at[2 + n]))
+        copies[-1].start()
+    for copy in copies:
+        copy.wait()
+
+
+def call(
+    body, out_shape, *args, place=None, scratch=(), held=0, sent=0, copies=0, limit=VMEM_LIMIT
+):
+    out_space = [pltpu.HBM if i < sent else pltpu.VMEM for i in range(len(out_shape))]
+    specs = [pl.BlockSpec(memory_space=pltpu.HBM if held else pltpu.VMEM) for _ in args]
+    shapes = [
+        s if isinstance(s, jax.ShapeDtypeStruct) else jax.ShapeDtypeStruct(s, F32) for s in out_shape
+    ]
     scratch = [pltpu.VMEM(s, F32) for s in scratch]
-    outer_space = pltpu.HBM if held else pltpu.VMEM
-    if held:
-        sems = pltpu.SemaphoreType.DMA((copies,))
-        scratch = [pltpu.VMEM(x.shape, x.dtype) for x in args[:held]] + [sems] + scratch
+    if copies:
+        scratch = [pltpu.SemaphoreType.DMA((copies,))] + scratch
+    scratch = [pltpu.VMEM(x.shape, x.dtype) for x in [*args[:held], *shapes[:sent]]] + scratch
     if place is not None:
         sizes, inner = place, body
 
@@ -700,12 +794,11 @@
             here = (lax.axis_index("gx"), lax.axis_index("gy"))
             inner(here + sizes, *refs)
 
-    shapes = [jax.ShapeDtypeStruct(s, F32) for s in out_shape]
     return pl.pallas_call(
         body,
         out_shape=shapes,
         in_specs=specs,
-        out_specs=[pl.BlockSpec(memory_space=outer_space) for _ in shapes],
+        out_specs=[pl.BlockSpec(memory_space=space) for space in out_space],
         scratch_shapes=scratch,
         compiler_params=pltpu.CompilerParams(vmem_limit_bytes=limit),
     )(*args)
@@ -759,19 +852,20 @@
     state = coefficients.reshape(solid)
     packed = (2 * HALF, 8 * CAP)
     for section in range(2):
-        fixed = (state, jacobian, star_mats, source_mat, deriv_mats, traces, send_faces)
         scratch = [spread, solid, solid, solid, (2 * HALF, 4 * CAP)]
         if section == 0:
+            fixed = (state, jacobian, star_mats, source_mat, deriv_mats, traces, send_faces)
             buffers = [(3 * HALF + OCEAN_ROWS, 128)] * 2 + [(HALF, 128)] * 2
             integral, table, p1, p2, own1, own2 = call(
                 start, [solid, faces] + buffers, *fixed, water_depth, momentum, bottom,
-                place=place, scratch=[(4, 8, tile_y)] * 2 + [solid, faces] + buffers + scratch,
-                held=len(fixed), copies=len(fixed) + 14, limit=START_LIMIT,
+                place=place, scratch=[(4, 8, tile_y)] * 2 + scratch,
+                held=len(fixed), sent=6, copies=len(fixed) + 14, limit=START_LIMIT,
             )
         else:
             buffers = [(3 * HALF, 128)] * 2 + [(HALF, 128)] * 2
             integral, table, p1, p2, own1, own2 = call(
-                front, [solid, faces] + buffers, *fixed, place=place, scratch=scratch
+                front_again, [solid, faces] + buffers,
+                state, jacobian, star4, *derivs, *traced, send_faces, place=place, scratch=scratch,
             )
         p2, p1 = swap(p2, "gx", 1), swap(p1, "gx", 0)
         inside = (state, jacobian, star_mats, stiff_mats, integral)
@@ -794,18 +888,34 @@
                 ocean_first,
                 [(4,) + wide_shape, (3,) + wide_shape],
                 water_depth, momentum, bottom, *halos,
-                place=place, scratch=[(5,) + wide_shape],
+                place=place, scratch=[(5,) + wide_shape, (3,) + wide_shape],
             )
             q1, q2, outer, wide, first = lax.optimization_barrier((q1, q2, outer, wide, first))
         else:
-            q1, q2, outer = lax.optimization_barrier((q1, q2, outer))
-        fixed = (normals, speed, star_mats, lifts)
+            half = lambda *shape: jax.ShapeDtypeStruct(shape, BF16)
+            size, sea = FIELDS * 8, sea_face.shape[0]
+            star4, star3, *ready = call(
+                prepared,
+                [half(8 * size, 2 * size), half(6 * size, 2 * size)]
+                + [half(2 * basis, 3 * basis), half(basis, 3 * basis)]
+                + [half(8 * FACE_PAD, basis), half(4 * FACE_PAD, basis)]
+                + [half(2 * basis, 4 * FACE_PAD), half(basis, 4 * FACE_PAD)]
+                + [half(8 * CAP, 4 * elements), half(4 * elements, sea), half(tiles, 4 * CAP, sea)],
+                star_mats, source_mat, deriv_mats, traces, lifts, face_partner,
+                sea_face.reshape(1, -1), sea_row.T,
+                place=place,
+            )
+            q1, q2, outer, *ready = lax.optimization_barrier((q1, q2, outer, *ready))
+            derivs, traced, lifting, (hot, sea_hot, slot_hot) = (
+                ready[0:2], ready[2:4], ready[4:6], ready[6:],
+            )
+        fixed = (normals, speed, star3, *lifting, hot)
         arrived = (p1, p2, q1, q2)
         flux = (FIELDS, 4 * FACE_PAD, elements)
         remote = (TABLE, 8 * CAP)
         if section == 0:
             (state,) = call(
-                back, [solid], base, table, outer, face_partner, *fixed, *arrived,
+                back, [solid], base, table, outer, *fixed, *arrived,
                 place=place, scratch=[flux, packed, remote],
             )
             halos = (p1, p2, q1, q2)
@@ -813,9 +923,9 @@
             state, outgoing = call(
                 finish,
                 [solid, (tiles, 32, 128)],
-                base, table, outer, face_partner, *fixed, *arrived,
-                traces, interp_mat, sea_face.reshape(1, -1), sea_base.T, sea_row.T,
-                place=place, scratch=[flux, packed, remote],
+                base, table, outer, *fixed, *arrived,
+                *traced, interp_mat, sea_base.T, sea_hot, slot_hot,
+                place=place, scratch=[flux, packed, remote], sent=1, copies=1,
             )
     incoming = lax.all_to_all(outgoing, "gy", split_axis=0, concat_axis=0, tiled=True)
     forcing, s1, s2 = call(
@@ -825,12 +935,12 @@
         place=place,
     )
     s2, s1 = swap(s2, "gx", 1, wrap=True), swap(s1, "gx", 0)
+    scratch = [(3,) + wide_shape, wide_shape, (5,) + wide_shape, (3,) + wide_shape]
+    water = [(3, tile_x, tile_y), (tile_x, tile_y)]
+    inner, raised = call(ocean_inner, water, wide, first, forcing, scratch=scratch)
     ocean_final, bed_final = call(
-        ocean_last,
-        [(3, tile_x, tile_y), (tile_x, tile_y)],
-        wide, first, forcing, s1, s2,
-        place=place,
-        scratch=[(3,) + wide_shape, wide_shape, (5,) + wide_shape],
+        ocean_ends, water, wide, first, forcing, s1, s2, inner, raised,
+        place=place, scratch=scratch, sent=2, copies=4,
     )
     return (state.reshape(coefficients.shape), ocean_final, bed_final)
 

time: 79.4 us -> 75.8 us (0.955)
  waiting for transfers between devices: 12.4 us -> 9.58 us
  Pallas kernels: 35.8 us -> 34.9 us
    ppermute x10, waiting for transfers between devices: 12.4 us -> 9.58 us  [swap(): return lax.ppermute(block, axis, pairs)]
    pallas_call x13 -> x15, Pallas kernels: 35.8 us -> 34.9 us  [call(): pl.pallas_call(body, out_shape=shapes, in_specs=specs, out_specs=[pl.Bloc...]
  transfers between devices with their start and end apart: 10 -> 10, of which waited for: 5 -> 4; matrix products, arithmetic and copies ran while one was open for 0% -> 0% of each run, Pallas kernels for 12% -> 18%
where the time goes in v3:
time: 75.8 us; the launch traced here: 75.2 us
  Pallas kernels  34.9 us (46%)
  starting transfers between devices  16.6 us (22%)
  blocking collectives  11.6 us (15%)
  waiting for transfers between devices  9.58 us (13%)
  between operations  1.27 us (2%)
  local copies, waits for them, and re-layouts  1.23 us (2%)
    pallas_call x15, Pallas kernels, call(): pl.pallas_call(body, out_shape=shapes, in_specs=specs, out_specs=[pl.Bloc...  34.9 us
    ppermute x10, starting transfers between devices, swap(): return lax.ppermute(block, axis, pairs)  16.6 us
    all_to_all x1, blocking collectives, per_device(): lax.all_to_all(outgoing, 'gy', split_axis=0, concat_axis=0, tiled=True)  11.6 us
    ppermute x10, waiting for transfers between devices, swap(): return lax.ppermute(block, axis, pairs)  9.58 us
  transfers between devices with their start and end apart: 10, of which 4 were waited for; matrix products, arithmetic and copies ran while one was open for 0% of the time, Pallas kernels for 18%

profile of v3, /device:TPU:1, one launch (start us, length us, event | category | flops | bytes accessed | tf_op | source)
XLA Modules:
  0.0 75.2 jit_solution(16079080691062527761)
XLA Ops:
  0.6 0.0 copy-start.6
  0.6 0.0 copy-start.9
  0.7 0.0 copy-start.4
  0.7 0.0 copy-start.1
  0.7 0.0 copy-start.3
  0.7 0.0 copy-start.2
  0.7 0.0 copy-start.8
  0.7 7.8 %shard_map.202 = (f32[728,256]{1,0:T(8,128)}, f32[312,1024]{1,0:T(8,128)}, f32[448,128]{1,0:T(8,128)}, f32[448,128]{1,0:T(8,128)}, f32[144,128]{1,0:T(8,128)}, /*index=5*/f32[144,128]{1,0:T(8,128)}) custom-call(f32[728,256]{1,0:T(8,128)} %bitcast.9, f32[3,3,256]{2,1,0:T(4,128)} %jac_ref.1, f32[3,13,13]{2,1,0:T(8,128)} %star_ref.1, f32[13,13]{1,0:T(8,128)} %refs_1_.7, ...), custom_call_target="tpu_custom_call" | custom-call | tf_op jit(solution)/shard_map/pallas_call | solution.py:797
  8.5 0.1 collective-permute-start
  8.6 4.5 %collective-permute-start.1 = (f32[448,128]{1,0:T(8,128)}, f32[448,128]{1,0:T(8,128)S(1)}, u32[]{:S(2)}, u32[]{:S(2)}) collective-permute-start(f32[448,128]{1,0:T(8,128)} %get-tuple-element.68), channel_id=1, source_target_pairs={{8,16},{16,8},{0,0},{24,24},{9,17},{17,9},{1,1},{25,25},{10,18},{1... | collective-permute-start | bytes 688136 | tf_op jit(solution)/shard_map/ppermute | solution.py:815
  13.1 0.0 copy-done.6
  13.1 0.0 copy-done.9
  13.2 0.0 copy-done.4
  13.2 0.0 copy-done.1
  13.2 0.0 copy-start.5
  13.2 1.1 %copy-done.5 = f32[728,256]{1,0:T(8,128)S(1)} copy-done((f32[728,256]{1,0:T(8,128)S(1)}, f32[728,256]{1,0:T(8,128)}, u32[]{:S(2)}) %copy-start.5) | copy-done | bytes 745496
  14.3 2.5 %shard_map.203 = (f32[728,256]{1,0:T(8,128)S(1)}, f32[16,128]{1,0:T(8,128)S(1)}, f32[16,128]{1,0:T(8,128)S(1)}) custom-call(f32[728,256]{1,0:T(8,128)S(1)} %bitcast.10, f32[3,3,256]{2,1,0:T(4,128)S(1)} %copy-done.9, f32[3,13,13]{2,1,0:T(8,128)S(1)} %copy-done.6, f32[3,56,56]{2,1,0:T(8,128)S(1)} %copy-done.8, f32[728,256]{1,0:T(8,128)S(1)} %copy-done.5, ...), custom_call_target="tpu_custom_call" | custom-call | tf_op jit(solution)/shard_map/pallas_call | solution.py:797
  16.9 0.0 collective-permute-done.refs_0_.refs_9_.refs_3_
  16.9 0.2 collective-permute-done.1.refs_1_.refs_10_.refs_4_
  17.1 1.9 %collective-permute-start.2 = (f32[464,128]{1,0:T(8,128)S(1)}, f32[464,128]{1,0:T(8,128)S(1)}, u32[]{:S(2)}, u32[]{:S(2)}) collective-permute-start(f32[464,128]{1,0:T(8,128)S(1)} %get-tuple-element.79), channel_id=1, source_target_pairs={{0,1},{1,0},{2,3},{3,2},{4,5},{5,4},{6,7},{7,6},{8,9},{9,8},{10,11... | collective-permute-start | bytes 712712 | tf_op jit(solution)/shard_map/ppermute | solution.py:815
  18.9 0.8 %collective-permute-start.3 = (f32[464,128]{1,0:T(8,128)S(1)}, f32[464,128]{1,0:T(8,128)S(1)}, u32[]{:S(2)}, u32[]{:S(2)}) collective-permute-start(f32[464,128]{1,0:T(8,128)S(1)} %get-tuple-element.80), channel_id=1, source_target_pairs={{1,2},{2,1},{3,4},{4,3},{5,6},{6,5},{0,0},{7,7},{9,10},{10,9},{11,... | collective-permute-start | bytes 712712 | tf_op jit(solution)/shard_map/ppermute | solution.py:815
  19.8 0.0 copy-start.7
  19.8 0.0 copy-start.10
  19.8 0.0 copy-start.14
  19.9 0.0 copy-start.16
  19.9 0.0 copy-start.21
  19.9 0.0 copy-start.22
  19.9 0.0 copy-start.13
  19.9 0.0 copy-start.19
  19.9 1.5 %shard_map.205.refs_2_ = f32[312,1024]{1,0:T(8,128)S(1)} custom-call(f32[312,1024]{1,0:T(8,128)S(1)} %copy-done, s32[4,256]{1,0:T(4,128)S(1)} %copy-done.15), custom_call_target="tpu_custom_call" | custom-call | tf_op jit(solution)/shard_map/pallas_call | solution.py:797
  21.4 0.0 copy-done.7
  21.5 0.0 copy-done.10
  21.5 0.0 copy-done.14
  21.5 0.0 copy-done.16
  21.5 0.0 copy-done.21
  21.5 0.0 copy-done.22
  21.5 1.3 %shard_map.206 = (bf16[832,208]{1,0:T(8,128)(2,1)S(1)}, bf16[624,208]{1,0:T(8,128)(2,1)S(1)}, bf16[112,168]{1,0:T(8,128)(2,1)S(1)}, bf16[56,168]{1,0:T(8,128)(2,...) custom-call(f32[3,13,13]{2,1,0:T(8,128)S(1)} %copy-done.6, ...), custom_call_target="tpu_custom_call" | custom-call | tf_op jit(solution)/shard_map/pallas_call | solution.py:797
  22.9 5.1 %collective-permute-done.2.refs_11_.refs_5_ = f32[464,128]{1,0:T(8,128)S(1)} collective-permute-done((f32[464,128]{1,0:T(8,128)S(1)}, f32[464,128]{1,0:T(8,128)S(1)}, u32[]{:S(2)}, u32[]{:S(2)}) %collective-permute-start.2) | collective-permute-done | bytes 237600 | tf_op jit(solution)/shard_map/ppermute | solution.py:815
  27.9 0.0 collective-permute-done.3.refs_12_.refs_6_
  28.0 2.6 %shard_map.207.refs_0_.q_ref = f32[728,256]{1,0:T(8,128)S(1)} custom-call(f32[728,256]{1,0:T(8,128)S(1)} %get-tuple-element.71.refs_0_, f32[312,1024]{1,0:T(8,128)S(1)} %copy-done, f32[312,1024]{1,0:T(8,128)S(1)} %shard_map.205.refs_2_, f32[3,4,256]{2,1,0:T(4,128)S(1)} %bitcast.13, f32[1,256]{1,0:T(1,128)S(1)} %bitcast.16, ...), custom_call_target="tpu_custom_call" | custom-call | tf_op jit(solution)/shard_map/pallas_call | solution.py:797
  30.6 5.0 %shard_map.208 = (f32[728,256]{1,0:T(8,128)S(1)}, f32[312,1024]{1,0:T(8,128)S(1)}, f32[432,128]{1,0:T(8,128)S(1)}, f32[432,128]{1,0:T(8,128)S(1)}, f32[144,128]{1,0:T(8,128)S(1)}, /*index=5*/f32[144,128]{1,0:T(8,128)S(1)}) custom-call(f32[728,256]{1,0:T(8,128)S(1)} %shard_map.207.refs_0_.q_ref, f32[3,3,256]{2,1,0:T(4,128)S(1)} %copy-done.9, ...), custom_call_target="tpu_custom_call" | custom-call | tf_op jit(solution)/shard_map/pallas_call | solution.py:797
  35.6 0.1 collective-permute-start.4
  35.6 3.1 %collective-permute-start.5 = (f32[432,128]{1,0:T(8,128)S(1)}, f32[432,128]{1,0:T(8,128)S(1)}, u32[]{:S(2)}, u32[]{:S(2)}) collective-permute-start(f32[432,128]{1,0:T(8,128)S(1)} %get-tuple-element.103), channel_id=1, source_target_pairs={{8,16},{16,8},{0,0},{24,24},{9,17},{17,9},{1,1},{25,25},{10,18},{1... | collective-permute-start | bytes 663560 | tf_op jit(solution)/shard_map/ppermute | solution.py:815
  38.7 1.8 %shard_map.209.refs_0_ = f32[728,256]{1,0:T(8,128)S(1)} custom-call(f32[728,256]{1,0:T(8,128)S(1)} %shard_map.207.refs_0_.q_ref, f32[3,3,256]{2,1,0:T(4,128)S(1)} %copy-done.9, f32[3,13,13]{2,1,0:T(8,128)S(1)} %copy-done.6, f32[3,56,56]{2,1,0:T(8,128)S(1)} %copy-done.8, f32[728,256]{1,0:T(8,128)S(1)} %get-tuple-element.104.integral_ref), custom_call_target="tpu_custom_call" | custom-call | tf_op jit(solution)/shard_map/pallas_call | solution.py:797
  40.5 0.0 collective-permute-done.4.refs_0_.refs_9_
  40.5 2.7 %collective-permute-done.5.refs_1_.refs_10_ = f32[432,128]{1,0:T(8,128)S(1)} collective-permute-done((f32[432,128]{1,0:T(8,128)S(1)}, f32[432,128]{1,0:T(8,128)S(1)}, u32[]{:S(2)}, u32[]{:S(2)}) %collective-permute-start.5) | collective-permute-done | bytes 221216 | tf_op jit(solution)/shard_map/ppermute | solution.py:815
  43.2 2.0 %collective-permute-start.6 = (f32[432,128]{1,0:T(8,128)S(1)}, f32[432,128]{1,0:T(8,128)S(1)}, u32[]{:S(2)}, u32[]{:S(2)}) collective-permute-start(f32[432,128]{1,0:T(8,128)S(1)} %get-tuple-element.111), channel_id=1, source_target_pairs={{0,1},{1,0},{2,3},{3,2},{4,5},{5,4},{6,7},{7,6},{8,9},{9,8},{10,11... | collective-permute-start | bytes 663560 | tf_op jit(solution)/shard_map/ppermute | solution.py:815
  45.2 0.9 %collective-permute-start.7 = (f32[432,128]{1,0:T(8,128)S(1)}, f32[432,128]{1,0:T(8,128)S(1)}, u32[]{:S(2)}, u32[]{:S(2)}) collective-permute-start(f32[432,128]{1,0:T(8,128)S(1)} %get-tuple-element.112), channel_id=1, source_target_pairs={{1,2},{2,1},{3,4},{4,3},{5,6},{6,5},{0,0},{7,7},{9,10},{10,9},{11,... | collective-permute-start | bytes 663560 | tf_op jit(solution)/shard_map/ppermute | solution.py:815
  46.1 2.3 %shard_map.212 = (f32[4,288,384]{2,1,0:T(8,128)S(1)}, f32[3,288,384]{2,1,0:T(8,128)S(1)}) custom-call(f32[256,256]{1,0:T(8,128)S(1)} %copy-done.3, f32[2,256,256]{2,1,0:T(8,128)S(1)} %copy-done.1, f32[256,256]{1,0:T(8,128)S(1)} %copy-done.4, f32[448,128]{1,0:T(8,128)S(1)} %collective-permute-done.refs_0_.refs_9_.refs_3_, ...), custom_call_target="tpu_custom_call" | custom-call | tf_op jit(solution)/shard_map/pallas_call | solution.py:797
  48.4 0.0 copy-start.18
  48.5 0.0 copy-start.20
  48.5 1.5 %shard_map.211.refs_2_ = f32[312,1024]{1,0:T(8,128)S(1)} custom-call(f32[312,1024]{1,0:T(8,128)S(1)} %get-tuple-element.106.table_ref.refs_1_, s32[4,256]{1,0:T(4,128)S(1)} %copy-done.15), custom_call_target="tpu_custom_call" | custom-call | tf_op jit(solution)/shard_map/pallas_call | solution.py:797
  50.0 1.6 %collective-permute-done.6.refs_11_ = f32[432,128]{1,0:T(8,128)S(1)} collective-permute-done((f32[432,128]{1,0:T(8,128)S(1)}, f32[432,128]{1,0:T(8,128)S(1)}, u32[]{:S(2)}, u32[]{:S(2)}) %collective-permute-start.6) | collective-permute-done | bytes 221216 | tf_op jit(solution)/shard_map/ppermute | solution.py:815
  51.6 0.0 collective-permute-done.7.refs_12_
  51.6 0.0 copy-done.18
  51.6 3.5 %shard_map.213 = (f32[728,256]{1,0:T(8,128)}, f32[8,32,128]{2,1,0:T(8,128)S(1)}) custom-call(f32[728,256]{1,0:T(8,128)S(1)} %shard_map.209.refs_0_, f32[312,1024]{1,0:T(8,128)S(1)} %get-tuple-element.106.table_ref.refs_1_, f32[312,1024]{1,0:T(8,128)S(1)} %shard_map.211.refs_2_, f32[3,4,256]{2,1,0:T(4,128)S(1)} %bitcast.14, f32[1,256]{1,0:T(1,128)S(1)} %bitcast.17, ...), custom_call_target="tpu_custom_call" | custom-call | tf_op jit(solution)/shard_map/pallas_call | solution.py:797
  55.1 11.6 %all_to_all.5.refs_0_ = f32[8,32,128]{2,1,0:T(8,128)S(1)} all-to-all(f32[8,32,128]{2,1,0:T(8,128)S(1)} %get-tuple-element.123), channel_id=1, replica_groups=mesh['gx'=4,'gy'=8] {'gy'}, dimensions={0} | all-to-all | bytes 262144 | tf_op jit(solution)/shard_map/all_to_all | solution.py:930
  66.7 1.6 %shard_map.214 = (f32[256,384]{1,0:T(8,128)S(1)}, f32[8,384]{1,0:T(8,128)S(1)}, f32[8,384]{1,0:T(8,128)S(1)}) custom-call(f32[8,32,128]{2,1,0:T(8,128)S(1)} %all_to_all.5.refs_0_), custom_call_target="tpu_custom_call" | custom-call | tf_op jit(solution)/shard_map/pallas_call | solution.py:797
  68.4 0.1 collective-permute-start.8
  68.4 3.2 %collective-permute-start.9 = (f32[8,384]{1,0:T(8,128)S(1)}, f32[8,384]{1,0:T(8,128)S(1)}, u32[]{:S(2)}, u32[]{:S(2)}) collective-permute-start(f32[8,384]{1,0:T(8,128)S(1)} %get-tuple-element.126), channel_id=1, source_target_pairs={{8,16},{16,8},{24,0},{0,24},{9,17},{17,9},{25,1},{1,25},{10,18},{1... | collective-permute-start | bytes 36872 | tf_op jit(solution)/shard_map/ppermute | solution.py:815
  71.6 2.3 %shard_map.215 = (f32[3,256,256]{2,1,0:T(8,128)S(1)}, f32[256,256]{1,0:T(8,128)S(1)}) custom-call(f32[4,288,384]{2,1,0:T(8,128)S(1)} %get-tuple-element.121.wide.refs_0_, f32[3,288,384]{2,1,0:T(8,128)S(1)} %get-tuple-element.122.first.refs_1_, f32[256,384]{1,0:T(8,128)S(1)} %get-tuple-element.124.forcing_ref.refs_2_), custom_call_target="tpu_custom_call" | custom-call | tf_op jit(solution)/shard_map/pallas_call | solution.py:797
  73.9 0.0 collective-permute-done.8.refs_3_
  73.9 0.0 collective-permute-done.9.refs_4_
  74.0 1.0 %shard_map.216 = (f32[3,256,256]{2,1,0:T(8,128)}, f32[256,256]{1,0:T(8,128)}) custom-call(f32[4,288,384]{2,1,0:T(8,128)S(1)} %get-tuple-element.121.wide.refs_0_, f32[3,288,384]{2,1,0:T(8,128)S(1)} %get-tuple-element.122.first.refs_1_, f32[256,384]{1,0:T(8,128)S(1)} %get-tuple-element.124.forcing_ref.refs_2_, f32[8,384]{1,0:T(8,128)S(1)} %collective-permute-done.8.refs_3_, ...), custom_call_target="tpu_custom_call" | custom-call | tf_op jit(solution)/shard_map/pallas_call | solution.py:797
  (18 shorter events, 0.1 us)
Async XLA Ops:
  0.6 12.5 %copy-start.6 = (f32[3,13,13]{2,1,0:T(8,128)S(1)}, f32[3,13,13]{2,1,0:T(8,128)}, u32[]{:S(2)}) copy-start(f32[3,13,13]{2,1,0:T(8,128)} %star_ref.1) | copy-start | bytes 6088
  0.6 12.5 %copy-start.9 = (f32[3,3,256]{2,1,0:T(4,128)S(1)}, f32[3,3,256]{2,1,0:T(4,128)}, u32[]{:S(2)}) copy-start(f32[3,3,256]{2,1,0:T(4,128)} %jac_ref.1) | copy-start | bytes 27652
  0.7 12.5 %copy-start.4 = (f32[256,256]{1,0:T(8,128)S(1)}, f32[256,256]{1,0:T(8,128)}, u32[]{:S(2)}) copy-start(f32[256,256]{1,0:T(8,128)} %refs_2_.7) | copy-start | bytes 786436
  0.7 12.5 %copy-start.1 = (f32[2,256,256]{2,1,0:T(8,128)S(1)}, f32[2,256,256]{2,1,0:T(8,128)}, u32[]{:S(2)}) copy-start(f32[2,256,256]{2,1,0:T(8,128)} %refs_1_.9) | copy-start | bytes 1572868
  0.7 12.5 %copy-start.3 = (f32[256,256]{1,0:T(8,128)S(1)}, f32[256,256]{1,0:T(8,128)}, u32[]{:S(2)}) copy-start(f32[256,256]{1,0:T(8,128)} %refs_0_.3) | copy-start | bytes 786436
  0.7 12.5 %copy-start.2 = (f32[13,56,256]{2,1,0:T(8,128)S(1)}, f32[13,56,256]{2,1,0:T(8,128)}, u32[]{:S(2)}) copy-start(f32[13,56,256]{2,1,0:T(8,128)} %param.19) | copy-start | bytes 2236420
  0.7 12.5 %copy-start.8 = (f32[3,56,56]{2,1,0:T(8,128)S(1)}, f32[3,56,56]{2,1,0:T(8,128)}, u32[]{:S(2)}) copy-start(f32[3,56,56]{2,1,0:T(8,128)} %stiff_ref.1) | copy-start | bytes 112900
  8.5 8.4 %collective-permute-start = (f32[448,128]{1,0:T(8,128)}, f32[448,128]{1,0:T(8,128)S(1)}, u32[]{:S(2)}, u32[]{:S(2)}) collective-permute-start(f32[448,128]{1,0:T(8,128)} %get-tuple-element.67), channel_id=1, source_target_pairs={{0,8},{8,0},{16,24},{24,16},{1,9},{9,1},{17,25},{25,17},{2,10},{10... | collective-permute-start | bytes 688136 | tf_op jit(solution)/shard_map/ppermute | solution.py:815
  8.6 8.4 %collective-permute-start.1 = (f32[448,128]{1,0:T(8,128)}, f32[448,128]{1,0:T(8,128)S(1)}, u32[]{:S(2)}, u32[]{:S(2)}) collective-permute-start(f32[448,128]{1,0:T(8,128)} %get-tuple-element.68), channel_id=1, source_target_pairs={{8,16},{16,8},{0,0},{24,24},{9,17},{17,9},{1,1},{25,25},{10,18},{1... | collective-permute-start | bytes 688136 | tf_op jit(solution)/shard_map/ppermute | solution.py:815
  13.2 1.1 %copy-start.5 = (f32[728,256]{1,0:T(8,128)S(1)}, f32[728,256]{1,0:T(8,128)}, u32[]{:S(2)}) copy-start(f32[728,256]{1,0:T(8,128)} %get-tuple-element.69.refs_4_) | copy-start | bytes 2236420
  14.3 2.7 %copy-start.11 = (f32[144,128]{1,0:T(8,128)S(1)}, f32[144,128]{1,0:T(8,128)}, u32[]{:S(2)}) copy-start(f32[144,128]{1,0:T(8,128)} %get-tuple-element.75.refs_2_) | copy-start | bytes 221188
  14.3 2.7 %copy-start.12 = (f32[144,128]{1,0:T(8,128)S(1)}, f32[144,128]{1,0:T(8,128)}, u32[]{:S(2)}) copy-start(f32[144,128]{1,0:T(8,128)} %get-tuple-element.76.refs_3_) | copy-start | bytes 221188
  14.3 5.5 %copy-start = (f32[312,1024]{1,0:T(8,128)S(1)}, f32[312,1024]{1,0:T(8,128)}, u32[]{:S(2)}) copy-start(f32[312,1024]{1,0:T(8,128)} %get-tuple-element.72.table_ref.refs_1_) | copy-start | bytes 3833860
  14.3 5.5 %copy-start.15 = (s32[4,256]{1,0:T(4,128)S(1)}, s32[4,256]{1,0:T(4,128)}, u32[]{:S(2)}) copy-start(s32[4,256]{1,0:T(4,128)} %partner_ref.3) | copy-start | bytes 12292
  17.1 10.9 %collective-permute-start.2 = (f32[464,128]{1,0:T(8,128)S(1)}, f32[464,128]{1,0:T(8,128)S(1)}, u32[]{:S(2)}, u32[]{:S(2)}) collective-permute-start(f32[464,128]{1,0:T(8,128)S(1)} %get-tuple-element.79), channel_id=1, source_target_pairs={{0,1},{1,0},{2,3},{3,2},{4,5},{5,4},{6,7},{7,6},{8,9},{9,8},{10,11... | collective-permute-start | bytes 712712 | tf_op jit(solution)/shard_map/ppermute | solution.py:815
  18.9 9.0 %collective-permute-start.3 = (f32[464,128]{1,0:T(8,128)S(1)}, f32[464,128]{1,0:T(8,128)S(1)}, u32[]{:S(2)}, u32[]{:S(2)}) collective-permute-start(f32[464,128]{1,0:T(8,128)S(1)} %get-tuple-element.80), channel_id=1, source_target_pairs={{1,2},{2,1},{3,4},{4,3},{5,6},{6,5},{0,0},{7,7},{9,10},{10,9},{11,... | collective-permute-start | bytes 712712 | tf_op jit(solution)/shard_map/ppermute | solution.py:815
  19.8 1.6 %copy-start.7 = (f32[3,56,56]{2,1,0:T(8,128)S(1)}, f32[3,56,56]{2,1,0:T(8,128)}, u32[]{:S(2)}) copy-start(f32[3,56,56]{2,1,0:T(8,128)} %refs_2_.6) | copy-start | bytes 112900
  19.8 1.6 %copy-start.10 = (f32[4,21,56]{2,0,1:T(4,128)S(1)}, f32[4,21,56]{2,0,1:T(4,128)}, u32[]{:S(2)}) copy-start(f32[4,21,56]{2,0,1:T(4,128)} %param.27) | copy-start | bytes 56452
  19.8 1.6 %copy-start.14 = (f32[4,56,21]{1,0,2:T(4,128)S(1)}, f32[4,56,21]{1,0,2:T(4,128)}, u32[]{:S(2)}) copy-start(f32[4,56,21]{1,0,2:T(4,128)} %param.28) | copy-start | bytes 56452
  19.9 1.6 %copy-start.16 = (f32[13,13]{1,0:T(8,128)S(1)}, f32[13,13]{1,0:T(8,128)}, u32[]{:S(2)}) copy-start(f32[13,13]{1,0:T(8,128)} %refs_1_.7) | copy-start | bytes 2032
  19.9 1.6 %copy-start.21 = (s32[256]{0:T(256)S(1)}, s32[256]{0:T(256)}, u32[]{:S(2)}) copy-start(s32[256]{0:T(256)} %param.31) | copy-start | bytes 3076
  19.9 1.6 %copy-start.22 = (s32[256,1]{0,1:T(1,128)S(1)}, s32[256,1]{0,1:T(1,128)}, u32[]{:S(2)}) copy-start(s32[256,1]{0,1:T(1,128)} %param.32) | copy-start | bytes 3076
  19.9 8.1 %copy-start.13 = (f32[4,3,256]{2,0,1:T(4,128)S(1)}, f32[4,3,256]{2,0,1:T(4,128)}, u32[]{:S(2)}) copy-start(f32[4,3,256]{2,0,1:T(4,128)} %param.21) | copy-start | bytes 36868
  19.9 8.1 %copy-start.19 = (f32[256]{0:T(256)S(1)}, f32[256]{0:T(256)}, u32[]{:S(2)}) copy-start(f32[256]{0:T(256)} %param.22) | copy-start | bytes 3076
  28.0 2.6 %copy-start.17 = (s32[8,64]{1,0:T(8,128)S(1)}, s32[8,64]{1,0:T(8,128)}, u32[]{:S(2)}) copy-start(s32[8,64]{1,0:T(8,128)} %refs_7_.5) | copy-start | bytes 6148
  35.6 4.9 %collective-permute-start.4 = (f32[432,128]{1,0:T(8,128)S(1)}, f32[432,128]{1,0:T(8,128)S(1)}, u32[]{:S(2)}, u32[]{:S(2)}) collective-permute-start(f32[432,128]{1,0:T(8,128)S(1)} %get-tuple-element.102), channel_id=1, source_target_pairs={{0,8},{8,0},{16,24},{24,16},{1,9},{9,1},{17,25},{25,17},{2,10},{10... | collective-permute-start | bytes 663560 | tf_op jit(solution)/shard_map/ppermute | solution.py:815
  35.6 7.5 %collective-permute-start.5 = (f32[432,128]{1,0:T(8,128)S(1)}, f32[432,128]{1,0:T(8,128)S(1)}, u32[]{:S(2)}, u32[]{:S(2)}) collective-permute-start(f32[432,128]{1,0:T(8,128)S(1)} %get-tuple-element.103), channel_id=1, source_target_pairs={{8,16},{16,8},{0,0},{24,24},{9,17},{17,9},{1,1},{25,25},{10,18},{1... | collective-permute-start | bytes 663560 | tf_op jit(solution)/shard_map/ppermute | solution.py:815
  43.2 8.4 %collective-permute-start.6 = (f32[432,128]{1,0:T(8,128)S(1)}, f32[432,128]{1,0:T(8,128)S(1)}, u32[]{:S(2)}, u32[]{:S(2)}) collective-permute-start(f32[432,128]{1,0:T(8,128)S(1)} %get-tuple-element.111), channel_id=1, source_target_pairs={{0,1},{1,0},{2,3},{3,2},{4,5},{5,4},{6,7},{7,6},{8,9},{9,8},{10,11... | collective-permute-start | bytes 663560 | tf_op jit(solution)/shard_map/ppermute | solution.py:815
  45.2 6.4 %collective-permute-start.7 = (f32[432,128]{1,0:T(8,128)S(1)}, f32[432,128]{1,0:T(8,128)S(1)}, u32[]{:S(2)}, u32[]{:S(2)}) collective-permute-start(f32[432,128]{1,0:T(8,128)S(1)} %get-tuple-element.112), channel_id=1, source_target_pairs={{1,2},{2,1},{3,4},{4,3},{5,6},{6,5},{0,0},{7,7},{9,10},{10,9},{11,... | collective-permute-start | bytes 663560 | tf_op jit(solution)/shard_map/ppermute | solution.py:815
  48.4 3.2 %copy-start.18 = (f32[16,21]{1,0:T(8,128)S(1)}, f32[16,21]{1,0:T(8,128)}, u32[]{:S(2)}) copy-start(f32[16,21]{1,0:T(8,128)} %refs_15_.1) | copy-start | bytes 4036
  48.5 3.2 %copy-start.20 = (s32[256,2]{0,1:T(2,128)S(1)}, s32[256,2]{0,1:T(2,128)}, u32[]{:S(2)}) copy-start(s32[256,2]{0,1:T(2,128)} %param.33) | copy-start | bytes 6148
  68.4 5.6 %collective-permute-start.8 = (f32[8,384]{1,0:T(8,128)S(1)}, f32[8,384]{1,0:T(8,128)S(1)}, u32[]{:S(2)}, u32[]{:S(2)}) collective-permute-start(f32[8,384]{1,0:T(8,128)S(1)} %get-tuple-element.125), channel_id=1, source_target_pairs={{0,8},{8,0},{16,24},{24,16},{1,9},{9,1},{17,25},{25,17},{2,10},{10... | collective-permute-start | bytes 36872 | tf_op jit(solution)/shard_map/ppermute | solution.py:815
  68.4 5.5 %collective-permute-start.9 = (f32[8,384]{1,0:T(8,128)S(1)}, f32[8,384]{1,0:T(8,128)S(1)}, u32[]{:S(2)}, u32[]{:S(2)}) collective-permute-start(f32[8,384]{1,0:T(8,128)S(1)} %get-tuple-element.126), channel_id=1, source_target_pairs={{8,16},{16,8},{24,0},{0,24},{9,17},{17,9},{25,1},{1,25},{10,18},{1... | collective-permute-start | bytes 36872 | tf_op jit(solution)/shard_map/ppermute | solution.py:815

commit v4 on v3

--- a/solution.py
+++ b/solution.py
@@ -14,7 +14,7 @@
 CAP = 64
 TABLE = FIELDS * FACE_PAD
 WIDE = 320
-HALF = 144
+HALF = 137
 OCEAN_ROWS = 16
 MARGIN = 16
 
@@ -66,6 +66,18 @@
 def weighted(stack, high, x):
     x_high, x_low = parts(x)
     return folded(dot(stack, x_high)) + dot(high, x_low)
+
+
+def side_weights(w):
+    columns = w.shape[1]
+    high, low = parts(w)
+    place = [selector(columns, 3 * columns, i * columns).astype(BF16) for i in range(3)]
+    return (dot(high, place[0] + place[1]) + dot(low, place[2])).astype(BF16)
+
+
+def side_weighted(stack, x):
+    high = x.astype(BF16).astype(F32)
+    return dot(stack, jnp.concatenate([high, x - high, high], axis=0).astype(BF16))
 
 
 def selector(rows, columns, shift):
@@ -149,11 +161,11 @@
     star = star_weights([star_ref[0], star_ref[1], star_ref[2], source_ref[...]])
     ready(4, 5)
     basis_weights = weights(side_by_side([deriv_ref[d] for d in range(3)]))
-    return star, basis_weights, weights(stacked_traces(trace_ref))
-
-
-def front_again(place, q_ref, jac_ref, star_ref, b1_ref, b2_ref, t1_ref, t2_ref, *refs):
-    held = star_ref[...], (b1_ref[...], b2_ref[...]), (t1_ref[...], t2_ref[...])
+    return star, basis_weights, side_weights(stacked_traces(trace_ref))
+
+
+def front_again(place, q_ref, jac_ref, star_ref, b1_ref, b2_ref, trace_ref, *refs):
+    held = star_ref[...], (b1_ref[...], b2_ref[...]), trace_ref[...]
     front(place, held, q_ref, jac_ref, *refs)
 
 
@@ -175,7 +187,7 @@
         rows = slice(g * basis, (g + 1) * basis)
         whole = first * q_ref[rows, :] + second * d1_ref[rows, :] + third * d2_ref[rows, :]
         integral_ref[rows, :] = whole
-        faces = weighted(*trace, whole)
+        faces = side_weighted(trace, whole)
         for f in range(4):
             table_ref[g * FACE_PAD : (g + 1) * FACE_PAD, f * elements : (f + 1) * elements] = faces[
                 f * FACE_PAD : (f + 1) * FACE_PAD
@@ -301,13 +313,36 @@
                     at += 2
 
 
-def local_faces(table_ref, partner_ref, outer_ref):
+def star_flux(star, normals, speed, inner, outer):
+    size = FIELDS * 8
+    y = folded(dot(star, both_parts(inner + outer)))
+    flux = speed * (inner - outer)
+    for c in range(3):
+        flux = flux + normals[c] * y[c * size : (c + 1) * size]
+    return flux
+
+
+def local_flux(table_ref, partner_ref, normal_ref, speed_ref, star_ref, flux_ref, outer_ref):
     elements = partner_ref.shape[1]
     stack = table_parts(table_ref)
     codes = iota((4 * elements, elements), 0)
+    star = star_ref[...]
+    speed = 0.5 * speed_ref[...]
     for f in range(4):
         hot = (codes == partner_ref[f : f + 1, :]).astype(F32).astype(BF16)
         outer_ref[:, f * elements : (f + 1) * elements] = folded(dot(stack, hot))[:TABLE]
+    for part in range(FACE_PAD // 8):
+        at = [slice(g * FACE_PAD + 8 * part, g * FACE_PAD + 8 * part + 8) for g in range(FIELDS)]
+        for f in range(4):
+            normals = [0.5 * normal_ref[c, f : f + 1, :] for c in range(3)]
+            columns = slice(f * elements, (f + 1) * elements)
+            inner = jnp.concatenate([table_ref[rows, columns] for rows in at], axis=0)
+            outer = jnp.concatenate([outer_ref[rows, columns] for rows in at], axis=0)
+            flux = star_flux(star, normals, speed, inner, outer)
+            for g in range(FIELDS):
+                flux_ref[g, f * FACE_PAD + 8 * part : f * FACE_PAD + 8 * part + 8, :] = flux[
+                    8 * g : 8 * g + 8
+                ]
 
 
 def remote_blocks(place, p1, p2, q1, q2):
@@ -326,10 +361,10 @@
 
 def prepared(
     place, star_ref, source_ref, deriv_ref, trace_ref, lift_ref, partner_ref,
-    sea_face_ref, sea_row_ref,
-    star4_ref, star3_ref, b1_ref, b2_ref, t1_ref, t2_ref, l1_ref, l2_ref, hot_ref, sea_ref, slot_ref,
+    sea_face_ref, sea_row_ref, normal_ref, speed_ref,
+    star4_ref, star3_ref, b1_ref, b2_ref, t_ref, l1_ref, l2_ref, hot_ref, sea_ref, slot_ref, scale_ref,
 ):
-    star, (b1_ref[...], b2_ref[...]), (t1_ref[...], t2_ref[...]) = front_weights(
+    star, (b1_ref[...], b2_ref[...]), t_ref[...] = front_weights(
         star_ref, source_ref, deriv_ref, trace_ref
     )
     star4_ref[...] = star
@@ -343,6 +378,14 @@
         hot_ref[:, f * elements : (f + 1) * elements] = jnp.concatenate(
             [(slot + CAP * block[2] == wanted).astype(F32) for block in blocks], axis=0
         ).astype(BF16)
+    scales = [
+        jnp.concatenate([normal_ref[c, f : f + 1, :] for f in range(4)], axis=1) for c in range(3)
+    ]
+    scales.append(jnp.concatenate([speed_ref[...]] * 4, axis=1))
+    scales = 0.5 * jnp.concatenate(scales + [jnp.zeros((4, 4 * elements), F32)], axis=0)
+    scale_ref[...] = folded(
+        lax.dot_general(both_parts(scales), hot_ref[...], NT, preferred_element_type=F32)
+    )
     faces = sea_face_ref.shape[1]
     sea_ref[...] = (iota((4 * elements, faces), 0) == sea_face_ref[...]).astype(F32).astype(BF16)
     row = sea_row_ref[...]
@@ -359,9 +402,9 @@
         slot_ref[j] = jnp.concatenate([edges.astype(F32), inside.astype(F32)], axis=0).astype(BF16)
 
 
-def remote_faces(place, outer_ref, hot_ref, table_refs, packed_ref, table_ref):
+def remote_flux(place, flux_ref, star_ref, hot_ref, scale_ref, arrived, packed_ref, table_ref):
     elements = hot_ref.shape[1] // 4
-    blocks = remote_blocks(place, *table_refs)
+    blocks = remote_blocks(place, *arrived)
     left = iota((HALF, 2 * CAP), 1) < CAP
     for n in range(0, 8, 2):
         one = blocks[n][0][blocks[n][1] : blocks[n][1] + HALF, :]
@@ -370,10 +413,28 @@
         packed_ref[0:HALF, lanes] = jnp.where(left, one, pltpu.roll(two, CAP, 1))
         packed_ref[HALF:, lanes] = jnp.where(left, pltpu.roll(one, CAP, 1), two)
     unpack(packed_ref, table_ref)
+    star = star_ref[...]
+    for part in range(FACE_PAD // 8):
+        at = [slice(g * FACE_PAD + 8 * part, g * FACE_PAD + 8 * part + 8) for g in range(FIELDS)]
+        for half in range(2):
+            lanes = slice(4 * CAP * half, 4 * CAP * (half + 1))
+            normals = [scale_ref[c : c + 1, lanes] for c in range(3)]
+            outer = jnp.concatenate([table_ref[rows, lanes] for rows in at], axis=0)
+            y = folded(dot(star, both_parts(outer)))
+            size = FIELDS * 8
+            flux = -scale_ref[3:4, lanes] * outer
+            for c in range(3):
+                flux = flux + normals[c] * y[c * size : (c + 1) * size]
+            for g, rows in enumerate(at):
+                table_ref[rows, lanes] = flux[8 * g : 8 * g + 8]
     remote = table_parts(table_ref)
     for f in range(4):
         columns = slice(f * elements, (f + 1) * elements)
-        outer_ref[:, columns] += folded(dot(remote, hot_ref[:, columns]))[:TABLE]
+        got = folded(dot(remote, hot_ref[:, columns]))
+        for g in range(FIELDS):
+            flux_ref[g, f * FACE_PAD : (f + 1) * FACE_PAD, :] += got[
+                g * FACE_PAD : (g + 1) * FACE_PAD
+            ]
 
 
 def lift_weights(lift_ref):
@@ -389,45 +450,24 @@
     )
 
 
-def lifted(base_ref, table_ref, outer_ref, normal_ref, speed_ref, star, lift, state_ref, flux_ref):
-    elements = base_ref.shape[1]
-    basis = base_ref.shape[0] // FIELDS
-    size = FIELDS * 8
-    for part in range(FACE_PAD // 8):
-        at = [slice(g * FACE_PAD + 8 * part, g * FACE_PAD + 8 * part + 8) for g in range(FIELDS)]
-        for f in range(4):
-            columns = slice(f * elements, (f + 1) * elements)
-            inner = jnp.concatenate([table_ref[rows, columns] for rows in at], axis=0)
-            outer = jnp.concatenate([outer_ref[rows, columns] for rows in at], axis=0)
-            y = folded(dot(star, both_parts(inner + outer)))
-            flux = 0.5 * speed_ref[...] * (inner - outer)
-            for c in range(3):
-                flux = flux + 0.5 * normal_ref[c, f : f + 1, :] * y[c * size : (c + 1) * size]
-            for g in range(FIELDS):
-                flux_ref[g, f * FACE_PAD + 8 * part : f * FACE_PAD + 8 * part + 8, :] = flux[
-                    8 * g : 8 * g + 8
-                ]
-    for g in range(FIELDS):
-        rows = slice(g * basis, (g + 1) * basis)
-        state_ref[rows, :] = base_ref[rows, :] - weighted(*lift, flux_ref[g])
-
-
 def back(
-    place, base_ref, table_ref, outer_ref, normal_ref, speed_ref, star_ref, l1_ref, l2_ref, hot_ref,
+    place, base_ref, local_ref, star_ref, l1_ref, l2_ref, hot_ref, scale_ref,
     p1_ref, p2_ref, q1_ref, q2_ref,
     state_ref, flux_ref, packed_ref, remote_ref,
 ):
     arrived = (p1_ref, p2_ref, q1_ref, q2_ref)
-    remote_faces(place, outer_ref, hot_ref, arrived, packed_ref, remote_ref)
+    flux_ref[...] = local_ref[...]
+    remote_flux(place, flux_ref, star_ref, hot_ref, scale_ref, arrived, packed_ref, remote_ref)
     lift = l1_ref[...], l2_ref[...]
-    lifted(
-        base_ref, table_ref, outer_ref, normal_ref, speed_ref, star_ref[...], lift, state_ref, flux_ref
-    )
-
-
-def rates_out(vertical, t1_ref, t2_ref, interp_ref, sea_base_ref, sea_ref, slot_ref, out_ref):
+    basis = base_ref.shape[0] // FIELDS
+    for g in range(FIELDS):
+        rows = slice(g * basis, (g + 1) * basis)
+        state_ref[rows, :] = base_ref[rows, :] - weighted(*lift, flux_ref[g])
+
+
+def rates_out(vertical, trace_ref, interp_ref, sea_base_ref, sea_ref, slot_ref, out_ref):
     tiles, _, faces = slot_ref.shape
-    sea = weighted(t1_ref[...], t2_ref[...], vertical)
+    sea = side_weighted(trace_ref[...], vertical)
     sea = jnp.concatenate([sea[f * FACE_PAD : (f + 1) * FACE_PAD] for f in range(4)], axis=1)
     coeffs = folded(dot(both_parts(sea), sea_ref[...]))[:FACE_BASIS]
     rates = exact_dot(interp_ref[...], coeffs)
@@ -448,7 +488,7 @@
 
 
 def finish(*refs):
-    solid, sea, refs = refs[:14], refs[14:20], refs[20:]
+    solid, sea, refs = refs[:12], refs[12:17], refs[17:]
     state_out, out_ref, state_ref, sems, *scratch = refs
     back(*solid, state_ref, *scratch)
     copy = pltpu.make_async_copy(state_ref, state_out, sems.at[0])
@@ -851,6 +891,7 @@
     wide_shape = (tile_x + 2 * MARGIN, tile_y + 128)
     state = coefficients.reshape(solid)
     packed = (2 * HALF, 8 * CAP)
+    flux_shape = (FIELDS, 4 * FACE_PAD, elements)
     for section in range(2):
         scratch = [spread, solid, solid, solid, (2 * HALF, 4 * CAP)]
         if section == 0:
@@ -882,7 +923,6 @@
         p1, p2, base = lax.optimization_barrier((p1, p2, base))
         q1, q2 = call(forward, [(size, 128)] * 2, p1, p2, own1, own2, *columns, place=place)
         q2, q1 = swap(q2, "gy", 1), swap(q1, "gy", 0)
-        (outer,) = call(local_faces, [faces], table, face_partner)
         if section == 1:
             wide, first = call(
                 ocean_first,
@@ -890,7 +930,11 @@
                 water_depth, momentum, bottom, *halos,
                 place=place, scratch=[(5,) + wide_shape, (3,) + wide_shape],
             )
-            q1, q2, outer, wide, first = lax.optimization_barrier((q1, q2, outer, wide, first))
+            (flux,) = call(
+                local_flux, [flux_shape], table, face_partner, normals, speed, star3,
+                scratch=[faces],
+            )
+            q1, q2, flux, wide, first = lax.optimization_barrier((q1, q2, flux, wide, first))
         else:
             half = lambda *shape: jax.ShapeDtypeStruct(shape, BF16)
             size, sea = FIELDS * 8, sea_face.shape[0]
@@ -898,34 +942,37 @@
                 prepared,
                 [half(8 * size, 2 * size), half(6 * size, 2 * size)]
                 + [half(2 * basis, 3 * basis), half(basis, 3 * basis)]
-                + [half(8 * FACE_PAD, basis), half(4 * FACE_PAD, basis)]
+                + [half(4 * FACE_PAD, 3 * basis)]
                 + [half(2 * basis, 4 * FACE_PAD), half(basis, 4 * FACE_PAD)]
-                + [half(8 * CAP, 4 * elements), half(4 * elements, sea), half(tiles, 4 * CAP, sea)],
+                + [half(8 * CAP, 4 * elements), half(4 * elements, sea), half(tiles, 4 * CAP, sea), (8, 8 * CAP)],
                 star_mats, source_mat, deriv_mats, traces, lifts, face_partner,
-                sea_face.reshape(1, -1), sea_row.T,
+                sea_face.reshape(1, -1), sea_row.T, normals, speed,
                 place=place,
             )
-            q1, q2, outer, *ready = lax.optimization_barrier((q1, q2, outer, *ready))
-            derivs, traced, lifting, (hot, sea_hot, slot_hot) = (
-                ready[0:2], ready[2:4], ready[4:6], ready[6:],
+            (flux,) = call(
+                local_flux, [flux_shape], table, face_partner, normals, speed, star3,
+                scratch=[faces],
             )
-        fixed = (normals, speed, star3, *lifting, hot)
+            q1, q2, flux, *ready = lax.optimization_barrier((q1, q2, flux, *ready))
+            derivs, traced, lifting, (hot, sea_hot, slot_hot, scales) = (
+                ready[0:2], ready[2:3], ready[3:5], ready[5:],
+            )
+        fixed = (star3, *lifting, hot, scales)
         arrived = (p1, p2, q1, q2)
-        flux = (FIELDS, 4 * FACE_PAD, elements)
         remote = (TABLE, 8 * CAP)
         if section == 0:
             (state,) = call(
-                back, [solid], base, table, outer, *fixed, *arrived,
-                place=place, scratch=[flux, packed, remote],
+                back, [solid], base, flux, *fixed, *arrived,
+                place=place, scratch=[flux_shape, packed, remote],
             )
             halos = (p1, p2, q1, q2)
         else:
             state, outgoing = call(
                 finish,
                 [solid, (tiles, 32, 128)],
-                base, table, outer, *fixed, *arrived,
+                base, flux, *fixed, *arrived,
                 *traced, interp_mat, sea_base.T, sea_hot, slot_hot,
-                place=place, scratch=[flux, packed, remote], sent=1, copies=1,
+                place=place, scratch=[flux_shape, packed, remote], sent=1, copies=1,
             )
     incoming = lax.all_to_all(outgoing, "gy", split_axis=0, concat_axis=0, tiled=True)
     forcing, s1, s2 = call(

time: 75.8 us -> 73.8 us (0.974)
  waiting for transfers between devices: 9.58 us -> 6.33 us
  Pallas kernels: 34.9 us -> 36 us
    ppermute x10, waiting for transfers between devices: 9.58 us -> 6.33 us  [swap(): return lax.ppermute(block, axis, pairs)]
    pallas_call x15, Pallas kernels: 34.9 us -> 36 us  [call(): pl.pallas_call(body, out_shape=shapes, in_specs=specs, out_specs=[pl.Bloc...]
  transfers between devices with their start and end apart: 10 -> 10, of which waited for: 4 -> 3; matrix products, arithmetic and copies ran while one was open for 0% -> 0% of each run, Pallas kernels for 18% -> 22%
where the time goes in v4:
time: 73.8 us; the launch traced here: 73.1 us
  Pallas kernels  36 us (49%)
  starting transfers between devices  16.3 us (22%)
  blocking collectives  11.9 us (16%)
  waiting for transfers between devices  6.33 us (9%)
  between operations  1.29 us (2%)
  local copies, waits for them, and re-layouts  1.25 us (2%)
    pallas_call x15, Pallas kernels, call(): pl.pallas_call(body, out_shape=shapes, in_specs=specs, out_specs=[pl.Bloc...  36 us
    ppermute x10, starting transfers between devices, swap(): return lax.ppermute(block, axis, pairs)  16.3 us
    all_to_all x1, blocking collectives, per_device(): lax.all_to_all(outgoing, 'gy', split_axis=0, concat_axis=0, tiled=True)  11.9 us
    ppermute x10, waiting for transfers between devices, swap(): return lax.ppermute(block, axis, pairs)  6.33 us
  transfers between devices with their start and end apart: 10, of which 3 were waited for; matrix products, arithmetic and copies ran while one was open for 0% of the time, Pallas kernels for 22%

profile of v4, /device:TPU:1, one launch (start us, length us, event | category | flops | bytes accessed | tf_op | source)
XLA Modules:
  0.0 73.1 jit_solution(8163285027817683601)
XLA Ops:
  0.6 0.0 copy-start.6
  0.6 0.0 copy-start.9
  0.7 0.0 copy-start.3
  0.7 0.0 copy-start
  0.7 0.0 copy-start.2
  0.7 0.0 copy-start.1
  0.7 0.0 copy-start.8
  0.7 7.6 %shard_map.202 = (f32[728,256]{1,0:T(8,128)}, f32[312,1024]{1,0:T(8,128)}, f32[427,128]{1,0:T(8,128)}, f32[427,128]{1,0:T(8,128)}, f32[137,128]{1,0:T(8,128)}, /*index=5*/f32[137,128]{1,0:T(8,128)}) custom-call(f32[728,256]{1,0:T(8,128)} %bitcast.9, f32[3,3,256]{2,1,0:T(4,128)} %jac_ref.1, f32[3,13,13]{2,1,0:T(8,128)} %star_ref.1, f32[13,13]{1,0:T(8,128)} %refs_1_.7, ...), custom_call_target="tpu_custom_call" | custom-call | tf_op jit(solution)/shard_map/pallas_call | solution.py:837
  8.3 0.1 collective-permute-start
  8.4 4.5 %collective-permute-start.1 = (f32[427,128]{1,0:T(8,128)}, f32[427,128]{1,0:T(8,128)S(1)}, u32[]{:S(2)}, u32[]{:S(2)}) collective-permute-start(f32[427,128]{1,0:T(8,128)} %get-tuple-element.68), channel_id=1, source_target_pairs={{8,16},{16,8},{0,0},{24,24},{9,17},{17,9},{1,1},{25,25},{10,18},{1... | collective-permute-start | bytes 655880 | tf_op jit(solution)/shard_map/ppermute | solution.py:855
  12.9 0.0 copy-done.6
  13.0 0.0 copy-done.9
  13.0 0.0 copy-done.3
  13.0 0.0 copy-done
  13.0 0.0 copy-done.2
  13.0 0.0 copy-done.1
  13.0 0.0 copy-done.8
  13.0 0.0 copy-start.5
  13.0 1.1 %copy-done.5 = f32[728,256]{1,0:T(8,128)S(1)} copy-done((f32[728,256]{1,0:T(8,128)S(1)}, f32[728,256]{1,0:T(8,128)}, u32[]{:S(2)}) %copy-start.5) | copy-done | bytes 745496
  14.1 0.0 copy-start.11
  14.2 0.0 copy-start.14
  14.2 0.0 copy-start.15
  14.2 0.0 copy-start.16
  14.2 0.0 copy-start.18
  14.2 0.0 copy-start.21
  14.2 0.0 copy-start.22
  14.2 0.0 copy-start.4
  14.2 2.5 %shard_map.203 = (f32[728,256]{1,0:T(8,128)S(1)}, f32[16,128]{1,0:T(8,128)S(1)}, f32[16,128]{1,0:T(8,128)S(1)}) custom-call(f32[728,256]{1,0:T(8,128)S(1)} %bitcast.10, f32[3,3,256]{2,1,0:T(4,128)S(1)} %copy-done.9, f32[3,13,13]{2,1,0:T(8,128)S(1)} %copy-done.6, f32[3,56,56]{2,1,0:T(8,128)S(1)} %copy-done.8, f32[728,256]{1,0:T(8,128)S(1)} %copy-done.5, ...), custom_call_target="tpu_custom_call" | custom-call | tf_op jit(solution)/shard_map/pallas_call | solution.py:837
  16.8 0.0 collective-permute-done.refs_0_.refs_7_.refs_3_
  16.8 0.0 collective-permute-done.1.refs_1_.refs_8_.refs_4_
  16.8 0.0 copy-done.12
  16.8 0.0 copy-done.13
  16.9 1.8 %collective-permute-start.2 = (f32[443,128]{1,0:T(8,128)S(1)}, f32[443,128]{1,0:T(8,128)S(1)}, u32[]{:S(2)}, u32[]{:S(2)}) collective-permute-start(f32[443,128]{1,0:T(8,128)S(1)} %get-tuple-element.78), channel_id=1, source_target_pairs={{0,1},{1,0},{2,3},{3,2},{4,5},{5,4},{6,7},{7,6},{8,9},{9,8},{10,11... | collective-permute-start | bytes 680456 | tf_op jit(solution)/shard_map/ppermute | solution.py:855
  18.7 0.8 %collective-permute-start.3 = (f32[443,128]{1,0:T(8,128)S(1)}, f32[443,128]{1,0:T(8,128)S(1)}, u32[]{:S(2)}, u32[]{:S(2)}) collective-permute-start(f32[443,128]{1,0:T(8,128)S(1)} %get-tuple-element.79), channel_id=1, source_target_pairs={{1,2},{2,1},{3,4},{4,3},{5,6},{6,5},{0,0},{7,7},{9,10},{10,9},{11,... | collective-permute-start | bytes 680456 | tf_op jit(solution)/shard_map/ppermute | solution.py:855
  19.5 0.0 copy-done.7
  19.6 0.0 copy-done.10
  19.6 1.5 %shard_map.205 = (bf16[832,208]{1,0:T(8,128)(2,1)S(1)}, bf16[624,208]{1,0:T(8,128)(2,1)S(1)}, bf16[112,168]{1,0:T(8,128)(2,1)S(1)}, bf16[56,168]{1,0:T(8,128)(2,...) custom-call(f32[3,13,13]{2,1,0:T(8,128)S(1)} %copy-done.6, ...), custom_call_target="tpu_custom_call" | custom-call | tf_op jit(solution)/shard_map/pallas_call | solution.py:837
  21.2 2.8 %shard_map.206.refs_1_ = f32[13,96,256]{2,1,0:T(8,128)S(1)} custom-call(f32[312,1024]{1,0:T(8,128)S(1)} %copy-done.4, s32[4,256]{1,0:T(4,128)S(1)} %copy-done.15, f32[3,4,256]{2,1,0:T(4,128)S(1)} %bitcast.14, f32[1,256]{1,0:T(1,128)S(1)} %bitcast.18, bf16[624,208]{1,0:T(8,128)(2,1)S(1)} %get-tuple-element.81.star_ref.refs_2_), custom_call_target="tpu_custom_call" | custom-call | tf_op jit(solution)/shard_map/pallas_call | solution.py:837
  24.0 3.5 %collective-permute-done.2.refs_9_.refs_5_ = f32[443,128]{1,0:T(8,128)S(1)} collective-permute-done((f32[443,128]{1,0:T(8,128)S(1)}, f32[443,128]{1,0:T(8,128)S(1)}, u32[]{:S(2)}, u32[]{:S(2)}) %collective-permute-start.2) | collective-permute-done | bytes 226848 | tf_op jit(solution)/shard_map/ppermute | solution.py:855
  27.5 0.0 collective-permute-done.3.refs_10_.refs_6_
  27.5 2.0 %shard_map.207.refs_0_.q_ref = f32[728,256]{1,0:T(8,128)S(1)} custom-call(f32[728,256]{1,0:T(8,128)S(1)} %get-tuple-element.71.refs_0_, f32[13,96,256]{2,1,0:T(8,128)S(1)} %shard_map.206.refs_1_, bf16[624,208]{1,0:T(8,128)(2,1)S(1)} %get-tuple-element.81.star_ref.refs_2_, bf16[112,96]{1,0:T(8,128)(2,1)S(1)} %get-tuple-element.92.refs_3_, ...), custom_call_target="tpu_custom_call" | custom-call | tf_op jit(solution)/shard_map/pallas_call | solution.py:837
  29.6 4.6 %shard_map.208 = (f32[728,256]{1,0:T(8,128)S(1)}, f32[312,1024]{1,0:T(8,128)S(1)}, f32[411,128]{1,0:T(8,128)S(1)}, f32[411,128]{1,0:T(8,128)S(1)}, f32[137,128]{1,0:T(8,128)S(1)}, /*index=5*/f32[137,128]{1,0:T(8,128)S(1)}) custom-call(f32[728,256]{1,0:T(8,128)S(1)} %shard_map.207.refs_0_.q_ref, f32[3,3,256]{2,1,0:T(4,128)S(1)} %copy-done.9, ...), custom_call_target="tpu_custom_call" | custom-call | tf_op jit(solution)/shard_map/pallas_call | solution.py:837
  34.1 0.1 collective-permute-start.4
  34.2 2.9 %collective-permute-start.5 = (f32[411,128]{1,0:T(8,128)S(1)}, f32[411,128]{1,0:T(8,128)S(1)}, u32[]{:S(2)}, u32[]{:S(2)}) collective-permute-start(f32[411,128]{1,0:T(8,128)S(1)} %get-tuple-element.103), channel_id=1, source_target_pairs={{8,16},{16,8},{0,0},{24,24},{9,17},{17,9},{1,1},{25,25},{10,18},{1... | collective-permute-start | bytes 631304 | tf_op jit(solution)/shard_map/ppermute | solution.py:855
  37.2 1.8 %shard_map.209.refs_0_ = f32[728,256]{1,0:T(8,128)S(1)} custom-call(f32[728,256]{1,0:T(8,128)S(1)} %shard_map.207.refs_0_.q_ref, f32[3,3,256]{2,1,0:T(4,128)S(1)} %copy-done.9, f32[3,13,13]{2,1,0:T(8,128)S(1)} %copy-done.6, f32[3,56,56]{2,1,0:T(8,128)S(1)} %copy-done.8, f32[728,256]{1,0:T(8,128)S(1)} %get-tuple-element.104.integral_ref), custom_call_target="tpu_custom_call" | custom-call | tf_op jit(solution)/shard_map/pallas_call | solution.py:837
  38.9 0.0 collective-permute-done.4.refs_0_.refs_7_
  38.9 2.7 %collective-permute-done.5.refs_1_.refs_8_ = f32[411,128]{1,0:T(8,128)S(1)} collective-permute-done((f32[411,128]{1,0:T(8,128)S(1)}, f32[411,128]{1,0:T(8,128)S(1)}, u32[]{:S(2)}, u32[]{:S(2)}) %collective-permute-start.5) | collective-permute-done | bytes 210464 | tf_op jit(solution)/shard_map/ppermute | solution.py:855
  41.7 2.0 %collective-permute-start.6 = (f32[411,128]{1,0:T(8,128)S(1)}, f32[411,128]{1,0:T(8,128)S(1)}, u32[]{:S(2)}, u32[]{:S(2)}) collective-permute-start(f32[411,128]{1,0:T(8,128)S(1)} %get-tuple-element.110), channel_id=1, source_target_pairs={{0,1},{1,0},{2,3},{3,2},{4,5},{5,4},{6,7},{7,6},{8,9},{9,8},{10,11... | collective-permute-start | bytes 631304 | tf_op jit(solution)/shard_map/ppermute | solution.py:855
  43.7 0.9 %collective-permute-start.7 = (f32[411,128]{1,0:T(8,128)S(1)}, f32[411,128]{1,0:T(8,128)S(1)}, u32[]{:S(2)}, u32[]{:S(2)}) collective-permute-start(f32[411,128]{1,0:T(8,128)S(1)} %get-tuple-element.111), channel_id=1, source_target_pairs={{1,2},{2,1},{3,4},{4,3},{5,6},{6,5},{0,0},{7,7},{9,10},{10,9},{11,... | collective-permute-start | bytes 631304 | tf_op jit(solution)/shard_map/ppermute | solution.py:855
  44.6 2.4 %shard_map.212 = (f32[4,288,384]{2,1,0:T(8,128)S(1)}, f32[3,288,384]{2,1,0:T(8,128)S(1)}) custom-call(f32[256,256]{1,0:T(8,128)S(1)} %copy-done.2, f32[2,256,256]{2,1,0:T(8,128)S(1)} %copy-done, f32[256,256]{1,0:T(8,128)S(1)} %copy-done.3, f32[427,128]{1,0:T(8,128)S(1)} %collective-permute-done.refs_0_.refs_7_.refs_3_, ...), custom_call_target="tpu_custom_call" | custom-call | tf_op jit(solution)/shard_map/pallas_call | solution.py:837
  47.0 0.0 copy-start.19
  47.0 0.0 copy-start.20
  47.0 2.8 %shard_map.211.refs_1_ = f32[13,96,256]{2,1,0:T(8,128)S(1)} custom-call(f32[312,1024]{1,0:T(8,128)S(1)} %get-tuple-element.112.table_ref, s32[4,256]{1,0:T(4,128)S(1)} %copy-done.15, f32[3,4,256]{2,1,0:T(4,128)S(1)} %bitcast.15, f32[1,256]{1,0:T(1,128)S(1)} %bitcast.19, bf16[624,208]{1,0:T(8,128)(2,1)S(1)} %get-tuple-element.81.star_ref.refs_2_), custom_call_target="tpu_custom_call" | custom-call | tf_op jit(solution)/shard_map/pallas_call | solution.py:837
  49.8 0.1 collective-permute-done.6.refs_9_
  49.9 0.0 collective-permute-done.7.refs_10_
  49.9 2.9 %shard_map.213 = (f32[728,256]{1,0:T(8,128)}, f32[8,32,128]{2,1,0:T(8,128)S(1)}) custom-call(f32[728,256]{1,0:T(8,128)S(1)} %shard_map.209.refs_0_, f32[13,96,256]{2,1,0:T(8,128)S(1)} %shard_map.211.refs_1_, bf16[624,208]{1,0:T(8,128)(2,1)S(1)} %get-tuple-element.81.star_ref.refs_2_, bf16[112,96]{1,0:T(8,128)(2,1)S(1)} %get-tuple-element.92.refs_3_, ...), custom_call_target="tpu_custom_call" | custom-call | tf_op jit(solution)/shard_map/pallas_call | solution.py:837
  52.8 11.9 %all_to_all.5.refs_0_ = f32[8,32,128]{2,1,0:T(8,128)S(1)} all-to-all(f32[8,32,128]{2,1,0:T(8,128)S(1)} %get-tuple-element.123), channel_id=1, replica_groups=mesh['gx'=4,'gy'=8] {'gy'}, dimensions={0} | all-to-all | bytes 262144 | tf_op jit(solution)/shard_map/all_to_all | solution.py:977
  64.7 1.6 %shard_map.214 = (f32[256,384]{1,0:T(8,128)S(1)}, f32[8,384]{1,0:T(8,128)S(1)}, f32[8,384]{1,0:T(8,128)S(1)}) custom-call(f32[8,32,128]{2,1,0:T(8,128)S(1)} %all_to_all.5.refs_0_), custom_call_target="tpu_custom_call" | custom-call | tf_op jit(solution)/shard_map/pallas_call | solution.py:837
  66.4 0.1 collective-permute-start.8
  66.4 3.1 %collective-permute-start.9 = (f32[8,384]{1,0:T(8,128)S(1)}, f32[8,384]{1,0:T(8,128)S(1)}, u32[]{:S(2)}, u32[]{:S(2)}) collective-permute-start(f32[8,384]{1,0:T(8,128)S(1)} %get-tuple-element.126), channel_id=1, source_target_pairs={{8,16},{16,8},{24,0},{0,24},{9,17},{17,9},{25,1},{1,25},{10,18},{1... | collective-permute-start | bytes 36872 | tf_op jit(solution)/shard_map/ppermute | solution.py:855
  69.5 2.3 %shard_map.215 = (f32[3,256,256]{2,1,0:T(8,128)S(1)}, f32[256,256]{1,0:T(8,128)S(1)}) custom-call(f32[4,288,384]{2,1,0:T(8,128)S(1)} %get-tuple-element.121.wide.refs_0_, f32[3,288,384]{2,1,0:T(8,128)S(1)} %get-tuple-element.122.first.refs_1_, f32[256,384]{1,0:T(8,128)S(1)} %get-tuple-element.124.forcing_ref.refs_2_), custom_call_target="tpu_custom_call" | custom-call | tf_op jit(solution)/shard_map/pallas_call | solution.py:837
  71.9 0.0 collective-permute-done.8.refs_3_
  71.9 0.0 collective-permute-done.9.refs_4_
  71.9 1.0 %shard_map.216 = (f32[3,256,256]{2,1,0:T(8,128)}, f32[256,256]{1,0:T(8,128)}) custom-call(f32[4,288,384]{2,1,0:T(8,128)S(1)} %get-tuple-element.121.wide.refs_0_, f32[3,288,384]{2,1,0:T(8,128)S(1)} %get-tuple-element.122.first.refs_1_, f32[256,384]{1,0:T(8,128)S(1)} %get-tuple-element.124.forcing_ref.refs_2_, f32[8,384]{1,0:T(8,128)S(1)} %collective-permute-done.8.refs_3_, ...), custom_call_target="tpu_custom_call" | custom-call | tf_op jit(solution)/shard_map/pallas_call | solution.py:837
  (18 shorter events, 0.1 us)
Async XLA Ops:
  0.6 12.3 %copy-start.6 = (f32[3,13,13]{2,1,0:T(8,128)S(1)}, f32[3,13,13]{2,1,0:T(8,128)}, u32[]{:S(2)}) copy-start(f32[3,13,13]{2,1,0:T(8,128)} %star_ref.1) | copy-start | bytes 6088
  0.6 12.3 %copy-start.9 = (f32[3,3,256]{2,1,0:T(4,128)S(1)}, f32[3,3,256]{2,1,0:T(4,128)}, u32[]{:S(2)}) copy-start(f32[3,3,256]{2,1,0:T(4,128)} %jac_ref.1) | copy-start | bytes 27652
  0.7 12.3 %copy-start.3 = (f32[256,256]{1,0:T(8,128)S(1)}, f32[256,256]{1,0:T(8,128)}, u32[]{:S(2)}) copy-start(f32[256,256]{1,0:T(8,128)} %refs_2_.7) | copy-start | bytes 786436
  0.7 12.3 %copy-start = (f32[2,256,256]{2,1,0:T(8,128)S(1)}, f32[2,256,256]{2,1,0:T(8,128)}, u32[]{:S(2)}) copy-start(f32[2,256,256]{2,1,0:T(8,128)} %refs_1_.9) | copy-start | bytes 1572868
  0.7 12.3 %copy-start.2 = (f32[256,256]{1,0:T(8,128)S(1)}, f32[256,256]{1,0:T(8,128)}, u32[]{:S(2)}) copy-start(f32[256,256]{1,0:T(8,128)} %refs_0_.3) | copy-start | bytes 786436
  0.7 12.3 %copy-start.1 = (f32[13,56,256]{2,1,0:T(8,128)S(1)}, f32[13,56,256]{2,1,0:T(8,128)}, u32[]{:S(2)}) copy-start(f32[13,56,256]{2,1,0:T(8,128)} %param.19) | copy-start | bytes 2236420
  0.7 12.3 %copy-start.8 = (f32[3,56,56]{2,1,0:T(8,128)S(1)}, f32[3,56,56]{2,1,0:T(8,128)}, u32[]{:S(2)}) copy-start(f32[3,56,56]{2,1,0:T(8,128)} %stiff_ref.1) | copy-start | bytes 112900
  8.3 8.5 %collective-permute-start = (f32[427,128]{1,0:T(8,128)}, f32[427,128]{1,0:T(8,128)S(1)}, u32[]{:S(2)}, u32[]{:S(2)}) collective-permute-start(f32[427,128]{1,0:T(8,128)} %get-tuple-element.67), channel_id=1, source_target_pairs={{0,8},{8,0},{16,24},{24,16},{1,9},{9,1},{17,25},{25,17},{2,10},{10... | collective-permute-start | bytes 655880 | tf_op jit(solution)/shard_map/ppermute | solution.py:855
  8.4 8.4 %collective-permute-start.1 = (f32[427,128]{1,0:T(8,128)}, f32[427,128]{1,0:T(8,128)S(1)}, u32[]{:S(2)}, u32[]{:S(2)}) collective-permute-start(f32[427,128]{1,0:T(8,128)} %get-tuple-element.68), channel_id=1, source_target_pairs={{8,16},{16,8},{0,0},{24,24},{9,17},{17,9},{1,1},{25,25},{10,18},{1... | collective-permute-start | bytes 655880 | tf_op jit(solution)/shard_map/ppermute | solution.py:855
  13.0 1.1 %copy-start.5 = (f32[728,256]{1,0:T(8,128)S(1)}, f32[728,256]{1,0:T(8,128)}, u32[]{:S(2)}) copy-start(f32[728,256]{1,0:T(8,128)} %get-tuple-element.69.refs_4_) | copy-start | bytes 2236420
  14.1 2.7 %copy-start.12 = (f32[137,128]{1,0:T(8,128)S(1)}, f32[137,128]{1,0:T(8,128)}, u32[]{:S(2)}) copy-start(f32[137,128]{1,0:T(8,128)} %get-tuple-element.74.refs_2_) | copy-start | bytes 210436
  14.1 2.7 %copy-start.13 = (f32[137,128]{1,0:T(8,128)S(1)}, f32[137,128]{1,0:T(8,128)}, u32[]{:S(2)}) copy-start(f32[137,128]{1,0:T(8,128)} %get-tuple-element.75.refs_3_) | copy-start | bytes 210436
  14.1 5.4 %copy-start.7 = (f32[3,56,56]{2,1,0:T(8,128)S(1)}, f32[3,56,56]{2,1,0:T(8,128)}, u32[]{:S(2)}) copy-start(f32[3,56,56]{2,1,0:T(8,128)} %refs_2_.6) | copy-start | bytes 112900
  14.1 5.4 %copy-start.10 = (f32[4,21,56]{2,0,1:T(4,128)S(1)}, f32[4,21,56]{2,0,1:T(4,128)}, u32[]{:S(2)}) copy-start(f32[4,21,56]{2,0,1:T(4,128)} %param.27) | copy-start | bytes 56452
  14.1 5.4 %copy-start.11 = (f32[4,3,256]{2,0,1:T(4,128)S(1)}, f32[4,3,256]{2,0,1:T(4,128)}, u32[]{:S(2)}) copy-start(f32[4,3,256]{2,0,1:T(4,128)} %param.21) | copy-start | bytes 36868
  14.2 5.4 %copy-start.14 = (f32[4,56,21]{1,0,2:T(4,128)S(1)}, f32[4,56,21]{1,0,2:T(4,128)}, u32[]{:S(2)}) copy-start(f32[4,56,21]{1,0,2:T(4,128)} %param.28) | copy-start | bytes 56452
  14.2 5.4 %copy-start.15 = (s32[4,256]{1,0:T(4,128)S(1)}, s32[4,256]{1,0:T(4,128)}, u32[]{:S(2)}) copy-start(s32[4,256]{1,0:T(4,128)} %partner_ref.3) | copy-start | bytes 12292
  14.2 5.4 %copy-start.16 = (f32[13,13]{1,0:T(8,128)S(1)}, f32[13,13]{1,0:T(8,128)}, u32[]{:S(2)}) copy-start(f32[13,13]{1,0:T(8,128)} %refs_1_.7) | copy-start | bytes 2032
  14.2 5.4 %copy-start.18 = (f32[256]{0:T(256)S(1)}, f32[256]{0:T(256)}, u32[]{:S(2)}) copy-start(f32[256]{0:T(256)} %param.22) | copy-start | bytes 3076
  14.2 5.4 %copy-start.21 = (s32[256]{0:T(256)S(1)}, s32[256]{0:T(256)}, u32[]{:S(2)}) copy-start(s32[256]{0:T(256)} %param.31) | copy-start | bytes 3076
  14.2 5.4 %copy-start.22 = (s32[256,1]{0,1:T(1,128)S(1)}, s32[256,1]{0,1:T(1,128)}, u32[]{:S(2)}) copy-start(s32[256,1]{0,1:T(1,128)} %param.32) | copy-start | bytes 3076
  14.2 7.0 %copy-start.4 = (f32[312,1024]{1,0:T(8,128)S(1)}, f32[312,1024]{1,0:T(8,128)}, u32[]{:S(2)}) copy-start(f32[312,1024]{1,0:T(8,128)} %get-tuple-element.80.table_ref) | copy-start | bytes 3833860
  16.9 10.6 %collective-permute-start.2 = (f32[443,128]{1,0:T(8,128)S(1)}, f32[443,128]{1,0:T(8,128)S(1)}, u32[]{:S(2)}, u32[]{:S(2)}) collective-permute-start(f32[443,128]{1,0:T(8,128)S(1)} %get-tuple-element.78), channel_id=1, source_target_pairs={{0,1},{1,0},{2,3},{3,2},{4,5},{5,4},{6,7},{7,6},{8,9},{9,8},{10,11... | collective-permute-start | bytes 680456 | tf_op jit(solution)/shard_map/ppermute | solution.py:855
  18.7 8.8 %collective-permute-start.3 = (f32[443,128]{1,0:T(8,128)S(1)}, f32[443,128]{1,0:T(8,128)S(1)}, u32[]{:S(2)}, u32[]{:S(2)}) collective-permute-start(f32[443,128]{1,0:T(8,128)S(1)} %get-tuple-element.79), channel_id=1, source_target_pairs={{1,2},{2,1},{3,4},{4,3},{5,6},{6,5},{0,0},{7,7},{9,10},{10,9},{11,... | collective-permute-start | bytes 680456 | tf_op jit(solution)/shard_map/ppermute | solution.py:855
  27.5 2.0 %copy-start.17 = (s32[8,64]{1,0:T(8,128)S(1)}, s32[8,64]{1,0:T(8,128)}, u32[]{:S(2)}) copy-start(s32[8,64]{1,0:T(8,128)} %refs_6_.5) | copy-start | bytes 6148
  34.1 4.8 %collective-permute-start.4 = (f32[411,128]{1,0:T(8,128)S(1)}, f32[411,128]{1,0:T(8,128)S(1)}, u32[]{:S(2)}, u32[]{:S(2)}) collective-permute-start(f32[411,128]{1,0:T(8,128)S(1)} %get-tuple-element.102), channel_id=1, source_target_pairs={{0,8},{8,0},{16,24},{24,16},{1,9},{9,1},{17,25},{25,17},{2,10},{10... | collective-permute-start | bytes 631304 | tf_op jit(solution)/shard_map/ppermute | solution.py:855
  34.2 7.5 %collective-permute-start.5 = (f32[411,128]{1,0:T(8,128)S(1)}, f32[411,128]{1,0:T(8,128)S(1)}, u32[]{:S(2)}, u32[]{:S(2)}) collective-permute-start(f32[411,128]{1,0:T(8,128)S(1)} %get-tuple-element.103), channel_id=1, source_target_pairs={{8,16},{16,8},{0,0},{24,24},{9,17},{17,9},{1,1},{25,25},{10,18},{1... | collective-permute-start | bytes 631304 | tf_op jit(solution)/shard_map/ppermute | solution.py:855
  41.7 8.2 %collective-permute-start.6 = (f32[411,128]{1,0:T(8,128)S(1)}, f32[411,128]{1,0:T(8,128)S(1)}, u32[]{:S(2)}, u32[]{:S(2)}) collective-permute-start(f32[411,128]{1,0:T(8,128)S(1)} %get-tuple-element.110), channel_id=1, source_target_pairs={{0,1},{1,0},{2,3},{3,2},{4,5},{5,4},{6,7},{7,6},{8,9},{9,8},{10,11... | collective-permute-start | bytes 631304 | tf_op jit(solution)/shard_map/ppermute | solution.py:855
  43.7 6.2 %collective-permute-start.7 = (f32[411,128]{1,0:T(8,128)S(1)}, f32[411,128]{1,0:T(8,128)S(1)}, u32[]{:S(2)}, u32[]{:S(2)}) collective-permute-start(f32[411,128]{1,0:T(8,128)S(1)} %get-tuple-element.111), channel_id=1, source_target_pairs={{1,2},{2,1},{3,4},{4,3},{5,6},{6,5},{0,0},{7,7},{9,10},{10,9},{11,... | collective-permute-start | bytes 631304 | tf_op jit(solution)/shard_map/ppermute | solution.py:855
  47.0 2.9 %copy-start.19 = (f32[16,21]{1,0:T(8,128)S(1)}, f32[16,21]{1,0:T(8,128)}, u32[]{:S(2)}) copy-start(f32[16,21]{1,0:T(8,128)} %refs_12_.1) | copy-start | bytes 4036
  47.0 2.9 %copy-start.20 = (s32[256,2]{0,1:T(2,128)S(1)}, s32[256,2]{0,1:T(2,128)}, u32[]{:S(2)}) copy-start(s32[256,2]{0,1:T(2,128)} %param.33) | copy-start | bytes 6148
  66.4 5.5 %collective-permute-start.8 = (f32[8,384]{1,0:T(8,128)S(1)}, f32[8,384]{1,0:T(8,128)S(1)}, u32[]{:S(2)}, u32[]{:S(2)}) collective-permute-start(f32[8,384]{1,0:T(8,128)S(1)} %get-tuple-element.125), channel_id=1, source_target_pairs={{0,8},{8,0},{16,24},{24,16},{1,9},{9,1},{17,25},{25,17},{2,10},{10... | collective-permute-start | bytes 36872 | tf_op jit(solution)/shard_map/ppermute | solution.py:855
  66.4 5.4 %collective-permute-start.9 = (f32[8,384]{1,0:T(8,128)S(1)}, f32[8,384]{1,0:T(8,128)S(1)}, u32[]{:S(2)}, u32[]{:S(2)}) collective-permute-start(f32[8,384]{1,0:T(8,128)S(1)} %get-tuple-element.126), channel_id=1, source_target_pairs={{8,16},{16,8},{24,0},{0,24},{9,17},{17,9},{25,1},{1,25},{10,18},{1... | collective-permute-start | bytes 36872 | tf_op jit(solution)/shard_map/ppermute | solution.py:855

commit v5 on v4

--- a/solution.py
+++ b/solution.py
@@ -14,9 +14,10 @@
 CAP = 64
 TABLE = FIELDS * FACE_PAD
 WIDE = 320
-HALF = 137
+HALF = (FIELDS * FACE_BASIS + 1) // 2
 OCEAN_ROWS = 16
 MARGIN = 16
+FOUR = 4
 
 step_solid = 0.4
 step_ocean = 0.2
@@ -115,23 +116,61 @@
     return jnp.concatenate([exact_dot(place, trace_ref[:, f, :]) for f in range(4)], axis=0)
 
 
+def star_quarters(mats):
+    size = FOUR * (FIELDS + FIELDS % 2)
+    columns = 3 * size
+    spread = ((iota((FIELDS, columns), 1) % size) // FOUR == iota((FIELDS, columns), 0)).astype(F32)
+    upper = iota((8, columns), 0) < FOUR
+    diagonal = iota((size, columns), 0) % FOUR == iota((size, columns), 1) % FOUR
+    first = iota((size, columns), 1) < 2 * size
+    out = []
+    for mat in mats:
+        wide = exact_dot(mat, spread)
+        wide = [jnp.broadcast_to(wide[g : g + 1], (8, columns)) for g in range(FIELDS)]
+        wide += [jnp.zeros((8, columns), F32)] * (FIELDS % 2)
+        tall = jnp.concatenate(
+            [jnp.where(upper, wide[g], wide[g + 1]) for g in range(0, FIELDS, 2)], axis=0
+        )
+        tall = jnp.where(diagonal, tall, 0.0)
+        high = tall.astype(BF16).astype(F32)
+        out.append(jnp.where(first, high, tall - high))
+    return jnp.concatenate(out, axis=0).astype(BF16)
+
+
+def interleaved(one, two, upper):
+    return jnp.where(upper, one, pltpu.roll(two, FOUR, 0)), jnp.where(
+        upper, pltpu.roll(one, FOUR, 0), two
+    )
+
+
 def spread_out(source, jac_ref, star, target, extra=None):
     basis = target.shape[1] // 3
-    size = FIELDS * 8
+    lanes = target.shape[2]
+    pairs = (FIELDS + 1) // 2
+    size = 8 * pairs
+    upper = iota((8, lanes), 0) < FOUR
     for j in range(basis // 8):
-        x = jnp.concatenate(
-            [source[g * basis + 8 * j : g * basis + 8 * j + 8, :] for g in range(FIELDS)], axis=0
-        )
-        y = folded(dot(star, both_parts(x)))
-        for d in range(3):
-            z = sum(jac_ref[d, c : c + 1, :] * y[c * size : (c + 1) * size] for c in range(3))
-            for g in range(FIELDS):
-                target[g, d * basis + 8 * j : d * basis + 8 * j + 8, :] = z[8 * g : 8 * g + 8]
-        if extra is not None:
-            for g in range(FIELDS):
-                extra[g * basis + 8 * j : g * basis + 8 * j + 8, :] = y[
-                    3 * size + 8 * g : 3 * size + 8 * g + 8
-                ]
+        x = [source[g * basis + 8 * j : g * basis + 8 * j + 8, :] for g in range(FIELDS)]
+        x += [jnp.zeros((8, lanes), F32)] * (2 * pairs - FIELDS)
+        mixed = [interleaved(x[2 * p], x[2 * p + 1], upper) for p in range(pairs)]
+        halves = []
+        for half in range(2):
+            y = side_weighted(star, jnp.concatenate([m[half] for m in mixed], axis=0))
+            z = [
+                sum(jac_ref[d, c : c + 1, :] * y[c * size : (c + 1) * size] for c in range(3))
+                for d in range(3)
+            ]
+            halves.append(z + ([] if extra is None else [y[3 * size :]]))
+        for d, (one, two) in enumerate(zip(*halves)):
+            for p in range(pairs):
+                rows = slice(8 * p, 8 * p + 8)
+                for g, value in zip(
+                    range(2 * p, FIELDS), interleaved(one[rows], two[rows], upper)
+                ):
+                    if d < 3:
+                        target[g, d * basis + 8 * j : d * basis + 8 * j + 8, :] = value
+                    else:
+                        extra[g * basis + 8 * j : g * basis + 8 * j + 8, :] = value
 
 
 def derivative(source, target, jac_ref, star, basis_weights, spread_ref, relaxed_ref):
@@ -158,7 +197,7 @@
 
 def front_weights(star_ref, source_ref, deriv_ref, trace_ref, ready=lambda *numbers: None):
     ready(2, 3)
-    star = star_weights([star_ref[0], star_ref[1], star_ref[2], source_ref[...]])
+    star = star_quarters([star_ref[0], star_ref[1], star_ref[2], source_ref[...]])
     ready(4, 5)
     basis_weights = weights(side_by_side([deriv_ref[d] for d in range(3)]))
     return star, basis_weights, side_weights(stacked_traces(trace_ref))
@@ -285,7 +324,7 @@
 
 def volume(q_ref, jac_ref, star_ref, stiff_ref, integral_ref, base_ref, spread_ref):
     basis = stiff_ref.shape[1]
-    star = star_weights([star_ref[0], star_ref[1], star_ref[2]])
+    star = star_quarters([star_ref[0], star_ref[1], star_ref[2]])
     basis_weights = weights(side_by_side([stiff_ref[d] for d in range(3)]))
     spread_out(integral_ref, jac_ref, star, spread_ref)
     for g in range(FIELDS):
@@ -361,8 +400,8 @@
 
 def prepared(
     place, star_ref, source_ref, deriv_ref, trace_ref, lift_ref, partner_ref,
-    sea_face_ref, sea_row_ref, normal_ref, speed_ref,
-    star4_ref, star3_ref, b1_ref, b2_ref, t_ref, l1_ref, l2_ref, hot_ref, sea_ref, slot_ref, scale_ref,
+    sea_face_ref, sea_row_ref, normal_ref, speed_ref, interp_ref,
+    star4_ref, star3_ref, b1_ref, b2_ref, t_ref, l1_ref, l2_ref, hot_ref, sea_ref, slot_ref, scale_ref, uplift_ref,
 ):
     star, (b1_ref[...], b2_ref[...]), t_ref[...] = front_weights(
         star_ref, source_ref, deriv_ref, trace_ref
@@ -385,6 +424,11 @@
     scales = 0.5 * jnp.concatenate(scales + [jnp.zeros((4, 4 * elements), F32)], axis=0)
     scale_ref[...] = folded(
         lax.dot_general(both_parts(scales), hot_ref[...], NT, preferred_element_type=F32)
+    )
+    uplift_ref[...] = side_weights(
+        jnp.concatenate(
+            [exact_dot(interp_ref[...], trace_ref[:, f, :]) for f in range(4)], axis=0
+        )
     )
     faces = sea_face_ref.shape[1]
     sea_ref[...] = (iota((4 * elements, faces), 0) == sea_face_ref[...]).astype(F32).astype(BF16)
@@ -465,12 +509,11 @@
         state_ref[rows, :] = base_ref[rows, :] - weighted(*lift, flux_ref[g])
 
 
-def rates_out(vertical, trace_ref, interp_ref, sea_base_ref, sea_ref, slot_ref, out_ref):
+def rates_out(vertical, uplift_ref, sea_base_ref, sea_ref, slot_ref, out_ref):
     tiles, _, faces = slot_ref.shape
-    sea = side_weighted(trace_ref[...], vertical)
-    sea = jnp.concatenate([sea[f * FACE_PAD : (f + 1) * FACE_PAD] for f in range(4)], axis=1)
-    coeffs = folded(dot(both_parts(sea), sea_ref[...]))[:FACE_BASIS]
-    rates = exact_dot(interp_ref[...], coeffs)
+    sea = side_weighted(uplift_ref[...], vertical)
+    sea = jnp.concatenate([sea[f * POINTS : (f + 1) * POINTS] for f in range(4)], axis=1)
+    rates = folded(dot(both_parts(sea), sea_ref[...]))
     corners = jnp.where(
         iota((8, faces), 0) == 0, sea_base_ref[0:1, :], sea_base_ref[1:2, :]
     ).astype(F32)
@@ -488,7 +531,7 @@
 
 
 def finish(*refs):
-    solid, sea, refs = refs[:12], refs[12:17], refs[17:]
+    solid, sea, refs = refs[:12], refs[12:16], refs[16:]
     state_out, out_ref, state_ref, sems, *scratch = refs
     back(*solid, state_ref, *scratch)
     copy = pltpu.make_async_copy(state_ref, state_out, sems.at[0])
@@ -597,12 +640,6 @@
             two_ref[at, :] = columns[2:4, lanes]
 
 
-def volume_and_columns(place, *refs):
-    solid, water, (base_ref, one_ref, two_ref, spread_ref) = refs[:5], refs[5:8], refs[8:]
-    volume(*solid, base_ref, spread_ref)
-    edge_columns(place, *water, one_ref, two_ref)
-
-
 def widened(place, depth_ref, momentum_ref, bottom_ref, p1_ref, p2_ref, q1_ref, q2_ref, out_ref):
     tile_x, tile_y = depth_ref.shape
     a1, c1 = unequal(place)
@@ -710,12 +747,18 @@
     return scale * slope_x, scale * slope_y
 
 
-def ocean_first(
-    place, depth_ref, momentum_ref, bottom_ref, p1_ref, p2_ref, q1_ref, q2_ref, wide, state, cell, face
+def ocean_cells(
+    place, depth_ref, momentum_ref, bottom_ref, p1_ref, p2_ref, q1_ref, q2_ref, wide, cell
 ):
-    tile_x, tile_y = depth_ref.shape
     widened(place, depth_ref, momentum_ref, bottom_ref, p1_ref, p2_ref, q1_ref, q2_ref, wide)
-    cells(wide, cell, 8, cell.shape[1] - 8)
+    height, span = wide.shape[1:]
+    cell[:, 0:8, :] = jnp.zeros((5, 8, span), F32)
+    cell[:, height - 8 :, :] = jnp.zeros((5, 8, span), F32)
+    cells(wide, cell, 8, height - 8)
+
+
+def ocean_first(place, wide, cell, state, face):
+    tile_x, tile_y = wide.shape[1] - 2 * MARGIN, wide.shape[2] - 128
     height, span = wide.shape[1:]
     lane = iota((STRIP, span), 1)
     outside = ((lane == span - 1) & (place[1] == 0)) | (
@@ -910,43 +953,49 @@
             )
         p2, p1 = swap(p2, "gx", 1), swap(p1, "gx", 0)
         inside = (state, jacobian, star_mats, stiff_mats, integral)
+        (base,) = call(volume, [solid], *inside, scratch=[spread])
         if section == 0:
-            base, *columns = call(
-                volume_and_columns, [solid] + [(OCEAN_ROWS, 128)] * 2,
-                *inside, water_depth, momentum, bottom,
-                place=place, scratch=[spread],
+            columns = call(
+                edge_columns, [(OCEAN_ROWS, 128)] * 2, water_depth, momentum, bottom, place=place
             )
             size = 3 * HALF + 2 * OCEAN_ROWS
         else:
-            (base,) = call(volume, [solid], *inside, scratch=[spread])
             columns, size = [], 3 * HALF
+            wide, cell = call(
+                ocean_cells,
+                [(4,) + wide_shape, (5,) + wide_shape],
+                water_depth, momentum, bottom, *halos,
+                place=place,
+            )
+            base, wide, cell = lax.optimization_barrier((base, wide, cell))
         p1, p2, base = lax.optimization_barrier((p1, p2, base))
         q1, q2 = call(forward, [(size, 128)] * 2, p1, p2, own1, own2, *columns, place=place)
         q2, q1 = swap(q2, "gy", 1), swap(q1, "gy", 0)
         if section == 1:
-            wide, first = call(
-                ocean_first,
-                [(4,) + wide_shape, (3,) + wide_shape],
-                water_depth, momentum, bottom, *halos,
-                place=place, scratch=[(5,) + wide_shape, (3,) + wide_shape],
-            )
             (flux,) = call(
                 local_flux, [flux_shape], table, face_partner, normals, speed, star3,
                 scratch=[faces],
             )
-            q1, q2, flux, wide, first = lax.optimization_barrier((q1, q2, flux, wide, first))
+            (first,) = call(
+                ocean_first,
+                [(3,) + wide_shape],
+                wide, cell,
+                place=place, scratch=[(3,) + wide_shape],
+            )
+            q1, q2, flux, first = lax.optimization_barrier((q1, q2, flux, first))
         else:
             half = lambda *shape: jax.ShapeDtypeStruct(shape, BF16)
             size, sea = FIELDS * 8, sea_face.shape[0]
             star4, star3, *ready = call(
                 prepared,
-                [half(8 * size, 2 * size), half(6 * size, 2 * size)]
+                [half(16 * (FIELDS + FIELDS % 2), 12 * (FIELDS + FIELDS % 2)), half(6 * size, 2 * size)]
                 + [half(2 * basis, 3 * basis), half(basis, 3 * basis)]
                 + [half(4 * FACE_PAD, 3 * basis)]
                 + [half(2 * basis, 4 * FACE_PAD), half(basis, 4 * FACE_PAD)]
-                + [half(8 * CAP, 4 * elements), half(4 * elements, sea), half(tiles, 4 * CAP, sea), (8, 8 * CAP)],
+                + [half(8 * CAP, 4 * elements), half(4 * elements, sea), half(tiles, 4 * CAP, sea), (8, 8 * CAP)]
+                + [half(4 * POINTS, 3 * basis)],
                 star_mats, source_mat, deriv_mats, traces, lifts, face_partner,
-                sea_face.reshape(1, -1), sea_row.T, normals, speed,
+                sea_face.reshape(1, -1), sea_row.T, normals, speed, interp_mat,
                 place=place,
             )
             (flux,) = call(
@@ -954,7 +1003,7 @@
                 scratch=[faces],
             )
             q1, q2, flux, *ready = lax.optimization_barrier((q1, q2, flux, *ready))
-            derivs, traced, lifting, (hot, sea_hot, slot_hot, scales) = (
+            derivs, traced, lifting, (hot, sea_hot, slot_hot, scales, uplift) = (
                 ready[0:2], ready[2:3], ready[3:5], ready[5:],
             )
         fixed = (star3, *lifting, hot, scales)
@@ -971,7 +1020,7 @@
                 finish,
                 [solid, (tiles, 32, 128)],
                 base, flux, *fixed, *arrived,
-                *traced, interp_mat, sea_base.T, sea_hot, slot_hot,
+                uplift, sea_base.T, sea_hot, slot_hot,
                 place=place, scratch=[flux_shape, packed, remote], sent=1, copies=1,
             )
     incoming = lax.all_to_all(outgoing, "gy", split_axis=0, concat_axis=0, tiled=True)

time: 73.8 us -> 73.2 us (level)
  starting transfers between devices: 16.3 us -> 17.5 us
  local copies, waits for them, and re-layouts: 1.25 us -> 0.12 us
    ppermute x10, starting transfers between devices: 16.3 us -> 17.5 us  [swap(): return lax.ppermute(block, axis, pairs)]
    unnamed x46, local copies, waits for them, and re-layouts: 1.25 us -> 0.12 us
    pallas_call x15 -> x17, Pallas kernels: 36 us -> 35.6 us  [call(): pl.pallas_call(body, out_shape=shapes, in_specs=specs, out_specs=[pl.Bloc...]
  transfers between devices with their start and end apart: 10 -> 10, of which waited for: 3 -> 4; matrix products, arithmetic and copies ran while one was open for 0% -> 0% of each run, Pallas kernels for 22% -> 22%
where the time goes in v5:
time: 73.2 us; the launch traced here: 72.6 us
  Pallas kernels  35.6 us (49%)
  starting transfers between devices  17.5 us (24%)
  blocking collectives  11.8 us (16%)
  waiting for transfers between devices  6.31 us (9%)
  between operations  1.33 us (2%)
    pallas_call x17, Pallas kernels, call(): pl.pallas_call(body, out_shape=shapes, in_specs=specs, out_specs=[pl.Bloc...  35.6 us
    ppermute x10, starting transfers between devices, swap(): return lax.ppermute(block, axis, pairs)  17.5 us
    all_to_all x1, blocking collectives, per_device(): lax.all_to_all(outgoing, 'gy', split_axis=0, concat_axis=0, tiled=True)  11.8 us
    ppermute x10, waiting for transfers between devices, swap(): return lax.ppermute(block, axis, pairs)  6.31 us
  transfers between devices with their start and end apart: 10, of which 4 were waited for; matrix products, arithmetic and copies ran while one was open for 0% of the time, Pallas kernels for 22%

profile of v5, /device:TPU:1, one launch (start us, length us, event | category | flops | bytes accessed | tf_op | source)
XLA Modules:
  0.0 72.6 jit_solution(2272230890165422811)
XLA Ops:
  0.6 0.0 copy-start.2
  0.7 7.4 %shard_map.202 = (f32[728,256]{1,0:T(8,128)}, f32[312,1024]{1,0:T(8,128)}, f32[427,128]{1,0:T(8,128)}, f32[427,128]{1,0:T(8,128)}, f32[137,128]{1,0:T(8,128)}, /*index=5*/f32[137,128]{1,0:T(8,128)}) custom-call(f32[728,256]{1,0:T(8,128)} %bitcast.9, f32[3,3,256]{2,1,0:T(4,128)} %jac_ref.3, f32[3,13,13]{2,1,0:T(8,128)} %star_ref.3, f32[13,13]{1,0:T(8,128)} %refs_1_.7, ...), custom_call_target="tpu_custom_call" | custom-call | tf_op jit(solution)/shard_map/pallas_call | solution.py:880
  8.1 0.0 copy-start.5
  8.2 0.1 collective-permute-start
  8.3 4.6 %collective-permute-start.1 = (f32[427,128]{1,0:T(8,128)}, f32[427,128]{1,0:T(8,128)S(1)}, u32[]{:S(2)}, u32[]{:S(2)}) collective-permute-start(f32[427,128]{1,0:T(8,128)} %get-tuple-element.71), channel_id=1, source_target_pairs={{8,16},{16,8},{0,0},{24,24},{9,17},{17,9},{1,1},{25,25},{10,18},{1... | collective-permute-start | bytes 655880 | tf_op jit(solution)/shard_map/ppermute | solution.py:898
  12.9 0.9 %shard_map.204 = (f32[16,128]{1,0:T(8,128)S(1)}, f32[16,128]{1,0:T(8,128)S(1)}) custom-call(f32[256,256]{1,0:T(8,128)S(1)} %copy-done.2, f32[2,256,256]{2,1,0:T(8,128)S(1)} %copy-done, f32[256,256]{1,0:T(8,128)S(1)} %copy-done.3), custom_call_target="tpu_custom_call" | custom-call | tf_op jit(solution)/shard_map/pallas_call | solution.py:880
  13.9 0.0 copy-done.6
  13.9 0.0 copy-done.7
  13.9 0.0 copy-done.9
  13.9 0.0 copy-done.5
  13.9 0.0 copy-start.8
  13.9 0.0 copy-start.10
  14.0 0.0 copy-start.11
  14.0 0.0 copy-start.14
  14.0 0.0 copy-start.15
  14.0 0.0 copy-start.16
  14.0 0.0 copy-start.18
  14.0 0.0 copy-start.19
  14.0 0.0 copy-start.21
  14.0 0.0 copy-start.22
  14.1 1.6 %shard_map.203.refs_0_ = f32[728,256]{1,0:T(8,128)S(1)} custom-call(f32[728,256]{1,0:T(8,128)S(1)} %bitcast.10, f32[3,3,256]{2,1,0:T(4,128)S(1)} %copy-done.9, f32[3,13,13]{2,1,0:T(8,128)S(1)} %copy-done.6, f32[3,56,56]{2,1,0:T(8,128)S(1)} %copy-done.7, f32[728,256]{1,0:T(8,128)S(1)} %copy-done.5), custom_call_target="tpu_custom_call" | custom-call | tf_op jit(solution)/shard_map/pallas_call | solution.py:880
  15.7 0.0 collective-permute-done.refs_0_.refs_7_.refs_3_
  15.7 1.0 %collective-permute-done.1.refs_1_.refs_8_.refs_4_ = f32[427,128]{1,0:T(8,128)S(1)} collective-permute-done((f32[427,128]{1,0:T(8,128)}, f32[427,128]{1,0:T(8,128)S(1)}, u32[]{:S(2)}, u32[]{:S(2)}) %collective-permute-start.1) | collective-permute-done | bytes 218656 | tf_op jit(solution)/shard_map/ppermute | solution.py:898
  16.8 1.7 %collective-permute-start.2 = (f32[443,128]{1,0:T(8,128)S(1)}, f32[443,128]{1,0:T(8,128)S(1)}, u32[]{:S(2)}, u32[]{:S(2)}) collective-permute-start(f32[443,128]{1,0:T(8,128)S(1)} %get-tuple-element.80), channel_id=1, source_target_pairs={{0,1},{1,0},{2,3},{3,2},{4,5},{5,4},{6,7},{7,6},{8,9},{9,8},{10,11... | collective-permute-start | bytes 680456 | tf_op jit(solution)/shard_map/ppermute | solution.py:898
  18.5 0.8 %collective-permute-start.3 = (f32[443,128]{1,0:T(8,128)S(1)}, f32[443,128]{1,0:T(8,128)S(1)}, u32[]{:S(2)}, u32[]{:S(2)}) collective-permute-start(f32[443,128]{1,0:T(8,128)S(1)} %get-tuple-element.81), channel_id=1, source_target_pairs={{1,2},{2,1},{3,4},{4,3},{5,6},{6,5},{0,0},{7,7},{9,10},{10,9},{11,... | collective-permute-start | bytes 680456 | tf_op jit(solution)/shard_map/ppermute | solution.py:898
  19.4 0.0 copy-done.8
  19.4 0.0 copy-done.10
  19.4 0.0 copy-done.11
  19.4 0.0 copy-done.14
  19.4 0.0 copy-done.15
  19.4 0.0 copy-done.16
  19.4 0.0 copy-done.18
  19.4 0.0 copy-done.19
  19.4 0.0 copy-done.21
  19.4 0.0 copy-done.22
  19.4 1.7 %shard_map.206 = (bf16[224,168]{1,0:T(8,128)(2,1)S(1)}, bf16[624,208]{1,0:T(8,128)(2,1)S(1)}, bf16[112,168]{1,0:T(8,128)(2,1)S(1)}, bf16[56,168]{1,0:T(8,128)(2,...) custom-call(f32[3,13,13]{2,1,0:T(8,128)S(1)} %copy-done.6, ...), custom_call_target="tpu_custom_call" | custom-call | tf_op jit(solution)/shard_map/pallas_call | solution.py:880
  21.2 2.7 %shard_map.207.refs_1_ = f32[13,96,256]{2,1,0:T(8,128)S(1)} custom-call(f32[312,1024]{1,0:T(8,128)S(1)} %copy-done.4, s32[4,256]{1,0:T(4,128)S(1)} %copy-done.15, f32[3,4,256]{2,1,0:T(4,128)S(1)} %bitcast.14, f32[1,256]{1,0:T(1,128)S(1)} %bitcast.18, bf16[624,208]{1,0:T(8,128)(2,1)S(1)} %get-tuple-element.83.star_ref.refs_2_), custom_call_target="tpu_custom_call" | custom-call | tf_op jit(solution)/shard_map/pallas_call | solution.py:880
  23.9 2.5 %collective-permute-done.2.refs_9_.refs_5_ = f32[443,128]{1,0:T(8,128)S(1)} collective-permute-done((f32[443,128]{1,0:T(8,128)S(1)}, f32[443,128]{1,0:T(8,128)S(1)}, u32[]{:S(2)}, u32[]{:S(2)}) %collective-permute-start.2) | collective-permute-done | bytes 226848 | tf_op jit(solution)/shard_map/ppermute | solution.py:898
  26.4 0.0 collective-permute-done.3.refs_10_.refs_6_
  26.4 2.0 %shard_map.208.refs_0_.q_ref = f32[728,256]{1,0:T(8,128)S(1)} custom-call(f32[728,256]{1,0:T(8,128)S(1)} %shard_map.203.refs_0_, f32[13,96,256]{2,1,0:T(8,128)S(1)} %shard_map.207.refs_1_, bf16[624,208]{1,0:T(8,128)(2,1)S(1)} %get-tuple-element.83.star_ref.refs_2_, bf16[112,96]{1,0:T(8,128)(2,1)S(1)} %get-tuple-element.95.refs_3_, ...), custom_call_target="tpu_custom_call" | custom-call | tf_op jit(solution)/shard_map/pallas_call | solution.py:880
  28.5 4.4 %shard_map.209 = (f32[728,256]{1,0:T(8,128)S(1)}, f32[312,1024]{1,0:T(8,128)S(1)}, f32[411,128]{1,0:T(8,128)S(1)}, f32[411,128]{1,0:T(8,128)S(1)}, f32[137,128]{1,0:T(8,128)S(1)}, /*index=5*/f32[137,128]{1,0:T(8,128)S(1)}) custom-call(f32[728,256]{1,0:T(8,128)S(1)} %shard_map.208.refs_0_.q_ref, f32[3,3,256]{2,1,0:T(4,128)S(1)} %copy-done.9, ...), custom_call_target="tpu_custom_call" | custom-call | tf_op jit(solution)/shard_map/pallas_call | solution.py:880
  32.9 0.1 collective-permute-start.4
  32.9 3.4 %collective-permute-start.5 = (f32[411,128]{1,0:T(8,128)S(1)}, f32[411,128]{1,0:T(8,128)S(1)}, u32[]{:S(2)}, u32[]{:S(2)}) collective-permute-start(f32[411,128]{1,0:T(8,128)S(1)} %get-tuple-element.106), channel_id=1, source_target_pairs={{8,16},{16,8},{0,0},{24,24},{9,17},{17,9},{1,1},{25,25},{10,18},{1... | collective-permute-start | bytes 631304 | tf_op jit(solution)/shard_map/ppermute | solution.py:898
  36.4 0.4 shard_map.211
  36.8 1.7 %shard_map.210.refs_0_ = f32[728,256]{1,0:T(8,128)S(1)} custom-call(f32[728,256]{1,0:T(8,128)S(1)} %shard_map.208.refs_0_.q_ref, f32[3,3,256]{2,1,0:T(4,128)S(1)} %copy-done.9, f32[3,13,13]{2,1,0:T(8,128)S(1)} %copy-done.6, f32[3,56,56]{2,1,0:T(8,128)S(1)} %copy-done.7, f32[728,256]{1,0:T(8,128)S(1)} %get-tuple-element.107.integral_ref), custom_call_target="tpu_custom_call" | custom-call | tf_op jit(solution)/shard_map/pallas_call | solution.py:880
  38.5 0.0 collective-permute-done.4.refs_0_.refs_7_
  38.5 1.9 %collective-permute-done.5.refs_1_.refs_8_ = f32[411,128]{1,0:T(8,128)S(1)} collective-permute-done((f32[411,128]{1,0:T(8,128)S(1)}, f32[411,128]{1,0:T(8,128)S(1)}, u32[]{:S(2)}, u32[]{:S(2)}) %collective-permute-start.5) | collective-permute-done | bytes 210464 | tf_op jit(solution)/shard_map/ppermute | solution.py:898
  40.4 2.0 %collective-permute-start.6 = (f32[411,128]{1,0:T(8,128)S(1)}, f32[411,128]{1,0:T(8,128)S(1)}, u32[]{:S(2)}, u32[]{:S(2)}) collective-permute-start(f32[411,128]{1,0:T(8,128)S(1)} %get-tuple-element.116), channel_id=1, source_target_pairs={{0,1},{1,0},{2,3},{3,2},{4,5},{5,4},{6,7},{7,6},{8,9},{9,8},{10,11... | collective-permute-start | bytes 631304 | tf_op jit(solution)/shard_map/ppermute | solution.py:898
  42.4 0.9 %collective-permute-start.7 = (f32[411,128]{1,0:T(8,128)S(1)}, f32[411,128]{1,0:T(8,128)S(1)}, u32[]{:S(2)}, u32[]{:S(2)}) collective-permute-start(f32[411,128]{1,0:T(8,128)S(1)} %get-tuple-element.117), channel_id=1, source_target_pairs={{1,2},{2,1},{3,4},{4,3},{5,6},{6,5},{0,0},{7,7},{9,10},{10,9},{11,... | collective-permute-start | bytes 631304 | tf_op jit(solution)/shard_map/ppermute | solution.py:898
  43.3 2.7 %shard_map.213.refs_1_ = f32[13,96,256]{2,1,0:T(8,128)S(1)} custom-call(f32[312,1024]{1,0:T(8,128)S(1)} %get-tuple-element.118.table_ref, s32[4,256]{1,0:T(4,128)S(1)} %copy-done.15, f32[3,4,256]{2,1,0:T(4,128)S(1)} %bitcast.15, f32[1,256]{1,0:T(1,128)S(1)} %bitcast.19, bf16[624,208]{1,0:T(8,128)(2,1)S(1)} %get-tuple-element.83.star_ref.refs_2_), custom_call_target="tpu_custom_call" | custom-call | tf_op jit(solution)/shard_map/pallas_call | solution.py:880
  46.1 0.0 copy-start.20
  46.1 2.0 %shard_map.214.first.refs_1_ = f32[3,288,384]{2,1,0:T(8,128)S(1)} custom-call(f32[4,288,384]{2,1,0:T(8,128)S(1)} %get-tuple-element.119.refs_0_.wide, f32[5,288,384]{2,1,0:T(8,128)S(1)} %get-tuple-element.120.refs_1_), custom_call_target="tpu_custom_call" | custom-call | tf_op jit(solution)/shard_map/pallas_call | solution.py:880
  48.1 0.9 %collective-permute-done.6.refs_9_ = f32[411,128]{1,0:T(8,128)S(1)} collective-permute-done((f32[411,128]{1,0:T(8,128)S(1)}, f32[411,128]{1,0:T(8,128)S(1)}, u32[]{:S(2)}, u32[]{:S(2)}) %collective-permute-start.6) | collective-permute-done | bytes 210464 | tf_op jit(solution)/shard_map/ppermute | solution.py:898
  49.0 0.0 collective-permute-done.7.refs_10_
  49.0 0.0 copy-done.20
  49.0 2.9 %shard_map.215 = (f32[728,256]{1,0:T(8,128)}, f32[8,32,128]{2,1,0:T(8,128)S(1)}) custom-call(f32[728,256]{1,0:T(8,128)S(1)} %shard_map.210.refs_0_, f32[13,96,256]{2,1,0:T(8,128)S(1)} %shard_map.213.refs_1_, bf16[624,208]{1,0:T(8,128)(2,1)S(1)} %get-tuple-element.83.star_ref.refs_2_, bf16[112,96]{1,0:T(8,128)(2,1)S(1)} %get-tuple-element.95.refs_3_, ...), custom_call_target="tpu_custom_call" | custom-call | tf_op jit(solution)/shard_map/pallas_call | solution.py:880
  51.9 11.8 %all_to_all.5.refs_0_ = f32[8,32,128]{2,1,0:T(8,128)S(1)} all-to-all(f32[8,32,128]{2,1,0:T(8,128)S(1)} %get-tuple-element.129), channel_id=1, replica_groups=mesh['gx'=4,'gy'=8] {'gy'}, dimensions={0} | all-to-all | bytes 262144 | tf_op jit(solution)/shard_map/all_to_all | solution.py:1026
  63.6 1.6 %shard_map.216 = (f32[256,384]{1,0:T(8,128)S(1)}, f32[8,384]{1,0:T(8,128)S(1)}, f32[8,384]{1,0:T(8,128)S(1)}) custom-call(f32[8,32,128]{2,1,0:T(8,128)S(1)} %all_to_all.5.refs_0_), custom_call_target="tpu_custom_call" | custom-call | tf_op jit(solution)/shard_map/pallas_call | solution.py:880
  65.3 0.1 collective-permute-start.8
  65.3 3.7 %collective-permute-start.9 = (f32[8,384]{1,0:T(8,128)S(1)}, f32[8,384]{1,0:T(8,128)S(1)}, u32[]{:S(2)}, u32[]{:S(2)}) collective-permute-start(f32[8,384]{1,0:T(8,128)S(1)} %get-tuple-element.132), channel_id=1, source_target_pairs={{8,16},{16,8},{24,0},{0,24},{9,17},{17,9},{25,1},{1,25},{10,18},{1... | collective-permute-start | bytes 36872 | tf_op jit(solution)/shard_map/ppermute | solution.py:898
  69.1 2.3 %shard_map.217 = (f32[3,256,256]{2,1,0:T(8,128)S(1)}, f32[256,256]{1,0:T(8,128)S(1)}) custom-call(f32[4,288,384]{2,1,0:T(8,128)S(1)} %get-tuple-element.119.refs_0_.wide, f32[3,288,384]{2,1,0:T(8,128)S(1)} %shard_map.214.first.refs_1_, f32[256,384]{1,0:T(8,128)S(1)} %get-tuple-element.130.forcing_ref.refs_2_), custom_call_target="tpu_custom_call" | custom-call | tf_op jit(solution)/shard_map/pallas_call | solution.py:880
  71.4 0.0 collective-permute-done.8.refs_3_
  71.4 0.0 collective-permute-done.9.refs_4_
  71.4 1.0 %shard_map.218 = (f32[3,256,256]{2,1,0:T(8,128)}, f32[256,256]{1,0:T(8,128)}) custom-call(f32[4,288,384]{2,1,0:T(8,128)S(1)} %get-tuple-element.119.refs_0_.wide, f32[3,288,384]{2,1,0:T(8,128)S(1)} %shard_map.214.first.refs_1_, f32[256,384]{1,0:T(8,128)S(1)} %get-tuple-element.130.forcing_ref.refs_2_, f32[8,384]{1,0:T(8,128)S(1)} %collective-permute-done.8.refs_3_, ...), custom_call_target="tpu_custom_call" | custom-call | tf_op jit(solution)/shard_map/pallas_call | solution.py:880
  (20 shorter events, 0.1 us)
Async XLA Ops:
  0.6 12.3 %copy-start.2 = (f32[256,256]{1,0:T(8,128)S(1)}, f32[256,256]{1,0:T(8,128)}, u32[]{:S(2)}) copy-start(f32[256,256]{1,0:T(8,128)} %refs_0_.5) | copy-start | bytes 786436
  0.6 12.3 %copy-start = (f32[2,256,256]{2,1,0:T(8,128)S(1)}, f32[2,256,256]{2,1,0:T(8,128)}, u32[]{:S(2)}) copy-start(f32[2,256,256]{2,1,0:T(8,128)} %refs_1_.9) | copy-start | bytes 1572868
  0.7 12.3 %copy-start.3 = (f32[256,256]{1,0:T(8,128)S(1)}, f32[256,256]{1,0:T(8,128)}, u32[]{:S(2)}) copy-start(f32[256,256]{1,0:T(8,128)} %refs_2_.7) | copy-start | bytes 786436
  0.7 13.2 %copy-start.1 = (f32[13,56,256]{2,1,0:T(8,128)S(1)}, f32[13,56,256]{2,1,0:T(8,128)}, u32[]{:S(2)}) copy-start(f32[13,56,256]{2,1,0:T(8,128)} %param.19) | copy-start | bytes 2236420
  0.7 13.2 %copy-start.6 = (f32[3,13,13]{2,1,0:T(8,128)S(1)}, f32[3,13,13]{2,1,0:T(8,128)}, u32[]{:S(2)}) copy-start(f32[3,13,13]{2,1,0:T(8,128)} %star_ref.3) | copy-start | bytes 6088
  0.7 13.2 %copy-start.7 = (f32[3,56,56]{2,1,0:T(8,128)S(1)}, f32[3,56,56]{2,1,0:T(8,128)}, u32[]{:S(2)}) copy-start(f32[3,56,56]{2,1,0:T(8,128)} %stiff_ref.3) | copy-start | bytes 112900
  0.7 13.2 %copy-start.9 = (f32[3,3,256]{2,1,0:T(4,128)S(1)}, f32[3,3,256]{2,1,0:T(4,128)}, u32[]{:S(2)}) copy-start(f32[3,3,256]{2,1,0:T(4,128)} %jac_ref.3) | copy-start | bytes 27652
  8.1 5.8 %copy-start.5 = (f32[728,256]{1,0:T(8,128)S(1)}, f32[728,256]{1,0:T(8,128)}, u32[]{:S(2)}) copy-start(f32[728,256]{1,0:T(8,128)} %get-tuple-element.72.integral_ref) | copy-start | bytes 2236420
  8.2 7.6 %collective-permute-start = (f32[427,128]{1,0:T(8,128)}, f32[427,128]{1,0:T(8,128)S(1)}, u32[]{:S(2)}, u32[]{:S(2)}) collective-permute-start(f32[427,128]{1,0:T(8,128)} %get-tuple-element.70), channel_id=1, source_target_pairs={{0,8},{8,0},{16,24},{24,16},{1,9},{9,1},{17,25},{25,17},{2,10},{10... | collective-permute-start | bytes 655880 | tf_op jit(solution)/shard_map/ppermute | solution.py:898
  8.3 8.4 %collective-permute-start.1 = (f32[427,128]{1,0:T(8,128)}, f32[427,128]{1,0:T(8,128)S(1)}, u32[]{:S(2)}, u32[]{:S(2)}) collective-permute-start(f32[427,128]{1,0:T(8,128)} %get-tuple-element.71), channel_id=1, source_target_pairs={{8,16},{16,8},{0,0},{24,24},{9,17},{17,9},{1,1},{25,25},{10,18},{1... | collective-permute-start | bytes 655880 | tf_op jit(solution)/shard_map/ppermute | solution.py:898
  13.9 2.8 %copy-start.12 = (f32[137,128]{1,0:T(8,128)S(1)}, f32[137,128]{1,0:T(8,128)}, u32[]{:S(2)}) copy-start(f32[137,128]{1,0:T(8,128)} %get-tuple-element.76.refs_2_) | copy-start | bytes 210436
  13.9 2.8 %copy-start.13 = (f32[137,128]{1,0:T(8,128)S(1)}, f32[137,128]{1,0:T(8,128)}, u32[]{:S(2)}) copy-start(f32[137,128]{1,0:T(8,128)} %get-tuple-element.77.refs_3_) | copy-start | bytes 210436
  13.9 5.4 %copy-start.8 = (f32[3,56,56]{2,1,0:T(8,128)S(1)}, f32[3,56,56]{2,1,0:T(8,128)}, u32[]{:S(2)}) copy-start(f32[3,56,56]{2,1,0:T(8,128)} %refs_2_.6) | copy-start | bytes 112900
  13.9 5.4 %copy-start.10 = (f32[4,21,56]{2,0,1:T(4,128)S(1)}, f32[4,21,56]{2,0,1:T(4,128)}, u32[]{:S(2)}) copy-start(f32[4,21,56]{2,0,1:T(4,128)} %param.27) | copy-start | bytes 56452
  14.0 5.4 %copy-start.11 = (f32[4,3,256]{2,0,1:T(4,128)S(1)}, f32[4,3,256]{2,0,1:T(4,128)}, u32[]{:S(2)}) copy-start(f32[4,3,256]{2,0,1:T(4,128)} %param.21) | copy-start | bytes 36868
  14.0 5.4 %copy-start.14 = (f32[4,56,21]{1,0,2:T(4,128)S(1)}, f32[4,56,21]{1,0,2:T(4,128)}, u32[]{:S(2)}) copy-start(f32[4,56,21]{1,0,2:T(4,128)} %param.28) | copy-start | bytes 56452
  14.0 5.4 %copy-start.15 = (s32[4,256]{1,0:T(4,128)S(1)}, s32[4,256]{1,0:T(4,128)}, u32[]{:S(2)}) copy-start(s32[4,256]{1,0:T(4,128)} %partner_ref.3) | copy-start | bytes 12292
  14.0 5.4 %copy-start.16 = (f32[13,13]{1,0:T(8,128)S(1)}, f32[13,13]{1,0:T(8,128)}, u32[]{:S(2)}) copy-start(f32[13,13]{1,0:T(8,128)} %refs_1_.7) | copy-start | bytes 2032
  14.0 5.4 %copy-start.18 = (f32[256]{0:T(256)S(1)}, f32[256]{0:T(256)}, u32[]{:S(2)}) copy-start(f32[256]{0:T(256)} %param.22) | copy-start | bytes 3076
  14.0 5.4 %copy-start.19 = (f32[16,21]{1,0:T(8,128)S(1)}, f32[16,21]{1,0:T(8,128)}, u32[]{:S(2)}) copy-start(f32[16,21]{1,0:T(8,128)} %refs_10_.1) | copy-start | bytes 4036
  14.0 5.4 %copy-start.21 = (s32[256]{0:T(256)S(1)}, s32[256]{0:T(256)}, u32[]{:S(2)}) copy-start(s32[256]{0:T(256)} %param.31) | copy-start | bytes 3076
  14.0 5.4 %copy-start.22 = (s32[256,1]{0,1:T(1,128)S(1)}, s32[256,1]{0,1:T(1,128)}, u32[]{:S(2)}) copy-start(s32[256,1]{0,1:T(1,128)} %param.32) | copy-start | bytes 3076
  14.1 7.1 %copy-start.4 = (f32[312,1024]{1,0:T(8,128)S(1)}, f32[312,1024]{1,0:T(8,128)}, u32[]{:S(2)}) copy-start(f32[312,1024]{1,0:T(8,128)} %get-tuple-element.82.table_ref) | copy-start | bytes 3833860
  16.8 9.6 %collective-permute-start.2 = (f32[443,128]{1,0:T(8,128)S(1)}, f32[443,128]{1,0:T(8,128)S(1)}, u32[]{:S(2)}, u32[]{:S(2)}) collective-permute-start(f32[443,128]{1,0:T(8,128)S(1)} %get-tuple-element.80), channel_id=1, source_target_pairs={{0,1},{1,0},{2,3},{3,2},{4,5},{5,4},{6,7},{7,6},{8,9},{9,8},{10,11... | collective-permute-start | bytes 680456 | tf_op jit(solution)/shard_map/ppermute | solution.py:898
  18.5 7.9 %collective-permute-start.3 = (f32[443,128]{1,0:T(8,128)S(1)}, f32[443,128]{1,0:T(8,128)S(1)}, u32[]{:S(2)}, u32[]{:S(2)}) collective-permute-start(f32[443,128]{1,0:T(8,128)S(1)} %get-tuple-element.81), channel_id=1, source_target_pairs={{1,2},{2,1},{3,4},{4,3},{5,6},{6,5},{0,0},{7,7},{9,10},{10,9},{11,... | collective-permute-start | bytes 680456 | tf_op jit(solution)/shard_map/ppermute | solution.py:898
  26.4 2.0 %copy-start.17 = (s32[8,64]{1,0:T(8,128)S(1)}, s32[8,64]{1,0:T(8,128)}, u32[]{:S(2)}) copy-start(s32[8,64]{1,0:T(8,128)} %refs_6_.3) | copy-start | bytes 6148
  32.9 5.6 %collective-permute-start.4 = (f32[411,128]{1,0:T(8,128)S(1)}, f32[411,128]{1,0:T(8,128)S(1)}, u32[]{:S(2)}, u32[]{:S(2)}) collective-permute-start(f32[411,128]{1,0:T(8,128)S(1)} %get-tuple-element.105), channel_id=1, source_target_pairs={{0,8},{8,0},{16,24},{24,16},{1,9},{9,1},{17,25},{25,17},{2,10},{10... | collective-permute-start | bytes 631304 | tf_op jit(solution)/shard_map/ppermute | solution.py:898
  32.9 7.5 %collective-permute-start.5 = (f32[411,128]{1,0:T(8,128)S(1)}, f32[411,128]{1,0:T(8,128)S(1)}, u32[]{:S(2)}, u32[]{:S(2)}) collective-permute-start(f32[411,128]{1,0:T(8,128)S(1)} %get-tuple-element.106), channel_id=1, source_target_pairs={{8,16},{16,8},{0,0},{24,24},{9,17},{17,9},{1,1},{25,25},{10,18},{1... | collective-permute-start | bytes 631304 | tf_op jit(solution)/shard_map/ppermute | solution.py:898
  40.4 8.5 %collective-permute-start.6 = (f32[411,128]{1,0:T(8,128)S(1)}, f32[411,128]{1,0:T(8,128)S(1)}, u32[]{:S(2)}, u32[]{:S(2)}) collective-permute-start(f32[411,128]{1,0:T(8,128)S(1)} %get-tuple-element.116), channel_id=1, source_target_pairs={{0,1},{1,0},{2,3},{3,2},{4,5},{5,4},{6,7},{7,6},{8,9},{9,8},{10,11... | collective-permute-start | bytes 631304 | tf_op jit(solution)/shard_map/ppermute | solution.py:898
  42.4 6.5 %collective-permute-start.7 = (f32[411,128]{1,0:T(8,128)S(1)}, f32[411,128]{1,0:T(8,128)S(1)}, u32[]{:S(2)}, u32[]{:S(2)}) collective-permute-start(f32[411,128]{1,0:T(8,128)S(1)} %get-tuple-element.117), channel_id=1, source_target_pairs={{1,2},{2,1},{3,4},{4,3},{5,6},{6,5},{0,0},{7,7},{9,10},{10,9},{11,... | collective-permute-start | bytes 631304 | tf_op jit(solution)/shard_map/ppermute | solution.py:898
  46.1 2.9 %copy-start.20 = (s32[256,2]{0,1:T(2,128)S(1)}, s32[256,2]{0,1:T(2,128)}, u32[]{:S(2)}) copy-start(s32[256,2]{0,1:T(2,128)} %param.33) | copy-start | bytes 6148
  65.3 6.1 %collective-permute-start.8 = (f32[8,384]{1,0:T(8,128)S(1)}, f32[8,384]{1,0:T(8,128)S(1)}, u32[]{:S(2)}, u32[]{:S(2)}) collective-permute-start(f32[8,384]{1,0:T(8,128)S(1)} %get-tuple-element.131), channel_id=1, source_target_pairs={{0,8},{8,0},{16,24},{24,16},{1,9},{9,1},{17,25},{25,17},{2,10},{10... | collective-permute-start | bytes 36872 | tf_op jit(solution)/shard_map/ppermute | solution.py:898
  65.3 6.0 %collective-permute-start.9 = (f32[8,384]{1,0:T(8,128)S(1)}, f32[8,384]{1,0:T(8,128)S(1)}, u32[]{:S(2)}, u32[]{:S(2)}) collective-permute-start(f32[8,384]{1,0:T(8,128)S(1)} %get-tuple-element.132), channel_id=1, source_target_pairs={{8,16},{16,8},{24,0},{0,24},{9,17},{17,9},{25,1},{1,25},{10,18},{1... | collective-permute-start | bytes 36872 | tf_op jit(solution)/shard_map/ppermute | solution.py:898

commit v6 on v5

--- a/solution.py
+++ b/solution.py
@@ -561,17 +561,20 @@
     arrived = x0.shape[1]
     hot = (iota((tile_x, arrived), 0).astype(F32) == x0).astype(F32).astype(BF16)
     from_y = iota((tile_y, arrived), 0).astype(F32) - y0
-    total = jnp.zeros((tile_x, tile_y), F32)
+    stack = []
     for pr in range(patch_side):
         source = lower if pr < 2 else upper
         value = jnp.zeros((tile_y, arrived), F32)
         for pc in range(patch_side):
             at = (pr * patch_side + pc) % 8
             value = jnp.where(from_y == pc, source[at : at + 1], value)
-        got = sum(
-            lax.dot_general(hot, part, NT, preferred_element_type=F32) for part in parts(value)
-        )
-        total += got if pr == 0 else pltpu.roll(got, pr, 0)
+        stack += parts(value)
+    got = lax.dot_general(jnp.concatenate(stack, axis=0), hot, NT, preferred_element_type=F32)
+    total = jnp.zeros((tile_y, tile_x), F32)
+    for pr in range(patch_side):
+        part = folded(got[2 * pr * tile_y : 2 * (pr + 1) * tile_y])
+        total += part if pr == 0 else pltpu.roll(part, pr, 1)
+    total = total.T
     forcing_ref[:, :tile_y] = total
     near = jnp.concatenate([got_ref[s, 0:POINTS, :] for s in range(tiles)], axis=1)
     x0 = jnp.concatenate([got_ref[s, 24:25, :] for s in range(tiles)], axis=1)
@@ -592,13 +595,14 @@
         chunks[(4 * pr - 1) % 16], chunks[4 * pr] = high, low
     blank = jnp.zeros((8, arrived), F32)
     value = jnp.concatenate([blank if c is None else c for c in chunks], axis=0)
-    got = sum(lax.dot_general(hot, part, NT, preferred_element_type=F32) for part in parts(value))
-    lane = iota((tile_x, 128), 1)
-    used = (lane < 2) | (lane >= 126)
+    got = folded(lax.dot_general(both_parts(value), hot, NT, preferred_element_type=F32))
+    row = iota((128, tile_x), 0)
+    used = (row < 2) | (row >= 126)
     total = jnp.where(used, got, 0.0)
     for pr in range(1, patch_side):
-        moved_back = pltpu.roll(pltpu.roll(got, 128 - 32 * pr, 1), pr, 0)
+        moved_back = pltpu.roll(pltpu.roll(got, 128 - 32 * pr, 0), pr, 1)
         total += jnp.where(used, moved_back, 0.0)
+    total = total.T
     forcing_ref[:, tile_y:] = total
     a1, _ = unequal(place)
     head, tail = forcing_ref[0:8, :], forcing_ref[tile_x - 8 : tile_x, :]

time: 73.2 us -> 73.1 us (level)
  no operation moved by 1% of the time
where the time goes in v6:
time: 73.1 us; the launch traced here: 72.4 us
  Pallas kernels  35.4 us (48%)
  starting transfers between devices  17.5 us (24%)
  blocking collectives  11.8 us (16%)
  waiting for transfers between devices  6.31 us (9%)
  between operations  1.32 us (2%)
    pallas_call x17, Pallas kernels, call(): pl.pallas_call(body, out_shape=shapes, in_specs=specs, out_specs=[pl.Bloc...  35.4 us
    ppermute x10, starting transfers between devices, swap(): return lax.ppermute(block, axis, pairs)  17.5 us
    all_to_all x1, blocking collectives, per_device(): lax.all_to_all(outgoing, 'gy', split_axis=0, concat_axis=0, tiled=True)  11.8 us
    ppermute x10, waiting for transfers between devices, swap(): return lax.ppermute(block, axis, pairs)  6.31 us
  transfers between devices with their start and end apart: 10, of which 4 were waited for; matrix products, arithmetic and copies ran while one was open for 0% of the time, Pallas kernels for 22%

profile of v6, /device:TPU:1, one launch (start us, length us, event | category | flops | bytes accessed | tf_op | source)
XLA Modules:
  0.0 72.4 jit_solution(6308249610522463263)
XLA Ops:
  0.6 0.0 copy-start.2
  0.7 7.4 %shard_map.202 = (f32[728,256]{1,0:T(8,128)}, f32[312,1024]{1,0:T(8,128)}, f32[427,128]{1,0:T(8,128)}, f32[427,128]{1,0:T(8,128)}, f32[137,128]{1,0:T(8,128)}, /*index=5*/f32[137,128]{1,0:T(8,128)}) custom-call(f32[728,256]{1,0:T(8,128)} %bitcast.9, f32[3,3,256]{2,1,0:T(4,128)} %jac_ref.3, f32[3,13,13]{2,1,0:T(8,128)} %star_ref.3, f32[13,13]{1,0:T(8,128)} %refs_1_.7, ...), custom_call_target="tpu_custom_call" | custom-call | tf_op jit(solution)/shard_map/pallas_call | solution.py:884
  8.1 0.0 copy-start.5
  8.2 0.1 collective-permute-start
  8.3 4.6 %collective-permute-start.1 = (f32[427,128]{1,0:T(8,128)}, f32[427,128]{1,0:T(8,128)S(1)}, u32[]{:S(2)}, u32[]{:S(2)}) collective-permute-start(f32[427,128]{1,0:T(8,128)} %get-tuple-element.71), channel_id=1, source_target_pairs={{8,16},{16,8},{0,0},{24,24},{9,17},{17,9},{1,1},{25,25},{10,18},{1... | collective-permute-start | bytes 655880 | tf_op jit(solution)/shard_map/ppermute | solution.py:902
  12.9 0.9 %shard_map.204 = (f32[16,128]{1,0:T(8,128)S(1)}, f32[16,128]{1,0:T(8,128)S(1)}) custom-call(f32[256,256]{1,0:T(8,128)S(1)} %copy-done.2, f32[2,256,256]{2,1,0:T(8,128)S(1)} %copy-done, f32[256,256]{1,0:T(8,128)S(1)} %copy-done.3), custom_call_target="tpu_custom_call" | custom-call | tf_op jit(solution)/shard_map/pallas_call | solution.py:884
  13.9 0.0 copy-done.6
  13.9 0.0 copy-done.7
  13.9 0.0 copy-done.9
  13.9 0.0 copy-done.5
  13.9 0.0 copy-start.8
  13.9 0.0 copy-start.10
  14.0 0.0 copy-start.11
  14.0 0.0 copy-start.14
  14.0 0.0 copy-start.15
  14.0 0.0 copy-start.16
  14.0 0.0 copy-start.18
  14.0 0.0 copy-start.19
  14.0 0.0 copy-start.21
  14.0 0.0 copy-start.22
  14.1 1.6 %shard_map.203.refs_0_ = f32[728,256]{1,0:T(8,128)S(1)} custom-call(f32[728,256]{1,0:T(8,128)S(1)} %bitcast.10, f32[3,3,256]{2,1,0:T(4,128)S(1)} %copy-done.9, f32[3,13,13]{2,1,0:T(8,128)S(1)} %copy-done.6, f32[3,56,56]{2,1,0:T(8,128)S(1)} %copy-done.7, f32[728,256]{1,0:T(8,128)S(1)} %copy-done.5), custom_call_target="tpu_custom_call" | custom-call | tf_op jit(solution)/shard_map/pallas_call | solution.py:884
  15.7 0.0 collective-permute-done.refs_0_.refs_7_.refs_3_
  15.7 1.0 %collective-permute-done.1.refs_1_.refs_8_.refs_4_ = f32[427,128]{1,0:T(8,128)S(1)} collective-permute-done((f32[427,128]{1,0:T(8,128)}, f32[427,128]{1,0:T(8,128)S(1)}, u32[]{:S(2)}, u32[]{:S(2)}) %collective-permute-start.1) | collective-permute-done | bytes 218656 | tf_op jit(solution)/shard_map/ppermute | solution.py:902
  16.8 1.7 %collective-permute-start.2 = (f32[443,128]{1,0:T(8,128)S(1)}, f32[443,128]{1,0:T(8,128)S(1)}, u32[]{:S(2)}, u32[]{:S(2)}) collective-permute-start(f32[443,128]{1,0:T(8,128)S(1)} %get-tuple-element.80), channel_id=1, source_target_pairs={{0,1},{1,0},{2,3},{3,2},{4,5},{5,4},{6,7},{7,6},{8,9},{9,8},{10,11... | collective-permute-start | bytes 680456 | tf_op jit(solution)/shard_map/ppermute | solution.py:902
  18.5 0.8 %collective-permute-start.3 = (f32[443,128]{1,0:T(8,128)S(1)}, f32[443,128]{1,0:T(8,128)S(1)}, u32[]{:S(2)}, u32[]{:S(2)}) collective-permute-start(f32[443,128]{1,0:T(8,128)S(1)} %get-tuple-element.81), channel_id=1, source_target_pairs={{1,2},{2,1},{3,4},{4,3},{5,6},{6,5},{0,0},{7,7},{9,10},{10,9},{11,... | collective-permute-start | bytes 680456 | tf_op jit(solution)/shard_map/ppermute | solution.py:902
  19.4 0.0 copy-done.8
  19.4 0.0 copy-done.10
  19.4 0.0 copy-done.11
  19.4 0.0 copy-done.14
  19.4 0.0 copy-done.15
  19.4 0.0 copy-done.16
  19.4 0.0 copy-done.18
  19.4 0.0 copy-done.19
  19.4 0.0 copy-done.21
  19.4 0.0 copy-done.22
  19.4 1.7 %shard_map.206 = (bf16[224,168]{1,0:T(8,128)(2,1)S(1)}, bf16[624,208]{1,0:T(8,128)(2,1)S(1)}, bf16[112,168]{1,0:T(8,128)(2,1)S(1)}, bf16[56,168]{1,0:T(8,128)(2,...) custom-call(f32[3,13,13]{2,1,0:T(8,128)S(1)} %copy-done.6, ...), custom_call_target="tpu_custom_call" | custom-call | tf_op jit(solution)/shard_map/pallas_call | solution.py:884
  21.2 2.7 %shard_map.207.refs_1_ = f32[13,96,256]{2,1,0:T(8,128)S(1)} custom-call(f32[312,1024]{1,0:T(8,128)S(1)} %copy-done.4, s32[4,256]{1,0:T(4,128)S(1)} %copy-done.15, f32[3,4,256]{2,1,0:T(4,128)S(1)} %bitcast.14, f32[1,256]{1,0:T(1,128)S(1)} %bitcast.18, bf16[624,208]{1,0:T(8,128)(2,1)S(1)} %get-tuple-element.83.star_ref.refs_2_), custom_call_target="tpu_custom_call" | custom-call | tf_op jit(solution)/shard_map/pallas_call | solution.py:884
  23.9 2.5 %collective-permute-done.2.refs_9_.refs_5_ = f32[443,128]{1,0:T(8,128)S(1)} collective-permute-done((f32[443,128]{1,0:T(8,128)S(1)}, f32[443,128]{1,0:T(8,128)S(1)}, u32[]{:S(2)}, u32[]{:S(2)}) %collective-permute-start.2) | collective-permute-done | bytes 226848 | tf_op jit(solution)/shard_map/ppermute | solution.py:902
  26.4 0.0 collective-permute-done.3.refs_10_.refs_6_
  26.4 2.0 %shard_map.208.refs_0_.q_ref = f32[728,256]{1,0:T(8,128)S(1)} custom-call(f32[728,256]{1,0:T(8,128)S(1)} %shard_map.203.refs_0_, f32[13,96,256]{2,1,0:T(8,128)S(1)} %shard_map.207.refs_1_, bf16[624,208]{1,0:T(8,128)(2,1)S(1)} %get-tuple-element.83.star_ref.refs_2_, bf16[112,96]{1,0:T(8,128)(2,1)S(1)} %get-tuple-element.95.refs_3_, ...), custom_call_target="tpu_custom_call" | custom-call | tf_op jit(solution)/shard_map/pallas_call | solution.py:884
  28.5 4.4 %shard_map.209 = (f32[728,256]{1,0:T(8,128)S(1)}, f32[312,1024]{1,0:T(8,128)S(1)}, f32[411,128]{1,0:T(8,128)S(1)}, f32[411,128]{1,0:T(8,128)S(1)}, f32[137,128]{1,0:T(8,128)S(1)}, /*index=5*/f32[137,128]{1,0:T(8,128)S(1)}) custom-call(f32[728,256]{1,0:T(8,128)S(1)} %shard_map.208.refs_0_.q_ref, f32[3,3,256]{2,1,0:T(4,128)S(1)} %copy-done.9, ...), custom_call_target="tpu_custom_call" | custom-call | tf_op jit(solution)/shard_map/pallas_call | solution.py:884
  32.9 0.1 collective-permute-start.4
  32.9 3.4 %collective-permute-start.5 = (f32[411,128]{1,0:T(8,128)S(1)}, f32[411,128]{1,0:T(8,128)S(1)}, u32[]{:S(2)}, u32[]{:S(2)}) collective-permute-start(f32[411,128]{1,0:T(8,128)S(1)} %get-tuple-element.106), channel_id=1, source_target_pairs={{8,16},{16,8},{0,0},{24,24},{9,17},{17,9},{1,1},{25,25},{10,18},{1... | collective-permute-start | bytes 631304 | tf_op jit(solution)/shard_map/ppermute | solution.py:902
  36.4 0.4 shard_map.211
  36.8 1.7 %shard_map.210.refs_0_ = f32[728,256]{1,0:T(8,128)S(1)} custom-call(f32[728,256]{1,0:T(8,128)S(1)} %shard_map.208.refs_0_.q_ref, f32[3,3,256]{2,1,0:T(4,128)S(1)} %copy-done.9, f32[3,13,13]{2,1,0:T(8,128)S(1)} %copy-done.6, f32[3,56,56]{2,1,0:T(8,128)S(1)} %copy-done.7, f32[728,256]{1,0:T(8,128)S(1)} %get-tuple-element.107.integral_ref), custom_call_target="tpu_custom_call" | custom-call | tf_op jit(solution)/shard_map/pallas_call | solution.py:884
  38.5 0.0 collective-permute-done.4.refs_0_.refs_7_
  38.5 1.9 %collective-permute-done.5.refs_1_.refs_8_ = f32[411,128]{1,0:T(8,128)S(1)} collective-permute-done((f32[411,128]{1,0:T(8,128)S(1)}, f32[411,128]{1,0:T(8,128)S(1)}, u32[]{:S(2)}, u32[]{:S(2)}) %collective-permute-start.5) | collective-permute-done | bytes 210464 | tf_op jit(solution)/shard_map/ppermute | solution.py:902
  40.4 2.0 %collective-permute-start.6 = (f32[411,128]{1,0:T(8,128)S(1)}, f32[411,128]{1,0:T(8,128)S(1)}, u32[]{:S(2)}, u32[]{:S(2)}) collective-permute-start(f32[411,128]{1,0:T(8,128)S(1)} %get-tuple-element.116), channel_id=1, source_target_pairs={{0,1},{1,0},{2,3},{3,2},{4,5},{5,4},{6,7},{7,6},{8,9},{9,8},{10,11... | collective-permute-start | bytes 631304 | tf_op jit(solution)/shard_map/ppermute | solution.py:902
  42.4 0.9 %collective-permute-start.7 = (f32[411,128]{1,0:T(8,128)S(1)}, f32[411,128]{1,0:T(8,128)S(1)}, u32[]{:S(2)}, u32[]{:S(2)}) collective-permute-start(f32[411,128]{1,0:T(8,128)S(1)} %get-tuple-element.117), channel_id=1, source_target_pairs={{1,2},{2,1},{3,4},{4,3},{5,6},{6,5},{0,0},{7,7},{9,10},{10,9},{11,... | collective-permute-start | bytes 631304 | tf_op jit(solution)/shard_map/ppermute | solution.py:902
  43.3 2.7 %shard_map.213.refs_1_ = f32[13,96,256]{2,1,0:T(8,128)S(1)} custom-call(f32[312,1024]{1,0:T(8,128)S(1)} %get-tuple-element.118.table_ref, s32[4,256]{1,0:T(4,128)S(1)} %copy-done.15, f32[3,4,256]{2,1,0:T(4,128)S(1)} %bitcast.15, f32[1,256]{1,0:T(1,128)S(1)} %bitcast.19, bf16[624,208]{1,0:T(8,128)(2,1)S(1)} %get-tuple-element.83.star_ref.refs_2_), custom_call_target="tpu_custom_call" | custom-call | tf_op jit(solution)/shard_map/pallas_call | solution.py:884
  46.1 0.0 copy-start.20
  46.1 2.0 %shard_map.214.first.refs_1_ = f32[3,288,384]{2,1,0:T(8,128)S(1)} custom-call(f32[4,288,384]{2,1,0:T(8,128)S(1)} %get-tuple-element.119.refs_0_.wide, f32[5,288,384]{2,1,0:T(8,128)S(1)} %get-tuple-element.120.refs_1_), custom_call_target="tpu_custom_call" | custom-call | tf_op jit(solution)/shard_map/pallas_call | solution.py:884
  48.1 0.9 %collective-permute-done.6.refs_9_ = f32[411,128]{1,0:T(8,128)S(1)} collective-permute-done((f32[411,128]{1,0:T(8,128)S(1)}, f32[411,128]{1,0:T(8,128)S(1)}, u32[]{:S(2)}, u32[]{:S(2)}) %collective-permute-start.6) | collective-permute-done | bytes 210464 | tf_op jit(solution)/shard_map/ppermute | solution.py:902
  49.0 0.0 collective-permute-done.7.refs_10_
  49.0 0.0 copy-done.20
  49.0 2.9 %shard_map.215 = (f32[728,256]{1,0:T(8,128)}, f32[8,32,128]{2,1,0:T(8,128)S(1)}) custom-call(f32[728,256]{1,0:T(8,128)S(1)} %shard_map.210.refs_0_, f32[13,96,256]{2,1,0:T(8,128)S(1)} %shard_map.213.refs_1_, bf16[624,208]{1,0:T(8,128)(2,1)S(1)} %get-tuple-element.83.star_ref.refs_2_, bf16[112,96]{1,0:T(8,128)(2,1)S(1)} %get-tuple-element.95.refs_3_, ...), custom_call_target="tpu_custom_call" | custom-call | tf_op jit(solution)/shard_map/pallas_call | solution.py:884
  51.9 11.8 %all_to_all.5.refs_0_ = f32[8,32,128]{2,1,0:T(8,128)S(1)} all-to-all(f32[8,32,128]{2,1,0:T(8,128)S(1)} %get-tuple-element.129), channel_id=1, replica_groups=mesh['gx'=4,'gy'=8] {'gy'}, dimensions={0} | all-to-all | bytes 262144 | tf_op jit(solution)/shard_map/all_to_all | solution.py:1030
  63.6 1.4 %shard_map.216 = (f32[256,384]{1,0:T(8,128)S(1)}, f32[8,384]{1,0:T(8,128)S(1)}, f32[8,384]{1,0:T(8,128)S(1)}) custom-call(f32[8,32,128]{2,1,0:T(8,128)S(1)} %all_to_all.5.refs_0_), custom_call_target="tpu_custom_call" | custom-call | tf_op jit(solution)/shard_map/pallas_call | solution.py:884
  65.1 0.1 collective-permute-start.8
  65.2 3.7 %collective-permute-start.9 = (f32[8,384]{1,0:T(8,128)S(1)}, f32[8,384]{1,0:T(8,128)S(1)}, u32[]{:S(2)}, u32[]{:S(2)}) collective-permute-start(f32[8,384]{1,0:T(8,128)S(1)} %get-tuple-element.132), channel_id=1, source_target_pairs={{8,16},{16,8},{24,0},{0,24},{9,17},{17,9},{25,1},{1,25},{10,18},{1... | collective-permute-start | bytes 36872 | tf_op jit(solution)/shard_map/ppermute | solution.py:902
  68.9 2.3 %shard_map.217 = (f32[3,256,256]{2,1,0:T(8,128)S(1)}, f32[256,256]{1,0:T(8,128)S(1)}) custom-call(f32[4,288,384]{2,1,0:T(8,128)S(1)} %get-tuple-element.119.refs_0_.wide, f32[3,288,384]{2,1,0:T(8,128)S(1)} %shard_map.214.first.refs_1_, f32[256,384]{1,0:T(8,128)S(1)} %get-tuple-element.130.forcing_ref.refs_2_), custom_call_target="tpu_custom_call" | custom-call | tf_op jit(solution)/shard_map/pallas_call | solution.py:884
  71.2 0.0 collective-permute-done.8.refs_3_
  71.2 0.0 collective-permute-done.9.refs_4_
  71.2 1.0 %shard_map.218 = (f32[3,256,256]{2,1,0:T(8,128)}, f32[256,256]{1,0:T(8,128)}) custom-call(f32[4,288,384]{2,1,0:T(8,128)S(1)} %get-tuple-element.119.refs_0_.wide, f32[3,288,384]{2,1,0:T(8,128)S(1)} %shard_map.214.first.refs_1_, f32[256,384]{1,0:T(8,128)S(1)} %get-tuple-element.130.forcing_ref.refs_2_, f32[8,384]{1,0:T(8,128)S(1)} %collective-permute-done.8.refs_3_, ...), custom_call_target="tpu_custom_call" | custom-call | tf_op jit(solution)/shard_map/pallas_call | solution.py:884
  (20 shorter events, 0.1 us)
Async XLA Ops:
  0.6 12.3 %copy-start.2 = (f32[256,256]{1,0:T(8,128)S(1)}, f32[256,256]{1,0:T(8,128)}, u32[]{:S(2)}) copy-start(f32[256,256]{1,0:T(8,128)} %refs_0_.5) | copy-start | bytes 786436
  0.6 12.3 %copy-start = (f32[2,256,256]{2,1,0:T(8,128)S(1)}, f32[2,256,256]{2,1,0:T(8,128)}, u32[]{:S(2)}) copy-start(f32[2,256,256]{2,1,0:T(8,128)} %refs_1_.9) | copy-start | bytes 1572868
  0.7 12.3 %copy-start.3 = (f32[256,256]{1,0:T(8,128)S(1)}, f32[256,256]{1,0:T(8,128)}, u32[]{:S(2)}) copy-start(f32[256,256]{1,0:T(8,128)} %refs_2_.7) | copy-start | bytes 786436
  0.7 13.2 %copy-start.1 = (f32[13,56,256]{2,1,0:T(8,128)S(1)}, f32[13,56,256]{2,1,0:T(8,128)}, u32[]{:S(2)}) copy-start(f32[13,56,256]{2,1,0:T(8,128)} %param.19) | copy-start | bytes 2236420
  0.7 13.2 %copy-start.6 = (f32[3,13,13]{2,1,0:T(8,128)S(1)}, f32[3,13,13]{2,1,0:T(8,128)}, u32[]{:S(2)}) copy-start(f32[3,13,13]{2,1,0:T(8,128)} %star_ref.3) | copy-start | bytes 6088
  0.7 13.2 %copy-start.7 = (f32[3,56,56]{2,1,0:T(8,128)S(1)}, f32[3,56,56]{2,1,0:T(8,128)}, u32[]{:S(2)}) copy-start(f32[3,56,56]{2,1,0:T(8,128)} %stiff_ref.3) | copy-start | bytes 112900
  0.7 13.2 %copy-start.9 = (f32[3,3,256]{2,1,0:T(4,128)S(1)}, f32[3,3,256]{2,1,0:T(4,128)}, u32[]{:S(2)}) copy-start(f32[3,3,256]{2,1,0:T(4,128)} %jac_ref.3) | copy-start | bytes 27652
  8.1 5.8 %copy-start.5 = (f32[728,256]{1,0:T(8,128)S(1)}, f32[728,256]{1,0:T(8,128)}, u32[]{:S(2)}) copy-start(f32[728,256]{1,0:T(8,128)} %get-tuple-element.72.integral_ref) | copy-start | bytes 2236420
  8.2 7.6 %collective-permute-start = (f32[427,128]{1,0:T(8,128)}, f32[427,128]{1,0:T(8,128)S(1)}, u32[]{:S(2)}, u32[]{:S(2)}) collective-permute-start(f32[427,128]{1,0:T(8,128)} %get-tuple-element.70), channel_id=1, source_target_pairs={{0,8},{8,0},{16,24},{24,16},{1,9},{9,1},{17,25},{25,17},{2,10},{10... | collective-permute-start | bytes 655880 | tf_op jit(solution)/shard_map/ppermute | solution.py:902
  8.3 8.4 %collective-permute-start.1 = (f32[427,128]{1,0:T(8,128)}, f32[427,128]{1,0:T(8,128)S(1)}, u32[]{:S(2)}, u32[]{:S(2)}) collective-permute-start(f32[427,128]{1,0:T(8,128)} %get-tuple-element.71), channel_id=1, source_target_pairs={{8,16},{16,8},{0,0},{24,24},{9,17},{17,9},{1,1},{25,25},{10,18},{1... | collective-permute-start | bytes 655880 | tf_op jit(solution)/shard_map/ppermute | solution.py:902
  13.9 2.8 %copy-start.12 = (f32[137,128]{1,0:T(8,128)S(1)}, f32[137,128]{1,0:T(8,128)}, u32[]{:S(2)}) copy-start(f32[137,128]{1,0:T(8,128)} %get-tuple-element.76.refs_2_) | copy-start | bytes 210436
  13.9 2.8 %copy-start.13 = (f32[137,128]{1,0:T(8,128)S(1)}, f32[137,128]{1,0:T(8,128)}, u32[]{:S(2)}) copy-start(f32[137,128]{1,0:T(8,128)} %get-tuple-element.77.refs_3_) | copy-start | bytes 210436
  13.9 5.4 %copy-start.8 = (f32[3,56,56]{2,1,0:T(8,128)S(1)}, f32[3,56,56]{2,1,0:T(8,128)}, u32[]{:S(2)}) copy-start(f32[3,56,56]{2,1,0:T(8,128)} %refs_2_.6) | copy-start | bytes 112900
  13.9 5.4 %copy-start.10 = (f32[4,21,56]{2,0,1:T(4,128)S(1)}, f32[4,21,56]{2,0,1:T(4,128)}, u32[]{:S(2)}) copy-start(f32[4,21,56]{2,0,1:T(4,128)} %param.27) | copy-start | bytes 56452
  14.0 5.4 %copy-start.11 = (f32[4,3,256]{2,0,1:T(4,128)S(1)}, f32[4,3,256]{2,0,1:T(4,128)}, u32[]{:S(2)}) copy-start(f32[4,3,256]{2,0,1:T(4,128)} %param.21) | copy-start | bytes 36868
  14.0 5.4 %copy-start.14 = (f32[4,56,21]{1,0,2:T(4,128)S(1)}, f32[4,56,21]{1,0,2:T(4,128)}, u32[]{:S(2)}) copy-start(f32[4,56,21]{1,0,2:T(4,128)} %param.28) | copy-start | bytes 56452
  14.0 5.4 %copy-start.15 = (s32[4,256]{1,0:T(4,128)S(1)}, s32[4,256]{1,0:T(4,128)}, u32[]{:S(2)}) copy-start(s32[4,256]{1,0:T(4,128)} %partner_ref.3) | copy-start | bytes 12292
  14.0 5.4 %copy-start.16 = (f32[13,13]{1,0:T(8,128)S(1)}, f32[13,13]{1,0:T(8,128)}, u32[]{:S(2)}) copy-start(f32[13,13]{1,0:T(8,128)} %refs_1_.7) | copy-start | bytes 2032
  14.0 5.4 %copy-start.18 = (f32[256]{0:T(256)S(1)}, f32[256]{0:T(256)}, u32[]{:S(2)}) copy-start(f32[256]{0:T(256)} %param.22) | copy-start | bytes 3076
  14.0 5.4 %copy-start.19 = (f32[16,21]{1,0:T(8,128)S(1)}, f32[16,21]{1,0:T(8,128)}, u32[]{:S(2)}) copy-start(f32[16,21]{1,0:T(8,128)} %refs_10_.1) | copy-start | bytes 4036
  14.0 5.4 %copy-start.21 = (s32[256]{0:T(256)S(1)}, s32[256]{0:T(256)}, u32[]{:S(2)}) copy-start(s32[256]{0:T(256)} %param.31) | copy-start | bytes 3076
  14.0 5.4 %copy-start.22 = (s32[256,1]{0,1:T(1,128)S(1)}, s32[256,1]{0,1:T(1,128)}, u32[]{:S(2)}) copy-start(s32[256,1]{0,1:T(1,128)} %param.32) | copy-start | bytes 3076
  14.1 7.1 %copy-start.4 = (f32[312,1024]{1,0:T(8,128)S(1)}, f32[312,1024]{1,0:T(8,128)}, u32[]{:S(2)}) copy-start(f32[312,1024]{1,0:T(8,128)} %get-tuple-element.82.table_ref) | copy-start | bytes 3833860
  16.8 9.6 %collective-permute-start.2 = (f32[443,128]{1,0:T(8,128)S(1)}, f32[443,128]{1,0:T(8,128)S(1)}, u32[]{:S(2)}, u32[]{:S(2)}) collective-permute-start(f32[443,128]{1,0:T(8,128)S(1)} %get-tuple-element.80), channel_id=1, source_target_pairs={{0,1},{1,0},{2,3},{3,2},{4,5},{5,4},{6,7},{7,6},{8,9},{9,8},{10,11... | collective-permute-start | bytes 680456 | tf_op jit(solution)/shard_map/ppermute | solution.py:902
  18.5 7.9 %collective-permute-start.3 = (f32[443,128]{1,0:T(8,128)S(1)}, f32[443,128]{1,0:T(8,128)S(1)}, u32[]{:S(2)}, u32[]{:S(2)}) collective-permute-start(f32[443,128]{1,0:T(8,128)S(1)} %get-tuple-element.81), channel_id=1, source_target_pairs={{1,2},{2,1},{3,4},{4,3},{5,6},{6,5},{0,0},{7,7},{9,10},{10,9},{11,... | collective-permute-start | bytes 680456 | tf_op jit(solution)/shard_map/ppermute | solution.py:902
  26.4 2.0 %copy-start.17 = (s32[8,64]{1,0:T(8,128)S(1)}, s32[8,64]{1,0:T(8,128)}, u32[]{:S(2)}) copy-start(s32[8,64]{1,0:T(8,128)} %refs_6_.3) | copy-start | bytes 6148
  32.9 5.6 %collective-permute-start.4 = (f32[411,128]{1,0:T(8,128)S(1)}, f32[411,128]{1,0:T(8,128)S(1)}, u32[]{:S(2)}, u32[]{:S(2)}) collective-permute-start(f32[411,128]{1,0:T(8,128)S(1)} %get-tuple-element.105), channel_id=1, source_target_pairs={{0,8},{8,0},{16,24},{24,16},{1,9},{9,1},{17,25},{25,17},{2,10},{10... | collective-permute-start | bytes 631304 | tf_op jit(solution)/shard_map/ppermute | solution.py:902
  32.9 7.5 %collective-permute-start.5 = (f32[411,128]{1,0:T(8,128)S(1)}, f32[411,128]{1,0:T(8,128)S(1)}, u32[]{:S(2)}, u32[]{:S(2)}) collective-permute-start(f32[411,128]{1,0:T(8,128)S(1)} %get-tuple-element.106), channel_id=1, source_target_pairs={{8,16},{16,8},{0,0},{24,24},{9,17},{17,9},{1,1},{25,25},{10,18},{1... | collective-permute-start | bytes 631304 | tf_op jit(solution)/shard_map/ppermute | solution.py:902
  40.4 8.5 %collective-permute-start.6 = (f32[411,128]{1,0:T(8,128)S(1)}, f32[411,128]{1,0:T(8,128)S(1)}, u32[]{:S(2)}, u32[]{:S(2)}) collective-permute-start(f32[411,128]{1,0:T(8,128)S(1)} %get-tuple-element.116), channel_id=1, source_target_pairs={{0,1},{1,0},{2,3},{3,2},{4,5},{5,4},{6,7},{7,6},{8,9},{9,8},{10,11... | collective-permute-start | bytes 631304 | tf_op jit(solution)/shard_map/ppermute | solution.py:902
  42.4 6.5 %collective-permute-start.7 = (f32[411,128]{1,0:T(8,128)S(1)}, f32[411,128]{1,0:T(8,128)S(1)}, u32[]{:S(2)}, u32[]{:S(2)}) collective-permute-start(f32[411,128]{1,0:T(8,128)S(1)} %get-tuple-element.117), channel_id=1, source_target_pairs={{1,2},{2,1},{3,4},{4,3},{5,6},{6,5},{0,0},{7,7},{9,10},{10,9},{11,... | collective-permute-start | bytes 631304 | tf_op jit(solution)/shard_map/ppermute | solution.py:902
  46.1 2.9 %copy-start.20 = (s32[256,2]{0,1:T(2,128)S(1)}, s32[256,2]{0,1:T(2,128)}, u32[]{:S(2)}) copy-start(s32[256,2]{0,1:T(2,128)} %param.33) | copy-start | bytes 6148
  65.1 6.1 %collective-permute-start.8 = (f32[8,384]{1,0:T(8,128)S(1)}, f32[8,384]{1,0:T(8,128)S(1)}, u32[]{:S(2)}, u32[]{:S(2)}) collective-permute-start(f32[8,384]{1,0:T(8,128)S(1)} %get-tuple-element.131), channel_id=1, source_target_pairs={{0,8},{8,0},{16,24},{24,16},{1,9},{9,1},{17,25},{25,17},{2,10},{10... | collective-permute-start | bytes 36872 | tf_op jit(solution)/shard_map/ppermute | solution.py:902
  65.2 6.0 %collective-permute-start.9 = (f32[8,384]{1,0:T(8,128)S(1)}, f32[8,384]{1,0:T(8,128)S(1)}, u32[]{:S(2)}, u32[]{:S(2)}) collective-permute-start(f32[8,384]{1,0:T(8,128)S(1)} %get-tuple-element.132), channel_id=1, source_target_pairs={{8,16},{16,8},{24,0},{0,24},{9,17},{17,9},{25,1},{1,25},{10,18},{1... | collective-permute-start | bytes 36872 | tf_op jit(solution)/shard_map/ppermute | solution.py:902

commit v7 on v6

--- a/solution.py
+++ b/solution.py
@@ -13,7 +13,6 @@
 STEPS_OCEAN = 2
 CAP = 64
 TABLE = FIELDS * FACE_PAD
-WIDE = 320
 HALF = (FIELDS * FACE_BASIS + 1) // 2
 OCEAN_ROWS = 16
 MARGIN = 16
@@ -316,10 +315,7 @@
 
 
 def table_parts(table_ref):
-    pad = jnp.zeros((WIDE - TABLE, table_ref.shape[1]), BF16)
-    high, low = parts(table_ref[...])
-    both = [high.astype(F32), pad.astype(F32), low.astype(F32), pad.astype(F32)]
-    return jnp.concatenate(both, axis=0).astype(BF16)
+    return both_parts(table_ref[...])
 
 
 def volume(q_ref, jac_ref, star_ref, stiff_ref, integral_ref, base_ref, spread_ref):

time: 73.1 us -> 73.1 us (level)
  no operation moved by 1% of the time
where the time goes in v7:
time: 73.1 us; the launch traced here: 72.5 us
  Pallas kernels  35.4 us (48%)
  starting transfers between devices  17.5 us (24%)
  blocking collectives  11.7 us (16%)
  waiting for transfers between devices  6.41 us (9%)
  between operations  1.32 us (2%)
    pallas_call x17, Pallas kernels, call(): pl.pallas_call(body, out_shape=shapes, in_specs=specs, out_specs=[pl.Bloc...  35.4 us
    ppermute x10, starting transfers between devices, swap(): return lax.ppermute(block, axis, pairs)  17.5 us
    all_to_all x1, blocking collectives, per_device(): lax.all_to_all(outgoing, 'gy', split_axis=0, concat_axis=0, tiled=True)  11.7 us
    ppermute x10, waiting for transfers between devices, swap(): return lax.ppermute(block, axis, pairs)  6.41 us
  transfers between devices with their start and end apart: 10, of which 4 were waited for; matrix products, arithmetic and copies ran while one was open for 0% of the time, Pallas kernels for 22%

profile of v7, /device:TPU:1, one launch (start us, length us, event | category | flops | bytes accessed | tf_op | source)
XLA Modules:
  0.0 72.5 jit_solution(12315030479007684602)
XLA Ops:
  0.6 0.0 copy-start.2
  0.6 0.0 copy-start
  0.7 0.0 copy-start.3
  0.7 0.0 copy-start.1
  0.7 7.4 %shard_map.202 = (f32[728,256]{1,0:T(8,128)}, f32[312,1024]{1,0:T(8,128)}, f32[427,128]{1,0:T(8,128)}, f32[427,128]{1,0:T(8,128)}, f32[137,128]{1,0:T(8,128)}, /*index=5*/f32[137,128]{1,0:T(8,128)}) custom-call(f32[728,256]{1,0:T(8,128)} %bitcast.9, f32[3,3,256]{2,1,0:T(4,128)} %jac_ref.3, f32[3,13,13]{2,1,0:T(8,128)} %star_ref.3, f32[13,13]{1,0:T(8,128)} %refs_1_.7, ...), custom_call_target="tpu_custom_call" | custom-call | tf_op jit(solution)/shard_map/pallas_call | solution.py:880
  8.1 0.0 copy-start.5
  8.1 0.1 collective-permute-start
  8.3 4.6 %collective-permute-start.1 = (f32[427,128]{1,0:T(8,128)}, f32[427,128]{1,0:T(8,128)S(1)}, u32[]{:S(2)}, u32[]{:S(2)}) collective-permute-start(f32[427,128]{1,0:T(8,128)} %get-tuple-element.71), channel_id=1, source_target_pairs={{8,16},{16,8},{0,0},{24,24},{9,17},{17,9},{1,1},{25,25},{10,18},{1... | collective-permute-start | bytes 655880 | tf_op jit(solution)/shard_map/ppermute | solution.py:898
  12.9 0.9 %shard_map.204 = (f32[16,128]{1,0:T(8,128)S(1)}, f32[16,128]{1,0:T(8,128)S(1)}) custom-call(f32[256,256]{1,0:T(8,128)S(1)} %copy-done.2, f32[2,256,256]{2,1,0:T(8,128)S(1)} %copy-done, f32[256,256]{1,0:T(8,128)S(1)} %copy-done.3), custom_call_target="tpu_custom_call" | custom-call | tf_op jit(solution)/shard_map/pallas_call | solution.py:880
  13.9 0.0 copy-done.6
  13.9 0.0 copy-start.8
  13.9 0.0 copy-start.10
  14.0 0.0 copy-start.11
  14.0 0.0 copy-start.14
  14.0 0.0 copy-start.15
  14.0 0.0 copy-start.16
  14.0 0.0 copy-start.18
  14.0 0.0 copy-start.19
  14.0 0.0 copy-start.21
  14.0 0.0 copy-start.22
  14.1 1.7 %shard_map.203.refs_0_ = f32[728,256]{1,0:T(8,128)S(1)} custom-call(f32[728,256]{1,0:T(8,128)S(1)} %bitcast.10, f32[3,3,256]{2,1,0:T(4,128)S(1)} %copy-done.9, f32[3,13,13]{2,1,0:T(8,128)S(1)} %copy-done.6, f32[3,56,56]{2,1,0:T(8,128)S(1)} %copy-done.7, f32[728,256]{1,0:T(8,128)S(1)} %copy-done.5), custom_call_target="tpu_custom_call" | custom-call | tf_op jit(solution)/shard_map/pallas_call | solution.py:880
  15.7 0.0 collective-permute-done.refs_0_.refs_7_.refs_3_
  15.7 1.0 %collective-permute-done.1.refs_1_.refs_8_.refs_4_ = f32[427,128]{1,0:T(8,128)S(1)} collective-permute-done((f32[427,128]{1,0:T(8,128)}, f32[427,128]{1,0:T(8,128)S(1)}, u32[]{:S(2)}, u32[]{:S(2)}) %collective-permute-start.1) | collective-permute-done | bytes 218656 | tf_op jit(solution)/shard_map/ppermute | solution.py:898
  16.7 0.0 copy-done.13
  16.8 1.7 %collective-permute-start.2 = (f32[443,128]{1,0:T(8,128)S(1)}, f32[443,128]{1,0:T(8,128)S(1)}, u32[]{:S(2)}, u32[]{:S(2)}) collective-permute-start(f32[443,128]{1,0:T(8,128)S(1)} %get-tuple-element.80), channel_id=1, source_target_pairs={{0,1},{1,0},{2,3},{3,2},{4,5},{5,4},{6,7},{7,6},{8,9},{9,8},{10,11... | collective-permute-start | bytes 680456 | tf_op jit(solution)/shard_map/ppermute | solution.py:898
  18.5 0.8 %collective-permute-start.3 = (f32[443,128]{1,0:T(8,128)S(1)}, f32[443,128]{1,0:T(8,128)S(1)}, u32[]{:S(2)}, u32[]{:S(2)}) collective-permute-start(f32[443,128]{1,0:T(8,128)S(1)} %get-tuple-element.81), channel_id=1, source_target_pairs={{1,2},{2,1},{3,4},{4,3},{5,6},{6,5},{0,0},{7,7},{9,10},{10,9},{11,... | collective-permute-start | bytes 680456 | tf_op jit(solution)/shard_map/ppermute | solution.py:898
  19.3 0.0 copy-done.8
  19.4 0.0 copy-done.10
  19.4 0.0 copy-done.11
  19.4 0.0 copy-done.14
  19.4 0.0 copy-done.15
  19.4 0.0 copy-done.16
  19.4 0.0 copy-done.18
  19.4 0.0 copy-done.19
  19.4 0.0 copy-done.21
  19.4 0.0 copy-done.22
  19.4 1.7 %shard_map.206 = (bf16[224,168]{1,0:T(8,128)(2,1)S(1)}, bf16[624,208]{1,0:T(8,128)(2,1)S(1)}, bf16[112,168]{1,0:T(8,128)(2,1)S(1)}, bf16[56,168]{1,0:T(8,128)(2,...) custom-call(f32[3,13,13]{2,1,0:T(8,128)S(1)} %copy-done.6, ...), custom_call_target="tpu_custom_call" | custom-call | tf_op jit(solution)/shard_map/pallas_call | solution.py:880
  21.1 2.7 %shard_map.207.refs_1_ = f32[13,96,256]{2,1,0:T(8,128)S(1)} custom-call(f32[312,1024]{1,0:T(8,128)S(1)} %copy-done.4, s32[4,256]{1,0:T(4,128)S(1)} %copy-done.15, f32[3,4,256]{2,1,0:T(4,128)S(1)} %bitcast.14, f32[1,256]{1,0:T(1,128)S(1)} %bitcast.18, bf16[624,208]{1,0:T(8,128)(2,1)S(1)} %get-tuple-element.83.star_ref.refs_2_), custom_call_target="tpu_custom_call" | custom-call | tf_op jit(solution)/shard_map/pallas_call | solution.py:880
  23.8 2.6 %collective-permute-done.2.refs_9_.refs_5_ = f32[443,128]{1,0:T(8,128)S(1)} collective-permute-done((f32[443,128]{1,0:T(8,128)S(1)}, f32[443,128]{1,0:T(8,128)S(1)}, u32[]{:S(2)}, u32[]{:S(2)}) %collective-permute-start.2) | collective-permute-done | bytes 226848 | tf_op jit(solution)/shard_map/ppermute | solution.py:898
  26.4 0.0 collective-permute-done.3.refs_10_.refs_6_
  26.4 2.1 %shard_map.208.refs_0_.q_ref = f32[728,256]{1,0:T(8,128)S(1)} custom-call(f32[728,256]{1,0:T(8,128)S(1)} %shard_map.203.refs_0_, f32[13,96,256]{2,1,0:T(8,128)S(1)} %shard_map.207.refs_1_, bf16[624,208]{1,0:T(8,128)(2,1)S(1)} %get-tuple-element.83.star_ref.refs_2_, bf16[112,96]{1,0:T(8,128)(2,1)S(1)} %get-tuple-element.95.refs_3_, ...), custom_call_target="tpu_custom_call" | custom-call | tf_op jit(solution)/shard_map/pallas_call | solution.py:880
  28.5 4.4 %shard_map.209 = (f32[728,256]{1,0:T(8,128)S(1)}, f32[312,1024]{1,0:T(8,128)S(1)}, f32[411,128]{1,0:T(8,128)S(1)}, f32[411,128]{1,0:T(8,128)S(1)}, f32[137,128]{1,0:T(8,128)S(1)}, /*index=5*/f32[137,128]{1,0:T(8,128)S(1)}) custom-call(f32[728,256]{1,0:T(8,128)S(1)} %shard_map.208.refs_0_.q_ref, f32[3,3,256]{2,1,0:T(4,128)S(1)} %copy-done.9, ...), custom_call_target="tpu_custom_call" | custom-call | tf_op jit(solution)/shard_map/pallas_call | solution.py:880
  32.9 0.1 collective-permute-start.4
  33.0 3.4 %collective-permute-start.5 = (f32[411,128]{1,0:T(8,128)S(1)}, f32[411,128]{1,0:T(8,128)S(1)}, u32[]{:S(2)}, u32[]{:S(2)}) collective-permute-start(f32[411,128]{1,0:T(8,128)S(1)} %get-tuple-element.106), channel_id=1, source_target_pairs={{8,16},{16,8},{0,0},{24,24},{9,17},{17,9},{1,1},{25,25},{10,18},{1... | collective-permute-start | bytes 631304 | tf_op jit(solution)/shard_map/ppermute | solution.py:898
  36.4 0.4 shard_map.211
  36.8 1.7 %shard_map.210.refs_0_ = f32[728,256]{1,0:T(8,128)S(1)} custom-call(f32[728,256]{1,0:T(8,128)S(1)} %shard_map.208.refs_0_.q_ref, f32[3,3,256]{2,1,0:T(4,128)S(1)} %copy-done.9, f32[3,13,13]{2,1,0:T(8,128)S(1)} %copy-done.6, f32[3,56,56]{2,1,0:T(8,128)S(1)} %copy-done.7, f32[728,256]{1,0:T(8,128)S(1)} %get-tuple-element.107.integral_ref), custom_call_target="tpu_custom_call" | custom-call | tf_op jit(solution)/shard_map/pallas_call | solution.py:880
  38.5 0.0 collective-permute-done.4.refs_0_.refs_7_
  38.5 1.9 %collective-permute-done.5.refs_1_.refs_8_ = f32[411,128]{1,0:T(8,128)S(1)} collective-permute-done((f32[411,128]{1,0:T(8,128)S(1)}, f32[411,128]{1,0:T(8,128)S(1)}, u32[]{:S(2)}, u32[]{:S(2)}) %collective-permute-start.5) | collective-permute-done | bytes 210464 | tf_op jit(solution)/shard_map/ppermute | solution.py:898
  40.4 2.0 %collective-permute-start.6 = (f32[411,128]{1,0:T(8,128)S(1)}, f32[411,128]{1,0:T(8,128)S(1)}, u32[]{:S(2)}, u32[]{:S(2)}) collective-permute-start(f32[411,128]{1,0:T(8,128)S(1)} %get-tuple-element.116), channel_id=1, source_target_pairs={{0,1},{1,0},{2,3},{3,2},{4,5},{5,4},{6,7},{7,6},{8,9},{9,8},{10,11... | collective-permute-start | bytes 631304 | tf_op jit(solution)/shard_map/ppermute | solution.py:898
  42.5 0.9 %collective-permute-start.7 = (f32[411,128]{1,0:T(8,128)S(1)}, f32[411,128]{1,0:T(8,128)S(1)}, u32[]{:S(2)}, u32[]{:S(2)}) collective-permute-start(f32[411,128]{1,0:T(8,128)S(1)} %get-tuple-element.117), channel_id=1, source_target_pairs={{1,2},{2,1},{3,4},{4,3},{5,6},{6,5},{0,0},{7,7},{9,10},{10,9},{11,... | collective-permute-start | bytes 631304 | tf_op jit(solution)/shard_map/ppermute | solution.py:898
  43.4 2.7 %shard_map.213.refs_1_ = f32[13,96,256]{2,1,0:T(8,128)S(1)} custom-call(f32[312,1024]{1,0:T(8,128)S(1)} %get-tuple-element.118.table_ref, s32[4,256]{1,0:T(4,128)S(1)} %copy-done.15, f32[3,4,256]{2,1,0:T(4,128)S(1)} %bitcast.15, f32[1,256]{1,0:T(1,128)S(1)} %bitcast.19, bf16[624,208]{1,0:T(8,128)(2,1)S(1)} %get-tuple-element.83.star_ref.refs_2_), custom_call_target="tpu_custom_call" | custom-call | tf_op jit(solution)/shard_map/pallas_call | solution.py:880
  46.1 0.0 copy-start.20
  46.1 2.0 %shard_map.214.first.refs_1_ = f32[3,288,384]{2,1,0:T(8,128)S(1)} custom-call(f32[4,288,384]{2,1,0:T(8,128)S(1)} %get-tuple-element.119.refs_0_.wide, f32[5,288,384]{2,1,0:T(8,128)S(1)} %get-tuple-element.120.refs_1_), custom_call_target="tpu_custom_call" | custom-call | tf_op jit(solution)/shard_map/pallas_call | solution.py:880
  48.1 0.9 %collective-permute-done.6.refs_9_ = f32[411,128]{1,0:T(8,128)S(1)} collective-permute-done((f32[411,128]{1,0:T(8,128)S(1)}, f32[411,128]{1,0:T(8,128)S(1)}, u32[]{:S(2)}, u32[]{:S(2)}) %collective-permute-start.6) | collective-permute-done | bytes 210464 | tf_op jit(solution)/shard_map/ppermute | solution.py:898
  49.0 0.0 collective-permute-done.7.refs_10_
  49.0 2.9 %shard_map.215 = (f32[728,256]{1,0:T(8,128)}, f32[8,32,128]{2,1,0:T(8,128)S(1)}) custom-call(f32[728,256]{1,0:T(8,128)S(1)} %shard_map.210.refs_0_, f32[13,96,256]{2,1,0:T(8,128)S(1)} %shard_map.213.refs_1_, bf16[624,208]{1,0:T(8,128)(2,1)S(1)} %get-tuple-element.83.star_ref.refs_2_, bf16[112,96]{1,0:T(8,128)(2,1)S(1)} %get-tuple-element.95.refs_3_, ...), custom_call_target="tpu_custom_call" | custom-call | tf_op jit(solution)/shard_map/pallas_call | solution.py:880
  51.9 11.7 %all_to_all.5.refs_0_ = f32[8,32,128]{2,1,0:T(8,128)S(1)} all-to-all(f32[8,32,128]{2,1,0:T(8,128)S(1)} %get-tuple-element.129), channel_id=1, replica_groups=mesh['gx'=4,'gy'=8] {'gy'}, dimensions={0} | all-to-all | bytes 262144 | tf_op jit(solution)/shard_map/all_to_all | solution.py:1026
  63.7 1.4 %shard_map.216 = (f32[256,384]{1,0:T(8,128)S(1)}, f32[8,384]{1,0:T(8,128)S(1)}, f32[8,384]{1,0:T(8,128)S(1)}) custom-call(f32[8,32,128]{2,1,0:T(8,128)S(1)} %all_to_all.5.refs_0_), custom_call_target="tpu_custom_call" | custom-call | tf_op jit(solution)/shard_map/pallas_call | solution.py:880
  65.1 0.1 collective-permute-start.8
  65.2 3.8 %collective-permute-start.9 = (f32[8,384]{1,0:T(8,128)S(1)}, f32[8,384]{1,0:T(8,128)S(1)}, u32[]{:S(2)}, u32[]{:S(2)}) collective-permute-start(f32[8,384]{1,0:T(8,128)S(1)} %get-tuple-element.132), channel_id=1, source_target_pairs={{8,16},{16,8},{24,0},{0,24},{9,17},{17,9},{25,1},{1,25},{10,18},{1... | collective-permute-start | bytes 36872 | tf_op jit(solution)/shard_map/ppermute | solution.py:898
  68.9 2.3 %shard_map.217 = (f32[3,256,256]{2,1,0:T(8,128)S(1)}, f32[256,256]{1,0:T(8,128)S(1)}) custom-call(f32[4,288,384]{2,1,0:T(8,128)S(1)} %get-tuple-element.119.refs_0_.wide, f32[3,288,384]{2,1,0:T(8,128)S(1)} %shard_map.214.first.refs_1_, f32[256,384]{1,0:T(8,128)S(1)} %get-tuple-element.130.forcing_ref.refs_2_), custom_call_target="tpu_custom_call" | custom-call | tf_op jit(solution)/shard_map/pallas_call | solution.py:880
  71.2 0.0 collective-permute-done.8.refs_3_
  71.2 0.0 collective-permute-done.9.refs_4_
  71.3 1.0 %shard_map.218 = (f32[3,256,256]{2,1,0:T(8,128)}, f32[256,256]{1,0:T(8,128)}) custom-call(f32[4,288,384]{2,1,0:T(8,128)S(1)} %get-tuple-element.119.refs_0_.wide, f32[3,288,384]{2,1,0:T(8,128)S(1)} %shard_map.214.first.refs_1_, f32[256,384]{1,0:T(8,128)S(1)} %get-tuple-element.130.forcing_ref.refs_2_, f32[8,384]{1,0:T(8,128)S(1)} %collective-permute-done.8.refs_3_, ...), custom_call_target="tpu_custom_call" | custom-call | tf_op jit(solution)/shard_map/pallas_call | solution.py:880
  (20 shorter events, 0.1 us)
Async XLA Ops:
  0.6 12.3 %copy-start.2 = (f32[256,256]{1,0:T(8,128)S(1)}, f32[256,256]{1,0:T(8,128)}, u32[]{:S(2)}) copy-start(f32[256,256]{1,0:T(8,128)} %refs_0_.5) | copy-start | bytes 786436
  0.6 12.3 %copy-start = (f32[2,256,256]{2,1,0:T(8,128)S(1)}, f32[2,256,256]{2,1,0:T(8,128)}, u32[]{:S(2)}) copy-start(f32[2,256,256]{2,1,0:T(8,128)} %refs_1_.9) | copy-start | bytes 1572868
  0.7 12.3 %copy-start.3 = (f32[256,256]{1,0:T(8,128)S(1)}, f32[256,256]{1,0:T(8,128)}, u32[]{:S(2)}) copy-start(f32[256,256]{1,0:T(8,128)} %refs_2_.7) | copy-start | bytes 786436
  0.7 13.2 %copy-start.1 = (f32[13,56,256]{2,1,0:T(8,128)S(1)}, f32[13,56,256]{2,1,0:T(8,128)}, u32[]{:S(2)}) copy-start(f32[13,56,256]{2,1,0:T(8,128)} %param.19) | copy-start | bytes 2236420
  0.7 13.2 %copy-start.6 = (f32[3,13,13]{2,1,0:T(8,128)S(1)}, f32[3,13,13]{2,1,0:T(8,128)}, u32[]{:S(2)}) copy-start(f32[3,13,13]{2,1,0:T(8,128)} %star_ref.3) | copy-start | bytes 6088
  0.7 13.2 %copy-start.7 = (f32[3,56,56]{2,1,0:T(8,128)S(1)}, f32[3,56,56]{2,1,0:T(8,128)}, u32[]{:S(2)}) copy-start(f32[3,56,56]{2,1,0:T(8,128)} %stiff_ref.3) | copy-start | bytes 112900
  0.7 13.2 %copy-start.9 = (f32[3,3,256]{2,1,0:T(4,128)S(1)}, f32[3,3,256]{2,1,0:T(4,128)}, u32[]{:S(2)}) copy-start(f32[3,3,256]{2,1,0:T(4,128)} %jac_ref.3) | copy-start | bytes 27652
  8.1 5.8 %copy-start.5 = (f32[728,256]{1,0:T(8,128)S(1)}, f32[728,256]{1,0:T(8,128)}, u32[]{:S(2)}) copy-start(f32[728,256]{1,0:T(8,128)} %get-tuple-element.72.integral_ref) | copy-start | bytes 2236420
  8.1 7.6 %collective-permute-start = (f32[427,128]{1,0:T(8,128)}, f32[427,128]{1,0:T(8,128)S(1)}, u32[]{:S(2)}, u32[]{:S(2)}) collective-permute-start(f32[427,128]{1,0:T(8,128)} %get-tuple-element.70), channel_id=1, source_target_pairs={{0,8},{8,0},{16,24},{24,16},{1,9},{9,1},{17,25},{25,17},{2,10},{10... | collective-permute-start | bytes 655880 | tf_op jit(solution)/shard_map/ppermute | solution.py:898
  8.3 8.4 %collective-permute-start.1 = (f32[427,128]{1,0:T(8,128)}, f32[427,128]{1,0:T(8,128)S(1)}, u32[]{:S(2)}, u32[]{:S(2)}) collective-permute-start(f32[427,128]{1,0:T(8,128)} %get-tuple-element.71), channel_id=1, source_target_pairs={{8,16},{16,8},{0,0},{24,24},{9,17},{17,9},{1,1},{25,25},{10,18},{1... | collective-permute-start | bytes 655880 | tf_op jit(solution)/shard_map/ppermute | solution.py:898
  13.9 2.8 %copy-start.12 = (f32[137,128]{1,0:T(8,128)S(1)}, f32[137,128]{1,0:T(8,128)}, u32[]{:S(2)}) copy-start(f32[137,128]{1,0:T(8,128)} %get-tuple-element.76.refs_2_) | copy-start | bytes 210436
  13.9 2.8 %copy-start.13 = (f32[137,128]{1,0:T(8,128)S(1)}, f32[137,128]{1,0:T(8,128)}, u32[]{:S(2)}) copy-start(f32[137,128]{1,0:T(8,128)} %get-tuple-element.77.refs_3_) | copy-start | bytes 210436
  13.9 5.4 %copy-start.8 = (f32[3,56,56]{2,1,0:T(8,128)S(1)}, f32[3,56,56]{2,1,0:T(8,128)}, u32[]{:S(2)}) copy-start(f32[3,56,56]{2,1,0:T(8,128)} %refs_2_.6) | copy-start | bytes 112900
  13.9 5.4 %copy-start.10 = (f32[4,21,56]{2,0,1:T(4,128)S(1)}, f32[4,21,56]{2,0,1:T(4,128)}, u32[]{:S(2)}) copy-start(f32[4,21,56]{2,0,1:T(4,128)} %param.27) | copy-start | bytes 56452
  14.0 5.4 %copy-start.11 = (f32[4,3,256]{2,0,1:T(4,128)S(1)}, f32[4,3,256]{2,0,1:T(4,128)}, u32[]{:S(2)}) copy-start(f32[4,3,256]{2,0,1:T(4,128)} %param.21) | copy-start | bytes 36868
  14.0 5.4 %copy-start.14 = (f32[4,56,21]{1,0,2:T(4,128)S(1)}, f32[4,56,21]{1,0,2:T(4,128)}, u32[]{:S(2)}) copy-start(f32[4,56,21]{1,0,2:T(4,128)} %param.28) | copy-start | bytes 56452
  14.0 5.4 %copy-start.15 = (s32[4,256]{1,0:T(4,128)S(1)}, s32[4,256]{1,0:T(4,128)}, u32[]{:S(2)}) copy-start(s32[4,256]{1,0:T(4,128)} %partner_ref.3) | copy-start | bytes 12292
  14.0 5.4 %copy-start.16 = (f32[13,13]{1,0:T(8,128)S(1)}, f32[13,13]{1,0:T(8,128)}, u32[]{:S(2)}) copy-start(f32[13,13]{1,0:T(8,128)} %refs_1_.7) | copy-start | bytes 2032
  14.0 5.4 %copy-start.18 = (f32[256]{0:T(256)S(1)}, f32[256]{0:T(256)}, u32[]{:S(2)}) copy-start(f32[256]{0:T(256)} %param.22) | copy-start | bytes 3076
  14.0 5.4 %copy-start.19 = (f32[16,21]{1,0:T(8,128)S(1)}, f32[16,21]{1,0:T(8,128)}, u32[]{:S(2)}) copy-start(f32[16,21]{1,0:T(8,128)} %refs_10_.1) | copy-start | bytes 4036
  14.0 5.4 %copy-start.21 = (s32[256]{0:T(256)S(1)}, s32[256]{0:T(256)}, u32[]{:S(2)}) copy-start(s32[256]{0:T(256)} %param.31) | copy-start | bytes 3076
  14.0 5.4 %copy-start.22 = (s32[256,1]{0,1:T(1,128)S(1)}, s32[256,1]{0,1:T(1,128)}, u32[]{:S(2)}) copy-start(s32[256,1]{0,1:T(1,128)} %param.32) | copy-start | bytes 3076
  14.1 7.1 %copy-start.4 = (f32[312,1024]{1,0:T(8,128)S(1)}, f32[312,1024]{1,0:T(8,128)}, u32[]{:S(2)}) copy-start(f32[312,1024]{1,0:T(8,128)} %get-tuple-element.82.table_ref) | copy-start | bytes 3833860
  16.8 9.6 %collective-permute-start.2 = (f32[443,128]{1,0:T(8,128)S(1)}, f32[443,128]{1,0:T(8,128)S(1)}, u32[]{:S(2)}, u32[]{:S(2)}) collective-permute-start(f32[443,128]{1,0:T(8,128)S(1)} %get-tuple-element.80), channel_id=1, source_target_pairs={{0,1},{1,0},{2,3},{3,2},{4,5},{5,4},{6,7},{7,6},{8,9},{9,8},{10,11... | collective-permute-start | bytes 680456 | tf_op jit(solution)/shard_map/ppermute | solution.py:898
  18.5 7.9 %collective-permute-start.3 = (f32[443,128]{1,0:T(8,128)S(1)}, f32[443,128]{1,0:T(8,128)S(1)}, u32[]{:S(2)}, u32[]{:S(2)}) collective-permute-start(f32[443,128]{1,0:T(8,128)S(1)} %get-tuple-element.81), channel_id=1, source_target_pairs={{1,2},{2,1},{3,4},{4,3},{5,6},{6,5},{0,0},{7,7},{9,10},{10,9},{11,... | collective-permute-start | bytes 680456 | tf_op jit(solution)/shard_map/ppermute | solution.py:898
  26.4 2.1 %copy-start.17 = (s32[8,64]{1,0:T(8,128)S(1)}, s32[8,64]{1,0:T(8,128)}, u32[]{:S(2)}) copy-start(s32[8,64]{1,0:T(8,128)} %refs_6_.3) | copy-start | bytes 6148
  32.9 5.6 %collective-permute-start.4 = (f32[411,128]{1,0:T(8,128)S(1)}, f32[411,128]{1,0:T(8,128)S(1)}, u32[]{:S(2)}, u32[]{:S(2)}) collective-permute-start(f32[411,128]{1,0:T(8,128)S(1)} %get-tuple-element.105), channel_id=1, source_target_pairs={{0,8},{8,0},{16,24},{24,16},{1,9},{9,1},{17,25},{25,17},{2,10},{10... | collective-permute-start | bytes 631304 | tf_op jit(solution)/shard_map/ppermute | solution.py:898
  33.0 7.5 %collective-permute-start.5 = (f32[411,128]{1,0:T(8,128)S(1)}, f32[411,128]{1,0:T(8,128)S(1)}, u32[]{:S(2)}, u32[]{:S(2)}) collective-permute-start(f32[411,128]{1,0:T(8,128)S(1)} %get-tuple-element.106), channel_id=1, source_target_pairs={{8,16},{16,8},{0,0},{24,24},{9,17},{17,9},{1,1},{25,25},{10,18},{1... | collective-permute-start | bytes 631304 | tf_op jit(solution)/shard_map/ppermute | solution.py:898
  40.4 8.5 %collective-permute-start.6 = (f32[411,128]{1,0:T(8,128)S(1)}, f32[411,128]{1,0:T(8,128)S(1)}, u32[]{:S(2)}, u32[]{:S(2)}) collective-permute-start(f32[411,128]{1,0:T(8,128)S(1)} %get-tuple-element.116), channel_id=1, source_target_pairs={{0,1},{1,0},{2,3},{3,2},{4,5},{5,4},{6,7},{7,6},{8,9},{9,8},{10,11... | collective-permute-start | bytes 631304 | tf_op jit(solution)/shard_map/ppermute | solution.py:898
  42.5 6.5 %collective-permute-start.7 = (f32[411,128]{1,0:T(8,128)S(1)}, f32[411,128]{1,0:T(8,128)S(1)}, u32[]{:S(2)}, u32[]{:S(2)}) collective-permute-start(f32[411,128]{1,0:T(8,128)S(1)} %get-tuple-element.117), channel_id=1, source_target_pairs={{1,2},{2,1},{3,4},{4,3},{5,6},{6,5},{0,0},{7,7},{9,10},{10,9},{11,... | collective-permute-start | bytes 631304 | tf_op jit(solution)/shard_map/ppermute | solution.py:898
  46.1 2.9 %copy-start.20 = (s32[256,2]{0,1:T(2,128)S(1)}, s32[256,2]{0,1:T(2,128)}, u32[]{:S(2)}) copy-start(s32[256,2]{0,1:T(2,128)} %param.33) | copy-start | bytes 6148
  65.1 6.2 %collective-permute-start.8 = (f32[8,384]{1,0:T(8,128)S(1)}, f32[8,384]{1,0:T(8,128)S(1)}, u32[]{:S(2)}, u32[]{:S(2)}) collective-permute-start(f32[8,384]{1,0:T(8,128)S(1)} %get-tuple-element.131), channel_id=1, source_target_pairs={{0,8},{8,0},{16,24},{24,16},{1,9},{9,1},{17,25},{25,17},{2,10},{10... | collective-permute-start | bytes 36872 | tf_op jit(solution)/shard_map/ppermute | solution.py:898
  65.2 6.1 %collective-permute-start.9 = (f32[8,384]{1,0:T(8,128)S(1)}, f32[8,384]{1,0:T(8,128)S(1)}, u32[]{:S(2)}, u32[]{:S(2)}) collective-permute-start(f32[8,384]{1,0:T(8,128)S(1)} %get-tuple-element.132), channel_id=1, source_target_pairs={{8,16},{16,8},{24,0},{0,24},{9,17},{17,9},{25,1},{1,25},{10,18},{1... | collective-permute-start | bytes 36872 | tf_op jit(solution)/shard_map/ppermute | solution.py:898
